TPU v7x, 32 devices: a whole 2x2x4 slice. The times are simulated.
32 devices in a mesh: ctx: 8 (over y, x, core), pair: 4 (over z).
Axes of the slice: x: 2, y: 2, z: 4, core: 2. Of those that a mesh axis runs over, the one named last changes fastest.
Arguments:
- prompt_x: bfloat16 [2, 2048, 16384], P(None, 'ctx', 'pair'), may hold values from -6 to 6
- prompt_bc: bfloat16 [2, 2, 16, 2048], P(None, None, None, 'ctx'), may hold values from -3 to 3
- prompt_logdec: float32 [2, 256, 2048], P(None, 'pair', 'ctx'), may hold values from -2.5 to 0, as said below
- branch_x: bfloat16 [8, 512, 16384], P('pair', None, 'ctx'), may hold values from -6 to 6
- branch_bc: bfloat16 [2, 8, 16, 512], P(None, 'pair'), may hold values from -3 to 3
- branch_logdec: float32 [8, 256, 512], P('pair', 'ctx'), may hold values from -2.5 to 0, as said below
- branch_prompt: int32 [4], P('pair'), may hold values from 0 to 1
- branch_len: int32 [8], P('pair'), may hold values from 128 to 512, as said below
Outputs:
- prompt_y: bfloat16 [2, 2048, 16384], P(None, 'ctx', 'pair')
- branch_y: bfloat16 [8, 512, 16384], P('pair', None, 'ctx')
Inputs may be any that keep to these rules, and one draw needn't show every extreme that they name: `prompt_logdec`: the logarithm of a position's decay for each head. `branch_logdec`: the logarithm of a position's decay for each head. `branch_len`: positions of a branch at or after its length are masked; some branch has all 512 positions live.
All inputs are finite; a program needn't handle non-finite values.
Results may differ from a plain program's by a relative error of at most 0.0049.
Values sent between devices are 32-bit elements; how exact they have to be, the bound alone decides.
No kernel may reach another device: no remote copies, remote signals or barrier semaphores. Data moves between devices by JAX's collectives and lax.ppermute only.
A program may use at most 128 MiB of HBM per device.

v0:
```python
import jax
import jax.numpy as jnp
from jax import lax
from jax.sharding import PartitionSpec as P

BLOCK = 256


def entering(array, axis, combine, identity):
    size, mine = (lax.axis_size(axis), lax.axis_index(axis))
    everything = jax.tree.map(lambda part: lax.all_gather(part, axis), array)
    start = jax.tree.map(
        lambda part, zero: jnp.broadcast_to(jnp.asarray(zero, part.dtype), part.shape),
        array,
        identity,
    )

    def lap(k, before):
        reached = k < mine
        new = combine(before, jax.tree.map(lambda part: part[k], everything))
        return jax.tree.map(lambda a, b: jnp.where(reached, a, b), new, before)

    return lax.fori_loop(0, size, lap, start)


def from_root(value, axis, source):
    kept = jnp.where(lax.axis_index(axis) == source, value, 0).astype(value.dtype)
    return lax.psum(kept, axis)


def block_pass(inputs, log_decay, b_rows, c_rows, start_state):
    block_rows, channels = inputs.shape
    head_count = log_decay.shape[0]
    head_width = channels // head_count
    running = jnp.cumsum(log_decay, axis=1)
    in_gain = jnp.sqrt(-jnp.expm1(2.0 * log_decay))
    scores = jnp.dot(c_rows.T, b_rows, preferred_element_type=jnp.float32)
    row_ids = lax.broadcasted_iota(jnp.int32, (block_rows, block_rows), 0)
    col_ids = lax.broadcasted_iota(jnp.int32, (block_rows, block_rows), 1)
    causal = (col_ids <= row_ids)[None, :, :]
    to_end = jnp.exp(running[:, -1:] - running) * in_gain
    inject = (b_rows.astype(jnp.float32)[None, :, :] * to_end[:, None, :]).astype(jnp.bfloat16)
    by_head = inputs.reshape(block_rows, head_count, head_width)
    differ = jnp.where(causal, running[:, :, None] - running[:, None, :], 0.0)
    weights = jnp.where(causal, jnp.exp(differ), 0.0)
    weights = (scores[None, :, :] * weights * in_gain[:, None, :]).astype(jnp.bfloat16)
    inner_out = jnp.einsum(
        "hts,shp->thp", weights, by_head, preferred_element_type=jnp.float32
    ).reshape(block_rows, channels)
    states = jnp.einsum("hns,shp->hnp", inject, by_head, preferred_element_type=jnp.float32)
    projected = jnp.einsum(
        "nt,hnp->thp", c_rows.astype(jnp.float32), start_state, precision=lax.Precision.HIGHEST
    )
    carried = (projected * jnp.exp(running).T[:, :, None]).reshape(block_rows, channels)
    end_state = jnp.exp(running[:, -1])[:, None, None] * start_state + states
    return (inner_out + carried, end_state)


def run_blocks(inputs, log_decay, b_and_c, start_state):
    sequence_length, channels = inputs.shape
    head_count = log_decay.shape[0]
    state_size = b_and_c.shape[1]
    block_count = sequence_length // BLOCK
    input_blocks = inputs.reshape(block_count, BLOCK, channels)
    decay_blocks = jnp.transpose(log_decay.reshape(head_count, block_count, BLOCK), (1, 0, 2))
    proj_blocks = jnp.transpose(b_and_c.reshape(2, state_size, block_count, BLOCK), (2, 0, 1, 3))

    def advance(carry_state, pieces):
        block_in, block_decay, block_proj = pieces
        block_out, end_state = block_pass(
            block_in, block_decay, block_proj[0], block_proj[1], carry_state
        )
        return (end_state, block_out)

    end_state, outputs = lax.scan(advance, start_state, (input_blocks, decay_blocks, proj_blocks))
    return (outputs.reshape(sequence_length, channels), end_state)


def carried_term(c_rows, log_decay, start_state):
    running = jnp.cumsum(log_decay, axis=1)
    projected = jnp.einsum(
        "nt,hnp->thp", c_rows.astype(jnp.float32), start_state, precision=lax.Precision.HIGHEST
    )
    return (projected * jnp.exp(running).T[:, :, None]).reshape(c_rows.shape[1], -1)


def chain_step(earlier, later):
    return (earlier[0] + later[0], jnp.exp(later[0])[:, :, None, None] * earlier[1] + later[1])


def body(
    prompt_x,
    prompt_bc,
    prompt_logdec,
    branch_x,
    branch_bc,
    branch_logdec,
    branch_prompt,
    branch_len,
):
    prompts = prompt_x.shape[0]
    branches = branch_x.shape[0]
    heads_here = prompt_logdec.shape[1]
    branch_heads = branch_logdec.shape[1]
    state_size = prompt_bc.shape[2]
    head_width = prompt_x.shape[2] // heads_here
    zero_state = jnp.zeros((heads_here, state_size, head_width), jnp.float32)
    local_outs = []
    local_ends = []
    for prompt_id in range(prompts):
        result, end_state = run_blocks(
            prompt_x[prompt_id], prompt_logdec[prompt_id], prompt_bc[:, prompt_id], zero_state
        )
        local_outs.append(result)
        local_ends.append(end_state)
    local_ends = jnp.stack(local_ends)
    totals = jnp.sum(prompt_logdec, axis=2)
    identity = (jnp.zeros_like(totals), jnp.zeros_like(local_ends))
    before_log, before = entering((totals, local_ends), "ctx", chain_step, identity)
    prompt_y = jnp.stack(
        [
            (
                local_outs[prompt_id]
                + carried_term(prompt_bc[1, prompt_id], prompt_logdec[prompt_id], before[prompt_id])
            ).astype(jnp.bfloat16)
            for prompt_id in range(prompts)
        ]
    )
    ctx_pos = lax.axis_index("ctx")
    final_here = jnp.exp(totals)[:, :, None, None] * before + local_ends
    final_state = from_root(final_here, "ctx", lax.axis_size("ctx") - 1)
    owner_id = ctx_pos * branch_heads // heads_here
    offset = ctx_pos * branch_heads - owner_id * heads_here
    my_piece = lax.dynamic_slice_in_dim(final_state, offset, branch_heads, 1)
    my_states = from_root(my_piece, "pair", owner_id)
    token_positions = lax.broadcasted_iota(jnp.int32, (branch_x.shape[1], 1), 0)
    outputs = []
    for branch_id in range(branches):
        source = branch_prompt[branch_id // 2]
        picked = source == jnp.arange(prompts, dtype=jnp.int32)
        start_state = jnp.sum(jnp.where(picked[:, None, None, None], my_states, 0.0), axis=0)
        branch_out, unused_end = run_blocks(
            branch_x[branch_id], branch_logdec[branch_id], branch_bc[:, branch_id], start_state
        )
        outputs.append(
            jnp.where(token_positions < branch_len[branch_id], branch_out, 0.0).astype(jnp.bfloat16)
        )
    return (prompt_y, jnp.stack(outputs))


def solution(mesh):
    return jax.shard_map(
        body,
        mesh=mesh,
        in_specs=(
            P(None, "ctx", "pair"),
            P(None, None, None, "ctx"),
            P(None, "pair", "ctx"),
            P("pair", None, "ctx"),
            P(None, "pair", None, None),
            P("pair", "ctx", None),
            P("pair"),
            P("pair"),
        ),
        out_specs=(P(None, "ctx", "pair"), P("pair", None, "ctx")),
        check_vma=False,
    )
```

profile of v0, /device:TPU:0, one launch (start us, length us, event | category | flops | bytes accessed | tf_op | source)
XLA Modules:
  0.0 270.5 jit_solution(10154447396486060368)
XLA Ops:
  7.2 1.6 sqrt_bitcast_fusion.1
  11.1 1.6 exponential_multiply_fusion.3
  12.7 3.9 %fusion.108 = (bf16[1,256,4096]{2,1,0:T(8,128)(2,1)}, bf16[1,256,4096]{2,1,0:T(8,128)(2,1)S(1)}) fusion(bf16[2,256,4096]{2,1,0:T(8,128)(2,1)} %param.14), kind=kLoop, calls=%fused_computation.182 | loop fusion | bytes 8388608 | tf_op jit(solution)/shard_map/slice | solution.py:112
  16.7 2.5 copy.77
  19.2 3.3 %copy.74 = bf16[1,256,4096]{1,2,0:T(8,128)(2,1)S(1)} copy(bf16[1,256,4096]{2,1,0:T(8,128)(2,1)} %get-tuple-element.293) | data formatting | bytes 4194304 | tf_op jit(solution)/shard_map/slice | solution.py:112
  22.5 2.3 fusion.69
  24.7 0.7 fusion.70
  25.5 0.8 copy-done.3
  26.4 1.0 pad_maximum_fusion.2
  28.3 0.9 fusion.109
  29.2 0.8 fusion.110
  30.1 10.3 %all-gather.2 = f32[8,2,64]{2,1,0:T(2,128)S(1)} all-gather(f32[1,2,64]{2,1,0:T(2,128)S(1)} %bitcast.307), channel_id=2, replica_groups=mesh['ctx'=8,'pair'=4] {'ctx'}, dimensions={0}, use_global_device_ids=true | all-gather | bytes 4608 | tf_op jit(solution)/shard_map/all_gather | solution.py:11
  41.7 0.7 iota_compare_fusion.4
  43.0 0.9 fusion.87
  43.9 0.9 fusion.92
  44.8 3.8 %fusion.81 = f32[64,64,256]{2,1,0:T(8,128)} fusion(bf16[2,2,16,256]{3,2,1,0:T(8,128)(2,1)S(1)} %copy-done.10), kind=kOutput, calls=%fused_computation.133 | convolution fusion | flops 201326592 | bytes 4202496 | tf_op jit(solution)/shard_map/while/body/eval_jaxpr/nt,hnp->thp/dot_general | solution.py:51
  48.6 3.7 %fusion.83 = f32[64,64,256]{2,1,0:T(8,128)} fusion(bf16[2,2,16,256]{3,2,1,0:T(8,128)(2,1)S(1)} %copy-done.10), kind=kOutput, calls=%fused_computation.135 | convolution fusion | flops 201326592 | bytes 4202496 | tf_op jit(solution)/shard_map/while/body/eval_jaxpr/nt,hnp->thp/dot_general | solution.py:51
  52.3 2.5 fusion.107
  54.8 29.8 %all-gather.5.cloned.1.call-done = f32[16,64,16,64]{3,2,1,0:T(8,128)} async-done(((f32[2,64,16,64]{3,2,1,0:T(8,128)}), f32[16,64,16,64]{3,2,1,0:T(8,128)}) %all-gather.5.cloned.1.call-update) | async-done | bytes 4194320 | tf_op jit(solution)/shard_map/all_gather | solution.py:11
  84.7 13.2 %while.50 = (s32[]{:T(128)}, f32[2,64,16,64]{3,2,1,0:T(8,128)S(1)}, s32[]{:T(128)}, f32[8,2,64]{2,1,0:T(2,128)S(1)}, f32[8,2,64,16,64]{4,3,2,1,0:T(8,128)}, /*index=5*/s32[]{:T(128)}, s32[]{:T(128)}) while((s32[]{:T(128)}, f32[2,64,16,64]{3,2,1,0:T(8,128)S(1)}, s32[]{:T(128)}, f32[8,2,64]{2,1,0:T(2,128)S(1)}, ...), condition=%wide.region_6.7_spmd.clone, body=%wide.region_5.6_spmd.clone.sunk | while | flops 524292 | bytes 1574513 | solution.py:23
  84.7 1.6 fusion.159
  86.3 1.6 fusion.159
  88.0 1.6 fusion.159
  89.6 1.6 fusion.159
  91.3 1.6 fusion.159
  93.0 1.6 fusion.159
  94.6 1.6 fusion.159
  96.3 1.6 fusion.159
  97.9 3.9 %fusion.71 = f32[64,64,256]{2,1,0:T(8,128)} fusion(f32[2,64,16,64]{3,2,1,0:T(8,128)S(1)} %get-tuple-element.196, bf16[2,2,16,256]{3,2,1,0:T(8,128)(2,1)S(1)} %copy-done.10), kind=kOutput, calls=%fused_computation.121 | convolution fusion | flops 201326592 | bytes 4726784 | tf_op jit(solution)/shard_map/nt,hnp->thp/dot_general | solution.py:81
  101.8 3.8 %fusion.73 = f32[64,64,256]{2,1,0:T(8,128)} fusion(f32[2,64,16,64]{3,2,1,0:T(8,128)S(1)} %get-tuple-element.196, bf16[2,2,16,256]{3,2,1,0:T(8,128)(2,1)S(1)} %copy-done.10), kind=kOutput, calls=%fused_computation.123 | convolution fusion | flops 201326592 | bytes 4726784 | tf_op jit(solution)/shard_map/nt,hnp->thp/dot_general | solution.py:81
  105.6 1.2 add_select_fusion
  107.1 10.1 %fusion.64 = bf16[256,64,64]{0,2,1:T(8,128)(2,1)} fusion(f32[64,64,256]{2,1,0:T(8,128)} %fusion.71, f32[64,64,256]{2,1,0:T(8,128)} %fusion.81, bf16[256,64,64]{0,2,1:T(8,128)(2,1)} %bitcast.293, f32[64,256]{1,0:T(8,128)} %get-tuple-element.298, f32[64,256]{1,0:T(8,128)S(1)} %bitcast.304, f32[256,256]{1,0:T(8,128)} %fusion.87, ...), kind=kOutput, calls=%fused_computation.105 | convolution fusion | flops 567279616 | bytes 13107200 | tf_op jit(solution)/shard_map/while/body/eval_jaxpr/hts,shp->thp/dot_general | solution.py:47
  117.3 8.0 %fusion.67 = bf16[256,64,64]{0,2,1:T(8,128)(2,1)} fusion(f32[64,64,256]{2,1,0:T(8,128)S(1)} %copy-done.5, f32[64,64,256]{2,1,0:T(8,128)S(1)} %copy-done.7, bf16[256,64,64]{0,2,1:T(8,128)(2,1)S(1)} %bitcast.291, f32[64,256]{1,0:T(8,128)S(1)} %copy-done.14, f32[64,256]{1,0:T(8,128)S(1)} %bitcast.302, f32[256,256]{1,0:T(8,128)S(1)} %copy-done.9, ...), kind=kOutput, calls=%fused_computation.110 | convolution fusion | flops 567279616 | bytes 13107200 | tf_op jit(solution)/shard_map/while/body/eval_jaxpr/hts,shp->thp/dot_general | solution.py:47
  125.3 2.9 %copy.79 = bf16[1,256,4096]{2,1,0:T(8,128)(2,1)S(1)} copy(bf16[1,256,4096]{1,2,0:T(8,128)(2,1)} %bitcast.297) | data formatting | bytes 4194304 | tf_op jit(solution)/shard_map/convert_element_type | solution.py:125
  128.2 4.1 %copy.78 = bf16[1,256,4096]{2,1,0:T(8,128)(2,1)} copy(bf16[1,256,4096]{1,2,0:T(8,128)(2,1)} %bitcast.298) | data formatting | bytes 4194304 | tf_op jit(solution)/shard_map/convert_element_type | solution.py:125
  132.4 31.3 %all-reduce.3.cloned.1.call-done = f32[2,64,16,64]{3,2,1,0:T(8,128)} async-done(((f32[2,64,16,64]{3,2,1,0:T(8,128)}), f32[2,64,16,64]{3,2,1,0:T(8,128)}) %all-reduce.3.cloned.1.call-update) | async-done | bytes 524304 | tf_op jit(solution)/shard_map/psum | solution.py:28
  163.6 1.9 dynamic-slice_select_fusion
  165.5 4.0 %pad_maximum_fusion = bf16[2,256,4096]{2,1,0:T(8,128)(2,1)} fusion(bf16[1,256,4096]{2,1,0:T(8,128)(2,1)S(1)} %copy.79, bf16[1,256,4096]{2,1,0:T(8,128)(2,1)} %copy.78), kind=kLoop, calls=%fused_computation.97 | loop fusion | flops 2097152 | bytes 8388608 | tf_op jit(solution)/shard_map/stack | solution.py:120
  169.5 34.4 %all-reduce.5.cloned.1.call-done = f32[2,32,16,64]{3,2,1,0:T(8,128)} async-done(((f32[2,32,16,64]{3,2,1,0:T(8,128)}), f32[2,32,16,64]{3,2,1,0:T(8,128)}) %all-reduce.5.cloned.1.call-update) | async-done | bytes 262160 | tf_op jit(solution)/shard_map/psum | solution.py:28
  203.9 1.2 select_reduce_fusion
  205.1 1.6 broadcast.191.clone2
  206.7 25.3 %while.13 = (s32[]{:T(128)}, f32[32,16,64]{2,1,0:T(8,128)S(1)}, bf16[2,256,2048]{2,1,0:T(8,128)(2,1)}, f32[2,32,256]{2,0,1:T(2,128)S(1)}, bf16[2,2,16,256]{3,2,1...) while((s32[]{:T(128)}, f32[32,16,64]{2,1,0:T(8,128)S(1)}, ...), condition=%wide.region_17.18_spmd, body=%wide.region_14.17_spmd.sunk | while | flops 403632224 | bytes 17568280 | solution.py:75
  206.7 2.4 fusion.156
  209.1 1.3 constant_dynamic-slice_fusion.10
  212.9 4.8 %bitcast_add_fusion.6 = bf16[256,32,64]{0,2,1:T(8,128)(2,1)S(1)} fusion(f32[256,32,64]{0,2,1:T(8,128)} %fusion.156, bf16[256,32,64]{0,2,1:T(8,128)(2,1)S(1)} %bitcast.281, f32[32,256]{1,0:T(8,128)S(1)} %fusion.157, f32[32,256]{1,0:T(8,128)S(1)} %copy_bitcast_fusion.7, f32[256,256]{1,0:T(8,128)S(1)} %fusion.158, ...), kind=kOutput, calls=%fused_computation.50.clone.1 | convolution fusion | flops 282591232 | bytes 4620288 | tf_op jit(solution)/shard_map/while/body/eval_jaxpr/hts,shp->thp/dot_general | solution.py:47
  217.7 0.6 copy.173
  218.3 1.0 constant_dynamic-update-slice_fusion.5
  219.4 2.4 fusion.156
  221.8 1.3 constant_dynamic-slice_fusion.10
  225.6 4.8 %bitcast_add_fusion.6 = bf16[256,32,64]{0,2,1:T(8,128)(2,1)S(1)} fusion(f32[256,32,64]{0,2,1:T(8,128)} %fusion.156, bf16[256,32,64]{0,2,1:T(8,128)(2,1)S(1)} %bitcast.281, f32[32,256]{1,0:T(8,128)S(1)} %fusion.157, f32[32,256]{1,0:T(8,128)S(1)} %copy_bitcast_fusion.7, f32[256,256]{1,0:T(8,128)S(1)} %fusion.158, ...), kind=kOutput, calls=%fused_computation.50.clone.1 | convolution fusion | flops 282591232 | bytes 4620288 | tf_op jit(solution)/shard_map/while/body/eval_jaxpr/hts,shp->thp/dot_general | solution.py:47
  230.4 0.6 copy.173
  231.0 1.0 constant_dynamic-update-slice_fusion.5
  232.1 1.6 broadcast.191.clone2.1
  233.7 25.3 %while.12 = (s32[]{:T(128)}, f32[32,16,64]{2,1,0:T(8,128)S(1)}, bf16[2,256,2048]{2,1,0:T(8,128)(2,1)}, f32[2,32,256]{2,0,1:T(2,128)S(1)}, bf16[2,2,16,256]{3,2,1...) while((s32[]{:T(128)}, f32[32,16,64]{2,1,0:T(8,128)S(1)}, ...), condition=%wide.region_13.14_spmd, body=%wide.region_10.13_spmd.sunk | while | flops 403632224 | bytes 17568280 | solution.py:75
  233.7 2.3 fusion.147
  236.0 1.3 constant_dynamic-slice_fusion.8
  239.8 4.8 %bitcast_add_fusion.5 = bf16[256,32,64]{0,2,1:T(8,128)(2,1)S(1)} fusion(f32[256,32,64]{0,2,1:T(8,128)} %fusion.147, bf16[256,32,64]{0,2,1:T(8,128)(2,1)S(1)} %bitcast.283, f32[32,256]{1,0:T(8,128)S(1)} %fusion.148, f32[32,256]{1,0:T(8,128)S(1)} %copy_bitcast_fusion.6, f32[256,256]{1,0:T(8,128)S(1)} %fusion.149, ...), kind=kOutput, calls=%fused_computation.11.clone.1 | convolution fusion | flops 282591232 | bytes 4620288 | tf_op jit(solution)/shard_map/while/body/eval_jaxpr/hts,shp->thp/dot_general | solution.py:47
  245.2 1.1 constant_dynamic-update-slice_fusion.4
  246.3 2.3 fusion.147
  248.6 1.3 constant_dynamic-slice_fusion.8
  252.4 4.8 %bitcast_add_fusion.5 = bf16[256,32,64]{0,2,1:T(8,128)(2,1)S(1)} fusion(f32[256,32,64]{0,2,1:T(8,128)} %fusion.147, bf16[256,32,64]{0,2,1:T(8,128)(2,1)S(1)} %bitcast.283, f32[32,256]{1,0:T(8,128)S(1)} %fusion.148, f32[32,256]{1,0:T(8,128)S(1)} %copy_bitcast_fusion.6, f32[256,256]{1,0:T(8,128)S(1)} %fusion.149, ...), kind=kOutput, calls=%fused_computation.11.clone.1 | convolution fusion | flops 282591232 | bytes 4620288 | tf_op jit(solution)/shard_map/while/body/eval_jaxpr/hts,shp->thp/dot_general | solution.py:47
  257.9 1.1 constant_dynamic-update-slice_fusion.4
  259.0 2.2 fusion.61
  261.6 2.4 pad_maximum_fusion.1
  (148 shorter events, 16.3 us)
Async XLA Ops:
  7.2 77.5 %all-gather.5.cloned.1.call-start = ((), (), s32[]{:S(2)}) async-start(), calls=%async_computation.2 | async-start | bytes 9437184 | tf_op jit(solution)/shard_map/all_gather | solution.py:11
  10.9 1.8 copy-start.11
  16.7 2.5 copy-start.10
  22.4 5.1 %copy-start.8 = (f32[2,64,256]{2,1,0:T(8,128)S(1)}, f32[2,64,256]{2,1,0:T(8,128)}, u32[]{:S(2)}) copy-start(f32[2,64,256]{2,1,0:T(8,128)} %param.16) | copy-start | bytes 393220
  22.4 18.0 %copy-start.16 = (s32[2]{0:T(128)S(1)}, s32[2]{0:T(128)}, u32[]{:S(2)}) copy-start(s32[2]{0:T(128)} %param.21) | copy-start | bytes 28
  24.7 0.8 copy-start.1
  25.5 0.8 copy-start.3
  27.4 136.2 %all-reduce.3.cloned.1.call-start = ((), (), s32[]{:S(2)}) async-start(), calls=%async_computation | async-start | bytes 2097152 | tf_op jit(solution)/shard_map/psum | solution.py:28
  44.8 7.5 %copy-start.6 = (bf16[2,512,2048]{2,1,0:T(8,128)(2,1)S(1)}, bf16[2,512,2048]{2,1,0:T(8,128)(2,1)}, u32[]{:S(2)}) copy-start(bf16[2,512,2048]{2,1,0:T(8,128)(2,1)} %param.17) | copy-start | bytes 12582916
  97.9 7.7 %copy-start.2 = (f32[1,64,16,64]{3,2,1,0:T(8,128)S(1)}, f32[1,64,16,64]{3,2,1,0:T(8,128)}, u32[]{:S(2)}) copy-start(f32[1,64,16,64]{3,2,1,0:T(8,128)} %copy-done.1) | copy-start | bytes 786436
  97.9 7.7 %copy-start.4 = (f32[1,64,16,64]{3,2,1,0:T(8,128)S(1)}, f32[1,64,16,64]{3,2,1,0:T(8,128)}, u32[]{:S(2)}) copy-start(f32[1,64,16,64]{3,2,1,0:T(8,128)} %copy-done.3) | copy-start | bytes 786436
  101.8 5.3 %copy-start.12 = (f32[2,8,8,128]{3,2,0,1:T(8,128)S(1)}, f32[2,8,8,128]{3,2,0,1:T(8,128)}, u32[]{:S(2)}) copy-start(f32[2,8,8,128]{3,2,0,1:T(8,128)} %copy-done.11) | copy-start | bytes 196612
  106.8 97.1 %all-reduce.5.cloned.1.call-start = ((), (), s32[]{:S(2)}) async-start(), calls=%async_computation.1 | async-start | bytes 1048576 | tf_op jit(solution)/shard_map/psum | solution.py:28
  107.1 10.2 %copy-start.5 = (f32[64,64,256]{2,1,0:T(8,128)S(1)}, f32[64,64,256]{2,1,0:T(8,128)}, u32[]{:S(2)}) copy-start(f32[64,64,256]{2,1,0:T(8,128)} %fusion.73) | copy-start | bytes 12582916
  107.1 10.2 %copy-start.7 = (f32[64,64,256]{2,1,0:T(8,128)S(1)}, f32[64,64,256]{2,1,0:T(8,128)}, u32[]{:S(2)}) copy-start(f32[64,64,256]{2,1,0:T(8,128)} %fusion.83) | copy-start | bytes 12582916
  107.1 10.2 %copy-start.9 = (f32[256,256]{1,0:T(8,128)S(1)}, f32[256,256]{1,0:T(8,128)}, u32[]{:S(2)}) copy-start(f32[256,256]{1,0:T(8,128)} %fusion.92) | copy-start | bytes 786436
  107.1 10.2 %copy-start.13 = (pred[256,256]{1,0:T(8,128)(4,1)S(1)}, pred[256,256]{1,0:T(8,128)(4,1)}, u32[]{:S(2)}) copy-start(pred[256,256]{1,0:T(8,128)(4,1)} %iota_compare_fusion.2) | copy-start | bytes 196612
  107.1 10.2 %copy-start.14 = (f32[64,256]{1,0:T(8,128)S(1)}, f32[64,256]{1,0:T(8,128)}, u32[]{:S(2)}) copy-start(f32[64,256]{1,0:T(8,128)} %get-tuple-element.297) | copy-start | bytes 196612
  107.1 10.2 %copy-start.15 = (f32[256,64]{0,1:T(8,128)S(1)}, f32[256,64]{0,1:T(8,128)}, u32[]{:S(2)}) copy-start(f32[256,64]{0,1:T(8,128)} %get-tuple-element.306) | copy-start | bytes 196612
  259.0 2.2 copy-start
Sparse Core Ops, SparseCore 0:
  27.5 57.0 all-gather.4
  106.9 56.6 all-reduce.2
  166.6 37.3 all-reduce.4
where the time goes:
time: 272 us; the launch traced here: 271 us
  waiting for transfers between devices  95.6 us (35%)
  matrix products  69.2 us (25%)
  local copies, waits for them, and re-layouts  42.4 us (16%)
  other arithmetic  37.3 us (14%)
  between operations  14.8 us (5%)
  blocking collectives  10.3 us (4%)
    psum x2, waiting for transfers between devices, from_root(): return lax.psum(kept, axis)  65.7 us
    dot_general x6, matrix products, block_pass(): jnp.einsum('hts,shp->thp', weights, by_head, preferred_element_type=jnp.f...  37.3 us
    all_gather x1, waiting for transfers between devices, entering(): everything = jax.tree.map(lambda part: lax.all_gather(part, axis), array)  29.8 us
    dot_general x6, matrix products, block_pass(): jnp.einsum('nt,hnp->thp', c_rows.astype(jnp.float32), start_state, precis...  16.9 us
    select_n x8, other arithmetic, lap(): return jax.tree.map(lambda a, b: jnp.where(reached, a, b), new, before)  12.9 us
    all_gather x1, blocking collectives, entering(): everything = jax.tree.map(lambda part: lax.all_gather(part, axis), array)  10.3 us
    slice x3, local copies, waits for them, and re-layouts, body(): prompt_x[prompt_id]  9.68 us
    dot_general x2, matrix products, carried_term(): jnp.einsum('nt,hnp->thp', c_rows.astype(jnp.float32), start_state, precis...  7.64 us
  transfers between devices with their start and end apart: 3, of which 3 were waited for; matrix products, arithmetic and copies ran while one was open for 17% of the time, Pallas kernels for 0%

commit v1 on v0

v1 whole, which is shorter than its diff:
```python
import functools
import jax
import jax.numpy as jnp
from jax import lax
from jax.experimental import pallas as pl
from jax.experimental.pallas import tpu as pltpu
from jax.sharding import PartitionSpec as P

BLOCK = 256
CHUNK = 32
F32 = jnp.float32
BF16 = jnp.bfloat16
VMEM_LIMIT = 40 * 1024 * 1024


def iota(shape, dim):
    return lax.broadcasted_iota(jnp.int32, shape, dim)


def exact_dot(a, b):
    return jnp.dot(a, b, preferred_element_type=F32, precision=lax.Precision.HIGHEST)


def gain_of(log_decay):
    z = 2.0 * log_decay
    series = 1.0 + z * (1.0 / 9.0)
    for k in (8, 7, 6, 5, 4, 3, 2):
        series = 1.0 + z * (1.0 / k) * series
    small = -z * series
    large = 1.0 - jnp.exp(z)
    return jnp.sqrt(jnp.maximum(jnp.where(z > -0.5, small, large), 0.0))


def hi_lo(value):
    high = value.astype(BF16).astype(F32)
    return jnp.concatenate([high, value - high], axis=0)


def spread(heads, width, lanes, first_head):
    rows = lax.rem(iota((2 * heads, lanes), 0), heads)
    cols = iota((2 * heads, lanes), 1) // width
    return jnp.where(rows - cols == first_head, 1.0, 0.0).astype(BF16)


def ends_kernel(x_ref, ld_ref, b_ref, end_ref, log_ref, push_ref, *, heads, width, state):
    tile = pl.program_id(0)
    positions = ld_ref.shape[2]
    lanes = x_ref.shape[2]

    @pl.when(tile == 0)
    def _():
        logs = ld_ref[0]
        after = jnp.where(iota((positions, positions), 0) > iota((positions, positions), 1), 1.0, 0.0)
        to_end = jnp.exp(exact_dot(logs, after)) * gain_of(logs)
        b_rows = b_ref[0, 0].astype(F32)
        push = b_rows[None, :, :] * to_end[:, None, :]
        push_ref[...] = push.reshape(heads * state, positions).astype(BF16)

    group = 256 // width
    tile_heads = lanes // width
    for g in range(tile_heads // group):
        first = tile * tile_heads + g * group
        rows = pl.ds(pl.multiple_of(first * state, group * state), group * state)
        cols = pl.ds(g * 256, 256)
        both = jnp.dot(push_ref[rows, :], x_ref[0, :, cols], preferred_element_type=F32)
        both = both.reshape(group, state, 256)
        own = iota(both.shape, 0) == iota(both.shape, 2) // width
        end_ref[:, cols] = jnp.sum(jnp.where(own, both, 0.0), axis=0)
    totals = lax.dot_general(
        jnp.ones((8, positions), F32), ld_ref[0], (((1,), (1,)), ((), ())),
        preferred_element_type=F32, precision=lax.Precision.HIGHEST)
    pick = iota((heads, lanes), 0) == iota((heads, lanes), 1) // width + tile * tile_heads
    log_ref[...] = exact_dot(totals, jnp.where(pick, 1.0, 0.0))


def local_ends(x, logdec, bc, which):
    _, positions, channels = x.shape
    heads, state = logdec.shape[1], bc.shape[2]
    width = channels // heads
    lanes = min(1024, channels)
    kernel = functools.partial(ends_kernel, heads=heads, width=width, state=state)
    return pl.pallas_call(
        kernel,
        grid=(channels // lanes,),
        in_specs=[
            pl.BlockSpec((1, positions, lanes), lambda j: (which, 0, j)),
            pl.BlockSpec((1, heads, positions), lambda j: (which, 0, 0)),
            pl.BlockSpec((1, 1, state, positions), lambda j: (0, which, 0, 0)),
        ],
        out_specs=[
            pl.BlockSpec((state, lanes), lambda j: (0, j)),
            pl.BlockSpec((8, lanes), lambda j: (0, j)),
        ],
        out_shape=[
            jax.ShapeDtypeStruct((state, channels), F32),
            jax.ShapeDtypeStruct((8, channels), F32),
        ],
        scratch_shapes=[pltpu.VMEM((heads * state, positions), BF16)],
        compiler_params=pltpu.CompilerParams(vmem_limit_bytes=VMEM_LIMIT),
        cost_estimate=pl.CostEstimate(
            flops=2 * 64 * positions * channels, bytes_accessed=2 * positions * channels, transcendentals=0),
        name="local_ends",
    )(x, logdec, bc)


def prepare(logs, b_rows, c_rows, w_ref, l_ref, c_ref, state):
    size = logs.shape[1]
    chunks = size // CHUNK
    half = CHUNK // 2
    src, dst = iota((size, size), 0), iota((size, size), 1)
    middle = dst // CHUNK * CHUNK + half - 1
    plus = (src > middle) & (src <= dst)
    minus = (src > dst) & (src <= middle)
    offset = exact_dot(logs, jnp.where(plus, 1.0, jnp.where(minus, -1.0, 0.0)))
    row_scale = hi_lo(jnp.exp(offset))
    in_scale = hi_lo(jnp.exp(-offset) * gain_of(logs))
    span = iota((size, 128), 1) == (iota((size, 128), 0) + half) // CHUNK
    steps = hi_lo(jnp.exp(exact_dot(logs, jnp.where(span, 1.0, 0.0))))
    w_ref[pl.ds(0, size), :] = in_scale.T.astype(BF16)
    w_ref[pl.ds(size, size), :] = row_scale.T.astype(BF16)
    w_ref[pl.ds(2 * size, 16), :] = steps.T[:16].astype(BF16)

    scores = lax.dot_general(c_rows, b_rows, (((0,), (0,)), ((), ())), preferred_element_type=F32)
    keep = (dst <= src) & (dst // CHUNK == src // CHUNK)
    l_ref[pl.ds(0, size), :] = jnp.where(keep, scores, 0.0).astype(BF16)
    rows = state * chunks
    mine = iota((rows, size), 0) // state == iota((rows, size), 1) // CHUNK
    b_all = jnp.concatenate([b_rows.astype(F32)] * chunks, axis=0)
    l_ref[pl.ds(size, rows), :] = jnp.where(mine, b_all, 0.0).astype(BF16)
    c_all = jnp.concatenate([c_rows.astype(F32)] * chunks, axis=0)
    c_ref[...] = jnp.where(mine, c_all, 0.0).T.astype(BF16)


def layer_kernel(*refs, heads, width, state, has_start, with_reach):
    x_ref, ld_ref, bc_ref = refs[:3]
    refs = refs[3:]
    if has_start:
        start_ref, refs = refs[0], refs[1:]
    y_ref, refs = refs[0], refs[1:]
    if with_reach:
        reach_ref, refs = refs[0], refs[1:]
        before_ref, refs = refs[-1], refs[:-1]
    w_ref, l_ref, c_ref, s_ref = refs
    block, tile = pl.program_id(1), pl.program_id(2)
    size, lanes = x_ref.shape[1], x_ref.shape[2]
    chunks = size // CHUNK
    tile_heads = lanes // width

    @pl.when(tile == 0)
    def _():
        logs = ld_ref[0]
        c_rows = bc_ref[1, 0]
        prepare(logs, bc_ref[0, 0], c_rows, w_ref, l_ref, c_ref, state)
        if with_reach:
            upto = jnp.where(iota((size, size), 0) <= iota((size, size), 1), 1.0, 0.0)
            run = exact_dot(logs, upto)
            entered = jnp.where(block == 0, 0.0, before_ref[:, 0:1])
            run = run + entered
            before_ref[...] = jnp.broadcast_to(run[:, size - 1:size], before_ref.shape)
            reach = c_rows.astype(F32)[None, :, :] * jnp.exp(run)[:, None, :]
            reach_ref[0] = reach.reshape(heads * state, size).T.astype(BF16)

    for g in range(lanes // 256):
        cols = pl.ds(g * 256, 256)
        here = pl.ds(pl.multiple_of(tile * lanes + g * 256, 256), 256)
        one_hot = spread(heads, width, 256, tile * tile_heads + g * (256 // width))
        scales = jnp.dot(w_ref[...], one_hot, preferred_element_type=F32)
        scaled = (x_ref[0, :, cols].astype(F32) * scales[:size]).astype(BF16)
        both = jnp.dot(l_ref[...], scaled, preferred_element_type=F32)
        if has_start:
            first = start_ref[0, :, cols]
        else:
            first = jnp.zeros((state, 256), F32)
        entering = jnp.where(block == 0, first, s_ref[:, here])
        carry = scales[2 * size:2 * size + 1] * entering
        carries = []
        for c in range(chunks):
            carries.append(carry.astype(BF16))
            local = both[size + c * state:size + (c + 1) * state]
            carry = scales[2 * size + c + 1:2 * size + c + 2] * (carry + local)
        s_ref[:, here] = carry
        carried = jnp.dot(c_ref[...], jnp.concatenate(carries, axis=0), preferred_element_type=F32)
        out = (both[:size] + carried) * scales[size:2 * size]
        y_ref[0, :, cols] = out.astype(y_ref.dtype)


def layer(x, logdec, bc, start, out_type, with_reach, name):
    count, positions, channels = x.shape
    heads, state = logdec.shape[1], bc.shape[2]
    width = channels // heads
    lanes = min(1024, channels)
    blocks = positions // BLOCK
    chunks = BLOCK // CHUNK
    kernel = functools.partial(
        layer_kernel, heads=heads, width=width, state=state,
        has_start=start is not None, with_reach=with_reach)
    in_specs = [
        pl.BlockSpec((1, BLOCK, lanes), lambda i, b, j: (i, b, j)),
        pl.BlockSpec((1, heads, BLOCK), lambda i, b, j: (i, 0, b)),
        pl.BlockSpec((2, 1, state, BLOCK), lambda i, b, j: (0, i, 0, b)),
    ]
    args = [x, logdec, bc]
    if start is not None:
        in_specs.append(pl.BlockSpec((1, state, lanes), lambda i, b, j: (i, 0, j)))
        args.append(start)
    out_specs = [pl.BlockSpec((1, BLOCK, lanes), lambda i, b, j: (i, b, j))]
    out_shape = [jax.ShapeDtypeStruct(x.shape, out_type)]
    scratch = [
        pltpu.VMEM((2 * BLOCK + 16, 2 * heads), BF16),
        pltpu.VMEM((BLOCK + chunks * state, BLOCK), BF16),
        pltpu.VMEM((BLOCK, chunks * state), BF16),
        pltpu.VMEM((state, channels), F32),
    ]
    if with_reach:
        out_specs.append(pl.BlockSpec((1, BLOCK, heads * state), lambda i, b, j: (i, b, 0)))
        out_shape.append(jax.ShapeDtypeStruct((count, positions, heads * state), BF16))
        scratch.append(pltpu.VMEM((heads, 128), F32))
    return pl.pallas_call(
        kernel,
        grid=(count, blocks, channels // lanes),
        in_specs=in_specs,
        out_specs=out_specs,
        out_shape=out_shape,
        scratch_shapes=scratch,
        compiler_params=pltpu.CompilerParams(vmem_limit_bytes=VMEM_LIMIT),
        cost_estimate=pl.CostEstimate(
            flops=2 * 1152 * x.size, bytes_accessed=4 * x.size, transcendentals=0),
        name=name,
    )(*args)


def finish_kernel(len_ref, own_ref, reach_ref, start_ref, y_ref, *, width, state):
    branch = pl.program_id(0)
    tile = pl.program_id(1)
    positions, lanes = own_ref.shape[1], own_ref.shape[2]
    group = 128 // state
    span = group * width
    live = iota((positions, 1), 0) < len_ref[branch]
    own_head = iota((group * state, span), 0) // state == iota((group * state, span), 1) // width
    for g in range(lanes // span):
        cols = pl.ds(g * span, span)
        first = (tile * (lanes // span) + g) * 128
        start = jnp.concatenate([start_ref[:, cols]] * group, axis=0)
        start = jnp.where(own_head, start, 0.0).astype(BF16)
        term = jnp.dot(reach_ref[0, :, pl.ds(pl.multiple_of(first, 128), 128)], start, preferred_element_type=F32)
        out = own_ref[0, :, cols].astype(F32) + term
        y_ref[0, :, cols] = jnp.where(live, out, 0.0).astype(BF16)


def finish(lengths, own, reach, start):
    count, positions, channels = own.shape
    state = start.shape[0]
    width = channels * state // reach.shape[2]
    lanes = min(1024, channels)
    return pl.pallas_call(
        functools.partial(finish_kernel, width=width, state=state),
        grid=(count, channels // lanes),
        in_specs=[
            pl.BlockSpec(memory_space=pltpu.SMEM),
            pl.BlockSpec((1, positions, lanes), lambda i, j: (i, 0, j)),
            pl.BlockSpec((1, positions, reach.shape[2]), lambda i, j: (i, 0, 0)),
            pl.BlockSpec((state, lanes), lambda i, j: (0, j)),
        ],
        out_specs=pl.BlockSpec((1, positions, lanes), lambda i, j: (i, 0, j)),
        out_shape=jax.ShapeDtypeStruct(own.shape, BF16),
        compiler_params=pltpu.CompilerParams(vmem_limit_bytes=VMEM_LIMIT),
        cost_estimate=pl.CostEstimate(
            flops=2 * 128 * own.size, bytes_accessed=6 * own.size, transcendentals=0),
        name="branch_finish",
    )(lengths, own, reach, start)


def swap_bit(value, bit, size):
    return lax.ppermute(value, "ctx", [(k, k ^ bit) for k in range(size)])


def prefix_and_total(end, log, size):
    mine = lax.axis_index("ctx")
    odd = (mine & 1) == 1
    width = end.shape[1] // 2
    log = log[:1]

    def halves(a):
        return a[:, :width], a[:, width:]

    low, high = halves(end)
    log_low, log_high = halves(log)
    got = swap_bit(jnp.where(odd, low, high), 1, size)
    got_log = swap_bit(jnp.where(odd, log_low, log_high), 1, size)
    keep, keep_log = jnp.where(odd, high, low), jnp.where(odd, log_high, log_low)
    first = jnp.where(odd, got, keep)
    first_log = jnp.where(odd, got_log, keep_log)
    second = jnp.where(odd, keep, got)
    second_log = jnp.where(odd, keep_log, got_log)
    total = jnp.exp(second_log) * first + second
    total_log = first_log + second_log
    before = jnp.zeros_like(total)
    before_log = jnp.zeros_like(total_log)
    bit = 2
    while bit < size:
        upper = (mine & bit) != 0
        other = swap_bit(total, bit, size)
        other_log = swap_bit(total_log, bit, size)
        before = jnp.where(upper, jnp.exp(before_log) * other + before, before)
        before_log = jnp.where(upper, before_log + other_log, before_log)
        total = jnp.where(
            upper, jnp.exp(total_log) * other + total, jnp.exp(other_log) * total + other)
        total_log = total_log + other_log
        bit *= 2
    next_before = jnp.exp(first_log) * before + first
    got = swap_bit(jnp.where(odd, before, next_before), 1, size)
    keep = jnp.where(odd, next_before, before)
    entering = jnp.concatenate([jnp.where(odd, got, keep), jnp.where(odd, keep, got)], axis=1)
    return entering, total


def branch_start(totals, chosen, ctx_size, pair_size):
    ctx, pair = lax.axis_index("ctx"), lax.axis_index("pair")
    owner = ctx * pair_size // ctx_size

    def shift(value, hop, back):
        links = []
        for k in range(ctx_size):
            z = k * pair_size // ctx_size
            ends = (k * pair_size + z, k * pair_size + (z + hop) % pair_size)
            links.append(ends[::-1] if back else ends)
        return lax.ppermute(value, ("ctx", "pair"), links)

    def pick(which):
        out = totals[0]
        for i in range(1, len(totals)):
            out = jnp.where(which == i, totals[i], out)
        return out

    start = jnp.where(pair == owner, pick(chosen[0]), 0.0)
    for hop in range(1, pair_size):
        wanted = shift(chosen, hop, True)[0]
        start = start + shift(pick(wanted), hop, False)
    return start


def body(
    prompt_x,
    prompt_bc,
    prompt_logdec,
    branch_x,
    branch_bc,
    branch_logdec,
    branch_prompt,
    branch_len,
):
    ctx_size, pair_size = lax.axis_size("ctx"), lax.axis_size("pair")
    entering, totals = [], []
    for which in range(prompt_x.shape[0]):
        end, log = local_ends(prompt_x, prompt_logdec, prompt_bc, which)
        before, total = prefix_and_total(end, log, ctx_size)
        entering.append(before)
        totals.append(total)
    own, reach = layer(branch_x, branch_logdec, branch_bc, None, F32, True, "branch_own")
    (prompt_y,) = layer(prompt_x, prompt_logdec, prompt_bc, jnp.stack(entering), BF16, False, "prompt_layer")
    start = branch_start(totals, branch_prompt, ctx_size, pair_size)
    branch_y = finish(branch_len, own, reach, start)
    return prompt_y, branch_y


def solution(mesh):
    return jax.shard_map(
        body,
        mesh=mesh,
        in_specs=(
            P(None, "ctx", "pair"),
            P(None, None, None, "ctx"),
            P(None, "pair", "ctx"),
            P("pair", None, "ctx"),
            P(None, "pair", None, None),
            P("pair", "ctx", None),
            P("pair"),
            P("pair"),
        ),
        out_specs=(P(None, "ctx", "pair"), P("pair", None, "ctx")),
        check_vma=False,
    )
```

time: 272 us -> 94.3 us (0.35)
  waiting for transfers between devices: 95.6 us -> 13.7 us
  matrix products: 69.2 us -> 0 us
  Pallas kernels: 0 us -> 39.8 us
  other arithmetic: 37.3 us -> 0.81 us
  local copies, waits for them, and re-layouts: 42.4 us -> 9.37 us
  starting transfers between devices: 0.3 us -> 26.8 us
  between operations: 14.8 us -> 3.49 us
  blocking collectives: 10.3 us -> 0 us
    dot_general x26 -> x0, matrix products: 69.2 us -> none  [the longest x6 37.3 us: block_pass(): jnp.einsum('hts,shp->thp', weights, by_head, preferred_element_type=jnp.f...]
    psum x2 -> x0, waiting for transfers between devices: 65.7 us -> none  [from_root(): return lax.psum(kept, axis)]
    pallas_call x0 -> x5, Pallas kernels: none -> 39.8 us  [the longest x2 30.1 us: layer(): pl.pallas_call(kernel, grid=(count, blocks, channels // lanes), in_specs=...]
    all_gather x1 -> x0, waiting for transfers between devices: 29.8 us -> none  [entering(): everything = jax.tree.map(lambda part: lax.all_gather(part, axis), array)]
    ppermute x0 -> x20, starting transfers between devices: none -> 26.8 us  [the longest x14 16.2 us: swap_bit(): return lax.ppermute(value, 'ctx', [(k, k ^ bit) for k in range(size)])]
    slice x13 -> x0, local copies, waits for them, and re-layouts: 15.5 us -> none  [the longest x3 9.68 us: body(): prompt_x[prompt_id]]
    select_n x10 -> x13, other arithmetic: 16 us -> 0.49 us  [the longest x2 0.15 us: pick(): out = jnp.where(which == i, totals[i], out)]
    ppermute x0 -> x20, waiting for transfers between devices: none -> 13.7 us  [the longest x14 8.78 us: swap_bit(): return lax.ppermute(value, 'ctx', [(k, k ^ bit) for k in range(size)])]
  transfers between devices with their start and end apart: 3 -> 20, of which waited for: 3 -> 6; matrix products, arithmetic and copies ran while one was open for 17% -> 1% of each run, Pallas kernels for 0% -> 38%
where the time goes in v1:
time: 94.3 us; the launch traced here: 93.9 us
  Pallas kernels  39.8 us (42%)
  starting transfers between devices  26.8 us (28%)
  waiting for transfers between devices  13.7 us (15%)
  local copies, waits for them, and re-layouts  9.37 us (10%)
  between operations  3.49 us (4%)
    pallas_call x2, Pallas kernels, layer(): pl.pallas_call(kernel, grid=(count, blocks, channels // lanes), in_specs=...  30.1 us
    ppermute x14, starting transfers between devices, swap_bit(): return lax.ppermute(value, 'ctx', [(k, k ^ bit) for k in range(size)])  16.2 us
    ppermute x6, starting transfers between devices, shift(): return lax.ppermute(value, ('ctx', 'pair'), links)  10.5 us
    unnamed x26, local copies, waits for them, and re-layouts  9.34 us
    ppermute x14, waiting for transfers between devices, swap_bit(): return lax.ppermute(value, 'ctx', [(k, k ^ bit) for k in range(size)])  8.78 us
    pallas_call x2, Pallas kernels, local_ends(): pl.pallas_call(kernel, grid=(channels // lanes,), in_specs=[pl.BlockSpec(...  5.57 us
    ppermute x6, waiting for transfers between devices, shift(): return lax.ppermute(value, ('ctx', 'pair'), links)  4.93 us
    pallas_call x1, Pallas kernels, finish(): pl.pallas_call(functools.partial(finish_kernel, width=width, state=state)...  4.15 us
  transfers between devices with their start and end apart: 20, of which 6 were waited for; matrix products, arithmetic and copies ran while one was open for 1% of the time, Pallas kernels for 38%

profile of v1, /device:TPU:0, one launch (start us, length us, event | category | flops | bytes accessed | tf_op | source)
XLA Modules:
  0.0 93.9 jit_solution(14775826642911963677)
XLA Ops:
  0.6 1.3 %collective-permute-start.14 = (s32[1]{0:T(128)}, s32[1]{0:T(128)}, u32[]{:S(2)}, u32[]{:S(2)}) collective-permute-start(s32[1]{0:T(128)} %param.14), channel_id=1, source_target_pairs={{1,0},{5,4},{10,9},{14,13},{19,18},{23,22},{24,27},{28,31}} | collective-permute-start | bytes 20 | tf_op jit(solution)/shard_map/ppermute | solution.py:327
  1.9 1.3 %collective-permute-start.16 = (s32[1]{0:T(128)}, s32[1]{0:T(128)}, u32[]{:S(2)}, u32[]{:S(2)}) collective-permute-start(s32[1]{0:T(128)} %param.14), channel_id=1, source_target_pairs={{2,0},{6,4},{11,9},{15,13},{16,18},{20,22},{25,27},{29,31}} | collective-permute-start | bytes 20 | tf_op jit(solution)/shard_map/ppermute | solution.py:327
  3.2 0.0 copy-start
  3.2 2.2 %copy-done = bf16[2,256,4096]{2,1,0:T(8,128)(2,1)S(1)} copy-done((bf16[2,256,4096]{2,1,0:T(8,128)(2,1)S(1)}, bf16[2,256,4096]{2,1,0:T(8,128)(2,1)}, u32[]{:S(2)}) %copy-start) | copy-done | bytes 4194328
  5.4 0.9 copy-done.3
  6.3 0.8 copy-done.5
  7.1 2.8 %local_ends.3 = (f32[16,4096]{1,0:T(8,128)S(1)}, f32[8,4096]{1,0:T(8,128)S(1)}) custom-call(bf16[2,256,4096]{2,1,0:T(8,128)(2,1)S(1)} %copy-done, f32[2,64,256]{2,1,0:T(8,128)S(1)} %copy-done.3, bf16[2,2,16,256]{3,2,1,0:T(8,128)(2,1)S(1)} %copy-done.5), custom_call_target="tpu_custom_call" | custom-call | flops 134217728 | bytes 2097152 | tf_op jit(solution)/shard_map/local_ends/pallas_call | solution.py:82
  9.9 0.5 collective-permute-start.6
  10.4 0.1 collective-permute-start.8
  10.6 2.8 %local_ends.2 = (f32[16,4096]{1,0:T(8,128)S(1)}, f32[8,4096]{1,0:T(8,128)S(1)}) custom-call(bf16[2,256,4096]{2,1,0:T(8,128)(2,1)S(1)} %copy-done, f32[2,64,256]{2,1,0:T(8,128)S(1)} %copy-done.3, bf16[2,2,16,256]{3,2,1,0:T(8,128)(2,1)S(1)} %copy-done.5), custom_call_target="tpu_custom_call" | custom-call | flops 134217728 | bytes 2097152 | tf_op jit(solution)/shard_map/local_ends/pallas_call | solution.py:82
  13.4 0.5 collective-permute-start
  13.9 0.0 collective-permute-done.6
  14.0 2.3 %collective-permute-start.7 = (f32[1,2048]{1,0:T(1,128)S(1)}, f32[1,2048]{1,0:T(1,128)S(1)}, u32[]{:S(2)}, u32[]{:S(2)}) collective-permute-start(f32[1,2048]{1,0:T(1,128)S(1)} %get-tuple-element.28), channel_id=1, source_target_pairs={{0,8},{4,12},{8,0},{12,4},{16,24},{20,28},{24,16},{28,20},{1,9},{5... | collective-permute-start | bytes 24584 | tf_op jit(solution)/shard_map/ppermute | solution.py:274
  16.2 0.0 collective-permute-done
  16.3 1.1 %collective-permute-start.1 = (f32[1,2048]{1,0:T(1,128)S(1)}, f32[1,2048]{1,0:T(1,128)S(1)}, u32[]{:S(2)}, u32[]{:S(2)}) collective-permute-start(f32[1,2048]{1,0:T(1,128)S(1)} %get-tuple-element.24), channel_id=1, source_target_pairs={{0,8},{4,12},{8,0},{12,4},{16,24},{20,28},{24,16},{28,20},{1,9},{5... | collective-permute-start | bytes 24584 | tf_op jit(solution)/shard_map/ppermute | solution.py:274
  17.4 0.5 collective-permute-done.7
  17.9 6.4 %collective-permute-start.12 = (f32[1,2048]{1,0:T(1,128)S(1)}, f32[1,2048]{1,0:T(1,128)S(1)}, u32[]{:S(2)}, u32[]{:S(2)}) collective-permute-start(f32[1,2048]{1,0:T(1,128)S(1)} %get-tuple-element.20), channel_id=1, source_target_pairs={{0,16},{4,20},{8,24},{12,28},{16,0},{20,4},{24,8},{28,12},{1,17},{... | collective-permute-start | bytes 24584 | tf_op jit(solution)/shard_map/ppermute | solution.py:274
  24.3 0.0 collective-permute-done.1
  24.4 2.1 %collective-permute-start.13 = (f32[1,2048]{1,0:T(1,128)S(1)}, f32[1,2048]{1,0:T(1,128)S(1)}, u32[]{:S(2)}, u32[]{:S(2)}) collective-permute-start(f32[1,2048]{1,0:T(1,128)S(1)} %get-tuple-element.18), channel_id=1, source_target_pairs={{0,16},{4,20},{8,24},{12,28},{16,0},{20,4},{24,8},{28,12},{1,17},{... | collective-permute-start | bytes 24584 | tf_op jit(solution)/shard_map/ppermute | solution.py:274
  26.5 0.0 copy-done.9
  26.5 0.0 copy-done.10
  26.5 2.2 %copy-done.8 = bf16[2,512,2048]{2,1,0:T(8,128)(2,1)S(1)} copy-done((bf16[2,512,2048]{2,1,0:T(8,128)(2,1)S(1)}, bf16[2,512,2048]{2,1,0:T(8,128)(2,1)}, u32[]{:S(2)}) %copy-start.8) | copy-done | bytes 4194328
  28.7 15.6 %branch_own.1 = (f32[2,512,2048]{2,1,0:T(8,128)S(1)}, bf16[2,512,512]{2,1,0:T(8,128)(2,1)S(1)}) custom-call(bf16[2,512,2048]{2,1,0:T(8,128)(2,1)S(1)} %copy-done.8, f32[2,32,512]{2,1,0:T(8,128)S(1)} %copy-done.9, bf16[2,2,16,512]{3,2,1,0:T(8,128)(2,1)S(1)} %copy-done.10), custom_call_target="tpu_custom_call" | custom-call | flops 4831838208 | bytes 8388608 | tf_op jit(solution)/shard_map/branch_own/pallas_call | solution.py:218
  44.3 0.0 copy-start.2
  44.3 3.3 %copy-done.2 = f32[2,512,2048]{2,1,0:T(8,128)} copy-done((f32[2,512,2048]{2,1,0:T(8,128)}, f32[2,512,2048]{2,1,0:T(8,128)S(1)}, u32[]{:S(2)}) %copy-start.2) | copy-done | bytes 8388632
  48.3 0.0 collective-permute-done.14
  48.3 1.3 %collective-permute-start.18 = (s32[1]{0:T(128)}, s32[1]{0:T(128)}, u32[]{:S(2)}, u32[]{:S(2)}) collective-permute-start(s32[1]{0:T(128)} %param.14), channel_id=1, source_target_pairs={{3,0},{7,4},{8,9},{12,13},{17,18},{21,22},{26,27},{30,31}} | collective-permute-start | bytes 20 | tf_op jit(solution)/shard_map/ppermute | solution.py:327
  50.1 0.0 collective-permute-done.16
  50.1 0.1 collective-permute-start.2
  50.8 4.9 %collective-permute-done.18 = s32[1]{0:T(128)} collective-permute-done((s32[1]{0:T(128)}, s32[1]{0:T(128)}, u32[]{:S(2)}, u32[]{:S(2)}) %collective-permute-start.18) | collective-permute-done | bytes 36 | tf_op jit(solution)/shard_map/ppermute | solution.py:327
  56.3 0.0 collective-permute-done.12
  56.4 0.0 collective-permute-done.13
  56.4 0.0 collective-permute-done.8
  56.4 0.1 collective-permute-start.9
  56.5 0.0 collective-permute-done.2
  56.6 2.1 %collective-permute-start.3 = (f32[16,2048]{1,0:T(8,128)S(1)}, f32[16,2048]{1,0:T(8,128)S(1)}, u32[]{:S(2)}, u32[]{:S(2)}) collective-permute-start(f32[16,2048]{1,0:T(8,128)S(1)} %select_add_fusion.1), channel_id=1, source_target_pairs={{0,8},{4,12},{8,0},{12,4},{16,24},{20,28},{24,16},{28,20},{1,9},{5... | collective-permute-start | bytes 393224 | tf_op jit(solution)/shard_map/ppermute | solution.py:274
  58.6 2.8 %collective-permute-done.9 = f32[16,2048]{1,0:T(8,128)S(1)} collective-permute-done((f32[16,2048]{1,0:T(8,128)S(1)}, f32[16,2048]{1,0:T(8,128)S(1)}, u32[]{:S(2)}, u32[]{:S(2)}) %collective-permute-start.9) | collective-permute-done | bytes 131104 | tf_op jit(solution)/shard_map/ppermute | solution.py:274
  61.5 0.1 collective-permute-start.10
  61.6 1.3 %collective-permute-done.3 = f32[16,2048]{1,0:T(8,128)S(1)} collective-permute-done((f32[16,2048]{1,0:T(8,128)S(1)}, f32[16,2048]{1,0:T(8,128)S(1)}, u32[]{:S(2)}, u32[]{:S(2)}) %collective-permute-start.3) | collective-permute-done | bytes 131104 | tf_op jit(solution)/shard_map/ppermute | solution.py:274
  62.9 0.8 collective-permute-start.4
  63.7 2.8 %collective-permute-done.10 = f32[16,2048]{1,0:T(8,128)S(1)} collective-permute-done((f32[16,2048]{1,0:T(8,128)S(1)}, f32[16,2048]{1,0:T(8,128)S(1)}, u32[]{:S(2)}, u32[]{:S(2)}) %collective-permute-start.10) | collective-permute-done | bytes 131104 | tf_op jit(solution)/shard_map/ppermute | solution.py:274
  66.5 0.1 fusion.1
  66.6 0.1 collective-permute-start.11
  66.7 1.3 %collective-permute-done.4 = f32[16,2048]{1,0:T(8,128)S(1)} collective-permute-done((f32[16,2048]{1,0:T(8,128)S(1)}, f32[16,2048]{1,0:T(8,128)S(1)}, u32[]{:S(2)}, u32[]{:S(2)}) %collective-permute-start.4) | collective-permute-done | bytes 131104 | tf_op jit(solution)/shard_map/ppermute | solution.py:274
  67.9 0.1 fusion.3
  68.0 0.1 collective-permute-start.5
  68.1 0.0 collective-permute-done.11
  68.1 0.1 broadcast_select_fusion.2
  68.3 1.3 %collective-permute-start.17 = (f32[16,2048]{1,0:T(8,128)S(1)}, f32[16,2048]{1,0:T(8,128)S(1)}, u32[]{:S(2)}, u32[]{:S(2)}) collective-permute-start(f32[16,2048]{1,0:T(8,128)S(1)} %get-tuple-element.29), channel_id=1, source_target_pairs={{0,2},{4,6},{9,11},{13,15},{18,16},{22,20},{27,25},{31,29}} | collective-permute-start | bytes 393224 | tf_op jit(solution)/shard_map/ppermute | solution.py:327
  69.6 4.0 %collective-permute-start.19 = (f32[16,2048]{1,0:T(8,128)S(1)}, f32[16,2048]{1,0:T(8,128)S(1)}, u32[]{:S(2)}, u32[]{:S(2)}) collective-permute-start(f32[16,2048]{1,0:T(8,128)S(1)} %get-tuple-element.30), channel_id=1, source_target_pairs={{0,3},{4,7},{9,8},{13,12},{18,17},{22,21},{27,26},{31,30}} | collective-permute-start | bytes 393224 | tf_op jit(solution)/shard_map/ppermute | solution.py:327
  73.6 1.3 %collective-permute-start.15 = (f32[16,2048]{1,0:T(8,128)S(1)}, f32[16,2048]{1,0:T(8,128)S(1)}, u32[]{:S(2)}, u32[]{:S(2)}) collective-permute-start(f32[16,2048]{1,0:T(8,128)S(1)} %get-tuple-element.14), channel_id=1, source_target_pairs={{0,1},{4,5},{9,10},{13,14},{18,19},{22,23},{27,24},{31,28}} | collective-permute-start | bytes 393224 | tf_op jit(solution)/shard_map/ppermute | solution.py:327
  74.9 0.0 collective-permute-done.5
  74.9 0.1 broadcast_select_fusion.7
  75.1 0.0 slice-start
  75.2 0.0 copy-done.1
  75.2 0.0 copy-done.4
  75.2 0.0 copy-done.6
  75.2 0.0 slice-start.1
  75.2 0.0 copy-start.7
  75.2 14.4 %prompt_layer.1 = bf16[2,256,4096]{2,1,0:T(8,128)(2,1)} custom-call(bf16[2,256,4096]{2,1,0:T(8,128)(2,1)S(1)} %copy-done.1, f32[2,64,256]{2,1,0:T(8,128)S(1)} %copy-done.4, bf16[2,2,16,256]{3,2,1,0:T(8,128)(2,1)S(1)} %copy-done.6, f32[2,16,4096]{2,1,0:T(8,128)S(1)} %pad_maximum_fusion.refs_3_), custom_call_target="tpu_custom_call" | custom-call | flops 4831838208 | bytes 8388608 | tf_op jit(solution)/shard_map/prompt_layer/pallas_call | solution.py:218
  89.7 0.0 collective-permute-done.17
  89.7 0.0 collective-permute-done.19
  89.7 0.0 collective-permute-done.15
  89.8 4.1 %branch_finish.1 = bf16[2,512,2048]{2,1,0:T(8,128)(2,1)} custom-call(s32[2]{0:T(128)S(1)} %copy-done.7, f32[2,512,2048]{2,1,0:T(8,128)S(1)} %bitcast.23, bf16[2,512,512]{2,1,0:T(8,128)(2,1)S(1)} %get-tuple-element.13.reach_ref, f32[16,2048]{1,0:T(8,128)S(1)} %add_add_fusion.start_ref), custom_call_target="tpu_custom_call" | custom-call | flops 536870912 | bytes 12582912 | tf_op jit(solution)/shard_map/branch_finish/pallas_call | solution.py:255
  (33 shorter events, 0.6 us)
Async XLA Ops:
  0.6 47.6 %collective-permute-start.14 = (s32[1]{0:T(128)}, s32[1]{0:T(128)}, u32[]{:S(2)}, u32[]{:S(2)}) collective-permute-start(s32[1]{0:T(128)} %param.14), channel_id=1, source_target_pairs={{1,0},{5,4},{10,9},{14,13},{19,18},{23,22},{24,27},{28,31}} | collective-permute-start | bytes 20 | tf_op jit(solution)/shard_map/ppermute | solution.py:327
  1.9 48.2 %collective-permute-start.16 = (s32[1]{0:T(128)}, s32[1]{0:T(128)}, u32[]{:S(2)}, u32[]{:S(2)}) collective-permute-start(s32[1]{0:T(128)} %param.14), channel_id=1, source_target_pairs={{2,0},{6,4},{11,9},{15,13},{16,18},{20,22},{25,27},{29,31}} | collective-permute-start | bytes 20 | tf_op jit(solution)/shard_map/ppermute | solution.py:327
  3.2 2.2 %copy-start = (bf16[2,256,4096]{2,1,0:T(8,128)(2,1)S(1)}, bf16[2,256,4096]{2,1,0:T(8,128)(2,1)}, u32[]{:S(2)}) copy-start(bf16[2,256,4096]{2,1,0:T(8,128)(2,1)} %refs_0_.2) | copy-start | bytes 12582916
  5.4 0.9 copy-start.3
  6.3 0.8 copy-start.5
  7.1 19.4 %copy-start.9 = (f32[2,32,512]{2,1,0:T(8,128)S(1)}, f32[2,32,512]{2,1,0:T(8,128)}, u32[]{:S(2)}) copy-start(f32[2,32,512]{2,1,0:T(8,128)} %refs_1_.3) | copy-start | bytes 393220
  7.1 19.4 %copy-start.10 = (bf16[2,2,16,512]{3,2,1,0:T(8,128)(2,1)S(1)}, bf16[2,2,16,512]{3,2,1,0:T(8,128)(2,1)}, u32[]{:S(2)}) copy-start(bf16[2,2,16,512]{3,2,1,0:T(8,128)(2,1)} %refs_2_.3) | copy-start | bytes 196612
  9.9 4.0 %collective-permute-start.6 = (f32[1,2048]{1,0:T(1,128)S(1)}, f32[1,2048]{1,0:T(1,128)S(1)}, u32[]{:S(2)}, u32[]{:S(2)}) collective-permute-start(f32[1,2048]{1,0:T(1,128)S(1)} %broadcast_select_fusion.12), channel_id=1, source_target_pairs={{0,4},{4,0},{8,12},{12,8},{16,20},{20,16},{24,28},{28,24},{1,5},{5... | collective-permute-start | bytes 24584 | tf_op jit(solution)/shard_map/ppermute | solution.py:274
  10.4 46.0 %collective-permute-start.8 = (f32[16,2048]{1,0:T(8,128)S(1)}, f32[16,2048]{1,0:T(8,128)S(1)}, u32[]{:S(2)}, u32[]{:S(2)}) collective-permute-start(f32[16,2048]{1,0:T(8,128)S(1)} %slice_select_fusion.1), channel_id=1, source_target_pairs={{0,4},{4,0},{8,12},{12,8},{16,20},{20,16},{24,28},{28,24},{1,5},{5... | collective-permute-start | bytes 393224 | tf_op jit(solution)/shard_map/ppermute | solution.py:274
  13.4 2.9 %collective-permute-start = (f32[1,2048]{1,0:T(1,128)S(1)}, f32[1,2048]{1,0:T(1,128)S(1)}, u32[]{:S(2)}, u32[]{:S(2)}) collective-permute-start(f32[1,2048]{1,0:T(1,128)S(1)} %broadcast_select_fusion.16), channel_id=1, source_target_pairs={{0,4},{4,0},{8,12},{12,8},{16,20},{20,16},{24,28},{28,24},{1,5},{5... | collective-permute-start | bytes 24584 | tf_op jit(solution)/shard_map/ppermute | solution.py:274
  14.0 3.9 %collective-permute-start.7 = (f32[1,2048]{1,0:T(1,128)S(1)}, f32[1,2048]{1,0:T(1,128)S(1)}, u32[]{:S(2)}, u32[]{:S(2)}) collective-permute-start(f32[1,2048]{1,0:T(1,128)S(1)} %get-tuple-element.28), channel_id=1, source_target_pairs={{0,8},{4,12},{8,0},{12,4},{16,24},{20,28},{24,16},{28,20},{1,9},{5... | collective-permute-start | bytes 24584 | tf_op jit(solution)/shard_map/ppermute | solution.py:274
  16.3 8.1 %collective-permute-start.1 = (f32[1,2048]{1,0:T(1,128)S(1)}, f32[1,2048]{1,0:T(1,128)S(1)}, u32[]{:S(2)}, u32[]{:S(2)}) collective-permute-start(f32[1,2048]{1,0:T(1,128)S(1)} %get-tuple-element.24), channel_id=1, source_target_pairs={{0,8},{4,12},{8,0},{12,4},{16,24},{20,28},{24,16},{28,20},{1,9},{5... | collective-permute-start | bytes 24584 | tf_op jit(solution)/shard_map/ppermute | solution.py:274
  17.9 38.4 %collective-permute-start.12 = (f32[1,2048]{1,0:T(1,128)S(1)}, f32[1,2048]{1,0:T(1,128)S(1)}, u32[]{:S(2)}, u32[]{:S(2)}) collective-permute-start(f32[1,2048]{1,0:T(1,128)S(1)} %get-tuple-element.20), channel_id=1, source_target_pairs={{0,16},{4,20},{8,24},{12,28},{16,0},{20,4},{24,8},{28,12},{1,17},{... | collective-permute-start | bytes 24584 | tf_op jit(solution)/shard_map/ppermute | solution.py:274
  24.4 32.0 %collective-permute-start.13 = (f32[1,2048]{1,0:T(1,128)S(1)}, f32[1,2048]{1,0:T(1,128)S(1)}, u32[]{:S(2)}, u32[]{:S(2)}) collective-permute-start(f32[1,2048]{1,0:T(1,128)S(1)} %get-tuple-element.18), channel_id=1, source_target_pairs={{0,16},{4,20},{8,24},{12,28},{16,0},{20,4},{24,8},{28,12},{1,17},{... | collective-permute-start | bytes 24584 | tf_op jit(solution)/shard_map/ppermute | solution.py:274
  26.5 2.2 %copy-start.8 = (bf16[2,512,2048]{2,1,0:T(8,128)(2,1)S(1)}, bf16[2,512,2048]{2,1,0:T(8,128)(2,1)}, u32[]{:S(2)}) copy-start(bf16[2,512,2048]{2,1,0:T(8,128)(2,1)} %refs_0_.3) | copy-start | bytes 12582916
  44.3 3.3 %copy-start.2 = (f32[2,512,2048]{2,1,0:T(8,128)}, f32[2,512,2048]{2,1,0:T(8,128)S(1)}, u32[]{:S(2)}) copy-start(f32[2,512,2048]{2,1,0:T(8,128)S(1)} %get-tuple-element.12.own_ref) | copy-start | bytes 25165828
  48.3 7.5 %collective-permute-start.18 = (s32[1]{0:T(128)}, s32[1]{0:T(128)}, u32[]{:S(2)}, u32[]{:S(2)}) collective-permute-start(s32[1]{0:T(128)} %param.14), channel_id=1, source_target_pairs={{3,0},{7,4},{8,9},{12,13},{17,18},{21,22},{26,27},{30,31}} | collective-permute-start | bytes 20 | tf_op jit(solution)/shard_map/ppermute | solution.py:327
  50.1 6.4 %collective-permute-start.2 = (f32[16,2048]{1,0:T(8,128)S(1)}, f32[16,2048]{1,0:T(8,128)S(1)}, u32[]{:S(2)}, u32[]{:S(2)}) collective-permute-start(f32[16,2048]{1,0:T(8,128)S(1)} %slice_select_fusion.3), channel_id=1, source_target_pairs={{0,4},{4,0},{8,12},{12,8},{16,20},{20,16},{24,28},{28,24},{1,5},{5... | collective-permute-start | bytes 393224 | tf_op jit(solution)/shard_map/ppermute | solution.py:274
  56.4 5.0 %collective-permute-start.9 = (f32[16,2048]{1,0:T(8,128)S(1)}, f32[16,2048]{1,0:T(8,128)S(1)}, u32[]{:S(2)}, u32[]{:S(2)}) collective-permute-start(f32[16,2048]{1,0:T(8,128)S(1)} %select_add_fusion), channel_id=1, source_target_pairs={{0,8},{4,12},{8,0},{12,4},{16,24},{20,28},{24,16},{28,20},{1,9},{5... | collective-permute-start | bytes 393224 | tf_op jit(solution)/shard_map/ppermute | solution.py:274
  56.6 6.3 %collective-permute-start.3 = (f32[16,2048]{1,0:T(8,128)S(1)}, f32[16,2048]{1,0:T(8,128)S(1)}, u32[]{:S(2)}, u32[]{:S(2)}) collective-permute-start(f32[16,2048]{1,0:T(8,128)S(1)} %select_add_fusion.1), channel_id=1, source_target_pairs={{0,8},{4,12},{8,0},{12,4},{16,24},{20,28},{24,16},{28,20},{1,9},{5... | collective-permute-start | bytes 393224 | tf_op jit(solution)/shard_map/ppermute | solution.py:274
  61.5 5.0 %collective-permute-start.10 = (f32[16,2048]{1,0:T(8,128)S(1)}, f32[16,2048]{1,0:T(8,128)S(1)}, u32[]{:S(2)}, u32[]{:S(2)}) collective-permute-start(f32[16,2048]{1,0:T(8,128)S(1)} %add_select_fusion.4), channel_id=1, source_target_pairs={{0,16},{4,20},{8,24},{12,28},{16,0},{20,4},{24,8},{28,12},{1,17},{... | collective-permute-start | bytes 393224 | tf_op jit(solution)/shard_map/ppermute | solution.py:274
  62.9 12.3 %copy-start.1 = (bf16[2,256,4096]{2,1,0:T(8,128)(2,1)S(1)}, bf16[2,256,4096]{2,1,0:T(8,128)(2,1)}, u32[]{:S(2)}) copy-start(bf16[2,256,4096]{2,1,0:T(8,128)(2,1)} %refs_0_.2) | copy-start | bytes 12582916
  62.9 12.3 %copy-start.4 = (f32[2,64,256]{2,1,0:T(8,128)S(1)}, f32[2,64,256]{2,1,0:T(8,128)}, u32[]{:S(2)}) copy-start(f32[2,64,256]{2,1,0:T(8,128)} %refs_1_.2) | copy-start | bytes 393220
  62.9 12.3 %copy-start.6 = (bf16[2,2,16,256]{3,2,1,0:T(8,128)(2,1)S(1)}, bf16[2,2,16,256]{3,2,1,0:T(8,128)(2,1)}, u32[]{:S(2)}) copy-start(bf16[2,2,16,256]{3,2,1,0:T(8,128)(2,1)} %refs_2_.2) | copy-start | bytes 98308
  62.9 5.0 %collective-permute-start.4 = (f32[16,2048]{1,0:T(8,128)S(1)}, f32[16,2048]{1,0:T(8,128)S(1)}, u32[]{:S(2)}, u32[]{:S(2)}) collective-permute-start(f32[16,2048]{1,0:T(8,128)S(1)} %add_select_fusion.5), channel_id=1, source_target_pairs={{0,16},{4,20},{8,24},{12,28},{16,0},{20,4},{24,8},{28,12},{1,17},{... | collective-permute-start | bytes 393224 | tf_op jit(solution)/shard_map/ppermute | solution.py:274
  66.6 1.5 %collective-permute-start.11 = (f32[16,2048]{1,0:T(8,128)S(1)}, f32[16,2048]{1,0:T(8,128)S(1)}, u32[]{:S(2)}, u32[]{:S(2)}) collective-permute-start(f32[16,2048]{1,0:T(8,128)S(1)} %fusion.1), channel_id=1, source_target_pairs={{0,4},{4,0},{8,12},{12,8},{16,20},{20,16},{24,28},{28,24},{1,5},{5... | collective-permute-start | bytes 393224 | tf_op jit(solution)/shard_map/ppermute | solution.py:274
  68.0 6.9 %collective-permute-start.5 = (f32[16,2048]{1,0:T(8,128)S(1)}, f32[16,2048]{1,0:T(8,128)S(1)}, u32[]{:S(2)}, u32[]{:S(2)}) collective-permute-start(f32[16,2048]{1,0:T(8,128)S(1)} %fusion.3), channel_id=1, source_target_pairs={{0,4},{4,0},{8,12},{12,8},{16,20},{20,16},{24,28},{28,24},{1,5},{5... | collective-permute-start | bytes 393224 | tf_op jit(solution)/shard_map/ppermute | solution.py:274
  68.3 21.4 %collective-permute-start.17 = (f32[16,2048]{1,0:T(8,128)S(1)}, f32[16,2048]{1,0:T(8,128)S(1)}, u32[]{:S(2)}, u32[]{:S(2)}) collective-permute-start(f32[16,2048]{1,0:T(8,128)S(1)} %get-tuple-element.29), channel_id=1, source_target_pairs={{0,2},{4,6},{9,11},{13,15},{18,16},{22,20},{27,25},{31,29}} | collective-permute-start | bytes 393224 | tf_op jit(solution)/shard_map/ppermute | solution.py:327
  69.6 20.1 %collective-permute-start.19 = (f32[16,2048]{1,0:T(8,128)S(1)}, f32[16,2048]{1,0:T(8,128)S(1)}, u32[]{:S(2)}, u32[]{:S(2)}) collective-permute-start(f32[16,2048]{1,0:T(8,128)S(1)} %get-tuple-element.30), channel_id=1, source_target_pairs={{0,3},{4,7},{9,8},{13,12},{18,17},{22,21},{27,26},{31,30}} | collective-permute-start | bytes 393224 | tf_op jit(solution)/shard_map/ppermute | solution.py:327
  73.6 16.1 %collective-permute-start.15 = (f32[16,2048]{1,0:T(8,128)S(1)}, f32[16,2048]{1,0:T(8,128)S(1)}, u32[]{:S(2)}, u32[]{:S(2)}) collective-permute-start(f32[16,2048]{1,0:T(8,128)S(1)} %get-tuple-element.14), channel_id=1, source_target_pairs={{0,1},{4,5},{9,10},{13,14},{18,19},{22,23},{27,24},{31,28}} | collective-permute-start | bytes 393224 | tf_op jit(solution)/shard_map/ppermute | solution.py:327
  75.1 14.6 %slice-start = ((s8[8388608]{0:T(1024)(128)(4,1)}), s8[4194304]{0:T(1024)(128)(4,1)S(1)}, s32[]{:S(2)}) async-start(s8[8388608]{0:T(1024)(128)(4,1)} %bitcast.22), calls=%async_computation | async-start | bytes 8388608
  75.2 14.5 %slice-start.1 = ((s8[8388608]{0:T(1024)(128)(4,1)}), s8[4194304]{0:T(1024)(128)(4,1)S(1)}, s32[]{:S(2)}) async-start(s8[8388608]{0:T(1024)(128)(4,1)} %bitcast.22), calls=%async_computation.1 | async-start | bytes 8388608
  75.2 14.5 %copy-start.7 = (s32[2]{0:T(128)S(1)}, s32[2]{0:T(128)}, u32[]{:S(2)}) copy-start(s32[2]{0:T(128)} %len_ref.1) | copy-start | bytes 28

commit v2 on v1

v2 whole, which is shorter than its diff:
```python
import functools
import jax
import jax.numpy as jnp
from jax import lax
from jax.experimental import pallas as pl
from jax.experimental.pallas import tpu as pltpu
from jax.sharding import PartitionSpec as P

BLOCK = 256
CHUNK = 32
F32 = jnp.float32
BF16 = jnp.bfloat16
VMEM_LIMIT = 40 * 1024 * 1024


def iota(shape, dim):
    return lax.broadcasted_iota(jnp.int32, shape, dim)


def quotient(index, divisor):
    if divisor & (divisor - 1) == 0:
        return lax.shift_right_logical(index, divisor.bit_length() - 1)
    return lax.div(index, divisor)


def remainder(index, divisor):
    if divisor & (divisor - 1) == 0:
        return index & (divisor - 1)
    return lax.rem(index, divisor)


def exact_dot(a, b):
    return jnp.dot(a, b, preferred_element_type=F32, precision=lax.Precision.HIGHEST)


def gain_of(log_decay):
    z = 2.0 * log_decay
    series = 1.0 + z * (1.0 / 9.0)
    for k in (8, 7, 6, 5, 4, 3, 2):
        series = 1.0 + z * (1.0 / k) * series
    small = -z * series
    large = 1.0 - jnp.exp(z)
    return jnp.sqrt(jnp.maximum(jnp.where(z > -0.5, small, large), 0.0))


def hi_lo(value):
    high = value.astype(BF16).astype(F32)
    return jnp.concatenate([high, value - high], axis=0)


def head_distance(heads, width, lanes):
    return remainder(iota((2 * heads, 1), 0), heads) - quotient(iota((1, lanes), 1), width)


def ends_kernel(x_ref, ld_ref, b_ref, end_ref, log_ref, push_ref, *, heads, width, state):
    tile = pl.program_id(1)
    positions = ld_ref.shape[2]
    lanes = x_ref.shape[2]

    @pl.when(tile == 0)
    def _():
        logs = ld_ref[0]
        after = jnp.where(iota((positions, 1), 0) > iota((1, positions), 1), 1.0, 0.0)
        to_end = jnp.exp(exact_dot(logs, after)) * gain_of(logs)
        b_rows = b_ref[0, 0].astype(F32)
        push = b_rows[None, :, :] * to_end[:, None, :]
        push_ref[...] = push.reshape(heads * state, positions).astype(BF16)

    group = 256 // width
    tile_heads = lanes // width
    lane_head = quotient(iota((1, 256), 1), width)
    for g in range(tile_heads // group):
        first = tile * tile_heads + g * group
        rows = pl.ds(pl.multiple_of(first * state, group * state), group * state)
        cols = pl.ds(g * 256, 256)
        both = jnp.dot(push_ref[rows, :], x_ref[0, :, cols], preferred_element_type=F32)
        end = jnp.where(lane_head == 0, both[:state], 0.0)
        for i in range(1, group):
            end = jnp.where(lane_head == i, both[i * state:(i + 1) * state], end)
        end_ref[0, :, cols] = end
    totals = lax.dot_general(
        jnp.ones((8, positions), F32), ld_ref[0], (((1,), (1,)), ((), ())),
        preferred_element_type=F32, precision=lax.Precision.HIGHEST)
    pick = iota((heads, 1), 0) == quotient(iota((1, lanes), 1), width) + tile * tile_heads
    log_ref[0] = exact_dot(totals, jnp.where(pick, 1.0, 0.0))


def local_ends(x, logdec, bc):
    count, positions, channels = x.shape
    heads, state = logdec.shape[1], bc.shape[2]
    width = channels // heads
    lanes = min(1024, channels)
    kernel = functools.partial(ends_kernel, heads=heads, width=width, state=state)
    return pl.pallas_call(
        kernel,
        grid=(count, channels // lanes),
        in_specs=[
            pl.BlockSpec((1, positions, lanes), lambda i, j: (i, 0, j)),
            pl.BlockSpec((1, heads, positions), lambda i, j: (i, 0, 0)),
            pl.BlockSpec((1, 1, state, positions), lambda i, j: (0, i, 0, 0)),
        ],
        out_specs=[
            pl.BlockSpec((1, state, lanes), lambda i, j: (i, 0, j)),
            pl.BlockSpec((1, 8, lanes), lambda i, j: (i, 0, j)),
        ],
        out_shape=[
            jax.ShapeDtypeStruct((count, state, channels), F32),
            jax.ShapeDtypeStruct((count, 8, channels), F32),
        ],
        scratch_shapes=[pltpu.VMEM((heads * state, positions), BF16)],
        compiler_params=pltpu.CompilerParams(vmem_limit_bytes=60 * 1024 * 1024),
        cost_estimate=pl.CostEstimate(
            flops=2 * 64 * x.size, bytes_accessed=2 * x.size, transcendentals=0),
        name="local_ends",
    )(x, logdec, bc)


def prepare(logs, b_rows, c_rows, w_ref, l_ref, c_ref, state):
    size = logs.shape[1]
    chunks = size // CHUNK
    half = CHUNK // 2
    src, dst = iota((size, 1), 0), iota((1, size), 1)
    middle = quotient(dst, CHUNK) * CHUNK + half - 1
    plus = (src > middle) & (src <= dst)
    minus = (src > dst) & (src <= middle)
    offset = exact_dot(logs, jnp.where(plus, 1.0, jnp.where(minus, -1.0, 0.0)))
    row_scale = hi_lo(jnp.exp(offset))
    in_scale = hi_lo(jnp.exp(-offset) * gain_of(logs))
    span = iota((1, 128), 1) == quotient(src + half, CHUNK)
    steps = hi_lo(jnp.exp(exact_dot(logs, jnp.where(span, 1.0, 0.0))))
    w_ref[pl.ds(0, size), :] = in_scale.T.astype(BF16)
    w_ref[pl.ds(size, size), :] = row_scale.T.astype(BF16)
    w_ref[pl.ds(2 * size, 16), :] = steps.T[:16].astype(BF16)

    scores = lax.dot_general(c_rows, b_rows, (((0,), (0,)), ((), ())), preferred_element_type=F32)
    keep = (dst <= src) & (quotient(dst, CHUNK) == quotient(src, CHUNK))
    l_ref[pl.ds(0, size), :] = jnp.where(keep, scores, 0.0).astype(BF16)
    rows = state * chunks
    mine = quotient(iota((rows, 1), 0), state) == quotient(dst, CHUNK)
    b_all = jnp.concatenate([b_rows.astype(F32)] * chunks, axis=0)
    l_ref[pl.ds(size, rows), :] = jnp.where(mine, b_all, 0.0).astype(BF16)
    c_all = jnp.concatenate([c_rows.astype(F32)] * chunks, axis=0)
    c_ref[...] = jnp.where(mine, c_all, 0.0).T.astype(BF16)


def layer_kernel(*refs, heads, width, state, has_start, with_reach, skip):
    x_ref, ld_ref, bc_ref = refs[:3]
    refs = refs[3 + skip:]
    if has_start:
        start_ref, refs = refs[0], refs[1:]
    y_ref, refs = refs[0], refs[1:]
    if with_reach:
        reach_ref, refs = refs[0], refs[1:]
        before_ref, refs = refs[-1], refs[:-1]
    w_ref, l_ref, c_ref, s_ref, far_ref = refs
    block, tile = pl.program_id(1), pl.program_id(2)
    size, lanes = x_ref.shape[1], x_ref.shape[2]
    chunks = size // CHUNK
    tile_heads = lanes // width

    @pl.when(tile == 0)
    def _():
        logs = ld_ref[0]
        c_rows = bc_ref[1, 0]
        prepare(logs, bc_ref[0, 0], c_rows, w_ref, l_ref, c_ref, state)
        far_ref[...] = head_distance(heads, width, 256)
        if with_reach:
            upto = jnp.where(iota((size, 1), 0) <= iota((1, size), 1), 1.0, 0.0)
            run = exact_dot(logs, upto)
            entered = jnp.where(block == 0, 0.0, before_ref[:, 0:1])
            run = run + entered
            before_ref[...] = jnp.broadcast_to(run[:, size - 1:size], before_ref.shape)
            reach = c_rows.astype(F32)[None, :, :] * jnp.exp(run)[:, None, :]
            reach_ref[0] = reach.reshape(heads * state, size).T.astype(BF16)

    for g in range(lanes // 256):
        cols = pl.ds(g * 256, 256)
        here = pl.ds(pl.multiple_of(tile * lanes + g * 256, 256), 256)
        first_head = tile * tile_heads + g * (256 // width)
        one_hot = jnp.where(far_ref[...] == first_head, 1.0, 0.0).astype(BF16)
        scales = jnp.dot(w_ref[...], one_hot, preferred_element_type=F32)
        scaled = (x_ref[0, :, cols].astype(F32) * scales[:size]).astype(BF16)
        both = jnp.dot(l_ref[...], scaled, preferred_element_type=F32)
        if has_start:
            first = start_ref[0, :, cols]
        else:
            first = jnp.zeros((state, 256), F32)
        entering = jnp.where(block == 0, first, s_ref[:, here])
        carry = scales[2 * size:2 * size + 1] * entering
        carries = []
        for c in range(chunks):
            carries.append(carry.astype(BF16))
            local = both[size + c * state:size + (c + 1) * state]
            carry = scales[2 * size + c + 1:2 * size + c + 2] * (carry + local)
        s_ref[:, here] = carry
        carried = jnp.dot(c_ref[...], jnp.concatenate(carries, axis=0), preferred_element_type=F32)
        out = (both[:size] + carried) * scales[size:2 * size]
        y_ref[0, :, cols] = out.astype(y_ref.dtype)


def layer(x, logdec, bc, start, out_type, with_reach, name, which=None, into=()):
    count, positions, channels = x.shape
    heads, state = logdec.shape[1], bc.shape[2]
    width = channels // heads
    lanes = min(1024, channels)
    blocks = positions // BLOCK
    chunks = BLOCK // CHUNK
    kernel = functools.partial(
        layer_kernel, heads=heads, width=width, state=state,
        has_start=start is not None, with_reach=with_reach, skip=len(into))
    base = 0 if which is None else which
    in_specs = [
        pl.BlockSpec((1, BLOCK, lanes), lambda i, b, j: (i + base, b, j)),
        pl.BlockSpec((1, heads, BLOCK), lambda i, b, j: (i + base, 0, b)),
        pl.BlockSpec((2, 1, state, BLOCK), lambda i, b, j: (0, i + base, 0, b)),
    ]
    args = [x, logdec, bc, *into]
    in_specs += [pl.BlockSpec(memory_space=pl.ANY)] * len(into)
    if start is not None:
        in_specs.append(pl.BlockSpec((1, state, lanes), lambda i, b, j: (i, 0, j)))
        args.append(start)
    out_specs = [pl.BlockSpec((1, BLOCK, lanes), lambda i, b, j: (i + base, b, j))]
    out_shape = [jax.ShapeDtypeStruct(x.shape, out_type)]
    scratch = [
        pltpu.VMEM((2 * BLOCK + 16, 2 * heads), BF16),
        pltpu.VMEM((BLOCK + chunks * state, BLOCK), BF16),
        pltpu.VMEM((BLOCK, chunks * state), BF16),
        pltpu.VMEM((state, channels), F32),
        pltpu.VMEM((2 * heads, 256), jnp.int32),
    ]
    if with_reach:
        out_specs.append(pl.BlockSpec((1, BLOCK, heads * state), lambda i, b, j: (i + base, b, 0)))
        out_shape.append(jax.ShapeDtypeStruct((count, positions, heads * state), BF16))
        scratch.append(pltpu.VMEM((heads, 128), F32))
    sequences = count if which is None else 1
    work = sequences * positions * channels
    return pl.pallas_call(
        kernel,
        grid=(sequences, blocks, channels // lanes),
        in_specs=in_specs,
        out_specs=out_specs,
        out_shape=out_shape,
        scratch_shapes=scratch,
        input_output_aliases={3 + i: i for i in range(len(into))},
        compiler_params=pltpu.CompilerParams(vmem_limit_bytes=VMEM_LIMIT),
        cost_estimate=pl.CostEstimate(
            flops=2 * 1152 * work, bytes_accessed=4 * work, transcendentals=0),
        name=name,
    )(*args)


def finish_kernel(len_ref, own_ref, reach_ref, start_ref, y_ref, *, width, state):
    branch = pl.program_id(0)
    tile = pl.program_id(1)
    positions, lanes = own_ref.shape[1], own_ref.shape[2]
    group = 128 // state
    span = group * width
    live = iota((positions, 1), 0) < len_ref[branch]
    own_head = quotient(iota((group * state, 1), 0), state) == quotient(iota((1, span), 1), width)
    for g in range(lanes // span):
        cols = pl.ds(g * span, span)
        first = (tile * (lanes // span) + g) * 128
        start = jnp.concatenate([start_ref[:, cols]] * group, axis=0)
        start = jnp.where(own_head, start, 0.0).astype(BF16)
        term = jnp.dot(reach_ref[0, :, pl.ds(pl.multiple_of(first, 128), 128)], start, preferred_element_type=F32)
        out = own_ref[0, :, cols].astype(F32) + term
        y_ref[0, :, cols] = jnp.where(live, out, 0.0).astype(BF16)


def finish(lengths, own, reach, start):
    count, positions, channels = own.shape
    state = start.shape[0]
    width = channels * state // reach.shape[2]
    lanes = min(1024, channels)
    return pl.pallas_call(
        functools.partial(finish_kernel, width=width, state=state),
        grid=(count, channels // lanes),
        in_specs=[
            pl.BlockSpec(memory_space=pltpu.SMEM),
            pl.BlockSpec((1, positions, lanes), lambda i, j: (i, 0, j)),
            pl.BlockSpec((1, positions, reach.shape[2]), lambda i, j: (i, 0, 0)),
            pl.BlockSpec((state, lanes), lambda i, j: (0, j)),
        ],
        out_specs=pl.BlockSpec((1, positions, lanes), lambda i, j: (i, 0, j)),
        out_shape=jax.ShapeDtypeStruct(own.shape, BF16),
        compiler_params=pltpu.CompilerParams(vmem_limit_bytes=VMEM_LIMIT),
        cost_estimate=pl.CostEstimate(
            flops=2 * 128 * own.size, bytes_accessed=6 * own.size, transcendentals=0),
        name="branch_finish",
    )(lengths, own, reach, start)


def swap_bit(value, bit, size):
    return lax.ppermute(value, "ctx", [(k, k ^ bit) for k in range(size)])


def pack(states, logs):
    lanes = states.shape[-1]
    return jnp.concatenate([states.reshape(-1, lanes), logs.reshape(-1, lanes)], axis=0)


def unpack(packed, count):
    lanes = packed.shape[-1]
    rows = packed.shape[0] - count
    return packed[:rows].reshape(count, rows // count, lanes), packed[rows:].reshape(count, 1, lanes)


def in_order(upper, mine, other):
    first = [jnp.where(upper, o, m) for m, o in zip(mine, other)]
    second = [jnp.where(upper, m, o) for m, o in zip(mine, other)]
    return first, second


def join(first, second):
    return jnp.exp(second[1]) * first[0] + second[0], first[1] + second[1]


def branch_prompts(chosen, pair_size):
    known = chosen
    while known.shape[0] < pair_size:
        step = known.shape[0]
        further = lax.ppermute(known, "pair", [((z + step) % pair_size, z) for z in range(pair_size)])
        known = jnp.concatenate([known, further])
    return known


def branch_start(total, wanted, ctx_size, pair_size):
    ctx, pair = lax.axis_index("ctx"), lax.axis_index("pair")
    owner = ctx * pair_size // ctx_size

    def pick(which):
        out = total[0]
        for i in range(1, total.shape[0]):
            out = jnp.where(which == i, total[i], out)
        return out

    parts = [jnp.where(pair == owner, pick(wanted[0]), 0.0)]
    for hop in range(1, pair_size):
        links = []
        for k in range(ctx_size):
            z = k * pair_size // ctx_size
            links.append((k * pair_size + z, k * pair_size + (z + hop) % pair_size))
        parts.append(lax.ppermute(pick(wanted[hop]), ("ctx", "pair"), links))
    return sum(parts)


def body(
    prompt_x,
    prompt_bc,
    prompt_logdec,
    branch_x,
    branch_bc,
    branch_logdec,
    branch_prompt,
    branch_len,
):
    size, pair_size = lax.axis_size("ctx"), lax.axis_size("pair")
    prompts, branches = prompt_x.shape[0], branch_x.shape[0]
    assert size == 2 * pair_size and size & (size - 1) == 0 and branch_prompt.shape[0] == 1
    mine = lax.axis_index("ctx")
    odd = (mine & 1) == 1
    wanted = branch_prompts(branch_prompt, pair_size)

    end, log = local_ends(prompt_x, prompt_logdec, prompt_bc)
    half = end.shape[2] // 2
    low, high = (end[:, :, :half], log[:, :1, :half]), (end[:, :, half:], log[:, :1, half:])
    keep = [jnp.where(odd, h, l) for l, h in zip(low, high)]
    send = [jnp.where(odd, l, h) for l, h in zip(low, high)]
    got = unpack(swap_bit(pack(*send), 1, size), prompts)
    first, second = in_order(odd, keep, got)
    total, total_log = join(first, second)
    before, before_log = jnp.zeros_like(total), jnp.zeros_like(total_log)

    own = ()
    works = iter(range(branches))
    bit = 2
    while bit < size:
        packed = pack(total, total_log)
        which = next(works, None)
        if which is not None:
            packed, branch_x = lax.optimization_barrier((packed, branch_x))
        got = swap_bit(packed, bit, size)
        if which is not None:
            own = layer(branch_x, branch_logdec, branch_bc, None, F32, True, "branch_own", which, own)
            got, own = lax.optimization_barrier((got, own))
        other = unpack(got, prompts)
        upper = (mine & bit) != 0
        before = jnp.where(upper, jnp.exp(before_log) * other[0] + before, before)
        before_log = jnp.where(upper, before_log + other[1], before_log)
        total, total_log = join(*in_order(upper, (total, total_log), other))
        bit *= 2
    for which in works:
        own = layer(branch_x, branch_logdec, branch_bc, None, F32, True, "branch_own", which, own)

    next_before = jnp.exp(first[1]) * before + first[0]
    got = swap_bit(jnp.where(odd, before, next_before), 1, size)
    keep = jnp.where(odd, next_before, before)
    entering = jnp.concatenate([jnp.where(odd, got, keep), jnp.where(odd, keep, got)], axis=2)
    start = branch_start(total, wanted, size, pair_size)
    (prompt_y,) = layer(prompt_x, prompt_logdec, prompt_bc, entering, BF16, False, "prompt_layer")
    start, prompt_y = lax.optimization_barrier((start, prompt_y))
    branch_y = finish(branch_len, *own, start)
    return prompt_y, branch_y


def solution(mesh):
    return jax.shard_map(
        body,
        mesh=mesh,
        in_specs=(
            P(None, "ctx", "pair"),
            P(None, None, None, "ctx"),
            P(None, "pair", "ctx"),
            P("pair", None, "ctx"),
            P(None, "pair", None, None),
            P("pair", "ctx", None),
            P("pair"),
            P("pair"),
        ),
        out_specs=(P(None, "ctx", "pair"), P("pair", None, "ctx")),
        check_vma=False,
    )
```

time: 94.3 us -> 72.1 us (0.76)
  waiting for transfers between devices: 13.7 us -> 1.49 us
  starting transfers between devices: 26.8 us -> 15.2 us
  local copies, waits for them, and re-layouts: 9.37 us -> 3.01 us
  other arithmetic: 0.81 us -> 5.46 us
  Pallas kernels: 39.8 us -> 42.8 us
    ppermute x14 -> x4, starting transfers between devices: 16.2 us -> 3.73 us  [swap_bit(): return lax.ppermute(value, 'ctx', [(k, k ^ bit) for k in range(size)])]
    ppermute x14 -> x4, waiting for transfers between devices: 8.78 us -> 1.47 us  [swap_bit(): return lax.ppermute(value, 'ctx', [(k, k ^ bit) for k in range(size)])]
    unnamed x26 -> x22, local copies, waits for them, and re-layouts: 9.34 us -> 2.29 us
    ppermute x6 -> x5, waiting for transfers between devices: 4.93 us -> 0.01 us  [the longest x3 0.01 us: branch_start(): parts.append(lax.ppermute(pick(wanted[hop]), ('ctx', 'pair'), links))]
    pallas_call x4, Pallas kernels: 35.6 us -> 38.6 us  [the longest x3 30 us: layer(): pl.pallas_call(kernel, grid=(sequences, blocks, channels // lanes), in_sp...]
    select_n x13 -> x6, other arithmetic: 0.49 us -> 2.33 us  [the longest x2 2.04 us: body(): send = [jnp.where(odd, l, h) for l, h in zip(low, high)]]
    add x3 -> x4, other arithmetic: 0.1 us -> 1.2 us  [the longest x3 1.16 us: join(): return (jnp.exp(second[1]) * first[0] + second[0], first[1] + second[1])]
    ppermute x6 -> x5, starting transfers between devices: 10.5 us -> 11.5 us  [the longest x3 6.8 us: branch_start(): parts.append(lax.ppermute(pick(wanted[hop]), ('ctx', 'pair'), links))]
  transfers between devices with their start and end apart: 20 -> 9, of which waited for: 6 -> 1; matrix products, arithmetic and copies ran while one was open for 1% -> 5% of each run, Pallas kernels for 38% -> 42%
where the time goes in v2:
time: 72.1 us; the launch traced here: 71.7 us
  Pallas kernels  42.8 us (59%)
  starting transfers between devices  15.2 us (21%)
  other arithmetic  5.46 us (8%)
  between operations  3.75 us (5%)
  local copies, waits for them, and re-layouts  3.01 us (4%)
  waiting for transfers between devices  1.49 us (2%)
    pallas_call x3, Pallas kernels, layer(): pl.pallas_call(kernel, grid=(sequences, blocks, channels // lanes), in_sp...  30 us
    pallas_call x1, Pallas kernels, local_ends(): pl.pallas_call(kernel, grid=(count, channels // lanes), in_specs=[pl.Bloc...  8.6 us
    ppermute x3, starting transfers between devices, branch_start(): parts.append(lax.ppermute(pick(wanted[hop]), ('ctx', 'pair'), links))  6.8 us
    ppermute x2, starting transfers between devices, branch_prompts(): lax.ppermute(known, 'pair', [((z + step) % pair_size, z) for z in range(p...  4.68 us
    pallas_call x1, Pallas kernels, finish(): pl.pallas_call(functools.partial(finish_kernel, width=width, state=state)...  4.16 us
    ppermute x4, starting transfers between devices, swap_bit(): return lax.ppermute(value, 'ctx', [(k, k ^ bit) for k in range(size)])  3.73 us
    unnamed x22, local copies, waits for them, and re-layouts  2.29 us
    select_n x2, other arithmetic, body(): send = [jnp.where(odd, l, h) for l, h in zip(low, high)]  2.04 us
  transfers between devices with their start and end apart: 9, of which 1 were waited for; matrix products, arithmetic and copies ran while one was open for 5% of the time, Pallas kernels for 42%

profile of v2, /device:TPU:0, one launch (start us, length us, event | category | flops | bytes accessed | tf_op | source)
XLA Modules:
  0.0 71.7 jit_solution(6789067880911809030)
XLA Ops:
  0.6 0.0 copy-start.2
  0.6 0.0 copy-start.4
  0.7 8.6 %local_ends.1 = (f32[2,16,4096]{2,1,0:T(8,128)}, f32[2,8,4096]{2,1,0:T(8,128)}) custom-call(bf16[2,256,4096]{2,1,0:T(8,128)(2,1)} %refs_0_.3, f32[2,64,256]{2,1,0:T(8,128)} %refs_1_.5, bf16[2,2,16,256]{3,2,1,0:T(8,128)(2,1)} %refs_2_.5), custom_call_target="tpu_custom_call" | custom-call | flops 268435456 | bytes 4194304 | tf_op jit(solution)/shard_map/local_ends/pallas_call | solution.py:94
  9.3 1.0 %broadcast_select_fusion.5 = f32[2,1,2048]{2,1,0:T(1,128)S(1)} fusion(pred[]{:T(512)S(6)} %eq.33, f32[2,8,4096]{2,1,0:T(8,128)} %get-tuple-element.20), kind=kLoop, calls=%fused_computation.24 | loop fusion | flops 4096 | bytes 49153 | tf_op jit(solution)/shard_map/jit(_where)/select_n | solution.py:368
  10.3 1.1 %slice_select_fusion.1 = f32[2,16,2048]{2,1,0:T(8,128)S(1)} fusion(f32[2,16,4096]{2,1,0:T(8,128)} %get-tuple-element.21, pred[]{:T(512)S(6)} %eq.33), kind=kLoop, calls=%fused_computation.12 | loop fusion | flops 65536 | bytes 786433 | tf_op jit(solution)/shard_map/jit(_where)/select_n | solution.py:368
  11.4 0.5 collective-permute-start
  11.9 4.7 %collective-permute-start.3 = (s32[1]{0:T(128)}, s32[1]{0:T(128)}, u32[]{:S(2)}, u32[]{:S(2)}) collective-permute-start(s32[1]{0:T(128)} %param.14), channel_id=1, source_target_pairs={{1,0},{2,1},{3,2},{0,3},{5,4},{6,5},{7,6},{4,7},{9,8},{10,9},{11,1... | collective-permute-start | bytes 20 | tf_op jit(solution)/shard_map/ppermute | solution.py:322
  17.3 0.0 collective-permute-done
  17.3 1.0 %fusion.9 = (f32[2,1,2048]{2,1,0:T(1,128)S(1)}, f32[2,1,2048]{2,1,0:T(1,128)S(1)}, f32[2,1,2048]{2,1,0:T(1,128)S(1)}) fusion(f32[2,2048]{1,0:T(2,128)S(1)} %slice.62, pred[]{:T(512)S(6)} %eq.33, f32[2,8,4096]{2,1,0:T(8,128)} %get-tuple-element.20), kind=kLoop, calls=%fused_computation.43 | loop fusion | flops 16384 | bytes 98305 | tf_op jit(solution)/shard_map/exp | solution.py:395
  18.4 1.1 %select_add_fusion.2 = f32[2,16,2048]{2,1,0:T(8,128)S(1)} fusion(f32[2,16,2048]{2,1,0:T(8,128)S(1)} %bitcast.41, f32[2,2048]{1,0:T(2,128)S(1)} %bitcast.53, pred[]{:T(512)S(6)} %eq.33, f32[2,16,4096]{2,1,0:T(8,128)} %get-tuple-element.21), kind=kLoop, calls=%fused_computation.10 | loop fusion | flops 327680 | bytes 1064961 | tf_op jit(solution)/shard_map/add | solution.py:315
  19.5 1.6 %collective-permute-start.1 = (f32[34,2048]{1,0:T(8,128)S(1)}, f32[34,2048]{1,0:T(8,128)S(1)}, u32[]{:S(2)}, u32[]{:S(2)}) collective-permute-start(f32[34,2048]{1,0:T(8,128)S(1)} %pad_maximum_fusion.2), channel_id=1, source_target_pairs={{0,8},{4,12},{8,0},{12,4},{16,24},{20,28},{24,16},{28,20},{1,9},{5... | collective-permute-start | bytes 835592 | tf_op jit(solution)/shard_map/ppermute | solution.py:294
  21.0 0.0 collective-permute-done.3
  21.0 0.7 %pad_add_fusion = s32[2]{0:T(128)S(1)} fusion(s32[1]{0:T(128)} %collective-permute-done.3, s32[1]{0:T(128)S(6)} %copy.33), kind=kLoop, calls=%fused_computation.40 | loop fusion | flops 2 | bytes 16 | tf_op jit(solution)/shard_map/concatenate | solution.py:323
  21.8 0.0 collective-permute-start.5
  22.5 0.0 copy-done.2
  22.5 0.0 copy-done.4
  22.5 0.0 copy-start
  22.5 2.2 %copy-done = bf16[2,512,2048]{2,1,0:T(8,128)(2,1)S(1)} copy-done((bf16[2,512,2048]{2,1,0:T(8,128)(2,1)S(1)}, bf16[2,512,2048]{2,1,0:T(8,128)(2,1)}, u32[]{:S(2)}) %copy-start) | copy-done | bytes 4194328
  24.7 7.8 %branch_own.2 = (f32[2,512,2048]{2,1,0:T(8,128)S(1)}, bf16[2,512,512]{2,1,0:T(8,128)(2,1)S(1)}) custom-call(bf16[2,512,2048]{2,1,0:T(8,128)(2,1)S(1)} %copy-done, f32[2,32,512]{2,1,0:T(8,128)S(1)} %copy-done.2, bf16[2,2,16,512]{3,2,1,0:T(8,128)(2,1)S(1)} %copy-done.4), custom_call_target="tpu_custom_call" | custom-call | flops 2415919104 | bytes 4194304 | tf_op jit(solution)/shard_map/branch_own/pallas_call | solution.py:237
  32.5 0.0 collective-permute-done.1
  32.7 1.6 %collective-permute-start.2 = (f32[34,2048]{1,0:T(8,128)S(1)}, f32[34,2048]{1,0:T(8,128)S(1)}, u32[]{:S(2)}, u32[]{:S(2)}) collective-permute-start(f32[34,2048]{1,0:T(8,128)S(1)} %pad_maximum_fusion.3), channel_id=1, source_target_pairs={{0,16},{4,20},{8,24},{12,28},{16,0},{20,4},{24,8},{28,12},{1,17},{... | collective-permute-start | bytes 835592 | tf_op jit(solution)/shard_map/ppermute | solution.py:294
  34.3 0.0 collective-permute-done.5
  34.3 0.6 fusion.11
  36.3 0.0 copy-start.7
  36.3 7.8 %branch_own.3 = (f32[2,512,2048]{2,1,0:T(8,128)S(1)}, bf16[2,512,512]{2,1,0:T(8,128)(2,1)S(1)}) custom-call(bf16[2,512,2048]{2,1,0:T(8,128)(2,1)S(1)} %copy-done, f32[2,32,512]{2,1,0:T(8,128)S(1)} %copy-done.2, bf16[2,2,16,512]{3,2,1,0:T(8,128)(2,1)S(1)} %copy-done.4, ...), custom_call_target="tpu_custom_call", output_to_operand_aliasing={{0}: (3, {}), {1}: (4, {})} | custom-call | flops 2415919104 | bytes 4194304 | tf_op jit(solution)/shard_map/branch_own/pallas_call | solution.py:237
  44.1 0.0 copy-start.1
  44.1 0.0 copy-start.3
  44.1 0.0 copy-start.5
  44.1 0.0 collective-permute-done.2
  44.2 0.0 copy-done.7
  44.2 0.1 fusion.1
  44.3 0.1 collective-permute-start.8
  44.4 1.5 %collective-permute-done.8 = f32[2,16,2048]{2,1,0:T(8,128)S(1)} collective-permute-done((f32[2,16,2048]{2,1,0:T(8,128)S(1)}, f32[2,16,2048]{2,1,0:T(8,128)S(1)}, u32[]{:S(2)}, u32[]{:S(2)}) %collective-permute-start.8) | collective-permute-done | bytes 262176 | tf_op jit(solution)/shard_map/ppermute | solution.py:294
  45.9 0.1 broadcast_select_fusion.1
  46.1 3.1 %collective-permute-start.7 = (f32[16,2048]{1,0:T(8,128)S(1)}, f32[16,2048]{1,0:T(8,128)S(1)}, u32[]{:S(2)}, u32[]{:S(2)}) collective-permute-start(f32[16,2048]{1,0:T(8,128)S(1)} %get-tuple-element.48), channel_id=1, source_target_pairs={{0,3},{4,7},{9,8},{13,12},{18,17},{22,21},{27,26},{31,30}} | collective-permute-start | bytes 393224 | tf_op jit(solution)/shard_map/ppermute | solution.py:343
  49.1 2.4 %collective-permute-start.6 = (f32[16,2048]{1,0:T(8,128)S(1)}, f32[16,2048]{1,0:T(8,128)S(1)}, u32[]{:S(2)}, u32[]{:S(2)}) collective-permute-start(f32[16,2048]{1,0:T(8,128)S(1)} %get-tuple-element.47), channel_id=1, source_target_pairs={{0,2},{4,6},{9,11},{13,15},{18,16},{22,20},{27,25},{31,29}} | collective-permute-start | bytes 393224 | tf_op jit(solution)/shard_map/ppermute | solution.py:343
  51.6 1.3 %collective-permute-start.4 = (f32[16,2048]{1,0:T(8,128)S(1)}, f32[16,2048]{1,0:T(8,128)S(1)}, u32[]{:S(2)}, u32[]{:S(2)}) collective-permute-start(f32[16,2048]{1,0:T(8,128)S(1)} %get-tuple-element.46), channel_id=1, source_target_pairs={{0,1},{4,5},{9,10},{13,14},{18,19},{22,23},{27,24},{31,28}} | collective-permute-start | bytes 393224 | tf_op jit(solution)/shard_map/ppermute | solution.py:343
  53.0 0.0 copy-done.1
  53.0 0.0 copy-done.3
  53.0 0.0 copy-done.5
  53.0 0.0 copy-start.6
  53.0 14.4 %prompt_layer.1 = bf16[2,256,4096]{2,1,0:T(8,128)(2,1)} custom-call(bf16[2,256,4096]{2,1,0:T(8,128)(2,1)S(1)} %copy-done.1, f32[2,64,256]{2,1,0:T(8,128)S(1)} %copy-done.3, bf16[2,2,16,256]{3,2,1,0:T(8,128)(2,1)S(1)} %copy-done.5, f32[2,16,4096]{2,1,0:T(8,128)S(1)} %pad_maximum_fusion.refs_3_), custom_call_target="tpu_custom_call" | custom-call | flops 4831838208 | bytes 8388608 | tf_op jit(solution)/shard_map/prompt_layer/pallas_call | solution.py:237
  67.4 0.0 collective-permute-done.7
  67.4 0.0 collective-permute-done.6
  67.5 0.0 collective-permute-done.4
  67.5 0.0 copy-done.6
  67.5 4.2 %branch_finish.1 = bf16[2,512,2048]{2,1,0:T(8,128)(2,1)} custom-call(s32[2]{0:T(128)S(1)} %copy-done.6, f32[2,512,2048]{2,1,0:T(8,128)S(1)} %get-tuple-element.35.own_ref, bf16[2,512,512]{2,1,0:T(8,128)(2,1)S(1)} %get-tuple-element.36.reach_ref, f32[16,2048]{1,0:T(8,128)S(1)} %fusion.3.start_ref), custom_call_target="tpu_custom_call" | custom-call | flops 536870912 | bytes 12582912 | tf_op jit(solution)/shard_map/branch_finish/pallas_call | solution.py:275
  (22 shorter events, 0.5 us)
Async XLA Ops:
  0.6 21.9 %copy-start.2 = (f32[2,32,512]{2,1,0:T(8,128)S(1)}, f32[2,32,512]{2,1,0:T(8,128)}, u32[]{:S(2)}) copy-start(f32[2,32,512]{2,1,0:T(8,128)} %refs_1_.4) | copy-start | bytes 393220
  0.6 21.9 %copy-start.4 = (bf16[2,2,16,512]{3,2,1,0:T(8,128)(2,1)S(1)}, bf16[2,2,16,512]{3,2,1,0:T(8,128)(2,1)}, u32[]{:S(2)}) copy-start(bf16[2,2,16,512]{3,2,1,0:T(8,128)(2,1)} %refs_2_.4) | copy-start | bytes 196612
  11.4 5.9 %collective-permute-start = (f32[34,2048]{1,0:T(8,128)S(1)}, f32[34,2048]{1,0:T(8,128)S(1)}, u32[]{:S(2)}, u32[]{:S(2)}) collective-permute-start(f32[34,2048]{1,0:T(8,128)S(1)} %pad_maximum_fusion.1), channel_id=1, source_target_pairs={{0,4},{4,0},{8,12},{12,8},{16,20},{20,16},{24,28},{28,24},{1,5},{5... | collective-permute-start | bytes 835592 | tf_op jit(solution)/shard_map/ppermute | solution.py:294
  11.9 9.2 %collective-permute-start.3 = (s32[1]{0:T(128)}, s32[1]{0:T(128)}, u32[]{:S(2)}, u32[]{:S(2)}) collective-permute-start(s32[1]{0:T(128)} %param.14), channel_id=1, source_target_pairs={{1,0},{2,1},{3,2},{0,3},{5,4},{6,5},{7,6},{4,7},{9,8},{10,9},{11,1... | collective-permute-start | bytes 20 | tf_op jit(solution)/shard_map/ppermute | solution.py:322
  19.5 13.0 %collective-permute-start.1 = (f32[34,2048]{1,0:T(8,128)S(1)}, f32[34,2048]{1,0:T(8,128)S(1)}, u32[]{:S(2)}, u32[]{:S(2)}) collective-permute-start(f32[34,2048]{1,0:T(8,128)S(1)} %pad_maximum_fusion.2), channel_id=1, source_target_pairs={{0,8},{4,12},{8,0},{12,4},{16,24},{20,28},{24,16},{28,20},{1,9},{5... | collective-permute-start | bytes 835592 | tf_op jit(solution)/shard_map/ppermute | solution.py:294
  21.8 12.5 %collective-permute-start.5 = (s32[2]{0:T(128)S(1)}, s32[2]{0:T(128)S(1)}, u32[]{:S(2)}, u32[]{:S(2)}) collective-permute-start(s32[2]{0:T(128)S(1)} %pad_add_fusion), channel_id=1, source_target_pairs={{2,0},{3,1},{0,2},{1,3},{6,4},{7,5},{4,6},{5,7},{10,8},{11,9},{8,1... | collective-permute-start | bytes 32 | tf_op jit(solution)/shard_map/ppermute | solution.py:322
  22.5 2.2 %copy-start = (bf16[2,512,2048]{2,1,0:T(8,128)(2,1)S(1)}, bf16[2,512,2048]{2,1,0:T(8,128)(2,1)}, u32[]{:S(2)}) copy-start(bf16[2,512,2048]{2,1,0:T(8,128)(2,1)} %refs_0_.2) | copy-start | bytes 12582916
  32.7 11.4 %collective-permute-start.2 = (f32[34,2048]{1,0:T(8,128)S(1)}, f32[34,2048]{1,0:T(8,128)S(1)}, u32[]{:S(2)}, u32[]{:S(2)}) collective-permute-start(f32[34,2048]{1,0:T(8,128)S(1)} %pad_maximum_fusion.3), channel_id=1, source_target_pairs={{0,16},{4,20},{8,24},{12,28},{16,0},{20,4},{24,8},{28,12},{1,17},{... | collective-permute-start | bytes 835592 | tf_op jit(solution)/shard_map/ppermute | solution.py:294
  36.3 7.9 %copy-start.7 = (f32[2,16,4096]{2,1,0:T(8,128)S(1)}, f32[2,16,4096]{2,1,0:T(8,128)}, u32[]{:S(2)}) copy-start(f32[2,16,4096]{2,1,0:T(8,128)} %get-tuple-element.21) | copy-start | bytes 1572868
  44.1 8.9 %copy-start.1 = (bf16[2,256,4096]{2,1,0:T(8,128)(2,1)S(1)}, bf16[2,256,4096]{2,1,0:T(8,128)(2,1)}, u32[]{:S(2)}) copy-start(bf16[2,256,4096]{2,1,0:T(8,128)(2,1)} %refs_0_.3) | copy-start | bytes 12582916
  44.1 8.9 %copy-start.3 = (f32[2,64,256]{2,1,0:T(8,128)S(1)}, f32[2,64,256]{2,1,0:T(8,128)}, u32[]{:S(2)}) copy-start(f32[2,64,256]{2,1,0:T(8,128)} %refs_1_.5) | copy-start | bytes 393220
  44.1 8.9 %copy-start.5 = (bf16[2,2,16,256]{3,2,1,0:T(8,128)(2,1)S(1)}, bf16[2,2,16,256]{3,2,1,0:T(8,128)(2,1)}, u32[]{:S(2)}) copy-start(bf16[2,2,16,256]{3,2,1,0:T(8,128)(2,1)} %refs_2_.5) | copy-start | bytes 98308
  44.3 1.6 %collective-permute-start.8 = (f32[2,16,2048]{2,1,0:T(8,128)S(1)}, f32[2,16,2048]{2,1,0:T(8,128)S(1)}, u32[]{:S(2)}, u32[]{:S(2)}) collective-permute-start(f32[2,16,2048]{2,1,0:T(8,128)S(1)} %fusion.1), channel_id=1, source_target_pairs={{0,4},{4,0},{8,12},{12,8},{16,20},{20,16},{24,28},{28,24},{1,5},{5... | collective-permute-start | bytes 786440 | tf_op jit(solution)/shard_map/ppermute | solution.py:294
  46.1 21.4 %collective-permute-start.7 = (f32[16,2048]{1,0:T(8,128)S(1)}, f32[16,2048]{1,0:T(8,128)S(1)}, u32[]{:S(2)}, u32[]{:S(2)}) collective-permute-start(f32[16,2048]{1,0:T(8,128)S(1)} %get-tuple-element.48), channel_id=1, source_target_pairs={{0,3},{4,7},{9,8},{13,12},{18,17},{22,21},{27,26},{31,30}} | collective-permute-start | bytes 393224 | tf_op jit(solution)/shard_map/ppermute | solution.py:343
  49.1 18.3 %collective-permute-start.6 = (f32[16,2048]{1,0:T(8,128)S(1)}, f32[16,2048]{1,0:T(8,128)S(1)}, u32[]{:S(2)}, u32[]{:S(2)}) collective-permute-start(f32[16,2048]{1,0:T(8,128)S(1)} %get-tuple-element.47), channel_id=1, source_target_pairs={{0,2},{4,6},{9,11},{13,15},{18,16},{22,20},{27,25},{31,29}} | collective-permute-start | bytes 393224 | tf_op jit(solution)/shard_map/ppermute | solution.py:343
  51.6 15.9 %collective-permute-start.4 = (f32[16,2048]{1,0:T(8,128)S(1)}, f32[16,2048]{1,0:T(8,128)S(1)}, u32[]{:S(2)}, u32[]{:S(2)}) collective-permute-start(f32[16,2048]{1,0:T(8,128)S(1)} %get-tuple-element.46), channel_id=1, source_target_pairs={{0,1},{4,5},{9,10},{13,14},{18,19},{22,23},{27,24},{31,28}} | collective-permute-start | bytes 393224 | tf_op jit(solution)/shard_map/ppermute | solution.py:343
  53.0 14.5 %copy-start.6 = (s32[2]{0:T(128)S(1)}, s32[2]{0:T(128)}, u32[]{:S(2)}) copy-start(s32[2]{0:T(128)} %len_ref.1) | copy-start | bytes 28

commit v3 on v2

v3 whole, which is shorter than its diff:
```python
import functools
import jax
import jax.numpy as jnp
from jax import lax
from jax.experimental import pallas as pl
from jax.experimental.pallas import tpu as pltpu
from jax.sharding import PartitionSpec as P

BLOCK = 256
CHUNK = 32
F32 = jnp.float32
BF16 = jnp.bfloat16
VMEM_LIMIT = 32 * 1024 * 1024


def iota(shape, dim):
    return lax.broadcasted_iota(jnp.int32, shape, dim)


def quotient(index, divisor):
    if divisor & (divisor - 1) == 0:
        return lax.shift_right_logical(index, divisor.bit_length() - 1)
    return lax.div(index, divisor)


def remainder(index, divisor):
    if divisor & (divisor - 1) == 0:
        return index & (divisor - 1)
    return lax.rem(index, divisor)


def exact_dot(a, b):
    return jnp.dot(a, b, preferred_element_type=F32, precision=lax.Precision.HIGHEST)


def gain_of(log_decay):
    z = 2.0 * log_decay
    series = 1.0 + z * (1.0 / 9.0)
    for k in (8, 7, 6, 5, 4, 3, 2):
        series = 1.0 + z * (1.0 / k) * series
    small = -z * series
    large = 1.0 - jnp.exp(z)
    return jnp.sqrt(jnp.maximum(jnp.where(z > -0.5, small, large), 0.0))


def hi_lo(value):
    high = value.astype(BF16).astype(F32)
    return jnp.concatenate([high, value - high], axis=0)


def in_hbm(array):
    return pltpu.with_memory_space_constraint(array, pltpu.HBM)


def split_dot(rows, one_hot):
    count = rows.shape[0]
    high = rows.astype(BF16).astype(F32)
    middle = (rows - high).astype(BF16).astype(F32)
    parts = jnp.concatenate([high, middle, rows - high - middle], axis=0).astype(BF16)
    out = jnp.dot(parts, one_hot, preferred_element_type=F32)
    return out[:count] + out[count:2 * count] + out[2 * count:]


def ends_kernel(
    x_ref, ld_in, bc_in, end_ref, log_ref, ld_ref, b_ref, held_ref, push_ref, sems, first_sems, *, width, lanes
):
    first_copies = [
        pltpu.make_async_copy(ld_in, ld_ref, first_sems.at[0]),
        pltpu.make_async_copy(bc_in.at[0], b_ref, first_sems.at[1]),
    ]
    for copy in first_copies:
        copy.start()
    count, heads, positions = ld_ref.shape
    state = end_ref.shape[1]
    channels = end_ref.shape[2]
    tiles = channels // lanes
    copies = {}
    for i in range(count):
        for j in range(tiles):
            cols = pl.ds(j * lanes, lanes)
            copies[i, j] = pltpu.make_async_copy(
                x_ref.at[i, :, cols], held_ref.at[i, :, cols], sems.at[i, j])
            copies[i, j].start()
    for copy in first_copies:
        copy.wait()
    logs = jnp.concatenate([ld_ref[i] for i in range(count)], axis=0)
    after = jnp.where(iota((positions, 1), 0) > iota((1, positions), 1), 1.0, 0.0)
    to_end = jnp.exp(exact_dot(logs, after)) * gain_of(logs)
    for i in range(count):
        b_rows = b_ref[i].astype(F32)
        push = b_rows[None, :, :] * to_end[i * heads:(i + 1) * heads][:, None, :]
        push_ref[i] = push.reshape(heads * state, positions).astype(BF16)
    group = 256 // width
    lane_head = quotient(iota((1, 256), 1), width)
    for i in range(count):
        totals = lax.dot_general(
            jnp.ones((16, positions), F32), ld_ref[i], (((1,), (1,)), ((), ())),
            preferred_element_type=F32, precision=lax.Precision.HIGHEST)
        for j in range(tiles):
            cols = pl.ds(j * lanes, lanes)
            pick = iota((heads, 1), 0) == quotient(iota((1, lanes), 1), width) + j * (lanes // width)
            log_ref[i, :, cols] = split_dot(totals, jnp.where(pick, 1.0, 0.0).astype(BF16))[:8]
    for i in range(count):
        for j in range(tiles):
            copies[i, j].wait()
            for g in range(lanes // 256):
                first = j * (lanes // width) + g * group
                cols = pl.ds(j * lanes + g * 256, 256)
                both = jnp.dot(
                    push_ref[i, pl.ds(first * state, group * state), :], held_ref[i, :, cols],
                    preferred_element_type=F32)
                end = jnp.where(lane_head == 0, both[:state], 0.0)
                for k in range(1, group):
                    end = jnp.where(lane_head == k, both[k * state:(k + 1) * state], end)
                end_ref[i, :, cols] = end


def local_ends(x, logdec, bc):
    count, positions, channels = x.shape
    heads, state = logdec.shape[1], bc.shape[2]
    width = channels // heads
    lanes = min(1024, channels)
    whole = pl.BlockSpec(memory_space=pltpu.VMEM)
    return pl.pallas_call(
        functools.partial(ends_kernel, width=width, lanes=lanes),
        in_specs=[pl.BlockSpec(memory_space=pltpu.HBM)] * 3,
        out_specs=[whole, whole],
        out_shape=[
            jax.ShapeDtypeStruct((count, state, channels), F32),
            jax.ShapeDtypeStruct((count, 8, channels), F32),
        ],
        scratch_shapes=[
            pltpu.VMEM(logdec.shape, F32),
            pltpu.VMEM(bc.shape[1:], BF16),
            pltpu.VMEM(x.shape, BF16),
            pltpu.VMEM((count, heads * state, positions), BF16),
            pltpu.SemaphoreType.DMA((count, channels // lanes)),
            pltpu.SemaphoreType.DMA((2,)),
        ],
        compiler_params=pltpu.CompilerParams(vmem_limit_bytes=VMEM_LIMIT),
        cost_estimate=pl.CostEstimate(
            flops=2 * 64 * x.size, bytes_accessed=2 * x.size, transcendentals=0),
        name="local_ends",
    )(in_hbm(x), in_hbm(logdec), in_hbm(bc))


def prepare(parts, logs, w_ref, lb_ref, lc_ref, state):
    size = logs.shape[1]
    heads = logs.shape[0] // len(parts)
    chunks = size // CHUNK
    half = CHUNK // 2
    src, dst = iota((size, 1), 0), iota((1, size), 1)
    middle = quotient(dst, CHUNK) * CHUNK + half - 1
    plus = (src > middle) & (src <= dst)
    minus = (src > dst) & (src <= middle)
    offset = exact_dot(logs, jnp.where(plus, 1.0, jnp.where(minus, -1.0, 0.0)))
    row_scale = jnp.exp(offset)
    in_scale = jnp.exp(-offset) * gain_of(logs)
    span = iota((1, 128), 1) == quotient(src + half, CHUNK)
    steps = jnp.exp(exact_dot(logs, jnp.where(span, 1.0, 0.0)))
    rows = state * chunks
    mine = quotient(iota((rows, 1), 0), state) == quotient(dst, CHUNK)
    keep = (dst <= src) & (quotient(dst, CHUNK) == quotient(src, CHUNK))
    for i, (b_rows, c_rows) in enumerate(parts):
        here = slice(i * heads, (i + 1) * heads)
        w_ref[i, pl.ds(0, size), :] = hi_lo(in_scale[here]).T.astype(BF16)
        w_ref[i, pl.ds(size, 16), :] = hi_lo(steps[here]).T[:16].astype(BF16)
        w_ref[i, pl.ds(size + 16, size), :] = hi_lo(row_scale[here]).T.astype(BF16)
        scores = lax.dot_general(c_rows, b_rows, (((0,), (0,)), ((), ())), preferred_element_type=F32)
        lc_ref[i, :, pl.ds(0, size)] = jnp.where(keep, scores, 0.0).astype(BF16)
        c_all = jnp.concatenate([c_rows.astype(F32)] * chunks, axis=0)
        lc_ref[i, :, pl.ds(size, rows)] = jnp.where(mine, c_all, 0.0).T.astype(BF16)
        b_all = jnp.concatenate([b_rows.astype(F32)] * chunks, axis=0)
        lb_ref[i] = jnp.where(mine, b_all, 0.0).astype(BF16)


def layer_kernel(*refs, width, has_start, with_reach, skip, lanes):
    x_ref, ld_ref, bc_ref = refs[:3]
    refs = refs[3 + skip:]
    if has_start:
        start_ref, refs = refs[0], refs[1:]
    y_ref, refs = refs[0], refs[1:]
    if with_reach:
        reach_ref, refs = refs[0], refs[1:]
    w_ref, lb_ref, lc_ref, hot_ref, s_ref = refs
    sequence, block, tile = pl.program_id(0), pl.program_id(1), pl.program_id(2)
    count, heads, positions = ld_ref.shape
    state, size = bc_ref.shape[2], x_ref.shape[1]
    blocks, chunks = positions // size, size // CHUNK
    channels = hot_ref.shape[1]

    @pl.when((sequence == 0) & (block == 0) & (tile == 0))
    def _():
        cuts = [(i, pl.ds(b * size, size)) for i in range(count) for b in range(blocks)]
        logs = jnp.concatenate([ld_ref[i, :, cut] for i, cut in cuts], axis=0)
        parts = [(bc_ref[0, i, :, cut], bc_ref[1, i, :, cut]) for i, cut in cuts]
        prepare(parts, logs, w_ref, lb_ref, lc_ref, state)
        row_head = remainder(iota((2 * heads, 1), 0), heads)
        for g in range(channels // 256):
            lane_head = quotient(iota((1, 256), 1), width) + g * (256 // width)
            hot_ref[:, pl.ds(g * 256, 256)] = jnp.where(row_head == lane_head, 1.0, 0.0).astype(BF16)
        if with_reach:
            upto = jnp.where(iota((size, 1), 0) <= iota((1, size), 1), 1.0, 0.0)
            runs = exact_dot(logs, upto)
            for k, (i, cut) in enumerate(cuts):
                run = runs[k * heads:(k + 1) * heads]
                if k % blocks:
                    run = run + entered
                entered = run[:, size - 1:size]
                reach = parts[k][1].astype(F32)[None, :, :] * jnp.exp(run)[:, None, :]
                reach_ref[i, cut, :] = reach.reshape(heads * state, size).T.astype(BF16)

    at = sequence * blocks + block
    tiles = lanes // 256
    scaled, steps, carries, ones = {}, {}, {}, {}

    def scale(g):
        ones[g] = hot_ref[:, pl.ds(pl.multiple_of(tile * lanes + g * 256, 256), 256)]
        wide = jnp.dot(w_ref[at, pl.ds(0, size + 16), :], ones[g], preferred_element_type=F32)
        steps[g] = wide[size:]
        scaled[g] = (x_ref[0, :, pl.ds(g * 256, 256)].astype(F32) * wide[:size]).astype(BF16)

    def pass_on(g):
        local = jnp.dot(lb_ref[at], scaled[g], preferred_element_type=F32)
        if has_start:
            entering = start_ref[0, :, pl.ds(g * 256, 256)]
        else:
            entering = jnp.zeros((state, 256), F32)
        if blocks > 1:
            here = pl.ds(pl.multiple_of(tile * lanes + g * 256, 256), 256)
            entering = jnp.where(block == 0, entering, s_ref[:, here])
        carry = steps[g][0:1] * entering
        rows = []
        for c in range(chunks):
            rows.append(carry.astype(BF16))
            if c < chunks - 1 or blocks > 1:
                carry = steps[g][c + 1:c + 2] * (carry + local[c * state:(c + 1) * state])
        if blocks > 1:
            s_ref[:, here] = carry
        carries[g] = jnp.concatenate(rows, axis=0)

    def give(g):
        both = jnp.concatenate([scaled[g], carries[g]], axis=0)
        out = jnp.dot(lc_ref[at], both, preferred_element_type=F32)
        rows = jnp.dot(w_ref[at, pl.ds(size + 16, size), :], ones[g], preferred_element_type=F32)
        y_ref[0, :, pl.ds(g * 256, 256)] = (out * rows).astype(y_ref.dtype)

    for g in range(tiles + 2):
        if g < tiles:
            scale(g)
        if 0 <= g - 1 < tiles:
            pass_on(g - 1)
        if 0 <= g - 2:
            give(g - 2)


def layer(x, logdec, bc, start, out_type, with_reach, name, which=None, into=()):
    count, positions, channels = x.shape
    heads, state = logdec.shape[1], bc.shape[2]
    width = channels // heads
    lanes = min(1024, channels)
    blocks = positions // BLOCK
    rows = BLOCK // CHUNK * state
    kernel = functools.partial(
        layer_kernel, width=width, has_start=start is not None, with_reach=with_reach,
        skip=len(into), lanes=lanes)
    base = 0 if which is None else which
    sequences = count if which is None else 1
    in_specs = [
        pl.BlockSpec((1, BLOCK, lanes), lambda i, b, j: (i + base, b, j)),
        pl.BlockSpec((sequences, heads, positions), lambda i, b, j: (base, 0, 0)),
        pl.BlockSpec((2, sequences, state, positions), lambda i, b, j: (0, base, 0, 0)),
    ]
    args = [in_hbm(x), logdec, bc, *into]
    in_specs += [pl.BlockSpec(memory_space=pl.ANY)] * len(into)
    if start is not None:
        in_specs.append(pl.BlockSpec((1, state, lanes), lambda i, b, j: (i, 0, j)))
        args.append(start)
    out_specs = [pl.BlockSpec((1, BLOCK, lanes), lambda i, b, j: (i + base, b, j))]
    out_shape = [jax.ShapeDtypeStruct(x.shape, out_type)]
    if with_reach:
        out_specs.append(pl.BlockSpec((sequences, positions, heads * state), lambda i, b, j: (base, 0, 0)))
        out_shape.append(jax.ShapeDtypeStruct((count, positions, heads * state), BF16))
    cuts = sequences * blocks
    work = sequences * positions * channels
    return pl.pallas_call(
        kernel,
        grid=(sequences, blocks, channels // lanes),
        in_specs=in_specs,
        out_specs=out_specs,
        out_shape=out_shape,
        scratch_shapes=[
            pltpu.VMEM((cuts, 2 * BLOCK + 16, 2 * heads), BF16),
            pltpu.VMEM((cuts, rows, BLOCK), BF16),
            pltpu.VMEM((cuts, BLOCK, BLOCK + rows), BF16),
            pltpu.VMEM((2 * heads, channels), BF16),
            pltpu.VMEM((state, channels), F32),
        ],
        input_output_aliases={3 + i: i for i in range(len(into))},
        compiler_params=pltpu.CompilerParams(vmem_limit_bytes=VMEM_LIMIT),
        cost_estimate=pl.CostEstimate(
            flops=2 * 1152 * work, bytes_accessed=4 * work, transcendentals=0),
        name=name,
    )(*args)


def finish_kernel(len_ref, own_ref, reach_ref, start_ref, y_ref, *, width):
    branch, tile = pl.program_id(0), pl.program_id(1)
    positions, lanes = y_ref.shape[1], y_ref.shape[2]
    state = start_ref.shape[0]
    group = 128 // state
    span = group * width
    live = iota((positions, span), 0) < len_ref[branch]
    own_head = quotient(iota((128, 1), 0), state) == quotient(iota((1, span), 1), width)
    for g in range(lanes // span):
        here = pl.ds(pl.multiple_of(tile * lanes + g * span, span), span)
        first = pl.ds(pl.multiple_of((tile * (lanes // span) + g) * 128, 128), 128)
        start = jnp.concatenate([start_ref[:, here]] * group, axis=0)
        start = jnp.where(own_head, start, 0.0).astype(BF16)
        term = jnp.dot(reach_ref[branch, :, first], start, preferred_element_type=F32)
        out = jnp.where(live, own_ref[branch, :, here] + term, 0.0)
        y_ref[0, :, pl.ds(g * span, span)] = out.astype(BF16)


def finish(lengths, own, reach, start):
    count, positions, channels = own.shape
    width = channels * start.shape[0] // reach.shape[2]
    lanes = min(1024, channels)
    whole = pl.BlockSpec(memory_space=pltpu.VMEM)
    return pl.pallas_call(
        functools.partial(finish_kernel, width=width),
        grid=(count, channels // lanes),
        in_specs=[pl.BlockSpec(memory_space=pltpu.SMEM), whole, whole, whole],
        out_specs=pl.BlockSpec((1, positions, lanes), lambda i, j: (i, 0, j)),
        out_shape=jax.ShapeDtypeStruct(own.shape, BF16),
        compiler_params=pltpu.CompilerParams(vmem_limit_bytes=VMEM_LIMIT),
        cost_estimate=pl.CostEstimate(
            flops=2 * 128 * own.size, bytes_accessed=6 * own.size, transcendentals=0),
        name="branch_finish",
    )(lengths, own, reach, start)


def swap_bit(value, bit, size):
    return lax.ppermute(value, "ctx", [(k, k ^ bit) for k in range(size)])


def pack(states, logs):
    lanes = states.shape[-1]
    return jnp.concatenate([states.reshape(-1, lanes), logs.reshape(-1, lanes)], axis=0)


def unpack(packed, count):
    lanes = packed.shape[-1]
    rows = packed.shape[0] - count
    return packed[:rows].reshape(count, rows // count, lanes), packed[rows:].reshape(count, 1, lanes)


def in_order(upper, mine, other):
    first = [jnp.where(upper, o, m) for m, o in zip(mine, other)]
    second = [jnp.where(upper, m, o) for m, o in zip(mine, other)]
    return first, second


def join(first, second):
    return jnp.exp(second[1]) * first[0] + second[0], first[1] + second[1]


def branch_prompts(chosen, pair_size):
    known = chosen
    while known.shape[0] < pair_size:
        step = known.shape[0]
        further = lax.ppermute(known, "pair", [((z + step) % pair_size, z) for z in range(pair_size)])
        known = jnp.concatenate([known, further])
    return known


def branch_start(total, wanted, ctx_size, pair_size):
    ctx, pair = lax.axis_index("ctx"), lax.axis_index("pair")
    owner = ctx * pair_size // ctx_size

    def pick(which):
        out = total[0]
        for i in range(1, total.shape[0]):
            out = jnp.where(which == i, total[i], out)
        return out

    parts = [jnp.where(pair == owner, pick(wanted[0]), 0.0)]
    for hop in range(1, pair_size):
        links = []
        for k in range(ctx_size):
            z = k * pair_size // ctx_size
            links.append((k * pair_size + z, k * pair_size + (z + hop) % pair_size))
        parts.append(lax.ppermute(pick(wanted[hop]), ("ctx", "pair"), links))
    return sum(parts)


def body(
    prompt_x,
    prompt_bc,
    prompt_logdec,
    branch_x,
    branch_bc,
    branch_logdec,
    branch_prompt,
    branch_len,
):
    size, pair_size = lax.axis_size("ctx"), lax.axis_size("pair")
    prompts, branches = prompt_x.shape[0], branch_x.shape[0]
    assert size == 2 * pair_size and size & (size - 1) == 0 and branch_prompt.shape[0] == 1
    mine = lax.axis_index("ctx")
    odd = (mine & 1) == 1
    wanted = branch_prompts(branch_prompt, pair_size)

    end, log = local_ends(prompt_x, prompt_logdec, prompt_bc)
    half = end.shape[2] // 2
    low, high = (end[:, :, :half], log[:, :1, :half]), (end[:, :, half:], log[:, :1, half:])
    keep = [jnp.where(odd, h, l) for l, h in zip(low, high)]
    send = [jnp.where(odd, l, h) for l, h in zip(low, high)]
    got = unpack(swap_bit(pack(*send), 1, size), prompts)
    first, second = in_order(odd, keep, got)
    total, total_log = join(first, second)
    before, before_log = jnp.zeros_like(total), jnp.zeros_like(total_log)

    own = ()
    works = iter(range(branches))
    bit = 2
    while bit < size:
        packed = pack(total, total_log)
        which = next(works, None)
        if which is not None:
            packed, branch_x = lax.optimization_barrier((packed, branch_x))
        got = swap_bit(packed, bit, size)
        if which is not None:
            own = layer(branch_x, branch_logdec, branch_bc, None, F32, True, "branch_own", which, own)
            got, own = lax.optimization_barrier((got, own))
        other = unpack(got, prompts)
        upper = (mine & bit) != 0
        before = jnp.where(upper, jnp.exp(before_log) * other[0] + before, before)
        before_log = jnp.where(upper, before_log + other[1], before_log)
        total, total_log = join(*in_order(upper, (total, total_log), other))
        bit *= 2
    for which in works:
        own = layer(branch_x, branch_logdec, branch_bc, None, F32, True, "branch_own", which, own)

    next_before = jnp.exp(first[1]) * before + first[0]
    got = swap_bit(jnp.where(odd, before, next_before), 1, size)
    keep = jnp.where(odd, next_before, before)
    entering = jnp.concatenate([jnp.where(odd, got, keep), jnp.where(odd, keep, got)], axis=2)
    start = branch_start(total, wanted, size, pair_size)
    (prompt_y,) = layer(prompt_x, prompt_logdec, prompt_bc, entering, BF16, False, "prompt_layer")
    start, prompt_y = lax.optimization_barrier((start, prompt_y))
    branch_y = finish(branch_len, *own, start)
    return prompt_y, branch_y


def solution(mesh):
    return jax.shard_map(
        body,
        mesh=mesh,
        in_specs=(
            P(None, "ctx", "pair"),
            P(None, None, None, "ctx"),
            P(None, "pair", "ctx"),
            P("pair", None, "ctx"),
            P(None, "pair", None, None),
            P("pair", "ctx", None),
            P("pair"),
            P("pair"),
        ),
        out_specs=(P(None, "ctx", "pair"), P("pair", None, "ctx")),
        check_vma=False,
    )
```

time: 72.1 us -> 55.4 us (0.77)
  Pallas kernels: 42.8 us -> 31.6 us
  other arithmetic: 5.46 us -> 1.41 us
  local copies, waits for them, and re-layouts: 3.01 us -> 0.76 us
  waiting for transfers between devices: 1.49 us -> 2.29 us
    pallas_call x3, Pallas kernels: 30 us -> 22.9 us  [layer(): pl.pallas_call(kernel, grid=(sequences, blocks, channels // lanes), in_sp...]
    pallas_call x2, Pallas kernels: 12.8 us -> 8.73 us  [the longest x1 4.91 us: local_ends(): pl.pallas_call(functools.partial(ends_kernel, width=width, lanes=lanes),...]
    unnamed x22 -> x16, local copies, waits for them, and re-layouts: 2.29 us -> 0.1 us
    select_n x2, other arithmetic: 2.04 us -> 0.05 us  [body(): send = [jnp.where(odd, l, h) for l, h in zip(low, high)]]
    add x3, other arithmetic: 1.16 us -> 0.13 us  [join(): return (jnp.exp(second[1]) * first[0] + second[0], first[1] + second[1])]
    exp x1, other arithmetic: 1.02 us -> 0.05 us  [body(): next_before = jnp.exp(first[1]) * before + first[0]]
    ppermute x4, waiting for transfers between devices: 1.47 us -> 2.28 us  [swap_bit(): return lax.ppermute(value, 'ctx', [(k, k ^ bit) for k in range(size)])]
  transfers between devices with their start and end apart: 9 -> 9, of which waited for: 1 -> 2; matrix products, arithmetic and copies ran while one was open for 5% -> 3% of each run, Pallas kernels for 42% -> 42%
where the time goes in v3:
time: 55.4 us; the launch traced here: 54.9 us
  Pallas kernels  31.6 us (57%)
  starting transfers between devices  15.2 us (27%)
  between operations  3.64 us (7%)
  waiting for transfers between devices  2.29 us (4%)
  other arithmetic  1.41 us (3%)
  local copies, waits for them, and re-layouts  0.76 us (1%)
    pallas_call x3, Pallas kernels, layer(): pl.pallas_call(kernel, grid=(sequences, blocks, channels // lanes), in_sp...  22.9 us
    ppermute x3, starting transfers between devices, branch_start(): parts.append(lax.ppermute(pick(wanted[hop]), ('ctx', 'pair'), links))  6.54 us
    ppermute x2, starting transfers between devices, branch_prompts(): lax.ppermute(known, 'pair', [((z + step) % pair_size, z) for z in range(p...  4.92 us
    pallas_call x1, Pallas kernels, local_ends(): pl.pallas_call(functools.partial(ends_kernel, width=width, lanes=lanes),...  4.91 us
    pallas_call x1, Pallas kernels, finish(): pl.pallas_call(functools.partial(finish_kernel, width=width), grid=(count...  3.82 us
    ppermute x4, starting transfers between devices, swap_bit(): return lax.ppermute(value, 'ctx', [(k, k ^ bit) for k in range(size)])  3.73 us
    ppermute x4, waiting for transfers between devices, swap_bit(): return lax.ppermute(value, 'ctx', [(k, k ^ bit) for k in range(size)])  2.28 us
  transfers between devices with their start and end apart: 9, of which 2 were waited for; matrix products, arithmetic and copies ran while one was open for 3% of the time, Pallas kernels for 42%

profile of v3, /device:TPU:0, one launch (start us, length us, event | category | flops | bytes accessed | tf_op | source)
XLA Modules:
  0.0 54.9 jit_solution(1956280060743028525)
XLA Ops:
  0.6 0.0 copy-start
  0.6 0.0 copy-start.2
  0.7 4.9 %local_ends.1 = (f32[2,16,4096]{2,1,0:T(8,128)S(1)}, f32[2,8,4096]{2,1,0:T(8,128)S(1)}) custom-call(bf16[2,256,4096]{2,1,0:T(8,128)(2,1)} %refs_0_.3, f32[2,64,256]{2,1,0:T(8,128)} %refs_1_.5, bf16[2,2,16,256]{3,2,1,0:T(8,128)(2,1)} %refs_2_.5), custom_call_target="tpu_custom_call" | custom-call | flops 268435456 | bytes 4194304 | tf_op jit(solution)/shard_map/local_ends/pallas_call | solution.py:124
  5.7 0.5 collective-permute-start
  6.2 4.7 %collective-permute-start.3 = (s32[1]{0:T(128)}, s32[1]{0:T(128)}, u32[]{:S(2)}, u32[]{:S(2)}) collective-permute-start(s32[1]{0:T(128)} %param.14), channel_id=1, source_target_pairs={{1,0},{2,1},{3,2},{0,3},{5,4},{6,5},{7,6},{4,7},{9,8},{10,9},{11,1... | collective-permute-start | bytes 20 | tf_op jit(solution)/shard_map/ppermute | solution.py:372
  11.6 0.0 collective-permute-done
  11.7 0.1 select_add_fusion.2
  11.8 1.6 %collective-permute-start.1 = (f32[34,2048]{1,0:T(8,128)S(1)}, f32[34,2048]{1,0:T(8,128)S(1)}, u32[]{:S(2)}, u32[]{:S(2)}) collective-permute-start(f32[34,2048]{1,0:T(8,128)S(1)} %pad_maximum_fusion.2), channel_id=1, source_target_pairs={{0,8},{4,12},{8,0},{12,4},{16,24},{20,28},{24,16},{28,20},{1,9},{5... | collective-permute-start | bytes 835592 | tf_op jit(solution)/shard_map/ppermute | solution.py:344
  13.4 0.0 collective-permute-done.3
  13.4 0.7 %pad_add_fusion = s32[2]{0:T(128)S(1)} fusion(s32[1]{0:T(128)} %collective-permute-done.3, s32[1]{0:T(128)S(6)} %copy.33), kind=kLoop, calls=%fused_computation.40 | loop fusion | flops 2 | bytes 16 | tf_op jit(solution)/shard_map/concatenate | solution.py:373
  14.1 0.3 collective-permute-start.5
  15.0 0.0 copy-done
  15.0 0.0 copy-done.2
  15.0 5.9 %branch_own.2 = (f32[2,512,2048]{2,1,0:T(8,128)S(1)}, bf16[2,512,512]{2,1,0:T(8,128)(2,1)S(1)}) custom-call(bf16[2,512,2048]{2,1,0:T(8,128)(2,1)} %refs_0_.2, f32[2,32,512]{2,1,0:T(8,128)S(1)} %copy-done, bf16[2,2,16,512]{3,2,1,0:T(8,128)(2,1)S(1)} %copy-done.2), custom_call_target="tpu_custom_call" | custom-call | flops 2415919104 | bytes 4194304 | tf_op jit(solution)/shard_map/branch_own/pallas_call | solution.py:286
  20.9 0.8 %collective-permute-done.1 = f32[34,2048]{1,0:T(8,128)S(1)} collective-permute-done((f32[34,2048]{1,0:T(8,128)S(1)}, f32[34,2048]{1,0:T(8,128)S(1)}, u32[]{:S(2)}, u32[]{:S(2)}) %collective-permute-start.1) | collective-permute-done | bytes 278560 | tf_op jit(solution)/shard_map/ppermute | solution.py:344
  21.9 1.6 %collective-permute-start.2 = (f32[34,2048]{1,0:T(8,128)S(1)}, f32[34,2048]{1,0:T(8,128)S(1)}, u32[]{:S(2)}, u32[]{:S(2)}) collective-permute-start(f32[34,2048]{1,0:T(8,128)S(1)} %pad_maximum_fusion.3), channel_id=1, source_target_pairs={{0,16},{4,20},{8,24},{12,28},{16,0},{20,4},{24,8},{28,12},{1,17},{... | collective-permute-start | bytes 835592 | tf_op jit(solution)/shard_map/ppermute | solution.py:344
  23.5 0.0 collective-permute-done.5
  23.5 0.6 %fusion.11 = (s32[1]{0:T(128)}, s32[1]{0:T(128)}) fusion(s32[2]{0:T(128)S(1)} %collective-permute-done.5), kind=kLoop, calls=%fused_computation.44 | loop fusion | bytes 16 | tf_op jit(solution)/shard_map/slice | solution.py:393
  25.3 5.9 %branch_own.3 = (f32[2,512,2048]{2,1,0:T(8,128)S(1)}, bf16[2,512,512]{2,1,0:T(8,128)(2,1)S(1)}) custom-call(bf16[2,512,2048]{2,1,0:T(8,128)(2,1)} %refs_0_.2, f32[2,32,512]{2,1,0:T(8,128)S(1)} %copy-done, bf16[2,2,16,512]{3,2,1,0:T(8,128)(2,1)S(1)} %copy-done.2, ...), custom_call_target="tpu_custom_call", output_to_operand_aliasing={{0}: (3, {}), {1}: (4, {})} | custom-call | flops 2415919104 | bytes 4194304 | tf_op jit(solution)/shard_map/branch_own/pallas_call | solution.py:286
  31.2 0.0 copy-start.1
  31.2 0.0 copy-start.3
  31.2 0.0 collective-permute-done.2
  31.3 0.1 fusion.1
  31.4 0.1 collective-permute-start.8
  31.5 1.5 %collective-permute-done.8 = f32[2,16,2048]{2,1,0:T(8,128)S(1)} collective-permute-done((f32[2,16,2048]{2,1,0:T(8,128)S(1)}, f32[2,16,2048]{2,1,0:T(8,128)S(1)}, u32[]{:S(2)}, u32[]{:S(2)}) %collective-permute-start.8) | collective-permute-done | bytes 262176 | tf_op jit(solution)/shard_map/ppermute | solution.py:344
  33.0 0.1 broadcast_select_fusion.1
  33.2 3.9 %collective-permute-start.7 = (f32[16,2048]{1,0:T(8,128)S(1)}, f32[16,2048]{1,0:T(8,128)S(1)}, u32[]{:S(2)}, u32[]{:S(2)}) collective-permute-start(f32[16,2048]{1,0:T(8,128)S(1)} %get-tuple-element.48), channel_id=1, source_target_pairs={{0,3},{4,7},{9,8},{13,12},{18,17},{22,21},{27,26},{31,30}} | collective-permute-start | bytes 393224 | tf_op jit(solution)/shard_map/ppermute | solution.py:393
  37.1 1.3 %collective-permute-start.6 = (f32[16,2048]{1,0:T(8,128)S(1)}, f32[16,2048]{1,0:T(8,128)S(1)}, u32[]{:S(2)}, u32[]{:S(2)}) collective-permute-start(f32[16,2048]{1,0:T(8,128)S(1)} %get-tuple-element.47), channel_id=1, source_target_pairs={{0,2},{4,6},{9,11},{13,15},{18,16},{22,20},{27,25},{31,29}} | collective-permute-start | bytes 393224 | tf_op jit(solution)/shard_map/ppermute | solution.py:393
  38.4 1.3 %collective-permute-start.4 = (f32[16,2048]{1,0:T(8,128)S(1)}, f32[16,2048]{1,0:T(8,128)S(1)}, u32[]{:S(2)}, u32[]{:S(2)}) collective-permute-start(f32[16,2048]{1,0:T(8,128)S(1)} %get-tuple-element.46), channel_id=1, source_target_pairs={{0,1},{4,5},{9,10},{13,14},{18,19},{22,23},{27,24},{31,28}} | collective-permute-start | bytes 393224 | tf_op jit(solution)/shard_map/ppermute | solution.py:393
  39.8 0.0 copy-done.1
  39.8 0.0 copy-done.3
  39.8 0.0 copy-start.4
  39.9 11.1 %prompt_layer.1 = bf16[2,256,4096]{2,1,0:T(8,128)(2,1)} custom-call(bf16[2,256,4096]{2,1,0:T(8,128)(2,1)} %refs_0_.3, f32[2,64,256]{2,1,0:T(8,128)S(1)} %copy-done.1, bf16[2,2,16,256]{3,2,1,0:T(8,128)(2,1)S(1)} %copy-done.3, f32[2,16,4096]{2,1,0:T(8,128)S(1)} %pad_maximum_fusion.refs_3_), custom_call_target="tpu_custom_call" | custom-call | flops 4831838208 | bytes 8388608 | tf_op jit(solution)/shard_map/prompt_layer/pallas_call | solution.py:286
  51.0 0.0 collective-permute-done.7
  51.0 0.0 collective-permute-done.6
  51.0 0.0 collective-permute-done.4
  51.0 0.0 copy-done.4
  51.0 3.8 %branch_finish.1 = bf16[2,512,2048]{2,1,0:T(8,128)(2,1)} custom-call(s32[2]{0:T(128)S(1)} %copy-done.4, f32[2,512,2048]{2,1,0:T(8,128)S(1)} %get-tuple-element.35.own_ref, bf16[2,512,512]{2,1,0:T(8,128)(2,1)S(1)} %get-tuple-element.36.reach_ref, f32[16,2048]{1,0:T(8,128)S(1)} %fusion.3.start_ref), custom_call_target="tpu_custom_call" | custom-call | flops 536870912 | bytes 12582912 | tf_op jit(solution)/shard_map/branch_finish/pallas_call | solution.py:330
  (25 shorter events, 0.6 us)
Async XLA Ops:
  0.6 14.3 %copy-start = (f32[2,32,512]{2,1,0:T(8,128)S(1)}, f32[2,32,512]{2,1,0:T(8,128)}, u32[]{:S(2)}) copy-start(f32[2,32,512]{2,1,0:T(8,128)} %refs_1_.4) | copy-start | bytes 393220
  0.6 14.3 %copy-start.2 = (bf16[2,2,16,512]{3,2,1,0:T(8,128)(2,1)S(1)}, bf16[2,2,16,512]{3,2,1,0:T(8,128)(2,1)}, u32[]{:S(2)}) copy-start(bf16[2,2,16,512]{3,2,1,0:T(8,128)(2,1)} %refs_2_.4) | copy-start | bytes 196612
  5.7 5.9 %collective-permute-start = (f32[34,2048]{1,0:T(8,128)S(1)}, f32[34,2048]{1,0:T(8,128)S(1)}, u32[]{:S(2)}, u32[]{:S(2)}) collective-permute-start(f32[34,2048]{1,0:T(8,128)S(1)} %pad_maximum_fusion.1), channel_id=1, source_target_pairs={{0,4},{4,0},{8,12},{12,8},{16,20},{20,16},{24,28},{28,24},{1,5},{5... | collective-permute-start | bytes 835592 | tf_op jit(solution)/shard_map/ppermute | solution.py:344
  6.2 7.2 %collective-permute-start.3 = (s32[1]{0:T(128)}, s32[1]{0:T(128)}, u32[]{:S(2)}, u32[]{:S(2)}) collective-permute-start(s32[1]{0:T(128)} %param.14), channel_id=1, source_target_pairs={{1,0},{2,1},{3,2},{0,3},{5,4},{6,5},{7,6},{4,7},{9,8},{10,9},{11,1... | collective-permute-start | bytes 20 | tf_op jit(solution)/shard_map/ppermute | solution.py:372
  11.8 9.8 %collective-permute-start.1 = (f32[34,2048]{1,0:T(8,128)S(1)}, f32[34,2048]{1,0:T(8,128)S(1)}, u32[]{:S(2)}, u32[]{:S(2)}) collective-permute-start(f32[34,2048]{1,0:T(8,128)S(1)} %pad_maximum_fusion.2), channel_id=1, source_target_pairs={{0,8},{4,12},{8,0},{12,4},{16,24},{20,28},{24,16},{28,20},{1,9},{5... | collective-permute-start | bytes 835592 | tf_op jit(solution)/shard_map/ppermute | solution.py:344
  14.1 9.4 %collective-permute-start.5 = (s32[2]{0:T(128)S(1)}, s32[2]{0:T(128)S(1)}, u32[]{:S(2)}, u32[]{:S(2)}) collective-permute-start(s32[2]{0:T(128)S(1)} %pad_add_fusion), channel_id=1, source_target_pairs={{2,0},{3,1},{0,2},{1,3},{6,4},{7,5},{4,6},{5,7},{10,8},{11,9},{8,1... | collective-permute-start | bytes 32 | tf_op jit(solution)/shard_map/ppermute | solution.py:372
  21.9 9.4 %collective-permute-start.2 = (f32[34,2048]{1,0:T(8,128)S(1)}, f32[34,2048]{1,0:T(8,128)S(1)}, u32[]{:S(2)}, u32[]{:S(2)}) collective-permute-start(f32[34,2048]{1,0:T(8,128)S(1)} %pad_maximum_fusion.3), channel_id=1, source_target_pairs={{0,16},{4,20},{8,24},{12,28},{16,0},{20,4},{24,8},{28,12},{1,17},{... | collective-permute-start | bytes 835592 | tf_op jit(solution)/shard_map/ppermute | solution.py:344
  31.2 8.6 %copy-start.1 = (f32[2,64,256]{2,1,0:T(8,128)S(1)}, f32[2,64,256]{2,1,0:T(8,128)}, u32[]{:S(2)}) copy-start(f32[2,64,256]{2,1,0:T(8,128)} %refs_1_.5) | copy-start | bytes 393220
  31.2 8.6 %copy-start.3 = (bf16[2,2,16,256]{3,2,1,0:T(8,128)(2,1)S(1)}, bf16[2,2,16,256]{3,2,1,0:T(8,128)(2,1)}, u32[]{:S(2)}) copy-start(bf16[2,2,16,256]{3,2,1,0:T(8,128)(2,1)} %refs_2_.5) | copy-start | bytes 98308
  31.4 1.6 %collective-permute-start.8 = (f32[2,16,2048]{2,1,0:T(8,128)S(1)}, f32[2,16,2048]{2,1,0:T(8,128)S(1)}, u32[]{:S(2)}, u32[]{:S(2)}) collective-permute-start(f32[2,16,2048]{2,1,0:T(8,128)S(1)} %fusion.1), channel_id=1, source_target_pairs={{0,4},{4,0},{8,12},{12,8},{16,20},{20,16},{24,28},{28,24},{1,5},{5... | collective-permute-start | bytes 786440 | tf_op jit(solution)/shard_map/ppermute | solution.py:344
  33.2 17.8 %collective-permute-start.7 = (f32[16,2048]{1,0:T(8,128)S(1)}, f32[16,2048]{1,0:T(8,128)S(1)}, u32[]{:S(2)}, u32[]{:S(2)}) collective-permute-start(f32[16,2048]{1,0:T(8,128)S(1)} %get-tuple-element.48), channel_id=1, source_target_pairs={{0,3},{4,7},{9,8},{13,12},{18,17},{22,21},{27,26},{31,30}} | collective-permute-start | bytes 393224 | tf_op jit(solution)/shard_map/ppermute | solution.py:393
  37.1 13.8 %collective-permute-start.6 = (f32[16,2048]{1,0:T(8,128)S(1)}, f32[16,2048]{1,0:T(8,128)S(1)}, u32[]{:S(2)}, u32[]{:S(2)}) collective-permute-start(f32[16,2048]{1,0:T(8,128)S(1)} %get-tuple-element.47), channel_id=1, source_target_pairs={{0,2},{4,6},{9,11},{13,15},{18,16},{22,20},{27,25},{31,29}} | collective-permute-start | bytes 393224 | tf_op jit(solution)/shard_map/ppermute | solution.py:393
  38.4 12.5 %collective-permute-start.4 = (f32[16,2048]{1,0:T(8,128)S(1)}, f32[16,2048]{1,0:T(8,128)S(1)}, u32[]{:S(2)}, u32[]{:S(2)}) collective-permute-start(f32[16,2048]{1,0:T(8,128)S(1)} %get-tuple-element.46), channel_id=1, source_target_pairs={{0,1},{4,5},{9,10},{13,14},{18,19},{22,23},{27,24},{31,28}} | collective-permute-start | bytes 393224 | tf_op jit(solution)/shard_map/ppermute | solution.py:393
  39.8 11.2 %copy-start.4 = (s32[2]{0:T(128)S(1)}, s32[2]{0:T(128)}, u32[]{:S(2)}) copy-start(s32[2]{0:T(128)} %len_ref.1) | copy-start | bytes 28

commit v4 on v3

v4 whole, which is shorter than its diff:
```python
import functools
import jax
import jax.numpy as jnp
from jax import lax
from jax.experimental import pallas as pl
from jax.experimental.pallas import tpu as pltpu
from jax.sharding import PartitionSpec as P

BLOCK = 256
CHUNK = 32
F32 = jnp.float32
BF16 = jnp.bfloat16
VMEM_LIMIT = 32 * 1024 * 1024


def iota(shape, dim):
    return lax.broadcasted_iota(jnp.int32, shape, dim)


def quotient(index, divisor):
    if divisor & (divisor - 1) == 0:
        return lax.shift_right_logical(index, divisor.bit_length() - 1)
    return lax.div(index, divisor)


def remainder(index, divisor):
    if divisor & (divisor - 1) == 0:
        return index & (divisor - 1)
    return lax.rem(index, divisor)


def exact_dot(a, b):
    return jnp.dot(a, b, preferred_element_type=F32, precision=lax.Precision.HIGHEST)


def gain_of(log_decay):
    z = 2.0 * log_decay
    series = 1.0 + z * (1.0 / 9.0)
    for k in (8, 7, 6, 5, 4, 3, 2):
        series = 1.0 + z * (1.0 / k) * series
    small = -z * series
    large = 1.0 - jnp.exp(z)
    return jnp.sqrt(jnp.maximum(jnp.where(z > -0.5, small, large), 0.0))


def hi_lo(value):
    high = value.astype(BF16).astype(F32)
    return jnp.concatenate([high, value - high], axis=0)


def in_hbm(array):
    return pltpu.with_memory_space_constraint(array, pltpu.HBM)


def split_dot(rows, one_hot):
    count = rows.shape[0]
    high = rows.astype(BF16).astype(F32)
    middle = (rows - high).astype(BF16).astype(F32)
    parts = jnp.concatenate([high, middle, rows - high - middle], axis=0).astype(BF16)
    out = jnp.dot(parts, one_hot, preferred_element_type=F32)
    return out[:count] + out[count:2 * count] + out[2 * count:]


def ends_kernel(
    x_ref, ld_in, bc_in, end_ref, log_ref, held_ref, ld_ref, b_ref, push_ref, sems, first_sems, *, width, lanes
):
    first_copies = [
        pltpu.make_async_copy(ld_in, ld_ref, first_sems.at[0]),
        pltpu.make_async_copy(bc_in.at[0], b_ref, first_sems.at[1]),
    ]
    for copy in first_copies:
        copy.start()
    count, heads, positions = ld_ref.shape
    state = end_ref.shape[1]
    channels = end_ref.shape[2]
    tiles = channels // lanes
    copies = {}
    for i in range(count):
        for j in range(tiles):
            cols = pl.ds(j * lanes, lanes)
            copies[i, j] = pltpu.make_async_copy(
                x_ref.at[i, :, cols], held_ref.at[i, :, cols], sems.at[i, j])
            copies[i, j].start()
    for copy in first_copies:
        copy.wait()
    logs = jnp.concatenate([ld_ref[i] for i in range(count)], axis=0)
    after = jnp.where(iota((positions, 1), 0) > iota((1, positions), 1), 1.0, 0.0)
    to_end = jnp.exp(exact_dot(logs, after)) * gain_of(logs)
    for i in range(count):
        b_rows = b_ref[i].astype(F32)
        push = b_rows[None, :, :] * to_end[i * heads:(i + 1) * heads][:, None, :]
        push_ref[i] = push.reshape(heads * state, positions).astype(BF16)
    group = 256 // width
    lane_head = quotient(iota((1, 256), 1), width)
    for i in range(count):
        totals = lax.dot_general(
            jnp.ones((16, positions), F32), ld_ref[i], (((1,), (1,)), ((), ())),
            preferred_element_type=F32, precision=lax.Precision.HIGHEST)
        for j in range(tiles):
            cols = pl.ds(j * lanes, lanes)
            pick = iota((heads, 1), 0) == quotient(iota((1, lanes), 1), width) + j * (lanes // width)
            log_ref[i, :, cols] = split_dot(totals, jnp.where(pick, 1.0, 0.0).astype(BF16))[:8]
    for i in range(count):
        for j in range(tiles):
            copies[i, j].wait()
            for g in range(lanes // 256):
                first = j * (lanes // width) + g * group
                cols = pl.ds(j * lanes + g * 256, 256)
                both = jnp.dot(
                    push_ref[i, pl.ds(first * state, group * state), :], held_ref[i, :, cols],
                    preferred_element_type=F32)
                end = jnp.where(lane_head == 0, both[:state], 0.0)
                for k in range(1, group):
                    end = jnp.where(lane_head == k, both[k * state:(k + 1) * state], end)
                end_ref[i, :, cols] = end


def local_ends(x, logdec, bc):
    count, positions, channels = x.shape
    heads, state = logdec.shape[1], bc.shape[2]
    width = channels // heads
    lanes = min(1024, channels)
    whole = pl.BlockSpec(memory_space=pltpu.VMEM)
    return pl.pallas_call(
        functools.partial(ends_kernel, width=width, lanes=lanes),
        in_specs=[pl.BlockSpec(memory_space=pltpu.HBM)] * 3,
        out_specs=[whole, whole, whole],
        out_shape=[
            jax.ShapeDtypeStruct((count, state, channels), F32),
            jax.ShapeDtypeStruct((count, 8, channels), F32),
            jax.ShapeDtypeStruct(x.shape, BF16),
        ],
        scratch_shapes=[
            pltpu.VMEM(logdec.shape, F32),
            pltpu.VMEM(bc.shape[1:], BF16),
            pltpu.VMEM((count, heads * state, positions), BF16),
            pltpu.SemaphoreType.DMA((count, channels // lanes)),
            pltpu.SemaphoreType.DMA((2,)),
        ],
        compiler_params=pltpu.CompilerParams(vmem_limit_bytes=VMEM_LIMIT),
        cost_estimate=pl.CostEstimate(
            flops=2 * 64 * x.size, bytes_accessed=2 * x.size, transcendentals=0),
        name="local_ends",
    )(in_hbm(x), in_hbm(logdec), in_hbm(bc))


def prepare(parts, logs, lv_ref, lc_ref, state):
    size = logs.shape[1]
    chunks = size // CHUNK
    half = CHUNK // 2
    src, dst = iota((size, 1), 0), iota((1, size), 1)
    middle = quotient(dst, CHUNK) * CHUNK + half - 1
    plus = (src > middle) & (src <= dst)
    minus = (src > dst) & (src <= middle)
    offset = exact_dot(logs, jnp.where(plus, 1.0, jnp.where(minus, -1.0, 0.0)))
    row_scale = jnp.exp(offset)
    in_scale = jnp.exp(-offset) * gain_of(logs)
    span = iota((1, 128), 1) == quotient(src + half, CHUNK)
    steps = jnp.exp(exact_dot(logs, jnp.where(span, 1.0, 0.0)))
    rows = state * chunks
    mine = quotient(iota((rows, 1), 0), state) == quotient(dst, CHUNK)
    keep = (dst <= src) & (quotient(dst, CHUNK) == quotient(src, CHUNK))
    for i, (b_rows, c_rows) in enumerate(parts):
        b_all = jnp.concatenate([b_rows.astype(F32)] * chunks, axis=0)
        lv_ref[i, pl.ds(0, rows), :] = jnp.where(mine, b_all, 0.0).astype(BF16)
        scores = lax.dot_general(c_rows, b_rows, (((0,), (0,)), ((), ())), preferred_element_type=F32)
        lv_ref[i, pl.ds(rows, size), :] = jnp.where(keep, scores, 0.0).astype(BF16)
        c_all = jnp.concatenate([c_rows.astype(F32)] * chunks, axis=0)
        lc_ref[i] = jnp.where(mine, c_all, 0.0).T.astype(BF16)
    return in_scale, row_scale, steps


def cuts_of(ld_ref):
    count, _, positions = ld_ref.shape
    return [(i, pl.ds(b * BLOCK, BLOCK)) for i in range(count) for b in range(positions // BLOCK)]


def prepare_kernel(
    pld_ref, pbc_ref, bld_ref, bbc_ref,
    pv_ref, pu_ref, ps_ref, plv_ref, plc_ref, w_ref, hot_ref, blv_ref, blc_ref, reach_ref, *, width
):
    state = pbc_ref.shape[2]

    def collect(ld_ref, bc_ref):
        cuts = cuts_of(ld_ref)
        logs = jnp.concatenate([ld_ref[i, :, cut] for i, cut in cuts], axis=0)
        return cuts, logs, [(bc_ref[0, i, :, cut], bc_ref[1, i, :, cut]) for i, cut in cuts]

    cuts, logs, parts = collect(bld_ref, bbc_ref)
    heads = bld_ref.shape[1]
    blocks = len(cuts) // bld_ref.shape[0]
    in_scale, row_scale, steps = prepare(parts, logs, blv_ref, blc_ref, state)
    for k in range(len(cuts)):
        here = slice(k * heads, (k + 1) * heads)
        w_ref[k, pl.ds(0, BLOCK), :] = hi_lo(in_scale[here]).T.astype(BF16)
        w_ref[k, pl.ds(BLOCK, 16), :] = hi_lo(steps[here]).T[:16].astype(BF16)
        w_ref[k, pl.ds(BLOCK + 16, BLOCK), :] = hi_lo(row_scale[here]).T.astype(BF16)
    row_head = remainder(iota((2 * heads, 1), 0), heads)
    for g in range(hot_ref.shape[1] // 256):
        lane_head = quotient(iota((1, 256), 1), width) + g * (256 // width)
        hot_ref[:, pl.ds(g * 256, 256)] = jnp.where(row_head == lane_head, 1.0, 0.0).astype(BF16)
    upto = jnp.where(iota((BLOCK, 1), 0) <= iota((1, BLOCK), 1), 1.0, 0.0)
    runs = exact_dot(logs, upto)
    for k, (i, cut) in enumerate(cuts):
        run = runs[k * heads:(k + 1) * heads]
        if k % blocks:
            run = run + entered
        entered = run[:, BLOCK - 1:BLOCK]
        reach = parts[k][1].astype(F32)[None, :, :] * jnp.exp(run)[:, None, :]
        reach_ref[i, cut, :] = reach.reshape(heads * state, BLOCK).T.astype(BF16)

    cuts, logs, parts = collect(pld_ref, pbc_ref)
    heads = pld_ref.shape[1] // 2
    in_scale, row_scale, steps = prepare(parts, logs, plv_ref, plc_ref, state)
    for k in range(len(cuts)):
        for h in range(2):
            here = slice((2 * k + h) * heads, (2 * k + h + 1) * heads)
            pv_ref[k, h] = in_scale[here].T
            pu_ref[k, h] = row_scale[here].T
            ps_ref[k, h] = steps[here].T[:16]


def prepare_all(prompt_logdec, prompt_bc, branch_logdec, branch_bc, branch_channels):
    state = prompt_bc.shape[2]
    rows = BLOCK // CHUNK * state
    prompt_cuts = prompt_logdec.shape[0] * (prompt_logdec.shape[2] // BLOCK)
    branches, heads, positions = branch_logdec.shape
    branch_cuts = branches * (positions // BLOCK)
    half = prompt_logdec.shape[1] // 2
    shapes = [
        ((prompt_cuts, 2, BLOCK, half), F32),
        ((prompt_cuts, 2, BLOCK, half), F32),
        ((prompt_cuts, 2, 16, half), F32),
        ((prompt_cuts, rows + BLOCK, BLOCK), BF16),
        ((prompt_cuts, BLOCK, rows), BF16),
        ((branch_cuts, 2 * BLOCK + 16, 2 * heads), BF16),
        ((2 * heads, branch_channels), BF16),
        ((branch_cuts, rows + BLOCK, BLOCK), BF16),
        ((branch_cuts, BLOCK, rows), BF16),
        ((branches, positions, heads * state), BF16),
    ]
    whole = pl.BlockSpec(memory_space=pltpu.VMEM)
    out = pl.pallas_call(
        functools.partial(prepare_kernel, width=branch_channels // heads),
        in_specs=[whole] * 4,
        out_specs=[whole] * len(shapes),
        out_shape=[jax.ShapeDtypeStruct(*shape) for shape in shapes],
        compiler_params=pltpu.CompilerParams(vmem_limit_bytes=VMEM_LIMIT),
        cost_estimate=pl.CostEstimate(flops=10**8, bytes_accessed=10**6, transcendentals=0),
        name="prepare",
    )(prompt_logdec, prompt_bc, branch_logdec, branch_bc)
    return out[:5], out[5:9], out[9]


def run_tiles(jobs):
    scaled, passed = {}, {}
    for g in range(len(jobs) + 2):
        if g < len(jobs):
            scaled[g] = jobs[g][0]()
        if 0 <= g - 1 < len(jobs):
            passed[g - 1] = jobs[g - 1][1](scaled.pop(g - 1))
        if 0 <= g - 2:
            jobs[g - 2][2](passed.pop(g - 2))


def through_chunks(both, steps, entering, state, chunks):
    rows, carry = [], steps[0:1] * entering
    for c in range(chunks):
        rows.append(carry.astype(BF16))
        carry = steps[c + 1:c + 2] * (carry + both[c * state:(c + 1) * state])
    return jnp.concatenate(rows, axis=0), carry


def branch_kernel(*refs, which, skip):
    x_in, w_ref, hot_ref, lv_ref, lc_ref = refs[:5]
    own_ref, x_ref, s_ref, sems = refs[5 + skip:]
    positions, channels = x_ref.shape
    state = s_ref.shape[0]
    chunks = BLOCK // CHUNK
    rows = chunks * state
    blocks = positions // BLOCK
    lanes = min(1024, channels)
    copies = {}
    for b in range(blocks):
        for j in range(channels // lanes):
            part = (pl.ds(b * BLOCK, BLOCK), pl.ds(j * lanes, lanes))
            copies[b, j] = pltpu.make_async_copy(x_in.at[(which, *part)], x_ref.at[part], sems.at[b, j])
            copies[b, j].start()

    def job(b, g):
        at = which * blocks + b
        spot = (pl.ds(b * BLOCK, BLOCK), pl.ds(g * 256, 256))

        def scale():
            if g * 256 % lanes == 0:
                copies[b, g * 256 // lanes].wait()
            wide = jnp.dot(w_ref[at], hot_ref[:, pl.ds(g * 256, 256)], preferred_element_type=F32)
            scaled = (x_ref[spot].astype(F32) * wide[:BLOCK]).astype(BF16)
            return scaled, wide[BLOCK:BLOCK + 16], wide[BLOCK + 16:]

        def pass_on(given):
            scaled, steps, out_scale = given
            both = jnp.dot(lv_ref[at], scaled, preferred_element_type=F32)
            here = pl.ds(g * 256, 256)
            entering = s_ref[:, here] if b else jnp.zeros((state, 256), F32)
            carries, carry = through_chunks(both, steps, entering, state, chunks)
            if b < blocks - 1:
                s_ref[:, here] = carry
            return both[rows:], carries, out_scale

        def give(given):
            inner, carries, out_scale = given
            carried = jnp.dot(lc_ref[at], carries, preferred_element_type=F32)
            own_ref[(which, *spot)] = (inner + carried) * out_scale

        return scale, pass_on, give

    run_tiles([job(b, g) for b in range(blocks) for g in range(channels // 256)])


def branch_own(x, ready, which, into):
    _, positions, channels = x.shape
    state = ready[3].shape[2] * CHUNK // BLOCK
    whole = pl.BlockSpec(memory_space=pltpu.VMEM)
    lanes = min(1024, channels)
    work = positions * channels
    return pl.pallas_call(
        functools.partial(branch_kernel, which=which, skip=len(into)),
        in_specs=[pl.BlockSpec(memory_space=pltpu.HBM)] + [whole] * (4 + len(into)),
        out_specs=whole,
        out_shape=jax.ShapeDtypeStruct(x.shape, F32),
        scratch_shapes=[
            pltpu.VMEM((positions, channels), BF16),
            pltpu.VMEM((state, channels), F32),
            pltpu.SemaphoreType.DMA((positions // BLOCK, channels // lanes)),
        ],
        input_output_aliases={5 + i: i for i in range(len(into))},
        compiler_params=pltpu.CompilerParams(vmem_limit_bytes=VMEM_LIMIT),
        cost_estimate=pl.CostEstimate(
            flops=2 * 1152 * work, bytes_accessed=4 * work, transcendentals=0),
        name="branch_own",
    )(in_hbm(x), *ready, *into)


def prompt_kernel(*refs, width, skip):
    half_ref, x_ref, v_ref, u_ref, s_ref, lv_ref, lc_ref, start_ref = refs[:8]
    y_out, y_ref, sems = refs[8 + skip:]
    count, positions, channels = y_ref.shape
    state = start_ref.shape[1]
    chunks = BLOCK // CHUNK
    rows = chunks * state
    blocks = positions // BLOCK
    lanes = min(512, channels)
    half = half_ref[0]
    left = iota((1, 128), 1) < width
    entered, copies = {}, []

    def widen(scales, g):
        def pair(k):
            return jnp.where(left, scales[:, k:k + 1], scales[:, k + 1:k + 2])

        first = g * (256 // width)
        return jnp.concatenate([pair(first + k) for k in range(0, 256 // width, 2)], axis=1)

    def job(i, b, g):
        at = i * blocks + b
        spot = (i, pl.ds(b * BLOCK, BLOCK), pl.ds(g * 256, 256))

        def scale():
            cols = pl.ds(pl.multiple_of(half * channels + g * 256, 256), 256)
            wide = widen(v_ref[at, half], g)
            return (x_ref[i, pl.ds(b * BLOCK, BLOCK), cols].astype(F32) * wide).astype(BF16)

        def pass_on(scaled):
            both = jnp.dot(lv_ref[at], scaled, preferred_element_type=F32)
            entering = entered[i, g] if b else start_ref[i, :, pl.ds(g * 256, 256)]
            steps = widen(s_ref[at, half], g)
            carries, entered[i, g] = through_chunks(both, steps, entering, state, chunks)
            return both[rows:], carries

        def give(given):
            inner, carries = given
            carried = jnp.dot(lc_ref[at], carries, preferred_element_type=F32)
            y_ref[spot] = ((inner + carried) * widen(u_ref[at, half], g)).astype(BF16)
            if (g + 1) * 256 % lanes == 0:
                j = (g + 1) * 256 // lanes - 1
                there = pl.ds(pl.multiple_of(half * channels + j * lanes, lanes), lanes)
                copy = pltpu.make_async_copy(
                    y_ref.at[i, pl.ds(b * BLOCK, BLOCK), pl.ds(j * lanes, lanes)],
                    y_out.at[i, pl.ds(b * BLOCK, BLOCK), there], sems.at[at, j])
                copy.start()
                copies.append(copy)

        return scale, pass_on, give

    run_tiles([job(i, b, g) for i in range(count) for b in range(blocks) for g in range(channels // 256)])
    for copy in copies:
        copy.wait()


def prompt_half(half, x, ready, start, into):
    count, positions, channels = x.shape
    width = channels // (2 * ready[0].shape[3])
    part = channels // 2
    whole = pl.BlockSpec(memory_space=pltpu.VMEM)
    hbm = pl.BlockSpec(memory_space=pltpu.HBM)
    work = count * positions * part
    return pl.pallas_call(
        functools.partial(prompt_kernel, width=width, skip=len(into)),
        in_specs=[pl.BlockSpec(memory_space=pltpu.SMEM)] + [whole] * 7 + [hbm] * len(into),
        out_specs=hbm,
        out_shape=jax.ShapeDtypeStruct(x.shape, BF16),
        scratch_shapes=[
            pltpu.VMEM((count, positions, part), BF16),
            pltpu.SemaphoreType.DMA((count * (positions // BLOCK), part // min(512, part))),
        ],
        input_output_aliases={8 + i: i for i in range(len(into))},
        compiler_params=pltpu.CompilerParams(vmem_limit_bytes=VMEM_LIMIT),
        cost_estimate=pl.CostEstimate(
            flops=2 * 1152 * work, bytes_accessed=4 * work, transcendentals=0),
        name="prompt_half",
    )(half, x, *ready, start, *into)


def finish_kernel(len_ref, own_ref, reach_ref, start_ref, y_ref, *, width):
    branch, tile = pl.program_id(0), pl.program_id(1)
    positions, lanes = y_ref.shape[1], y_ref.shape[2]
    state = start_ref.shape[0]
    group = 128 // state
    span = group * width
    live = iota((positions, span), 0) < len_ref[branch]
    own_head = quotient(iota((128, 1), 0), state) == quotient(iota((1, span), 1), width)
    for g in range(lanes // span):
        here = pl.ds(pl.multiple_of(tile * lanes + g * span, span), span)
        first = pl.ds(pl.multiple_of((tile * (lanes // span) + g) * 128, 128), 128)
        start = jnp.concatenate([start_ref[:, here]] * group, axis=0)
        start = jnp.where(own_head, start, 0.0).astype(BF16)
        term = jnp.dot(reach_ref[branch, :, first], start, preferred_element_type=F32)
        out = jnp.where(live, own_ref[branch, :, here] + term, 0.0)
        y_ref[0, :, pl.ds(g * span, span)] = out.astype(BF16)


def finish(lengths, own, reach, start):
    count, positions, channels = own.shape
    width = channels * start.shape[0] // reach.shape[2]
    lanes = min(1024, channels)
    whole = pl.BlockSpec(memory_space=pltpu.VMEM)
    return pl.pallas_call(
        functools.partial(finish_kernel, width=width),
        grid=(count, channels // lanes),
        in_specs=[pl.BlockSpec(memory_space=pltpu.SMEM), whole, whole, whole],
        out_specs=pl.BlockSpec((1, positions, lanes), lambda i, j: (i, 0, j)),
        out_shape=jax.ShapeDtypeStruct(own.shape, BF16),
        compiler_params=pltpu.CompilerParams(vmem_limit_bytes=VMEM_LIMIT),
        cost_estimate=pl.CostEstimate(
            flops=2 * 128 * own.size, bytes_accessed=6 * own.size, transcendentals=0),
        name="branch_finish",
    )(lengths, own, reach, start)


def swap_bit(value, bit, size):
    return lax.ppermute(value, "ctx", [(k, k ^ bit) for k in range(size)])


def pack(states, logs):
    lanes = states.shape[-1]
    return jnp.concatenate([states.reshape(-1, lanes), logs.reshape(-1, lanes)], axis=0)


def unpack(packed, count):
    lanes = packed.shape[-1]
    rows = packed.shape[0] - count
    return packed[:rows].reshape(count, rows // count, lanes), packed[rows:].reshape(count, 1, lanes)


def in_order(upper, mine, other):
    first = [jnp.where(upper, o, m) for m, o in zip(mine, other)]
    second = [jnp.where(upper, m, o) for m, o in zip(mine, other)]
    return first, second


def join(first, second):
    return jnp.exp(second[1]) * first[0] + second[0], first[1] + second[1]


def spread_step(value, hop, ctx_size, pair_size):
    owner = lax.axis_index("ctx") * pair_size // ctx_size
    known = [m for m in range(pair_size) if m & (2 * hop - 1) == 0]
    links = []
    for k in range(ctx_size):
        z = k * pair_size // ctx_size
        links += [(k * pair_size + (z ^ m), k * pair_size + (z ^ m ^ hop)) for m in known]
    got = lax.ppermute(value, ("ctx", "pair"), links)
    has = ((lax.axis_index("pair") ^ owner) & (2 * hop - 1)) == 0
    return got, has


def body(
    prompt_x,
    prompt_bc,
    prompt_logdec,
    branch_x,
    branch_bc,
    branch_logdec,
    branch_prompt,
    branch_len,
):
    size, pair_size = lax.axis_size("ctx"), lax.axis_size("pair")
    prompts, branches = prompt_x.shape[0], branch_x.shape[0]
    assert size == 2 * pair_size and size & (size - 1) == 0 and branch_prompt.shape[0] == 1
    mine = lax.axis_index("ctx")
    odd = (mine & 1) == 1

    def beside(exchange, value, work, *given):
        value, given = lax.optimization_barrier((value, given))
        got = exchange(value)
        return lax.optimization_barrier((got, work(*given)))

    end, log, held = local_ends(prompt_x, prompt_logdec, prompt_bc)
    half = end.shape[2] // 2
    low, high = (end[:, :, :half], log[:, :1, :half]), (end[:, :, half:], log[:, :1, half:])
    keep = [jnp.where(odd, h, l) for l, h in zip(low, high)]
    send = [jnp.where(odd, l, h) for l, h in zip(low, high)]
    got, (prompt_ready, branch_ready, reach) = beside(
        lambda v: swap_bit(v, 1, size),
        pack(*send),
        lambda ld: prepare_all(prompt_logdec, prompt_bc, ld, branch_bc, branch_x.shape[2]),
        branch_logdec,
    )
    got = unpack(got, prompts)
    first, second = in_order(odd, keep, got)
    total, total_log = join(first, second)
    before, before_log = jnp.zeros_like(total), jnp.zeros_like(total_log)

    own = ()
    works = iter(range(branches))
    bit = 2
    while bit < size:
        which = next(works, None)
        swap = functools.partial(swap_bit, bit=bit, size=size)
        if which is None:
            got = swap(pack(total, total_log))
        else:
            got, own = beside(
                swap, pack(total, total_log),
                lambda x, own: (branch_own(x, branch_ready, which, own),), branch_x, own)
        other = unpack(got, prompts)
        upper = (mine & bit) != 0
        before = jnp.where(upper, jnp.exp(before_log) * other[0] + before, before)
        before_log = jnp.where(upper, before_log + other[1], before_log)
        total, total_log = join(*in_order(upper, (total, total_log), other))
        bit *= 2
    for which in works:
        own = (branch_own(branch_x, branch_ready, which, own),)

    next_before = jnp.exp(first[1]) * before + first[0]
    keep = jnp.where(odd, next_before, before)
    others = swap_bit(jnp.where(odd, before, next_before), 1, size)
    here = jnp.reshape(mine & 1, (1,))
    sides = [(here, keep), (1 - here, others)]
    prompt_y = ()
    hop = pair_size // 2
    while hop:
        step = functools.partial(spread_step, hop=hop, ctx_size=size, pair_size=pair_size)
        if sides:
            side, entering = sides.pop(0)
            (got, has), prompt_y = beside(
                step, total,
                lambda entering, y: (prompt_half(side, held, prompt_ready, entering, y),), entering, prompt_y)
        else:
            got, has = step(total)
        total = jnp.where(has, total, got)
        hop //= 2
    for side, entering in sides:
        prompt_y = (prompt_half(side, held, prompt_ready, entering, prompt_y),)
    start = total[0]
    for which in range(1, prompts):
        start = jnp.where(branch_prompt[0] == which, total[which], start)
    branch_y = finish(branch_len, *own, reach, start)
    return prompt_y[0], branch_y


def solution(mesh):
    return jax.shard_map(
        body,
        mesh=mesh,
        in_specs=(
            P(None, "ctx", "pair"),
            P(None, None, None, "ctx"),
            P(None, "pair", "ctx"),
            P("pair", None, "ctx"),
            P(None, "pair", None, None),
            P("pair", "ctx", None),
            P("pair"),
            P("pair"),
        ),
        out_specs=(P(None, "ctx", "pair"), P("pair", None, "ctx")),
        check_vma=False,
    )
```

time: 55.4 us -> 76.8 us (1.39)
  local copies, waits for them, and re-layouts: 0.76 us -> 28.5 us
  starting transfers between devices: 15.2 us -> 10.7 us
  waiting for transfers between devices: 2.29 us -> 0.02 us
  other arithmetic: 1.41 us -> 3.52 us
  between operations: 3.64 us -> 1.81 us
    unnamed x16 -> x80, local copies, waits for them, and re-layouts: 0.1 us -> 25.7 us
    ppermute x5 -> x2, starting transfers between devices: 11.5 us -> 5.99 us  [spread_step(): got = lax.ppermute(value, ('ctx', 'pair'), links)]
    ppermute x4, waiting for transfers between devices: 2.28 us -> 0.01 us  [swap_bit(): return lax.ppermute(value, 'ctx', [(k, k ^ bit) for k in range(size)])]
    slice x3, local copies, waits for them, and re-layouts: 0.06 us -> 1.96 us  [unpack(): packed[:rows].reshape(count, rows // count, lanes)]
    exp x1, other arithmetic: 0.02 us -> 1.53 us  [body(): before = jnp.where(upper, jnp.exp(before_log) * other[0] + before, before)]
    concatenate x3, other arithmetic: 0.07 us -> 1.52 us  [pack(): jnp.concatenate([states.reshape(-1, lanes), logs.reshape(-1, lanes)], axi...]
    ppermute x4, starting transfers between devices: 3.73 us -> 4.71 us  [swap_bit(): return lax.ppermute(value, 'ctx', [(k, k ^ bit) for k in range(size)])]
    slice x2, local copies, waits for them, and re-layouts: 0.01 us -> 0.85 us  [unpack(): packed[rows:].reshape(count, 1, lanes)]
  transfers between devices with their start and end apart: 9 -> 6, of which waited for: 2 -> 0; matrix products, arithmetic and copies ran while one was open for 3% -> 0% of each run, Pallas kernels for 42% -> 30%
where the time goes in v4:
time: 76.8 us; the launch traced here: 76.2 us
  Pallas kernels  31.6 us (41%)
  local copies, waits for them, and re-layouts  28.5 us (37%)
  starting transfers between devices  10.7 us (14%)
  other arithmetic  3.52 us (5%)
  between operations  1.81 us (2%)
    unnamed x80, local copies, waits for them, and re-layouts  25.7 us
    pallas_call x2, Pallas kernels, prompt_half(): pl.pallas_call(functools.partial(prompt_kernel, width=width, skip=len(int...  11.7 us
    pallas_call x2, Pallas kernels, branch_own(): pl.pallas_call(functools.partial(branch_kernel, which=which, skip=len(int...  9.17 us
    ppermute x2, starting transfers between devices, spread_step(): got = lax.ppermute(value, ('ctx', 'pair'), links)  5.99 us
    pallas_call x1, Pallas kernels, local_ends(): pl.pallas_call(functools.partial(ends_kernel, width=width, lanes=lanes),...  4.99 us
    ppermute x4, starting transfers between devices, swap_bit(): return lax.ppermute(value, 'ctx', [(k, k ^ bit) for k in range(size)])  4.71 us
    pallas_call x1, Pallas kernels, finish(): pl.pallas_call(functools.partial(finish_kernel, width=width), grid=(count...  3.83 us
    slice x3, local copies, waits for them, and re-layouts, unpack(): packed[:rows].reshape(count, rows // count, lanes)  1.96 us
  transfers between devices with their start and end apart: 6, of which 0 were waited for; matrix products, arithmetic and copies ran while one was open for 0% of the time, Pallas kernels for 30%

profile of v4, /device:TPU:0, one launch (start us, length us, event | category | flops | bytes accessed | tf_op | source)
XLA Modules:
  0.0 76.2 jit_solution(7231389630156463927)
XLA Ops:
  0.6 0.0 copy-start.16
  0.6 0.0 copy-start.17
  0.7 0.0 copy-start.19
  0.7 0.0 copy-start.20
  0.7 5.0 %local_ends.1 = (f32[2,16,4096]{2,1,0:T(8,128)S(1)}, f32[2,8,4096]{2,1,0:T(8,128)S(1)}, bf16[2,256,4096]{2,1,0:T(8,128)(2,1)S(1)}) custom-call(bf16[2,256,4096]{2,1,0:T(8,128)(2,1)} %x_ref.1, f32[2,64,256]{2,1,0:T(8,128)} %pld_ref.1, bf16[2,2,16,256]{3,2,1,0:T(8,128)(2,1)} %pbc_ref.1), custom_call_target="tpu_custom_call" | custom-call | flops 268435456 | bytes 4194304 | tf_op jit(solution)/shard_map/local_ends/pallas_call | solution.py:124
  5.7 0.0 copy-start.3
  5.7 2.0 %copy-done.3 = bf16[2,256,4096]{2,1,0:T(8,128)(2,1)} copy-done((bf16[2,256,4096]{2,1,0:T(8,128)(2,1)}, bf16[2,256,4096]{2,1,0:T(8,128)(2,1)S(1)}, u32[]{:S(2)}) %copy-start.3) | copy-done | bytes 4194328
  7.8 0.5 collective-permute-start
  8.3 0.0 copy-done.16
  8.3 0.0 copy-done.17
  8.3 0.0 copy-done.19
  8.3 1.9 %prepare.1 = (f32[2,2,256,32]{3,2,1,0:T(8,128)S(1)}, f32[2,2,256,32]{3,2,1,0:T(8,128)S(1)}, f32[2,2,16,32]{3,2,1,0:T(8,128)S(1)}, bf16[2,384,256]{2,1,0:T(8,128)...) custom-call(f32[2,64,256]{2,1,0:T(8,128)S(1)} %copy-done.16, ...), custom_call_target="tpu_custom_call" | custom-call | flops 100000000 | bytes 1000000 | tf_op jit(solution)/shard_map/prepare/pallas_call | solution.py:243
  10.3 0.7 copy-done.6
  11.0 1.0 %copy-done.9 = bf16[2,512,512]{2,1,0:T(8,128)(2,1)} copy-done((bf16[2,512,512]{2,1,0:T(8,128)(2,1)}, bf16[2,512,512]{2,1,0:T(8,128)(2,1)S(1)}, u32[]{:S(2)}) %copy-start.9) | copy-done | bytes 1048600
  11.9 0.6 copy-done.11
  12.6 0.6 copy-done.14
  13.2 0.0 collective-permute-done
  13.2 0.0 copy-start.23
  13.3 0.6 copy_bitcast_fusion
  14.0 0.0 copy-done.31
  14.0 0.7 copy-done.27
  14.7 0.7 pad_maximum_fusion.1
  15.5 2.5 %collective-permute-start.1 = (f32[34,2048]{1,0:T(8,128)}, f32[34,2048]{1,0:T(8,128)}, u32[]{:S(2)}, u32[]{:S(2)}) collective-permute-start(f32[34,2048]{1,0:T(8,128)} %pad_maximum_fusion.1), channel_id=1, source_target_pairs={{0,8},{4,12},{8,0},{12,4},{16,24},{20,28},{24,16},{28,20},{1,9},{5... | collective-permute-start | bytes 835592 | tf_op jit(solution)/shard_map/ppermute | solution.py:462
  18.0 0.9 %copy-done.7 = bf16[4,256,128]{2,1,0:T(8,128)(2,1)S(1)} copy-done((bf16[4,256,128]{2,1,0:T(8,128)(2,1)S(1)}, bf16[4,256,128]{2,1,0:T(8,128)(2,1)}, u32[]{:S(2)}) %copy-start.7) | copy-done | bytes 262168
  18.9 4.6 %branch_own.2.refs_5_ = f32[2,512,2048]{2,1,0:T(8,128)S(1)} custom-call(bf16[2,512,2048]{2,1,0:T(8,128)(2,1)} %refs_0_.1, bf16[4,528,64]{2,1,0:T(8,128)(2,1)S(1)} %get-tuple-element.65.refs_1_, bf16[64,2048]{1,0:T(8,128)(2,1)S(1)} %get-tuple-element.66.refs_2_, bf16[4,384,256]{2,1,0:T(8,128)(2,1)S(1)} %get-tuple-element.67.refs_3_, ...), custom_call_target="tpu_custom_call" | custom-call | flops 2415919104 | bytes 4194304 | tf_op jit(solution)/shard_map/branch_own/pallas_call | solution.py:327
  23.5 3.3 %copy-done = f32[2,512,2048]{2,1,0:T(8,128)} copy-done((f32[2,512,2048]{2,1,0:T(8,128)}, f32[2,512,2048]{2,1,0:T(8,128)S(1)}, u32[]{:S(2)}) %copy-start) | copy-done | bytes 8388632
  26.8 0.0 collective-permute-done.1
  26.8 1.0 %slice.43 = f32[32,2048]{1,0:T(8,128)S(1)} slice(f32[34,2048]{1,0:T(8,128)} %collective-permute-done.1), slice={[0:32], [0:2048]} | slice | bytes 524288 | tf_op jit(solution)/shard_map/slice | solution.py:473
  27.8 1.5 %select_exponential_fusion = (f32[2,2048]{1,0:T(2,128)}, f32[2,2048]{1,0:T(2,128)S(1)}) fusion(pred[]{:T(512)S(6)} %ne.17, f32[34,2048]{1,0:T(8,128)} %collective-permute-done.1), kind=kLoop, calls=%fused_computation.33 | loop fusion | flops 4096 | bytes 49153 | tf_op jit(solution)/shard_map/exp | solution.py:549
  29.4 0.6 copy-done.29
  30.0 0.1 select_add_fusion.1
  30.0 0.7 copy-done.21
  30.7 0.7 pad_maximum_fusion.2
  31.5 0.0 copy-done.25
  31.5 1.6 %collective-permute-start.2 = (f32[34,2048]{1,0:T(8,128)}, f32[34,2048]{1,0:T(8,128)}, u32[]{:S(2)}, u32[]{:S(2)}) collective-permute-start(f32[34,2048]{1,0:T(8,128)} %pad_maximum_fusion.2), channel_id=1, source_target_pairs={{0,16},{4,20},{8,24},{12,28},{16,0},{20,4},{24,8},{28,12},{1,17},{... | collective-permute-start | bytes 835592 | tf_op jit(solution)/shard_map/ppermute | solution.py:462
  33.1 3.4 %copy-done.1 = f32[2,512,2048]{2,1,0:T(8,128)S(1)} copy-done((f32[2,512,2048]{2,1,0:T(8,128)S(1)}, f32[2,512,2048]{2,1,0:T(8,128)}, u32[]{:S(2)}) %copy-start.1) | copy-done | bytes 8388632
  36.5 0.9 %copy-done.8 = bf16[4,256,128]{2,1,0:T(8,128)(2,1)S(1)} copy-done((bf16[4,256,128]{2,1,0:T(8,128)(2,1)S(1)}, bf16[4,256,128]{2,1,0:T(8,128)(2,1)}, u32[]{:S(2)}) %copy-start.8) | copy-done | bytes 262168
  37.5 4.6 %branch_own.3.own_ref = f32[2,512,2048]{2,1,0:T(8,128)S(1)} custom-call(bf16[2,512,2048]{2,1,0:T(8,128)(2,1)} %refs_0_.1, bf16[4,528,64]{2,1,0:T(8,128)(2,1)S(1)} %get-tuple-element.65.refs_1_, bf16[64,2048]{1,0:T(8,128)(2,1)S(1)} %get-tuple-element.66.refs_2_, bf16[4,384,256]{2,1,0:T(8,128)(2,1)S(1)} %get-tuple-element.67.refs_3_, ...), custom_call_target="tpu_custom_call", output_to_operand_aliasing={{}: (5, {})} | custom-call | flops 2415919104 | bytes 4194304 | tf_op jit(solution)/shard_map/branch_own/pallas_call | solution.py:327
  42.1 0.0 copy-start.2
  42.1 3.3 %copy-done.2 = f32[2,512,2048]{2,1,0:T(8,128)} copy-done((f32[2,512,2048]{2,1,0:T(8,128)}, f32[2,512,2048]{2,1,0:T(8,128)S(1)}, u32[]{:S(2)}) %copy-start.2) | copy-done | bytes 8388632
  45.4 0.0 collective-permute-done.2
  45.4 1.0 %slice.45 = f32[32,2048]{1,0:T(8,128)S(1)} slice(f32[34,2048]{1,0:T(8,128)} %collective-permute-done.2), slice={[0:32], [0:2048]} | slice | bytes 524288 | tf_op jit(solution)/shard_map/slice | solution.py:473
  46.3 0.8 %slice.44 = f32[2,2048]{1,0:T(2,128)S(1)} slice(f32[34,2048]{1,0:T(8,128)} %collective-permute-done.2), slice={[32:34], [0:2048]} | slice | bytes 32768 | tf_op jit(solution)/shard_map/slice | solution.py:473
  47.3 0.1 fusion
  47.4 4.7 %collective-permute-start.3 = (f32[2,16,2048]{2,1,0:T(8,128)S(1)}, f32[2,16,2048]{2,1,0:T(8,128)S(1)}, u32[]{:S(2)}, u32[]{:S(2)}) collective-permute-start(f32[2,16,2048]{2,1,0:T(8,128)S(1)} %get-tuple-element.75), channel_id=1, source_target_pairs={{0,2},{4,6},{9,11},{13,15},{18,16},{22,20},{27,25},{31,29}} | collective-permute-start | bytes 786440 | tf_op jit(solution)/shard_map/ppermute | solution.py:493
  52.1 0.1 collective-permute-start.4
  52.2 0.0 copy-start.4
  52.2 2.2 %copy-done.4 = bf16[2,256,4096]{2,1,0:T(8,128)(2,1)S(1)} copy-done((bf16[2,256,4096]{2,1,0:T(8,128)(2,1)S(1)}, bf16[2,256,4096]{2,1,0:T(8,128)(2,1)}, u32[]{:S(2)}) %copy-start.4) | copy-done | bytes 4194328
  54.4 0.9 %copy-done.12 = bf16[2,256,128]{2,1,0:T(8,128)(2,1)S(1)} copy-done((bf16[2,256,128]{2,1,0:T(8,128)(2,1)S(1)}, bf16[2,256,128]{2,1,0:T(8,128)(2,1)}, u32[]{:S(2)}) %copy-start.12) | copy-done | bytes 131096
  55.3 0.8 copy-done.15
  56.1 5.9 %prompt_half.2.refs_8_ = bf16[2,256,4096]{2,1,0:T(8,128)(2,1)} custom-call(s32[1]{0:T(128)} %bitcast.6.refs_0_, bf16[2,256,4096]{2,1,0:T(8,128)(2,1)S(1)} %copy-done.4, f32[2,2,256,32]{3,2,1,0:T(8,128)S(1)} %get-tuple-element.77.refs_2_, f32[2,2,256,32]{3,2,1,0:T(8,128)S(1)} %get-tuple-element.78.refs_3_, f32[2,2,16,32]{3,2,1,0:T(8,128)S(1)} %copy-done.15, ...), custom_call_target="tpu_custom_call" | custom-call | flops 2415919104 | bytes 4194304 | tf_op jit(solution)/shard_map/prompt_half/pallas_call | solution.py:408
  61.9 0.0 collective-permute-done.3
  62.0 0.0 collective-permute-done.4.refs_7_
  62.0 1.3 %collective-permute-start.5 = (f32[2,16,2048]{2,1,0:T(8,128)S(1)}, f32[2,16,2048]{2,1,0:T(8,128)S(1)}, u32[]{:S(2)}, u32[]{:S(2)}) collective-permute-start(f32[2,16,2048]{2,1,0:T(8,128)S(1)} %broadcast_select_fusion.1), channel_id=1, source_target_pairs={{0,1},{2,3},{4,5},{6,7},{9,8},{11,10},{13,12},{15,14},{18,19},{16,... | collective-permute-start | bytes 786440 | tf_op jit(solution)/shard_map/ppermute | solution.py:493
  64.0 0.0 slice-start
  64.0 0.0 copy-start.5
  64.0 2.3 %copy-done.5 = bf16[2,256,4096]{2,1,0:T(8,128)(2,1)S(1)} copy-done((bf16[2,256,4096]{2,1,0:T(8,128)(2,1)S(1)}, bf16[2,256,4096]{2,1,0:T(8,128)(2,1)}, u32[]{:S(2)}) %copy-start.5) | copy-done | bytes 4194328
  66.3 5.9 %prompt_half.3 = bf16[2,256,4096]{2,1,0:T(8,128)(2,1)} custom-call(s32[1]{0:T(128)S(6)} %sub.9.refs_0_, bf16[2,256,4096]{2,1,0:T(8,128)(2,1)S(1)} %copy-done.5, f32[2,2,256,32]{3,2,1,0:T(8,128)S(1)} %get-tuple-element.77.refs_2_, f32[2,2,256,32]{3,2,1,0:T(8,128)S(1)} %get-tuple-element.78.refs_3_, ...), custom_call_target="tpu_custom_call", output_to_operand_aliasing={{}: (8, {})} | custom-call | flops 2415919104 | bytes 4194304 | tf_op jit(solution)/shard_map/prompt_half/pallas_call | solution.py:408
  72.2 0.0 collective-permute-done.5
  72.3 0.0 slice-done
  72.3 0.0 slice-done.1
  72.3 0.0 copy-done.10
  72.3 0.0 copy-done.18
  72.3 3.8 %branch_finish.1 = bf16[2,512,2048]{2,1,0:T(8,128)(2,1)} custom-call(s32[2]{0:T(128)S(1)} %copy-done.18, f32[2,512,2048]{2,1,0:T(8,128)S(1)} %bitcast.30, bf16[2,512,512]{2,1,0:T(8,128)(2,1)S(1)} %copy-done.10, f32[16,2048]{1,0:T(8,128)S(1)} %fusion.2.start_ref), custom_call_target="tpu_custom_call" | custom-call | flops 536870912 | bytes 12582912 | tf_op jit(solution)/shard_map/branch_finish/pallas_call | solution.py:448
  (56 shorter events, 0.5 us)
Async XLA Ops:
  0.6 7.7 %copy-start.16 = (f32[2,64,256]{2,1,0:T(8,128)S(1)}, f32[2,64,256]{2,1,0:T(8,128)}, u32[]{:S(2)}) copy-start(f32[2,64,256]{2,1,0:T(8,128)} %pld_ref.1) | copy-start | bytes 393220
  0.6 7.7 %copy-start.17 = (bf16[2,2,16,256]{3,2,1,0:T(8,128)(2,1)S(1)}, bf16[2,2,16,256]{3,2,1,0:T(8,128)(2,1)}, u32[]{:S(2)}) copy-start(bf16[2,2,16,256]{3,2,1,0:T(8,128)(2,1)} %pbc_ref.1) | copy-start | bytes 98308
  0.7 7.7 %copy-start.19 = (f32[2,32,512]{2,1,0:T(8,128)S(1)}, f32[2,32,512]{2,1,0:T(8,128)}, u32[]{:S(2)}) copy-start(f32[2,32,512]{2,1,0:T(8,128)} %bld_ref) | copy-start | bytes 393220
  0.7 7.7 %copy-start.20 = (bf16[2,2,16,512]{3,2,1,0:T(8,128)(2,1)S(1)}, bf16[2,2,16,512]{3,2,1,0:T(8,128)(2,1)}, u32[]{:S(2)}) copy-start(bf16[2,2,16,512]{3,2,1,0:T(8,128)(2,1)} %bbc_ref.1) | copy-start | bytes 196612
  5.7 2.0 %copy-start.3 = (bf16[2,256,4096]{2,1,0:T(8,128)(2,1)}, bf16[2,256,4096]{2,1,0:T(8,128)(2,1)S(1)}, u32[]{:S(2)}) copy-start(bf16[2,256,4096]{2,1,0:T(8,128)(2,1)S(1)} %get-tuple-element.76.refs_1_) | copy-start | bytes 12582916
  7.8 5.4 %collective-permute-start = (f32[34,2048]{1,0:T(8,128)S(1)}, f32[34,2048]{1,0:T(8,128)S(1)}, u32[]{:S(2)}, u32[]{:S(2)}) collective-permute-start(f32[34,2048]{1,0:T(8,128)S(1)} %pad_maximum_fusion), channel_id=1, source_target_pairs={{0,4},{4,0},{8,12},{12,8},{16,20},{20,16},{24,28},{28,24},{1,5},{5... | collective-permute-start | bytes 835592 | tf_op jit(solution)/shard_map/ppermute | solution.py:462
  10.3 0.7 copy-start.6
  11.0 1.0 %copy-start.9 = (bf16[2,512,512]{2,1,0:T(8,128)(2,1)}, bf16[2,512,512]{2,1,0:T(8,128)(2,1)S(1)}, u32[]{:S(2)}) copy-start(bf16[2,512,512]{2,1,0:T(8,128)(2,1)S(1)} %get-tuple-element.91.reach_ref) | copy-start | bytes 3145732
  11.9 0.7 copy-start.11
  12.6 0.6 copy-start.14
  13.2 0.7 copy-start.23
  13.3 0.7 copy-start.31
  14.0 0.7 copy-start.27
  15.5 11.4 %collective-permute-start.1 = (f32[34,2048]{1,0:T(8,128)}, f32[34,2048]{1,0:T(8,128)}, u32[]{:S(2)}, u32[]{:S(2)}) collective-permute-start(f32[34,2048]{1,0:T(8,128)} %pad_maximum_fusion.1), channel_id=1, source_target_pairs={{0,8},{4,12},{8,0},{12,4},{16,24},{20,28},{24,16},{28,20},{1,9},{5... | collective-permute-start | bytes 835592 | tf_op jit(solution)/shard_map/ppermute | solution.py:462
  18.0 0.9 %copy-start.7 = (bf16[4,256,128]{2,1,0:T(8,128)(2,1)S(1)}, bf16[4,256,128]{2,1,0:T(8,128)(2,1)}, u32[]{:S(2)}) copy-start(bf16[4,256,128]{2,1,0:T(8,128)(2,1)} %copy-done.6) | copy-start | bytes 786436
  18.9 10.4 %copy-start.32 = (f32[2,1,2048]{2,1,0:T(1,128)S(1)}, f32[2,1,2048]{2,1,0:T(1,128)}, u32[]{:S(2)}) copy-start(f32[2,1,2048]{2,1,0:T(1,128)} %copy-done.31) | copy-start | bytes 49156
  18.9 11.0 %copy-start.28 = (f32[2,16,2048]{2,1,0:T(8,128)S(1)}, f32[2,16,2048]{2,1,0:T(8,128)}, u32[]{:S(2)}) copy-start(f32[2,16,2048]{2,1,0:T(8,128)} %copy-done.27) | copy-start | bytes 786436
  23.5 3.3 %copy-start = (f32[2,512,2048]{2,1,0:T(8,128)}, f32[2,512,2048]{2,1,0:T(8,128)S(1)}, u32[]{:S(2)}) copy-start(f32[2,512,2048]{2,1,0:T(8,128)S(1)} %branch_own.2.refs_5_) | copy-start | bytes 25165828
  27.8 3.7 %copy-start.25 = (f32[32,2048]{1,0:T(8,128)}, f32[32,2048]{1,0:T(8,128)S(1)}, u32[]{:S(2)}) copy-start(f32[32,2048]{1,0:T(8,128)S(1)} %slice.43) | copy-start | bytes 786436
  29.4 0.6 copy-start.29
  30.0 0.7 copy-start.21
  31.5 13.9 %collective-permute-start.2 = (f32[34,2048]{1,0:T(8,128)}, f32[34,2048]{1,0:T(8,128)}, u32[]{:S(2)}, u32[]{:S(2)}) collective-permute-start(f32[34,2048]{1,0:T(8,128)} %pad_maximum_fusion.2), channel_id=1, source_target_pairs={{0,16},{4,20},{8,24},{12,28},{16,0},{20,4},{24,8},{28,12},{1,17},{... | collective-permute-start | bytes 835592 | tf_op jit(solution)/shard_map/ppermute | solution.py:462
  33.1 3.4 %copy-start.1 = (f32[2,512,2048]{2,1,0:T(8,128)S(1)}, f32[2,512,2048]{2,1,0:T(8,128)}, u32[]{:S(2)}) copy-start(f32[2,512,2048]{2,1,0:T(8,128)} %copy-done) | copy-start | bytes 25165828
  36.5 0.9 %copy-start.8 = (bf16[4,256,128]{2,1,0:T(8,128)(2,1)S(1)}, bf16[4,256,128]{2,1,0:T(8,128)(2,1)}, u32[]{:S(2)}) copy-start(bf16[4,256,128]{2,1,0:T(8,128)(2,1)} %copy-done.6) | copy-start | bytes 786436
  37.4 9.8 %copy-start.30 = (f32[2,1,2048]{2,1,0:T(1,128)S(1)}, f32[2,1,2048]{2,1,0:T(1,128)}, u32[]{:S(2)}) copy-start(f32[2,1,2048]{2,1,0:T(1,128)} %copy-done.29) | copy-start | bytes 49156
  37.4 9.8 %copy-start.22 = (f32[2,16,2048]{2,1,0:T(8,128)S(1)}, f32[2,16,2048]{2,1,0:T(8,128)}, u32[]{:S(2)}) copy-start(f32[2,16,2048]{2,1,0:T(8,128)} %copy-done.21) | copy-start | bytes 786436
  37.4 9.8 %copy-start.24 = (f32[32,2048]{1,0:T(8,128)S(1)}, f32[32,2048]{1,0:T(8,128)}, u32[]{:S(2)}) copy-start(f32[32,2048]{1,0:T(8,128)} %copy-done.23) | copy-start | bytes 786436
  37.4 9.8 %copy-start.26 = (f32[32,2048]{1,0:T(8,128)S(1)}, f32[32,2048]{1,0:T(8,128)}, u32[]{:S(2)}) copy-start(f32[32,2048]{1,0:T(8,128)} %copy-done.25) | copy-start | bytes 786436
  37.4 9.8 %copy-start.33 = (f32[2,2048]{1,0:T(2,128)S(1)}, f32[2,2048]{1,0:T(2,128)}, u32[]{:S(2)}) copy-start(f32[2,2048]{1,0:T(2,128)} %get-tuple-element.96) | copy-start | bytes 49156
  37.4 9.8 %copy-start.34 = (f32[2,2048]{1,0:T(2,128)S(1)}, f32[2,2048]{1,0:T(2,128)}, u32[]{:S(2)}) copy-start(f32[2,2048]{1,0:T(2,128)} %get-tuple-element.104) | copy-start | bytes 49156
  42.1 3.3 %copy-start.2 = (f32[2,512,2048]{2,1,0:T(8,128)}, f32[2,512,2048]{2,1,0:T(8,128)S(1)}, u32[]{:S(2)}) copy-start(f32[2,512,2048]{2,1,0:T(8,128)S(1)} %branch_own.3.own_ref) | copy-start | bytes 25165828
  47.4 14.5 %collective-permute-start.3 = (f32[2,16,2048]{2,1,0:T(8,128)S(1)}, f32[2,16,2048]{2,1,0:T(8,128)S(1)}, u32[]{:S(2)}, u32[]{:S(2)}) collective-permute-start(f32[2,16,2048]{2,1,0:T(8,128)S(1)} %get-tuple-element.75), channel_id=1, source_target_pairs={{0,2},{4,6},{9,11},{13,15},{18,16},{22,20},{27,25},{31,29}} | collective-permute-start | bytes 786440 | tf_op jit(solution)/shard_map/ppermute | solution.py:493
  52.1 9.9 %collective-permute-start.4 = (f32[2,16,2048]{2,1,0:T(8,128)S(1)}, f32[2,16,2048]{2,1,0:T(8,128)S(1)}, u32[]{:S(2)}, u32[]{:S(2)}) collective-permute-start(f32[2,16,2048]{2,1,0:T(8,128)S(1)} %get-tuple-element.94), channel_id=1, source_target_pairs={{0,4},{4,0},{8,12},{12,8},{16,20},{20,16},{24,28},{28,24},{1,5},{5... | collective-permute-start | bytes 786440 | tf_op jit(solution)/shard_map/ppermute | solution.py:462
  52.2 2.2 %copy-start.4 = (bf16[2,256,4096]{2,1,0:T(8,128)(2,1)S(1)}, bf16[2,256,4096]{2,1,0:T(8,128)(2,1)}, u32[]{:S(2)}) copy-start(bf16[2,256,4096]{2,1,0:T(8,128)(2,1)} %copy-done.3) | copy-start | bytes 12582916
  54.4 0.9 %copy-start.12 = (bf16[2,256,128]{2,1,0:T(8,128)(2,1)S(1)}, bf16[2,256,128]{2,1,0:T(8,128)(2,1)}, u32[]{:S(2)}) copy-start(bf16[2,256,128]{2,1,0:T(8,128)(2,1)} %copy-done.11) | copy-start | bytes 393220
  55.3 0.8 copy-start.15
  56.1 7.9 %copy-start.13 = (bf16[2,256,128]{2,1,0:T(8,128)(2,1)S(1)}, bf16[2,256,128]{2,1,0:T(8,128)(2,1)}, u32[]{:S(2)}) copy-start(bf16[2,256,128]{2,1,0:T(8,128)(2,1)} %copy-done.11) | copy-start | bytes 393220
  62.0 10.2 %collective-permute-start.5 = (f32[2,16,2048]{2,1,0:T(8,128)S(1)}, f32[2,16,2048]{2,1,0:T(8,128)S(1)}, u32[]{:S(2)}, u32[]{:S(2)}) collective-permute-start(f32[2,16,2048]{2,1,0:T(8,128)S(1)} %broadcast_select_fusion.1), channel_id=1, source_target_pairs={{0,1},{2,3},{4,5},{6,7},{9,8},{11,10},{13,12},{15,14},{18,19},{16,... | collective-permute-start | bytes 786440 | tf_op jit(solution)/shard_map/ppermute | solution.py:493
  64.0 8.3 %slice-start = ((s8[8388608]{0:T(1024)(128)(4,1)}), s8[4194304]{0:T(1024)(128)(4,1)S(1)}, s32[]{:S(2)}) async-start(s8[8388608]{0:T(1024)(128)(4,1)} %bitcast.29), calls=%async_computation | async-start | bytes 8388608
  64.0 2.3 %copy-start.5 = (bf16[2,256,4096]{2,1,0:T(8,128)(2,1)S(1)}, bf16[2,256,4096]{2,1,0:T(8,128)(2,1)}, u32[]{:S(2)}) copy-start(bf16[2,256,4096]{2,1,0:T(8,128)(2,1)} %copy-done.3) | copy-start | bytes 12582916
  66.3 6.0 %slice-start.1 = ((s8[8388608]{0:T(1024)(128)(4,1)}), s8[4194304]{0:T(1024)(128)(4,1)S(1)}, s32[]{:S(2)}) async-start(s8[8388608]{0:T(1024)(128)(4,1)} %bitcast.29), calls=%async_computation.1 | async-start | bytes 8388608
  66.3 6.0 %copy-start.10 = (bf16[2,512,512]{2,1,0:T(8,128)(2,1)S(1)}, bf16[2,512,512]{2,1,0:T(8,128)(2,1)}, u32[]{:S(2)}) copy-start(bf16[2,512,512]{2,1,0:T(8,128)(2,1)} %copy-done.9) | copy-start | bytes 3145732
  66.3 6.0 %copy-start.18 = (s32[2]{0:T(128)S(1)}, s32[2]{0:T(128)}, u32[]{:S(2)}) copy-start(s32[2]{0:T(128)} %len_ref.1) | copy-start | bytes 28

commit v5 on v4

--- a/solution.py
+++ b/solution.py
@@ -10,7 +10,7 @@
 CHUNK = 32
 F32 = jnp.float32
 BF16 = jnp.bfloat16
-VMEM_LIMIT = 32 * 1024 * 1024
+VMEM_LIMIT = 16 * 1024 * 1024
 
 
 def iota(shape, dim):
@@ -124,13 +124,13 @@
     return pl.pallas_call(
         functools.partial(ends_kernel, width=width, lanes=lanes),
         in_specs=[pl.BlockSpec(memory_space=pltpu.HBM)] * 3,
-        out_specs=[whole, whole, whole],
+        out_specs=[whole, whole],
         out_shape=[
             jax.ShapeDtypeStruct((count, state, channels), F32),
             jax.ShapeDtypeStruct((count, 8, channels), F32),
-            jax.ShapeDtypeStruct(x.shape, BF16),
         ],
         scratch_shapes=[
+            pltpu.VMEM(x.shape, BF16),
             pltpu.VMEM(logdec.shape, F32),
             pltpu.VMEM(bc.shape[1:], BF16),
             pltpu.VMEM((count, heads * state, positions), BF16),
@@ -144,7 +144,7 @@
     )(in_hbm(x), in_hbm(logdec), in_hbm(bc))
 
 
-def prepare(parts, logs, lv_ref, lc_ref, state):
+def prepare(parts, logs, lv_ref, lc_ref, state, heads):
     size = logs.shape[1]
     chunks = size // CHUNK
     half = CHUNK // 2
@@ -167,7 +167,12 @@
         lv_ref[i, pl.ds(rows, size), :] = jnp.where(keep, scores, 0.0).astype(BF16)
         c_all = jnp.concatenate([c_rows.astype(F32)] * chunks, axis=0)
         lc_ref[i] = jnp.where(mine, c_all, 0.0).T.astype(BF16)
-    return in_scale, row_scale, steps
+    scales = []
+    for first in range(0, logs.shape[0], heads):
+        here = slice(first, first + heads)
+        columns = [hi_lo(in_scale[here]).T, hi_lo(steps[here]).T[:16], hi_lo(row_scale[here]).T]
+        scales.append(jnp.concatenate(columns, axis=0).astype(BF16))
+    return scales
 
 
 def cuts_of(ld_ref):
@@ -177,7 +182,7 @@
 
 def prepare_kernel(
     pld_ref, pbc_ref, bld_ref, bbc_ref,
-    pv_ref, pu_ref, ps_ref, plv_ref, plc_ref, w_ref, hot_ref, blv_ref, blc_ref, reach_ref, *, width
+    hot_ref, pw_ref, plv_ref, plc_ref, bw_ref, blv_ref, blc_ref, reach_ref, *, width
 ):
     state = pbc_ref.shape[2]
 
@@ -189,12 +194,8 @@
     cuts, logs, parts = collect(bld_ref, bbc_ref)
     heads = bld_ref.shape[1]
     blocks = len(cuts) // bld_ref.shape[0]
-    in_scale, row_scale, steps = prepare(parts, logs, blv_ref, blc_ref, state)
-    for k in range(len(cuts)):
-        here = slice(k * heads, (k + 1) * heads)
-        w_ref[k, pl.ds(0, BLOCK), :] = hi_lo(in_scale[here]).T.astype(BF16)
-        w_ref[k, pl.ds(BLOCK, 16), :] = hi_lo(steps[here]).T[:16].astype(BF16)
-        w_ref[k, pl.ds(BLOCK + 16, BLOCK), :] = hi_lo(row_scale[here]).T.astype(BF16)
+    for k, w in enumerate(prepare(parts, logs, blv_ref, blc_ref, state, heads)):
+        bw_ref[k] = w
     row_head = remainder(iota((2 * heads, 1), 0), heads)
     for g in range(hot_ref.shape[1] // 256):
         lane_head = quotient(iota((1, 256), 1), width) + g * (256 // width)
@@ -211,13 +212,8 @@
 
     cuts, logs, parts = collect(pld_ref, pbc_ref)
     heads = pld_ref.shape[1] // 2
-    in_scale, row_scale, steps = prepare(parts, logs, plv_ref, plc_ref, state)
-    for k in range(len(cuts)):
-        for h in range(2):
-            here = slice((2 * k + h) * heads, (2 * k + h + 1) * heads)
-            pv_ref[k, h] = in_scale[here].T
-            pu_ref[k, h] = row_scale[here].T
-            ps_ref[k, h] = steps[here].T[:16]
+    for k, w in enumerate(prepare(parts, logs, plv_ref, plc_ref, state, heads)):
+        pw_ref[k // 2, k % 2] = w
 
 
 def prepare_all(prompt_logdec, prompt_bc, branch_logdec, branch_bc, branch_channels):
@@ -228,13 +224,11 @@
     branch_cuts = branches * (positions // BLOCK)
     half = prompt_logdec.shape[1] // 2
     shapes = [
-        ((prompt_cuts, 2, BLOCK, half), F32),
-        ((prompt_cuts, 2, BLOCK, half), F32),
-        ((prompt_cuts, 2, 16, half), F32),
+        ((2 * heads, branch_channels), BF16),
+        ((prompt_cuts, 2, 2 * BLOCK + 16, 2 * half), BF16),
         ((prompt_cuts, rows + BLOCK, BLOCK), BF16),
         ((prompt_cuts, BLOCK, rows), BF16),
         ((branch_cuts, 2 * BLOCK + 16, 2 * heads), BF16),
-        ((2 * heads, branch_channels), BF16),
         ((branch_cuts, rows + BLOCK, BLOCK), BF16),
         ((branch_cuts, BLOCK, rows), BF16),
         ((branches, positions, heads * state), BF16),
@@ -243,13 +237,13 @@
     out = pl.pallas_call(
         functools.partial(prepare_kernel, width=branch_channels // heads),
         in_specs=[whole] * 4,
-        out_specs=[whole] * len(shapes),
+        out_specs=[pl.BlockSpec(shape, lambda rank=len(shape): (0,) * rank) for shape, _ in shapes],
         out_shape=[jax.ShapeDtypeStruct(*shape) for shape in shapes],
         compiler_params=pltpu.CompilerParams(vmem_limit_bytes=VMEM_LIMIT),
         cost_estimate=pl.CostEstimate(flops=10**8, bytes_accessed=10**6, transcendentals=0),
         name="prepare",
     )(prompt_logdec, prompt_bc, branch_logdec, branch_bc)
-    return out[:5], out[5:9], out[9]
+    return out[:4], (out[0], *out[4:7]), out[7]
 
 
 def run_tiles(jobs):
@@ -263,76 +257,117 @@
             jobs[g - 2][2](passed.pop(g - 2))
 
 
-def through_chunks(both, steps, entering, state, chunks):
-    rows, carry = [], steps[0:1] * entering
-    for c in range(chunks):
-        rows.append(carry.astype(BF16))
-        carry = steps[c + 1:c + 2] * (carry + both[c * state:(c + 1) * state])
-    return jnp.concatenate(rows, axis=0), carry
+def tile_job(ready_refs, at, g, x_of, entering_of, leave, write):
+    hot_ref, w_ref, lv_ref, lc_ref = ready_refs
+    w_at, at = at
+    rows = lc_ref.shape[2]
+    chunks = BLOCK // CHUNK
+    state = rows // chunks
+
+    def scale():
+        wide = jnp.dot(w_ref[w_at], hot_ref[:, pl.ds(g * 256, 256)], preferred_element_type=F32)
+        scaled = (x_of().astype(F32) * wide[:BLOCK]).astype(BF16)
+        return scaled, wide[BLOCK:BLOCK + 16], wide[BLOCK + 16:]
+
+    def pass_on(given):
+        scaled, steps, out_scale = given
+        both = jnp.dot(lv_ref[at], scaled, preferred_element_type=F32)
+        carries, carry = [], steps[0:1] * entering_of()
+        for c in range(chunks):
+            carries.append(carry.astype(BF16))
+            carry = steps[c + 1:c + 2] * (carry + both[c * state:(c + 1) * state])
+        leave(carry)
+        return both[rows:], jnp.concatenate(carries, axis=0), out_scale
+
+    def give(given):
+        inner, carries, out_scale = given
+        carried = jnp.dot(lc_ref[at], carries, preferred_element_type=F32)
+        write((inner + carried) * out_scale)
+
+    return scale, pass_on, give
+
+
+class Copies:
+    def __init__(self, sems):
+        self.sems, self.started = sems, {}
+
+    def start(self, key, source, target):
+        copy = pltpu.make_async_copy(source, target, self.sems.at[key])
+        copy.start()
+        self.started[key] = copy
+
+    def wait(self, key):
+        self.started.pop(key).wait()
+
+    def wait_all(self):
+        for key in list(self.started):
+            self.wait(key)
 
 
 def branch_kernel(*refs, which, skip):
-    x_in, w_ref, hot_ref, lv_ref, lc_ref = refs[:5]
-    own_ref, x_ref, s_ref, sems = refs[5 + skip:]
+    x_in, ready = refs[0], refs[1:5]
+    own_out, x_ref, own_ref, s_ref, in_sems, out_sems = refs[5 + skip:]
     positions, channels = x_ref.shape
     state = s_ref.shape[0]
-    chunks = BLOCK // CHUNK
-    rows = chunks * state
     blocks = positions // BLOCK
-    lanes = min(1024, channels)
-    copies = {}
+    lanes = channels // in_sems.shape[1]
+    came, left = Copies(in_sems), Copies(out_sems)
+
+    def spot(b, j):
+        return pl.ds(b * BLOCK, BLOCK), pl.ds(j * lanes, lanes)
+
     for b in range(blocks):
         for j in range(channels // lanes):
-            part = (pl.ds(b * BLOCK, BLOCK), pl.ds(j * lanes, lanes))
-            copies[b, j] = pltpu.make_async_copy(x_in.at[(which, *part)], x_ref.at[part], sems.at[b, j])
-            copies[b, j].start()
+            came.start((b, j), x_in.at[(which, *spot(b, j))], x_ref.at[spot(b, j)])
 
     def job(b, g):
+        cols = pl.ds(g * 256, 256)
+        here = (pl.ds(b * BLOCK, BLOCK), cols)
+
+        def x_of():
+            if g * 256 % lanes == 0:
+                came.wait((b, g * 256 // lanes))
+            return x_ref[here]
+
+        def leave(carry):
+            if b < blocks - 1:
+                s_ref[:, cols] = carry
+
+        def write(out):
+            own_ref[here] = out
+            if (g + 1) * 256 % lanes == 0:
+                j = g * 256 // lanes
+                left.start((b, j), own_ref.at[spot(b, j)], own_out.at[(which, *spot(b, j))])
+
+        def entering_of():
+            return s_ref[:, cols] if b else jnp.zeros((state, 256), F32)
+
         at = which * blocks + b
-        spot = (pl.ds(b * BLOCK, BLOCK), pl.ds(g * 256, 256))
-
-        def scale():
-            if g * 256 % lanes == 0:
-                copies[b, g * 256 // lanes].wait()
-            wide = jnp.dot(w_ref[at], hot_ref[:, pl.ds(g * 256, 256)], preferred_element_type=F32)
-            scaled = (x_ref[spot].astype(F32) * wide[:BLOCK]).astype(BF16)
-            return scaled, wide[BLOCK:BLOCK + 16], wide[BLOCK + 16:]
-
-        def pass_on(given):
-            scaled, steps, out_scale = given
-            both = jnp.dot(lv_ref[at], scaled, preferred_element_type=F32)
-            here = pl.ds(g * 256, 256)
-            entering = s_ref[:, here] if b else jnp.zeros((state, 256), F32)
-            carries, carry = through_chunks(both, steps, entering, state, chunks)
-            if b < blocks - 1:
-                s_ref[:, here] = carry
-            return both[rows:], carries, out_scale
-
-        def give(given):
-            inner, carries, out_scale = given
-            carried = jnp.dot(lc_ref[at], carries, preferred_element_type=F32)
-            own_ref[(which, *spot)] = (inner + carried) * out_scale
-
-        return scale, pass_on, give
+        return tile_job(ready, (at, at), g, x_of, entering_of, leave, write)
 
     run_tiles([job(b, g) for b in range(blocks) for g in range(channels // 256)])
+    left.wait_all()
 
 
 def branch_own(x, ready, which, into):
     _, positions, channels = x.shape
     state = ready[3].shape[2] * CHUNK // BLOCK
     whole = pl.BlockSpec(memory_space=pltpu.VMEM)
-    lanes = min(1024, channels)
+    hbm = pl.BlockSpec(memory_space=pltpu.HBM)
+    anywhere = pl.BlockSpec(memory_space=pl.ANY)
+    parts = (positions // BLOCK, channels // min(512, channels))
     work = positions * channels
     return pl.pallas_call(
         functools.partial(branch_kernel, which=which, skip=len(into)),
-        in_specs=[pl.BlockSpec(memory_space=pltpu.HBM)] + [whole] * (4 + len(into)),
-        out_specs=whole,
+        in_specs=[hbm] + [whole] * 4 + [anywhere] * len(into),
+        out_specs=anywhere,
         out_shape=jax.ShapeDtypeStruct(x.shape, F32),
         scratch_shapes=[
             pltpu.VMEM((positions, channels), BF16),
+            pltpu.VMEM((positions, channels), F32),
             pltpu.VMEM((state, channels), F32),
-            pltpu.SemaphoreType.DMA((positions // BLOCK, channels // lanes)),
+            pltpu.SemaphoreType.DMA(parts),
+            pltpu.SemaphoreType.DMA(parts),
         ],
         input_output_aliases={5 + i: i for i in range(len(into))},
         compiler_params=pltpu.CompilerParams(vmem_limit_bytes=VMEM_LIMIT),
@@ -342,115 +377,118 @@
     )(in_hbm(x), *ready, *into)
 
 
-def prompt_kernel(*refs, width, skip):
-    half_ref, x_ref, v_ref, u_ref, s_ref, lv_ref, lc_ref, start_ref = refs[:8]
-    y_out, y_ref, sems = refs[8 + skip:]
+def prompt_kernel(*refs, skip):
+    half_ref, x_in, *ready, start_ref = refs[:7]
+    y_out, x_ref, y_ref, in_sems, out_sems = refs[7 + skip:]
     count, positions, channels = y_ref.shape
-    state = start_ref.shape[1]
-    chunks = BLOCK // CHUNK
-    rows = chunks * state
     blocks = positions // BLOCK
-    lanes = min(512, channels)
+    lanes = channels // in_sems.shape[2]
     half = half_ref[0]
-    left = iota((1, 128), 1) < width
-    entered, copies = {}, []
-
-    def widen(scales, g):
-        def pair(k):
-            return jnp.where(left, scales[:, k:k + 1], scales[:, k + 1:k + 2])
-
-        first = g * (256 // width)
-        return jnp.concatenate([pair(first + k) for k in range(0, 256 // width, 2)], axis=1)
+    came, left = Copies(in_sems), Copies(out_sems)
+    entered = {}
+
+    def spots(i, b, j):
+        there = pl.ds(pl.multiple_of(half * channels + j * lanes, lanes), lanes)
+        rows = pl.ds(b * BLOCK, BLOCK)
+        return (i, rows, there), (i, rows, pl.ds(j * lanes, lanes))
+
+    for i in range(count):
+        for b in range(blocks):
+            for j in range(channels // lanes):
+                there, here = spots(i, b, j)
+                came.start((i, b, j), x_in.at[there], x_ref.at[here])
 
     def job(i, b, g):
+        here = (i, pl.ds(b * BLOCK, BLOCK), pl.ds(g * 256, 256))
+        j = g * 256 // lanes
+
+        def x_of():
+            if g * 256 % lanes == 0:
+                came.wait((i, b, j))
+            return x_ref[here]
+
+        def leave(carry):
+            entered[i, g] = carry
+
+        def entering_of():
+            return entered[i, g] if b else start_ref[i, :, pl.ds(g * 256, 256)]
+
+        def write(out):
+            y_ref[here] = out.astype(BF16)
+            if (g + 1) * 256 % lanes == 0:
+                there, staged = spots(i, b, j)
+                left.start((i, b, j), y_ref.at[staged], y_out.at[there])
+
         at = i * blocks + b
-        spot = (i, pl.ds(b * BLOCK, BLOCK), pl.ds(g * 256, 256))
-
-        def scale():
-            cols = pl.ds(pl.multiple_of(half * channels + g * 256, 256), 256)
-            wide = widen(v_ref[at, half], g)
-            return (x_ref[i, pl.ds(b * BLOCK, BLOCK), cols].astype(F32) * wide).astype(BF16)
-
-        def pass_on(scaled):
-            both = jnp.dot(lv_ref[at], scaled, preferred_element_type=F32)
-            entering = entered[i, g] if b else start_ref[i, :, pl.ds(g * 256, 256)]
-            steps = widen(s_ref[at, half], g)
-            carries, entered[i, g] = through_chunks(both, steps, entering, state, chunks)
-            return both[rows:], carries
-
-        def give(given):
-            inner, carries = given
-            carried = jnp.dot(lc_ref[at], carries, preferred_element_type=F32)
-            y_ref[spot] = ((inner + carried) * widen(u_ref[at, half], g)).astype(BF16)
-            if (g + 1) * 256 % lanes == 0:
-                j = (g + 1) * 256 // lanes - 1
-                there = pl.ds(pl.multiple_of(half * channels + j * lanes, lanes), lanes)
-                copy = pltpu.make_async_copy(
-                    y_ref.at[i, pl.ds(b * BLOCK, BLOCK), pl.ds(j * lanes, lanes)],
-                    y_out.at[i, pl.ds(b * BLOCK, BLOCK), there], sems.at[at, j])
-                copy.start()
-                copies.append(copy)
-
-        return scale, pass_on, give
+        return tile_job(ready, ((at, half), at), g, x_of, entering_of, leave, write)
 
     run_tiles([job(i, b, g) for i in range(count) for b in range(blocks) for g in range(channels // 256)])
-    for copy in copies:
-        copy.wait()
+    left.wait_all()
 
 
 def prompt_half(half, x, ready, start, into):
     count, positions, channels = x.shape
-    width = channels // (2 * ready[0].shape[3])
     part = channels // 2
     whole = pl.BlockSpec(memory_space=pltpu.VMEM)
     hbm = pl.BlockSpec(memory_space=pltpu.HBM)
+    parts = (count, positions // BLOCK, part // min(512, part))
     work = count * positions * part
     return pl.pallas_call(
-        functools.partial(prompt_kernel, width=width, skip=len(into)),
-        in_specs=[pl.BlockSpec(memory_space=pltpu.SMEM)] + [whole] * 7 + [hbm] * len(into),
+        functools.partial(prompt_kernel, skip=len(into)),
+        in_specs=[pl.BlockSpec(memory_space=pltpu.SMEM), hbm] + [whole] * 5 + [hbm] * len(into),
         out_specs=hbm,
         out_shape=jax.ShapeDtypeStruct(x.shape, BF16),
         scratch_shapes=[
             pltpu.VMEM((count, positions, part), BF16),
-            pltpu.SemaphoreType.DMA((count * (positions // BLOCK), part // min(512, part))),
+            pltpu.VMEM((count, positions, part), BF16),
+            pltpu.SemaphoreType.DMA(parts),
+            pltpu.SemaphoreType.DMA(parts),
         ],
-        input_output_aliases={8 + i: i for i in range(len(into))},
+        input_output_aliases={7 + i: i for i in range(len(into))},
         compiler_params=pltpu.CompilerParams(vmem_limit_bytes=VMEM_LIMIT),
         cost_estimate=pl.CostEstimate(
             flops=2 * 1152 * work, bytes_accessed=4 * work, transcendentals=0),
         name="prompt_half",
-    )(half, x, *ready, start, *into)
-
-
-def finish_kernel(len_ref, own_ref, reach_ref, start_ref, y_ref, *, width):
-    branch, tile = pl.program_id(0), pl.program_id(1)
-    positions, lanes = y_ref.shape[1], y_ref.shape[2]
+    )(half, in_hbm(x), *ready, start, *into)
+
+
+def finish_kernel(len_ref, own_ref, reach_ref, start_ref, y_out, y_ref, sems, *, width):
+    count, positions, channels = y_ref.shape
     state = start_ref.shape[0]
     group = 128 // state
     span = group * width
-    live = iota((positions, span), 0) < len_ref[branch]
+    left = Copies(sems)
     own_head = quotient(iota((128, 1), 0), state) == quotient(iota((1, span), 1), width)
-    for g in range(lanes // span):
-        here = pl.ds(pl.multiple_of(tile * lanes + g * span, span), span)
-        first = pl.ds(pl.multiple_of((tile * (lanes // span) + g) * 128, 128), 128)
-        start = jnp.concatenate([start_ref[:, here]] * group, axis=0)
-        start = jnp.where(own_head, start, 0.0).astype(BF16)
-        term = jnp.dot(reach_ref[branch, :, first], start, preferred_element_type=F32)
-        out = jnp.where(live, own_ref[branch, :, here] + term, 0.0)
-        y_ref[0, :, pl.ds(g * span, span)] = out.astype(BF16)
+    starts = []
+    for g in range(channels // span):
+        start = jnp.concatenate([start_ref[:, pl.ds(g * span, span)]] * group, axis=0)
+        starts.append(jnp.where(own_head, start, 0.0).astype(BF16))
+    for i in range(count):
+        for g in range(channels // span):
+            for b in range(positions // BLOCK):
+                rows, cols = pl.ds(b * BLOCK, BLOCK), pl.ds(g * span, span)
+                term = jnp.dot(
+                    reach_ref[i, rows, pl.ds(g * 128, 128)], starts[g], preferred_element_type=F32)
+                live = iota((BLOCK, span), 0) < len_ref[i] - b * BLOCK
+                y_ref[i, rows, cols] = jnp.where(live, own_ref[i, rows, cols] + term, 0.0).astype(BF16)
+                left.start((i, b, g), y_ref.at[i, rows, cols], y_out.at[i, rows, cols])
+    left.wait_all()
 
 
 def finish(lengths, own, reach, start):
     count, positions, channels = own.shape
-    width = channels * start.shape[0] // reach.shape[2]
-    lanes = min(1024, channels)
+    state = start.shape[0]
+    width = channels * state // reach.shape[2]
     whole = pl.BlockSpec(memory_space=pltpu.VMEM)
     return pl.pallas_call(
         functools.partial(finish_kernel, width=width),
-        grid=(count, channels // lanes),
         in_specs=[pl.BlockSpec(memory_space=pltpu.SMEM), whole, whole, whole],
-        out_specs=pl.BlockSpec((1, positions, lanes), lambda i, j: (i, 0, j)),
+        out_specs=pl.BlockSpec(memory_space=pltpu.HBM),
         out_shape=jax.ShapeDtypeStruct(own.shape, BF16),
+        scratch_shapes=[
+            pltpu.VMEM(own.shape, BF16),
+            pltpu.SemaphoreType.DMA((count, positions // BLOCK, reach.shape[2] // 128)),
+        ],
         compiler_params=pltpu.CompilerParams(vmem_limit_bytes=VMEM_LIMIT),
         cost_estimate=pl.CostEstimate(
             flops=2 * 128 * own.size, bytes_accessed=6 * own.size, transcendentals=0),
@@ -516,7 +554,7 @@
         got = exchange(value)
         return lax.optimization_barrier((got, work(*given)))
 
-    end, log, held = local_ends(prompt_x, prompt_logdec, prompt_bc)
+    end, log = local_ends(prompt_x, prompt_logdec, prompt_bc)
     half = end.shape[2] // 2
     low, high = (end[:, :, :half], log[:, :1, :half]), (end[:, :, half:], log[:, :1, half:])
     keep = [jnp.where(odd, h, l) for l, h in zip(low, high)]
@@ -566,13 +604,13 @@
             side, entering = sides.pop(0)
             (got, has), prompt_y = beside(
                 step, total,
-                lambda entering, y: (prompt_half(side, held, prompt_ready, entering, y),), entering, prompt_y)
+                lambda entering, y: (prompt_half(side, prompt_x, prompt_ready, entering, y),), entering, prompt_y)
         else:
             got, has = step(total)
         total = jnp.where(has, total, got)
         hop //= 2
     for side, entering in sides:
-        prompt_y = (prompt_half(side, held, prompt_ready, entering, prompt_y),)
+        prompt_y = (prompt_half(side, prompt_x, prompt_ready, entering, prompt_y),)
     start = total[0]
     for which in range(1, prompts):
         start = jnp.where(branch_prompt[0] == which, total[which], start)

time: 76.8 us -> 67.9 us (0.88)
  local copies, waits for them, and re-layouts: 28.5 us -> 15.8 us
  Pallas kernels: 31.6 us -> 36 us
    unnamed x80 -> x46, local copies, waits for them, and re-layouts: 25.7 us -> 13 us
    pallas_call x2, Pallas kernels: 9.17 us -> 14.4 us  [branch_own(): pl.pallas_call(functools.partial(branch_kernel, which=which, skip=len(int...]
    pallas_call x3, Pallas kernels: 15.6 us -> 14.7 us  [the longest x2 11.8 us: prompt_half(): pl.pallas_call(functools.partial(prompt_kernel, skip=len(into)), in_specs...]
  transfers between devices with their start and end apart: 6 -> 6, of which waited for: 0 -> 0; matrix products, arithmetic and copies ran while one was open for 0% -> 0% of each run, Pallas kernels for 30% -> 42%
where the time goes in v5:
time: 67.9 us; the launch traced here: 67.4 us
  Pallas kernels  36 us (53%)
  local copies, waits for them, and re-layouts  15.8 us (23%)
  starting transfers between devices  10.7 us (16%)
  other arithmetic  2.96 us (4%)
  between operations  1.95 us (3%)
    pallas_call x2, Pallas kernels, branch_own(): pl.pallas_call(functools.partial(branch_kernel, which=which, skip=len(int...  14.4 us
    unnamed x46, local copies, waits for them, and re-layouts  13 us
    pallas_call x2, Pallas kernels, prompt_half(): pl.pallas_call(functools.partial(prompt_kernel, skip=len(into)), in_specs...  11.8 us
    ppermute x2, starting transfers between devices, spread_step(): got = lax.ppermute(value, ('ctx', 'pair'), links)  6.03 us
    pallas_call x1, Pallas kernels, local_ends(): pl.pallas_call(functools.partial(ends_kernel, width=width, lanes=lanes),...  5 us
    ppermute x4, starting transfers between devices, swap_bit(): return lax.ppermute(value, 'ctx', [(k, k ^ bit) for k in range(size)])  4.64 us
    pallas_call x1, Pallas kernels, finish(): pl.pallas_call(functools.partial(finish_kernel, width=width), in_specs=[p...  2.89 us
    slice x3, local copies, waits for them, and re-layouts, unpack(): packed[:rows].reshape(count, rows // count, lanes)  1.96 us
  transfers between devices with their start and end apart: 6, of which 0 were waited for; matrix products, arithmetic and copies ran while one was open for 0% of the time, Pallas kernels for 42%

profile of v5, /device:TPU:0, one launch (start us, length us, event | category | flops | bytes accessed | tf_op | source)
XLA Modules:
  0.0 67.4 jit_solution(14610414529581533470)
XLA Ops:
  0.6 0.0 copy-start.6
  0.6 0.0 copy-start.9
  0.7 0.0 copy-start.5
  0.7 0.0 copy-start.8
  0.7 5.0 %local_ends.1 = (f32[2,16,4096]{2,1,0:T(8,128)S(1)}, f32[2,8,4096]{2,1,0:T(8,128)S(1)}) custom-call(bf16[2,256,4096]{2,1,0:T(8,128)(2,1)} %refs_1_.3, f32[2,64,256]{2,1,0:T(8,128)} %pld_ref.1, bf16[2,2,16,256]{3,2,1,0:T(8,128)(2,1)} %pbc_ref.1), custom_call_target="tpu_custom_call" | custom-call | flops 268435456 | bytes 4194304 | tf_op jit(solution)/shard_map/local_ends/pallas_call | solution.py:124
  5.8 0.5 collective-permute-start
  6.3 0.0 copy-done.6
  6.3 0.0 copy-done.9
  6.3 0.0 copy-done.5
  6.3 0.0 copy-done.8
  6.3 1.9 %prepare.1 = (bf16[64,2048]{1,0:T(8,128)(2,1)S(1)}, bf16[2,2,528,64]{3,2,1,0:T(8,128)(2,1)S(1)}, bf16[2,384,256]{2,1,0:T(8,128)(2,1)S(1)}, bf16[2,256,128]{2,1,0...) custom-call(f32[2,64,256]{2,1,0:T(8,128)S(1)} %copy-done.5, ...), custom_call_target="tpu_custom_call" | custom-call | flops 100000000 | bytes 1000000 | tf_op jit(solution)/shard_map/prepare/pallas_call | solution.py:237
  8.2 0.0 copy-start.3
  8.2 1.0 %copy-done.3 = bf16[2,512,512]{2,1,0:T(8,128)(2,1)} copy-done((bf16[2,512,512]{2,1,0:T(8,128)(2,1)}, bf16[2,512,512]{2,1,0:T(8,128)(2,1)S(1)}, u32[]{:S(2)}) %copy-start.3) | copy-done | bytes 1048600
  9.2 0.0 collective-permute-done
  9.2 0.0 copy-start.12
  9.4 0.6 copy-done.12
  10.0 0.1 select_add_fusion.2
  10.0 0.0 copy-start.16
  10.0 0.7 %copy-done.16 = f32[2,16,2048]{2,1,0:T(8,128)} copy-done((f32[2,16,2048]{2,1,0:T(8,128)}, f32[2,16,2048]{2,1,0:T(8,128)S(1)}, u32[]{:S(2)}) %copy-start.16) | copy-done | bytes 262168
  10.7 0.7 %pad_maximum_fusion.1 = f32[34,2048]{1,0:T(8,128)} fusion(f32[2,2048]{1,0:T(2,128)S(1)} %get-tuple-element.97, f32[32,2048]{1,0:T(8,128)S(1)} %bitcast.36), kind=kLoop, calls=%fused_computation.2 | loop fusion | flops 69632 | bytes 557056 | tf_op jit(solution)/shard_map/concatenate | solution.py:505
  11.5 2.5 %collective-permute-start.1 = (f32[34,2048]{1,0:T(8,128)}, f32[34,2048]{1,0:T(8,128)}, u32[]{:S(2)}, u32[]{:S(2)}) collective-permute-start(f32[34,2048]{1,0:T(8,128)} %pad_maximum_fusion.1), channel_id=1, source_target_pairs={{0,8},{4,12},{8,0},{12,4},{16,24},{20,28},{24,16},{28,20},{1,9},{5... | collective-permute-start | bytes 835592 | tf_op jit(solution)/shard_map/ppermute | solution.py:500
  14.0 0.0 copy-start.17
  14.0 7.3 %branch_own.2.refs_5_ = f32[2,512,2048]{2,1,0:T(8,128)S(1)} custom-call(bf16[2,512,2048]{2,1,0:T(8,128)(2,1)} %refs_0_.1, bf16[64,2048]{1,0:T(8,128)(2,1)S(1)} %get-tuple-element.70.refs_1_.refs_2_, bf16[4,528,64]{2,1,0:T(8,128)(2,1)S(1)} %get-tuple-element.60.refs_2_, bf16[4,384,256]{2,1,0:T(8,128)(2,1)S(1)} %get-tuple-element.61.refs_3_, ...), custom_call_target="tpu_custom_call" | custom-call | flops 2415919104 | bytes 4194304 | tf_op jit(solution)/shard_map/branch_own/pallas_call | solution.py:360
  21.3 0.0 copy-start
  21.3 3.3 %copy-done = f32[2,512,2048]{2,1,0:T(8,128)} copy-done((f32[2,512,2048]{2,1,0:T(8,128)}, f32[2,512,2048]{2,1,0:T(8,128)S(1)}, u32[]{:S(2)}) %copy-start) | copy-done | bytes 8388632
  24.6 0.0 collective-permute-done.1
  24.6 1.0 %slice.43 = f32[32,2048]{1,0:T(8,128)S(1)} slice(f32[34,2048]{1,0:T(8,128)} %collective-permute-done.1), slice={[0:32], [0:2048]} | slice | bytes 524288 | tf_op jit(solution)/shard_map/slice | solution.py:511
  25.6 0.0 copy-start.14
  25.6 0.9 %select_exponential_fusion = (f32[2,2048]{1,0:T(2,128)S(1)}, f32[2,2048]{1,0:T(2,128)S(1)}) fusion(pred[]{:T(512)S(6)} %ne.17, f32[34,2048]{1,0:T(8,128)} %collective-permute-done.1), kind=kLoop, calls=%fused_computation.33 | loop fusion | flops 4096 | bytes 49153 | tf_op jit(solution)/shard_map/exp | solution.py:587
  26.6 0.0 copy-done.17
  26.6 0.1 select_add_fusion.1
  26.7 0.0 copy-start.10
  26.7 0.7 %copy-done.10 = f32[2,16,2048]{2,1,0:T(8,128)} copy-done((f32[2,16,2048]{2,1,0:T(8,128)}, f32[2,16,2048]{2,1,0:T(8,128)S(1)}, u32[]{:S(2)}) %copy-start.10) | copy-done | bytes 262168
  27.4 0.7 %pad_maximum_fusion.2 = f32[34,2048]{1,0:T(8,128)} fusion(f32[2,2048]{1,0:T(2,128)S(1)} %bitcast.41, f32[32,2048]{1,0:T(8,128)S(1)} %bitcast.31), kind=kLoop, calls=%fused_computation.3 | loop fusion | flops 69632 | bytes 557056 | tf_op jit(solution)/shard_map/concatenate | solution.py:505
  28.1 0.0 copy-done.14
  28.1 1.5 %collective-permute-start.2 = (f32[34,2048]{1,0:T(8,128)}, f32[34,2048]{1,0:T(8,128)}, u32[]{:S(2)}, u32[]{:S(2)}) collective-permute-start(f32[34,2048]{1,0:T(8,128)} %pad_maximum_fusion.2), channel_id=1, source_target_pairs={{0,16},{4,20},{8,24},{12,28},{16,0},{20,4},{24,8},{28,12},{1,17},{... | collective-permute-start | bytes 835592 | tf_op jit(solution)/shard_map/ppermute | solution.py:500
  29.6 3.4 %copy-done.1 = f32[2,512,2048]{2,1,0:T(8,128)S(1)} copy-done((f32[2,512,2048]{2,1,0:T(8,128)S(1)}, f32[2,512,2048]{2,1,0:T(8,128)}, u32[]{:S(2)}) %copy-start.1) | copy-done | bytes 8388632
  33.0 7.1 %branch_own.3.own_ref = f32[2,512,2048]{2,1,0:T(8,128)S(1)} custom-call(bf16[2,512,2048]{2,1,0:T(8,128)(2,1)} %refs_0_.1, bf16[64,2048]{1,0:T(8,128)(2,1)S(1)} %get-tuple-element.70.refs_1_.refs_2_, bf16[4,528,64]{2,1,0:T(8,128)(2,1)S(1)} %get-tuple-element.60.refs_2_, ...), custom_call_target="tpu_custom_call", output_to_operand_aliasing={{}: (5, {})} | custom-call | flops 2415919104 | bytes 4194304 | tf_op jit(solution)/shard_map/branch_own/pallas_call | solution.py:360
  40.2 0.0 copy-start.2
  40.2 3.3 %copy-done.2 = f32[2,512,2048]{2,1,0:T(8,128)} copy-done((f32[2,512,2048]{2,1,0:T(8,128)}, f32[2,512,2048]{2,1,0:T(8,128)S(1)}, u32[]{:S(2)}) %copy-start.2) | copy-done | bytes 8388632
  43.4 0.0 collective-permute-done.2
  43.5 1.0 %slice.45 = f32[32,2048]{1,0:T(8,128)S(1)} slice(f32[34,2048]{1,0:T(8,128)} %collective-permute-done.2), slice={[0:32], [0:2048]} | slice | bytes 524288 | tf_op jit(solution)/shard_map/slice | solution.py:511
  44.4 0.8 %slice.44 = f32[2,2048]{1,0:T(2,128)S(1)} slice(f32[34,2048]{1,0:T(8,128)} %collective-permute-done.2), slice={[32:34], [0:2048]} | slice | bytes 32768 | tf_op jit(solution)/shard_map/slice | solution.py:511
  45.3 0.0 copy-done.11
  45.3 0.0 copy-done.13
  45.3 0.0 copy-done.15
  45.3 0.1 fusion
  45.5 4.5 %collective-permute-start.3 = (f32[2,16,2048]{2,1,0:T(8,128)S(1)}, f32[2,16,2048]{2,1,0:T(8,128)S(1)}, u32[]{:S(2)}, u32[]{:S(2)}) collective-permute-start(f32[2,16,2048]{2,1,0:T(8,128)S(1)} %get-tuple-element.69), channel_id=1, source_target_pairs={{0,2},{4,6},{9,11},{13,15},{18,16},{22,20},{27,25},{31,29}} | collective-permute-start | bytes 786440 | tf_op jit(solution)/shard_map/ppermute | solution.py:531
  50.0 0.1 collective-permute-start.4
  50.1 5.8 %prompt_half.2.refs_7_ = bf16[2,256,4096]{2,1,0:T(8,128)(2,1)} custom-call(s32[1]{0:T(128)} %bitcast.6.refs_0_, bf16[2,256,4096]{2,1,0:T(8,128)(2,1)} %refs_1_.3, bf16[64,2048]{1,0:T(8,128)(2,1)S(1)} %get-tuple-element.70.refs_1_.refs_2_, bf16[2,2,528,64]{3,2,1,0:T(8,128)(2,1)S(1)} %get-tuple-element.71.refs_3_, ...), custom_call_target="tpu_custom_call" | custom-call | flops 2415919104 | bytes 4194304 | tf_op jit(solution)/shard_map/prompt_half/pallas_call | solution.py:436
  55.9 0.0 collective-permute-done.3
  56.0 0.0 collective-permute-done.4.refs_6_
  56.0 1.5 %collective-permute-start.5 = (f32[2,16,2048]{2,1,0:T(8,128)S(1)}, f32[2,16,2048]{2,1,0:T(8,128)S(1)}, u32[]{:S(2)}, u32[]{:S(2)}) collective-permute-start(f32[2,16,2048]{2,1,0:T(8,128)S(1)} %broadcast_select_fusion.1), channel_id=1, source_target_pairs={{0,1},{2,3},{4,5},{6,7},{9,8},{11,10},{13,12},{15,14},{18,19},{16,... | collective-permute-start | bytes 786440 | tf_op jit(solution)/shard_map/ppermute | solution.py:531
  58.2 0.0 slice-start
  58.2 0.0 slice-start.1
  58.2 0.0 copy-start.4
  58.2 0.0 copy-start.7
  58.2 6.0 %prompt_half.3 = bf16[2,256,4096]{2,1,0:T(8,128)(2,1)} custom-call(s32[1]{0:T(128)S(6)} %sub.9.refs_0_, bf16[2,256,4096]{2,1,0:T(8,128)(2,1)} %refs_1_.3, bf16[64,2048]{1,0:T(8,128)(2,1)S(1)} %get-tuple-element.70.refs_1_.refs_2_, bf16[2,2,528,64]{3,2,1,0:T(8,128)(2,1)S(1)} %get-tuple-element.71.refs_3_, ...), custom_call_target="tpu_custom_call", output_to_operand_aliasing={{}: (7, {})} | custom-call | flops 2415919104 | bytes 4194304 | tf_op jit(solution)/shard_map/prompt_half/pallas_call | solution.py:436
  64.2 0.0 collective-permute-done.5
  64.3 0.0 slice-done
  64.3 0.0 slice-done.1
  64.3 0.0 copy-done.4
  64.3 0.0 copy-done.7
  64.3 2.9 %branch_finish.1 = bf16[2,512,2048]{2,1,0:T(8,128)(2,1)} custom-call(s32[2]{0:T(128)S(1)} %copy-done.7, f32[2,512,2048]{2,1,0:T(8,128)S(1)} %bitcast.30, bf16[2,512,512]{2,1,0:T(8,128)(2,1)S(1)} %copy-done.4, f32[16,2048]{1,0:T(8,128)S(1)} %fusion.2.start_ref), custom_call_target="tpu_custom_call" | custom-call | flops 536870912 | bytes 12582912 | tf_op jit(solution)/shard_map/branch_finish/pallas_call | solution.py:483
  (22 shorter events, 0.4 us)
Async XLA Ops:
  0.6 5.7 %copy-start.6 = (bf16[2,2,16,256]{3,2,1,0:T(8,128)(2,1)S(1)}, bf16[2,2,16,256]{3,2,1,0:T(8,128)(2,1)}, u32[]{:S(2)}) copy-start(bf16[2,2,16,256]{3,2,1,0:T(8,128)(2,1)} %pbc_ref.1) | copy-start | bytes 98308
  0.6 5.7 %copy-start.9 = (bf16[2,2,16,512]{3,2,1,0:T(8,128)(2,1)S(1)}, bf16[2,2,16,512]{3,2,1,0:T(8,128)(2,1)}, u32[]{:S(2)}) copy-start(bf16[2,2,16,512]{3,2,1,0:T(8,128)(2,1)} %bbc_ref.1) | copy-start | bytes 196612
  0.7 5.7 %copy-start.5 = (f32[2,64,256]{2,1,0:T(8,128)S(1)}, f32[2,64,256]{2,1,0:T(8,128)}, u32[]{:S(2)}) copy-start(f32[2,64,256]{2,1,0:T(8,128)} %pld_ref.1) | copy-start | bytes 393220
  0.7 5.7 %copy-start.8 = (f32[2,32,512]{2,1,0:T(8,128)S(1)}, f32[2,32,512]{2,1,0:T(8,128)}, u32[]{:S(2)}) copy-start(f32[2,32,512]{2,1,0:T(8,128)} %bld_ref) | copy-start | bytes 393220
  5.8 3.4 %collective-permute-start = (f32[34,2048]{1,0:T(8,128)S(1)}, f32[34,2048]{1,0:T(8,128)S(1)}, u32[]{:S(2)}, u32[]{:S(2)}) collective-permute-start(f32[34,2048]{1,0:T(8,128)S(1)} %pad_maximum_fusion), channel_id=1, source_target_pairs={{0,4},{4,0},{8,12},{12,8},{16,20},{20,16},{24,28},{28,24},{1,5},{5... | collective-permute-start | bytes 835592 | tf_op jit(solution)/shard_map/ppermute | solution.py:500
  8.2 1.0 %copy-start.3 = (bf16[2,512,512]{2,1,0:T(8,128)(2,1)}, bf16[2,512,512]{2,1,0:T(8,128)(2,1)S(1)}, u32[]{:S(2)}) copy-start(bf16[2,512,512]{2,1,0:T(8,128)(2,1)S(1)} %get-tuple-element.83.reach_ref) | copy-start | bytes 3145732
  9.2 0.7 %copy-start.12 = (f32[32,2048]{1,0:T(8,128)}, f32[32,2048]{1,0:T(8,128)S(1)}, u32[]{:S(2)}) copy-start(f32[32,2048]{1,0:T(8,128)S(1)} %slice.41) | copy-start | bytes 786436
  10.0 0.7 %copy-start.16 = (f32[2,16,2048]{2,1,0:T(8,128)}, f32[2,16,2048]{2,1,0:T(8,128)S(1)}, u32[]{:S(2)}) copy-start(f32[2,16,2048]{2,1,0:T(8,128)S(1)} %select_add_fusion.2) | copy-start | bytes 786436
  11.5 13.1 %collective-permute-start.1 = (f32[34,2048]{1,0:T(8,128)}, f32[34,2048]{1,0:T(8,128)}, u32[]{:S(2)}, u32[]{:S(2)}) collective-permute-start(f32[34,2048]{1,0:T(8,128)} %pad_maximum_fusion.1), channel_id=1, source_target_pairs={{0,8},{4,12},{8,0},{12,4},{16,24},{20,28},{24,16},{28,20},{1,9},{5... | collective-permute-start | bytes 835592 | tf_op jit(solution)/shard_map/ppermute | solution.py:500
  14.0 12.6 %copy-start.17 = (f32[2,16,2048]{2,1,0:T(8,128)S(1)}, f32[2,16,2048]{2,1,0:T(8,128)}, u32[]{:S(2)}) copy-start(f32[2,16,2048]{2,1,0:T(8,128)} %copy-done.16) | copy-start | bytes 786436
  21.3 3.3 %copy-start = (f32[2,512,2048]{2,1,0:T(8,128)}, f32[2,512,2048]{2,1,0:T(8,128)S(1)}, u32[]{:S(2)}) copy-start(f32[2,512,2048]{2,1,0:T(8,128)S(1)} %branch_own.2.refs_5_) | copy-start | bytes 25165828
  25.6 2.5 %copy-start.14 = (f32[32,2048]{1,0:T(8,128)}, f32[32,2048]{1,0:T(8,128)S(1)}, u32[]{:S(2)}) copy-start(f32[32,2048]{1,0:T(8,128)S(1)} %slice.43) | copy-start | bytes 786436
  26.7 0.7 %copy-start.10 = (f32[2,16,2048]{2,1,0:T(8,128)}, f32[2,16,2048]{2,1,0:T(8,128)S(1)}, u32[]{:S(2)}) copy-start(f32[2,16,2048]{2,1,0:T(8,128)S(1)} %select_add_fusion.1) | copy-start | bytes 786436
  28.1 15.3 %collective-permute-start.2 = (f32[34,2048]{1,0:T(8,128)}, f32[34,2048]{1,0:T(8,128)}, u32[]{:S(2)}, u32[]{:S(2)}) collective-permute-start(f32[34,2048]{1,0:T(8,128)} %pad_maximum_fusion.2), channel_id=1, source_target_pairs={{0,16},{4,20},{8,24},{12,28},{16,0},{20,4},{24,8},{28,12},{1,17},{... | collective-permute-start | bytes 835592 | tf_op jit(solution)/shard_map/ppermute | solution.py:500
  29.6 3.4 %copy-start.1 = (f32[2,512,2048]{2,1,0:T(8,128)S(1)}, f32[2,512,2048]{2,1,0:T(8,128)}, u32[]{:S(2)}) copy-start(f32[2,512,2048]{2,1,0:T(8,128)} %copy-done) | copy-start | bytes 25165828
  33.0 12.3 %copy-start.11 = (f32[2,16,2048]{2,1,0:T(8,128)S(1)}, f32[2,16,2048]{2,1,0:T(8,128)}, u32[]{:S(2)}) copy-start(f32[2,16,2048]{2,1,0:T(8,128)} %copy-done.10) | copy-start | bytes 786436
  33.0 12.3 %copy-start.13 = (f32[32,2048]{1,0:T(8,128)S(1)}, f32[32,2048]{1,0:T(8,128)}, u32[]{:S(2)}) copy-start(f32[32,2048]{1,0:T(8,128)} %copy-done.12) | copy-start | bytes 786436
  33.0 12.3 %copy-start.15 = (f32[32,2048]{1,0:T(8,128)S(1)}, f32[32,2048]{1,0:T(8,128)}, u32[]{:S(2)}) copy-start(f32[32,2048]{1,0:T(8,128)} %copy-done.14) | copy-start | bytes 786436
  40.2 3.3 %copy-start.2 = (f32[2,512,2048]{2,1,0:T(8,128)}, f32[2,512,2048]{2,1,0:T(8,128)S(1)}, u32[]{:S(2)}) copy-start(f32[2,512,2048]{2,1,0:T(8,128)S(1)} %branch_own.3.own_ref) | copy-start | bytes 25165828
  45.5 10.4 %collective-permute-start.3 = (f32[2,16,2048]{2,1,0:T(8,128)S(1)}, f32[2,16,2048]{2,1,0:T(8,128)S(1)}, u32[]{:S(2)}, u32[]{:S(2)}) collective-permute-start(f32[2,16,2048]{2,1,0:T(8,128)S(1)} %get-tuple-element.69), channel_id=1, source_target_pairs={{0,2},{4,6},{9,11},{13,15},{18,16},{22,20},{27,25},{31,29}} | collective-permute-start | bytes 786440 | tf_op jit(solution)/shard_map/ppermute | solution.py:531
  50.0 5.9 %collective-permute-start.4 = (f32[2,16,2048]{2,1,0:T(8,128)S(1)}, f32[2,16,2048]{2,1,0:T(8,128)S(1)}, u32[]{:S(2)}, u32[]{:S(2)}) collective-permute-start(f32[2,16,2048]{2,1,0:T(8,128)S(1)} %get-tuple-element.86), channel_id=1, source_target_pairs={{0,4},{4,0},{8,12},{12,8},{16,20},{20,16},{24,28},{28,24},{1,5},{5... | collective-permute-start | bytes 786440 | tf_op jit(solution)/shard_map/ppermute | solution.py:500
  56.0 8.2 %collective-permute-start.5 = (f32[2,16,2048]{2,1,0:T(8,128)S(1)}, f32[2,16,2048]{2,1,0:T(8,128)S(1)}, u32[]{:S(2)}, u32[]{:S(2)}) collective-permute-start(f32[2,16,2048]{2,1,0:T(8,128)S(1)} %broadcast_select_fusion.1), channel_id=1, source_target_pairs={{0,1},{2,3},{4,5},{6,7},{9,8},{11,10},{13,12},{15,14},{18,19},{16,... | collective-permute-start | bytes 786440 | tf_op jit(solution)/shard_map/ppermute | solution.py:531
  58.2 6.1 %slice-start = ((s8[8388608]{0:T(1024)(128)(4,1)}), s8[4194304]{0:T(1024)(128)(4,1)S(1)}, s32[]{:S(2)}) async-start(s8[8388608]{0:T(1024)(128)(4,1)} %bitcast.29), calls=%async_computation | async-start | bytes 8388608
  58.2 6.1 %slice-start.1 = ((s8[8388608]{0:T(1024)(128)(4,1)}), s8[4194304]{0:T(1024)(128)(4,1)S(1)}, s32[]{:S(2)}) async-start(s8[8388608]{0:T(1024)(128)(4,1)} %bitcast.29), calls=%async_computation.1 | async-start | bytes 8388608
  58.2 6.1 %copy-start.4 = (bf16[2,512,512]{2,1,0:T(8,128)(2,1)S(1)}, bf16[2,512,512]{2,1,0:T(8,128)(2,1)}, u32[]{:S(2)}) copy-start(bf16[2,512,512]{2,1,0:T(8,128)(2,1)} %copy-done.3) | copy-start | bytes 3145732
  58.2 6.1 %copy-start.7 = (s32[2]{0:T(128)S(1)}, s32[2]{0:T(128)}, u32[]{:S(2)}) copy-start(s32[2]{0:T(128)} %len_ref.1) | copy-start | bytes 28

commit v6 on v5

--- a/solution.py
+++ b/solution.py
@@ -304,21 +304,18 @@
             self.wait(key)
 
 
-def branch_kernel(*refs, which, skip):
-    x_in, ready = refs[0], refs[1:5]
-    own_out, x_ref, own_ref, s_ref, in_sems, out_sems = refs[5 + skip:]
+def branch_kernel(x_in, *refs, which):
+    ready = refs[:4]
+    own_ref, x_ref, s_ref, in_sems = refs[4:]
     positions, channels = x_ref.shape
     state = s_ref.shape[0]
     blocks = positions // BLOCK
     lanes = channels // in_sems.shape[1]
-    came, left = Copies(in_sems), Copies(out_sems)
-
-    def spot(b, j):
-        return pl.ds(b * BLOCK, BLOCK), pl.ds(j * lanes, lanes)
-
+    came = Copies(in_sems)
     for b in range(blocks):
         for j in range(channels // lanes):
-            came.start((b, j), x_in.at[(which, *spot(b, j))], x_ref.at[spot(b, j)])
+            spot = (pl.ds(b * BLOCK, BLOCK), pl.ds(j * lanes, lanes))
+            came.start((b, j), x_in.at[(which, *spot)], x_ref.at[spot])
 
     def job(b, g):
         cols = pl.ds(g * 256, 256)
@@ -335,9 +332,6 @@
 
         def write(out):
             own_ref[here] = out
-            if (g + 1) * 256 % lanes == 0:
-                j = g * 256 // lanes
-                left.start((b, j), own_ref.at[spot(b, j)], own_out.at[(which, *spot(b, j))])
 
         def entering_of():
             return s_ref[:, cols] if b else jnp.zeros((state, 256), F32)
@@ -346,41 +340,34 @@
         return tile_job(ready, (at, at), g, x_of, entering_of, leave, write)
 
     run_tiles([job(b, g) for b in range(blocks) for g in range(channels // 256)])
-    left.wait_all()
-
-
-def branch_own(x, ready, which, into):
+
+
+def branch_own(x, ready, which):
     _, positions, channels = x.shape
     state = ready[3].shape[2] * CHUNK // BLOCK
     whole = pl.BlockSpec(memory_space=pltpu.VMEM)
-    hbm = pl.BlockSpec(memory_space=pltpu.HBM)
-    anywhere = pl.BlockSpec(memory_space=pl.ANY)
-    parts = (positions // BLOCK, channels // min(512, channels))
     work = positions * channels
     return pl.pallas_call(
-        functools.partial(branch_kernel, which=which, skip=len(into)),
-        in_specs=[hbm] + [whole] * 4 + [anywhere] * len(into),
-        out_specs=anywhere,
-        out_shape=jax.ShapeDtypeStruct(x.shape, F32),
+        functools.partial(branch_kernel, which=which),
+        in_specs=[pl.BlockSpec(memory_space=pltpu.HBM)] + [whole] * 4,
+        out_specs=whole,
+        out_shape=jax.ShapeDtypeStruct(x.shape[1:], F32),
         scratch_shapes=[
             pltpu.VMEM((positions, channels), BF16),
-            pltpu.VMEM((positions, channels), F32),
             pltpu.VMEM((state, channels), F32),
-            pltpu.SemaphoreType.DMA(parts),
-            pltpu.SemaphoreType.DMA(parts),
+            pltpu.SemaphoreType.DMA((positions // BLOCK, channels // min(512, channels))),
         ],
-        input_output_aliases={5 + i: i for i in range(len(into))},
         compiler_params=pltpu.CompilerParams(vmem_limit_bytes=VMEM_LIMIT),
         cost_estimate=pl.CostEstimate(
             flops=2 * 1152 * work, bytes_accessed=4 * work, transcendentals=0),
         name="branch_own",
-    )(in_hbm(x), *ready, *into)
+    )(in_hbm(x), *ready)
 
 
 def prompt_kernel(*refs, skip):
     half_ref, x_in, *ready, start_ref = refs[:7]
-    y_out, x_ref, y_ref, in_sems, out_sems = refs[7 + skip:]
-    count, positions, channels = y_ref.shape
+    y_out, x_ref, in_sems, out_sems = refs[7 + skip:]
+    count, positions, channels = x_ref.shape
     blocks = positions // BLOCK
     lanes = channels // in_sems.shape[2]
     half = half_ref[0]
@@ -414,10 +401,10 @@
             return entered[i, g] if b else start_ref[i, :, pl.ds(g * 256, 256)]
 
         def write(out):
-            y_ref[here] = out.astype(BF16)
+            x_ref[here] = out.astype(BF16)
             if (g + 1) * 256 % lanes == 0:
                 there, staged = spots(i, b, j)
-                left.start((i, b, j), y_ref.at[staged], y_out.at[there])
+                left.start((i, b, j), x_ref.at[staged], y_out.at[there])
 
         at = i * blocks + b
         return tile_job(ready, ((at, half), at), g, x_of, entering_of, leave, write)
@@ -440,7 +427,6 @@
         out_shape=jax.ShapeDtypeStruct(x.shape, BF16),
         scratch_shapes=[
             pltpu.VMEM((count, positions, part), BF16),
-            pltpu.VMEM((count, positions, part), BF16),
             pltpu.SemaphoreType.DMA(parts),
             pltpu.SemaphoreType.DMA(parts),
         ],
@@ -452,7 +438,8 @@
     )(half, in_hbm(x), *ready, start, *into)
 
 
-def finish_kernel(len_ref, own_ref, reach_ref, start_ref, y_out, y_ref, sems, *, width):
+def finish_kernel(len_ref, reach_ref, start_ref, *refs, width):
+    own_refs, (y_out, y_ref, sems) = refs[:-3], refs[-3:]
     count, positions, channels = y_ref.shape
     state = start_ref.shape[0]
     group = 128 // state
@@ -470,30 +457,30 @@
                 term = jnp.dot(
                     reach_ref[i, rows, pl.ds(g * 128, 128)], starts[g], preferred_element_type=F32)
                 live = iota((BLOCK, span), 0) < len_ref[i] - b * BLOCK
-                y_ref[i, rows, cols] = jnp.where(live, own_ref[i, rows, cols] + term, 0.0).astype(BF16)
+                y_ref[i, rows, cols] = jnp.where(live, own_refs[i][rows, cols] + term, 0.0).astype(BF16)
                 left.start((i, b, g), y_ref.at[i, rows, cols], y_out.at[i, rows, cols])
     left.wait_all()
 
 
-def finish(lengths, own, reach, start):
-    count, positions, channels = own.shape
+def finish(lengths, reach, start, own):
+    count, (positions, channels) = len(own), own[0].shape
     state = start.shape[0]
     width = channels * state // reach.shape[2]
     whole = pl.BlockSpec(memory_space=pltpu.VMEM)
     return pl.pallas_call(
         functools.partial(finish_kernel, width=width),
-        in_specs=[pl.BlockSpec(memory_space=pltpu.SMEM), whole, whole, whole],
+        in_specs=[pl.BlockSpec(memory_space=pltpu.SMEM)] + [whole] * (2 + count),
         out_specs=pl.BlockSpec(memory_space=pltpu.HBM),
-        out_shape=jax.ShapeDtypeStruct(own.shape, BF16),
+        out_shape=jax.ShapeDtypeStruct((count, positions, channels), BF16),
         scratch_shapes=[
-            pltpu.VMEM(own.shape, BF16),
+            pltpu.VMEM((count, positions, channels), BF16),
             pltpu.SemaphoreType.DMA((count, positions // BLOCK, reach.shape[2] // 128)),
         ],
         compiler_params=pltpu.CompilerParams(vmem_limit_bytes=VMEM_LIMIT),
         cost_estimate=pl.CostEstimate(
-            flops=2 * 128 * own.size, bytes_accessed=6 * own.size, transcendentals=0),
+            flops=2**28, bytes_accessed=2**23, transcendentals=0),
         name="branch_finish",
-    )(lengths, own, reach, start)
+    )(lengths, reach, start, *own)
 
 
 def swap_bit(value, bit, size):
@@ -581,7 +568,7 @@
         else:
             got, own = beside(
                 swap, pack(total, total_log),
-                lambda x, own: (branch_own(x, branch_ready, which, own),), branch_x, own)
+                lambda x, own: (*own, branch_own(x, branch_ready, which)), branch_x, own)
         other = unpack(got, prompts)
         upper = (mine & bit) != 0
         before = jnp.where(upper, jnp.exp(before_log) * other[0] + before, before)
@@ -589,7 +576,7 @@
         total, total_log = join(*in_order(upper, (total, total_log), other))
         bit *= 2
     for which in works:
-        own = (branch_own(branch_x, branch_ready, which, own),)
+        own = (*own, branch_own(branch_x, branch_ready, which))
 
     next_before = jnp.exp(first[1]) * before + first[0]
     keep = jnp.where(odd, next_before, before)
@@ -614,7 +601,7 @@
     start = total[0]
     for which in range(1, prompts):
         start = jnp.where(branch_prompt[0] == which, total[which], start)
-    branch_y = finish(branch_len, *own, reach, start)
+    branch_y = finish(branch_len, reach, start, own)
     return prompt_y[0], branch_y
 
 

time: 67.9 us -> 60.9 us (0.90)
  local copies, waits for them, and re-layouts: 15.8 us -> 9.89 us
  Pallas kernels: 36 us -> 31.7 us
  waiting for transfers between devices: 0.02 us -> 2.61 us
    unnamed x46 -> x44, local copies, waits for them, and re-layouts: 13 us -> 7.08 us
    pallas_call x2, Pallas kernels: 14.4 us -> 10.1 us  [branch_own(): pl.pallas_call(functools.partial(branch_kernel, which=which), in_specs=[p...]
    ppermute x4, waiting for transfers between devices: 0.01 us -> 2.6 us  [swap_bit(): return lax.ppermute(value, 'ctx', [(k, k ^ bit) for k in range(size)])]
  transfers between devices with their start and end apart: 6 -> 6, of which waited for: 0 -> 2; matrix products, arithmetic and copies ran while one was open for 0% -> 0% of each run, Pallas kernels for 42% -> 40%
where the time goes in v6:
time: 60.9 us; the launch traced here: 60 us
  Pallas kernels  31.7 us (52%)
  starting transfers between devices  10.9 us (18%)
  local copies, waits for them, and re-layouts  9.89 us (16%)
  other arithmetic  2.96 us (5%)
  waiting for transfers between devices  2.61 us (4%)
  between operations  1.92 us (3%)
    pallas_call x2, Pallas kernels, prompt_half(): pl.pallas_call(functools.partial(prompt_kernel, skip=len(into)), in_specs...  11.8 us
    pallas_call x2, Pallas kernels, branch_own(): pl.pallas_call(functools.partial(branch_kernel, which=which), in_specs=[p...  10.1 us
    unnamed x44, local copies, waits for them, and re-layouts  7.08 us
    ppermute x2, starting transfers between devices, spread_step(): got = lax.ppermute(value, ('ctx', 'pair'), links)  6.03 us
    pallas_call x1, Pallas kernels, local_ends(): pl.pallas_call(functools.partial(ends_kernel, width=width, lanes=lanes),...  5.05 us
    ppermute x4, starting transfers between devices, swap_bit(): return lax.ppermute(value, 'ctx', [(k, k ^ bit) for k in range(size)])  4.88 us
    pallas_call x1, Pallas kernels, finish(): pl.pallas_call(functools.partial(finish_kernel, width=width), in_specs=[p...  2.9 us
    ppermute x4, waiting for transfers between devices, swap_bit(): return lax.ppermute(value, 'ctx', [(k, k ^ bit) for k in range(size)])  2.6 us
  transfers between devices with their start and end apart: 6, of which 2 were waited for; matrix products, arithmetic and copies ran while one was open for 0% of the time, Pallas kernels for 40%

profile of v6, /device:TPU:0, one launch (start us, length us, event | category | flops | bytes accessed | tf_op | source)
XLA Modules:
  0.0 60.0 jit_solution(3149397256275251648)
XLA Ops:
  0.6 0.0 copy-start.7
  0.6 0.0 copy-start.10
  0.7 0.0 copy-start.6
  0.7 0.0 copy-start.9
  0.7 5.1 %local_ends.1 = (f32[2,16,4096]{2,1,0:T(8,128)S(1)}, f32[2,8,4096]{2,1,0:T(8,128)S(1)}) custom-call(bf16[2,256,4096]{2,1,0:T(8,128)(2,1)} %refs_1_.3, f32[2,64,256]{2,1,0:T(8,128)} %pld_ref.1, bf16[2,2,16,256]{3,2,1,0:T(8,128)(2,1)} %pbc_ref.1), custom_call_target="tpu_custom_call" | custom-call | flops 268435456 | bytes 4194304 | tf_op jit(solution)/shard_map/local_ends/pallas_call | solution.py:124
  5.9 0.5 collective-permute-start
  6.4 0.0 copy-done.7
  6.4 0.0 copy-done.10
  6.4 0.0 copy-done.6
  6.4 0.0 copy-done.9
  6.4 1.9 %prepare.1 = (bf16[64,2048]{1,0:T(8,128)(2,1)S(1)}, bf16[2,2,528,64]{3,2,1,0:T(8,128)(2,1)S(1)}, bf16[2,384,256]{2,1,0:T(8,128)(2,1)S(1)}, bf16[2,256,128]{2,1,0...) custom-call(f32[2,64,256]{2,1,0:T(8,128)S(1)} %copy-done.6, ...), custom_call_target="tpu_custom_call" | custom-call | flops 100000000 | bytes 1000000 | tf_op jit(solution)/shard_map/prepare/pallas_call | solution.py:237
  8.3 0.0 copy-start.4
  8.3 1.0 %copy-done.4 = bf16[2,512,512]{2,1,0:T(8,128)(2,1)} copy-done((bf16[2,512,512]{2,1,0:T(8,128)(2,1)}, bf16[2,512,512]{2,1,0:T(8,128)(2,1)S(1)}, u32[]{:S(2)}) %copy-start.4) | copy-done | bytes 1048600
  9.3 0.0 collective-permute-done
  9.3 0.0 copy-start.13
  9.4 0.6 %copy-done.13 = f32[32,2048]{1,0:T(8,128)} copy-done((f32[32,2048]{1,0:T(8,128)}, f32[32,2048]{1,0:T(8,128)S(1)}, u32[]{:S(2)}) %copy-start.13) | copy-done | bytes 262168
  10.0 0.1 select_add_fusion.2
  10.1 0.0 copy-start.17
  10.1 0.7 %copy-done.17 = f32[2,16,2048]{2,1,0:T(8,128)} copy-done((f32[2,16,2048]{2,1,0:T(8,128)}, f32[2,16,2048]{2,1,0:T(8,128)S(1)}, u32[]{:S(2)}) %copy-start.17) | copy-done | bytes 262168
  10.8 0.7 %pad_maximum_fusion.1 = f32[34,2048]{1,0:T(8,128)} fusion(f32[2,2048]{1,0:T(2,128)S(1)} %get-tuple-element.99, f32[32,2048]{1,0:T(8,128)S(1)} %bitcast.34), kind=kLoop, calls=%fused_computation.2 | loop fusion | flops 69632 | bytes 557056 | tf_op jit(solution)/shard_map/concatenate | solution.py:492
  11.6 2.5 %collective-permute-start.1 = (f32[34,2048]{1,0:T(8,128)}, f32[34,2048]{1,0:T(8,128)}, u32[]{:S(2)}, u32[]{:S(2)}) collective-permute-start(f32[34,2048]{1,0:T(8,128)} %pad_maximum_fusion.1), channel_id=1, source_target_pairs={{0,8},{4,12},{8,0},{12,4},{16,24},{20,28},{24,16},{28,20},{1,9},{5... | collective-permute-start | bytes 835592 | tf_op jit(solution)/shard_map/ppermute | solution.py:487
  14.1 0.0 copy-start.18
  14.1 5.0 %branch_own.2.refs_0_ = f32[512,2048]{1,0:T(8,128)S(1)} custom-call(bf16[2,512,2048]{2,1,0:T(8,128)(2,1)} %x_in.1, bf16[64,2048]{1,0:T(8,128)(2,1)S(1)} %get-tuple-element.71.refs_0_.refs_2_, bf16[4,528,64]{2,1,0:T(8,128)(2,1)S(1)} %get-tuple-element.61.refs_1_, bf16[4,384,256]{2,1,0:T(8,128)(2,1)S(1)} %get-tuple-element.62.refs_2_, ...), custom_call_target="tpu_custom_call" | custom-call | flops 2415919104 | bytes 4194304 | tf_op jit(solution)/shard_map/branch_own/pallas_call | solution.py:350
  19.1 0.0 copy-start
  19.1 2.0 %copy-done = f32[512,2048]{1,0:T(8,128)} copy-done((f32[512,2048]{1,0:T(8,128)}, f32[512,2048]{1,0:T(8,128)S(1)}, u32[]{:S(2)}) %copy-start) | copy-done | bytes 4194328
  21.1 1.6 %collective-permute-done.1 = f32[34,2048]{1,0:T(8,128)} collective-permute-done((f32[34,2048]{1,0:T(8,128)}, f32[34,2048]{1,0:T(8,128)}, u32[]{:S(2)}, u32[]{:S(2)}) %collective-permute-start.1) | collective-permute-done | bytes 278560 | tf_op jit(solution)/shard_map/ppermute | solution.py:487
  22.7 1.0 %slice.43 = f32[32,2048]{1,0:T(8,128)S(1)} slice(f32[34,2048]{1,0:T(8,128)} %collective-permute-done.1), slice={[0:32], [0:2048]} | slice | bytes 524288 | tf_op jit(solution)/shard_map/slice | solution.py:498
  23.7 0.0 copy-start.15
  23.7 0.9 %select_exponential_fusion = (f32[2,2048]{1,0:T(2,128)S(1)}, f32[2,2048]{1,0:T(2,128)S(1)}) fusion(pred[]{:T(512)S(6)} %ne.17, f32[34,2048]{1,0:T(8,128)} %collective-permute-done.1), kind=kLoop, calls=%fused_computation.33 | loop fusion | flops 4096 | bytes 49153 | tf_op jit(solution)/shard_map/exp | solution.py:574
  24.7 0.0 copy-done.18
  24.7 0.1 select_add_fusion.1
  24.8 0.0 copy-start.11
  24.8 0.7 %copy-done.11 = f32[2,16,2048]{2,1,0:T(8,128)} copy-done((f32[2,16,2048]{2,1,0:T(8,128)}, f32[2,16,2048]{2,1,0:T(8,128)S(1)}, u32[]{:S(2)}) %copy-start.11) | copy-done | bytes 262168
  25.5 0.7 %pad_maximum_fusion.2 = f32[34,2048]{1,0:T(8,128)} fusion(f32[2,2048]{1,0:T(2,128)S(1)} %bitcast.40, f32[32,2048]{1,0:T(8,128)S(1)} %bitcast.29), kind=kLoop, calls=%fused_computation.3 | loop fusion | flops 69632 | bytes 557056 | tf_op jit(solution)/shard_map/concatenate | solution.py:492
  26.3 0.0 copy-done.15
  26.3 1.8 %collective-permute-start.2 = (f32[34,2048]{1,0:T(8,128)}, f32[34,2048]{1,0:T(8,128)}, u32[]{:S(2)}, u32[]{:S(2)}) collective-permute-start(f32[34,2048]{1,0:T(8,128)} %pad_maximum_fusion.2), channel_id=1, source_target_pairs={{0,16},{4,20},{8,24},{12,28},{16,0},{20,4},{24,8},{28,12},{1,17},{... | collective-permute-start | bytes 835592 | tf_op jit(solution)/shard_map/ppermute | solution.py:487
  28.0 0.0 copy-start.12
  28.0 5.1 %branch_own.3.refs_1_ = f32[512,2048]{1,0:T(8,128)S(1)} custom-call(bf16[2,512,2048]{2,1,0:T(8,128)(2,1)} %x_in.1, bf16[64,2048]{1,0:T(8,128)(2,1)S(1)} %get-tuple-element.71.refs_0_.refs_2_, bf16[4,528,64]{2,1,0:T(8,128)(2,1)S(1)} %get-tuple-element.61.refs_1_, bf16[4,384,256]{2,1,0:T(8,128)(2,1)S(1)} %get-tuple-element.62.refs_2_, ...), custom_call_target="tpu_custom_call" | custom-call | flops 2415919104 | bytes 4194304 | tf_op jit(solution)/shard_map/branch_own/pallas_call | solution.py:350
  33.1 0.0 copy-start.2
  33.1 2.0 %copy-done.2 = f32[512,2048]{1,0:T(8,128)} copy-done((f32[512,2048]{1,0:T(8,128)}, f32[512,2048]{1,0:T(8,128)S(1)}, u32[]{:S(2)}) %copy-start.2) | copy-done | bytes 4194328
  35.1 1.0 %collective-permute-done.2 = f32[34,2048]{1,0:T(8,128)} collective-permute-done((f32[34,2048]{1,0:T(8,128)}, f32[34,2048]{1,0:T(8,128)}, u32[]{:S(2)}, u32[]{:S(2)}) %collective-permute-start.2) | collective-permute-done | bytes 278560 | tf_op jit(solution)/shard_map/ppermute | solution.py:487
  36.1 0.8 %slice.44 = f32[2,2048]{1,0:T(2,128)S(1)} slice(f32[34,2048]{1,0:T(8,128)} %collective-permute-done.2), slice={[32:34], [0:2048]} | slice | bytes 32768 | tf_op jit(solution)/shard_map/slice | solution.py:498
  36.9 1.0 %slice.45 = f32[32,2048]{1,0:T(8,128)S(1)} slice(f32[34,2048]{1,0:T(8,128)} %collective-permute-done.2), slice={[0:32], [0:2048]} | slice | bytes 524288 | tf_op jit(solution)/shard_map/slice | solution.py:498
  38.0 0.0 copy-done.12
  38.0 0.0 copy-done.14
  38.0 0.0 copy-done.16
  38.0 0.1 fusion
  38.1 4.7 %collective-permute-start.3 = (f32[2,16,2048]{2,1,0:T(8,128)S(1)}, f32[2,16,2048]{2,1,0:T(8,128)S(1)}, u32[]{:S(2)}, u32[]{:S(2)}) collective-permute-start(f32[2,16,2048]{2,1,0:T(8,128)S(1)} %get-tuple-element.70), channel_id=1, source_target_pairs={{0,2},{4,6},{9,11},{13,15},{18,16},{22,20},{27,25},{31,29}} | collective-permute-start | bytes 786440 | tf_op jit(solution)/shard_map/ppermute | solution.py:518
  42.9 0.1 collective-permute-start.4
  43.0 5.8 %prompt_half.2.refs_7_ = bf16[2,256,4096]{2,1,0:T(8,128)(2,1)} custom-call(s32[1]{0:T(128)} %bitcast.6.refs_0_, bf16[2,256,4096]{2,1,0:T(8,128)(2,1)} %refs_1_.3, bf16[64,2048]{1,0:T(8,128)(2,1)S(1)} %get-tuple-element.71.refs_0_.refs_2_, bf16[2,2,528,64]{3,2,1,0:T(8,128)(2,1)S(1)} %get-tuple-element.72.refs_3_, ...), custom_call_target="tpu_custom_call" | custom-call | flops 2415919104 | bytes 4194304 | tf_op jit(solution)/shard_map/prompt_half/pallas_call | solution.py:423
  48.8 0.0 collective-permute-done.3
  48.8 0.0 collective-permute-done.4.refs_6_
  48.8 1.3 %collective-permute-start.5 = (f32[2,16,2048]{2,1,0:T(8,128)S(1)}, f32[2,16,2048]{2,1,0:T(8,128)S(1)}, u32[]{:S(2)}, u32[]{:S(2)}) collective-permute-start(f32[2,16,2048]{2,1,0:T(8,128)S(1)} %broadcast_select_fusion.1), channel_id=1, source_target_pairs={{0,1},{2,3},{4,5},{6,7},{9,8},{11,10},{13,12},{15,14},{18,19},{16,... | collective-permute-start | bytes 786440 | tf_op jit(solution)/shard_map/ppermute | solution.py:518
  50.8 0.0 copy-start.1
  50.8 0.0 copy-start.3
  50.8 0.0 copy-start.5
  50.8 0.0 copy-start.8
  50.9 6.0 %prompt_half.3 = bf16[2,256,4096]{2,1,0:T(8,128)(2,1)} custom-call(s32[1]{0:T(128)S(6)} %sub.9.refs_0_, bf16[2,256,4096]{2,1,0:T(8,128)(2,1)} %refs_1_.3, bf16[64,2048]{1,0:T(8,128)(2,1)S(1)} %get-tuple-element.71.refs_0_.refs_2_, bf16[2,2,528,64]{3,2,1,0:T(8,128)(2,1)S(1)} %get-tuple-element.72.refs_3_, ...), custom_call_target="tpu_custom_call", output_to_operand_aliasing={{}: (7, {})} | custom-call | flops 2415919104 | bytes 4194304 | tf_op jit(solution)/shard_map/prompt_half/pallas_call | solution.py:423
  56.8 0.0 collective-permute-done.5
  56.9 0.0 copy-done.1
  56.9 0.0 copy-done.3
  56.9 0.0 copy-done.5
  56.9 0.0 copy-done.8
  57.0 2.9 %branch_finish.1 = bf16[2,512,2048]{2,1,0:T(8,128)(2,1)} custom-call(s32[2]{0:T(128)S(1)} %copy-done.8, bf16[2,512,512]{2,1,0:T(8,128)(2,1)S(1)} %copy-done.5, f32[16,2048]{1,0:T(8,128)S(1)} %fusion.2.start_ref, f32[512,2048]{1,0:T(8,128)S(1)} %copy-done.1, f32[512,2048]{1,0:T(8,128)S(1)} %copy-done.3), custom_call_target="tpu_custom_call" | custom-call | flops 268435456 | bytes 8388608 | tf_op jit(solution)/shard_map/branch_finish/pallas_call | solution.py:470
  (19 shorter events, 0.4 us)
Async XLA Ops:
  0.6 5.7 %copy-start.7 = (bf16[2,2,16,256]{3,2,1,0:T(8,128)(2,1)S(1)}, bf16[2,2,16,256]{3,2,1,0:T(8,128)(2,1)}, u32[]{:S(2)}) copy-start(bf16[2,2,16,256]{3,2,1,0:T(8,128)(2,1)} %pbc_ref.1) | copy-start | bytes 98308
  0.6 5.7 %copy-start.10 = (bf16[2,2,16,512]{3,2,1,0:T(8,128)(2,1)S(1)}, bf16[2,2,16,512]{3,2,1,0:T(8,128)(2,1)}, u32[]{:S(2)}) copy-start(bf16[2,2,16,512]{3,2,1,0:T(8,128)(2,1)} %bbc_ref.1) | copy-start | bytes 196612
  0.7 5.7 %copy-start.6 = (f32[2,64,256]{2,1,0:T(8,128)S(1)}, f32[2,64,256]{2,1,0:T(8,128)}, u32[]{:S(2)}) copy-start(f32[2,64,256]{2,1,0:T(8,128)} %pld_ref.1) | copy-start | bytes 393220
  0.7 5.7 %copy-start.9 = (f32[2,32,512]{2,1,0:T(8,128)S(1)}, f32[2,32,512]{2,1,0:T(8,128)}, u32[]{:S(2)}) copy-start(f32[2,32,512]{2,1,0:T(8,128)} %bld_ref) | copy-start | bytes 393220
  5.9 3.5 %collective-permute-start = (f32[34,2048]{1,0:T(8,128)S(1)}, f32[34,2048]{1,0:T(8,128)S(1)}, u32[]{:S(2)}, u32[]{:S(2)}) collective-permute-start(f32[34,2048]{1,0:T(8,128)S(1)} %pad_maximum_fusion), channel_id=1, source_target_pairs={{0,4},{4,0},{8,12},{12,8},{16,20},{20,16},{24,28},{28,24},{1,5},{5... | collective-permute-start | bytes 835592 | tf_op jit(solution)/shard_map/ppermute | solution.py:487
  8.3 1.0 %copy-start.4 = (bf16[2,512,512]{2,1,0:T(8,128)(2,1)}, bf16[2,512,512]{2,1,0:T(8,128)(2,1)S(1)}, u32[]{:S(2)}) copy-start(bf16[2,512,512]{2,1,0:T(8,128)(2,1)S(1)} %get-tuple-element.83.reach_ref) | copy-start | bytes 3145732
  9.3 0.7 %copy-start.13 = (f32[32,2048]{1,0:T(8,128)}, f32[32,2048]{1,0:T(8,128)S(1)}, u32[]{:S(2)}) copy-start(f32[32,2048]{1,0:T(8,128)S(1)} %slice.41) | copy-start | bytes 786436
  10.1 0.7 %copy-start.17 = (f32[2,16,2048]{2,1,0:T(8,128)}, f32[2,16,2048]{2,1,0:T(8,128)S(1)}, u32[]{:S(2)}) copy-start(f32[2,16,2048]{2,1,0:T(8,128)S(1)} %select_add_fusion.2) | copy-start | bytes 786436
  11.6 11.2 %collective-permute-start.1 = (f32[34,2048]{1,0:T(8,128)}, f32[34,2048]{1,0:T(8,128)}, u32[]{:S(2)}, u32[]{:S(2)}) collective-permute-start(f32[34,2048]{1,0:T(8,128)} %pad_maximum_fusion.1), channel_id=1, source_target_pairs={{0,8},{4,12},{8,0},{12,4},{16,24},{20,28},{24,16},{28,20},{1,9},{5... | collective-permute-start | bytes 835592 | tf_op jit(solution)/shard_map/ppermute | solution.py:487
  14.1 10.7 %copy-start.18 = (f32[2,16,2048]{2,1,0:T(8,128)S(1)}, f32[2,16,2048]{2,1,0:T(8,128)}, u32[]{:S(2)}) copy-start(f32[2,16,2048]{2,1,0:T(8,128)} %copy-done.17) | copy-start | bytes 786436
  19.1 2.0 %copy-start = (f32[512,2048]{1,0:T(8,128)}, f32[512,2048]{1,0:T(8,128)S(1)}, u32[]{:S(2)}) copy-start(f32[512,2048]{1,0:T(8,128)S(1)} %branch_own.2.refs_0_) | copy-start | bytes 12582916
  23.7 2.5 %copy-start.15 = (f32[32,2048]{1,0:T(8,128)}, f32[32,2048]{1,0:T(8,128)S(1)}, u32[]{:S(2)}) copy-start(f32[32,2048]{1,0:T(8,128)S(1)} %slice.43) | copy-start | bytes 786436
  24.8 0.7 %copy-start.11 = (f32[2,16,2048]{2,1,0:T(8,128)}, f32[2,16,2048]{2,1,0:T(8,128)S(1)}, u32[]{:S(2)}) copy-start(f32[2,16,2048]{2,1,0:T(8,128)S(1)} %select_add_fusion.1) | copy-start | bytes 786436
  26.3 9.8 %collective-permute-start.2 = (f32[34,2048]{1,0:T(8,128)}, f32[34,2048]{1,0:T(8,128)}, u32[]{:S(2)}, u32[]{:S(2)}) collective-permute-start(f32[34,2048]{1,0:T(8,128)} %pad_maximum_fusion.2), channel_id=1, source_target_pairs={{0,16},{4,20},{8,24},{12,28},{16,0},{20,4},{24,8},{28,12},{1,17},{... | collective-permute-start | bytes 835592 | tf_op jit(solution)/shard_map/ppermute | solution.py:487
  28.0 9.9 %copy-start.12 = (f32[2,16,2048]{2,1,0:T(8,128)S(1)}, f32[2,16,2048]{2,1,0:T(8,128)}, u32[]{:S(2)}) copy-start(f32[2,16,2048]{2,1,0:T(8,128)} %copy-done.11) | copy-start | bytes 786436
  28.0 9.9 %copy-start.14 = (f32[32,2048]{1,0:T(8,128)S(1)}, f32[32,2048]{1,0:T(8,128)}, u32[]{:S(2)}) copy-start(f32[32,2048]{1,0:T(8,128)} %copy-done.13) | copy-start | bytes 786436
  28.0 9.9 %copy-start.16 = (f32[32,2048]{1,0:T(8,128)S(1)}, f32[32,2048]{1,0:T(8,128)}, u32[]{:S(2)}) copy-start(f32[32,2048]{1,0:T(8,128)} %copy-done.15) | copy-start | bytes 786436
  33.1 2.0 %copy-start.2 = (f32[512,2048]{1,0:T(8,128)}, f32[512,2048]{1,0:T(8,128)S(1)}, u32[]{:S(2)}) copy-start(f32[512,2048]{1,0:T(8,128)S(1)} %branch_own.3.refs_1_) | copy-start | bytes 12582916
  38.1 10.6 %collective-permute-start.3 = (f32[2,16,2048]{2,1,0:T(8,128)S(1)}, f32[2,16,2048]{2,1,0:T(8,128)S(1)}, u32[]{:S(2)}, u32[]{:S(2)}) collective-permute-start(f32[2,16,2048]{2,1,0:T(8,128)S(1)} %get-tuple-element.70), channel_id=1, source_target_pairs={{0,2},{4,6},{9,11},{13,15},{18,16},{22,20},{27,25},{31,29}} | collective-permute-start | bytes 786440 | tf_op jit(solution)/shard_map/ppermute | solution.py:518
  42.9 5.9 %collective-permute-start.4 = (f32[2,16,2048]{2,1,0:T(8,128)S(1)}, f32[2,16,2048]{2,1,0:T(8,128)S(1)}, u32[]{:S(2)}, u32[]{:S(2)}) collective-permute-start(f32[2,16,2048]{2,1,0:T(8,128)S(1)} %get-tuple-element.88), channel_id=1, source_target_pairs={{0,4},{4,0},{8,12},{12,8},{16,20},{20,16},{24,28},{28,24},{1,5},{5... | collective-permute-start | bytes 786440 | tf_op jit(solution)/shard_map/ppermute | solution.py:487
  48.8 8.0 %collective-permute-start.5 = (f32[2,16,2048]{2,1,0:T(8,128)S(1)}, f32[2,16,2048]{2,1,0:T(8,128)S(1)}, u32[]{:S(2)}, u32[]{:S(2)}) collective-permute-start(f32[2,16,2048]{2,1,0:T(8,128)S(1)} %broadcast_select_fusion.1), channel_id=1, source_target_pairs={{0,1},{2,3},{4,5},{6,7},{9,8},{11,10},{13,12},{15,14},{18,19},{16,... | collective-permute-start | bytes 786440 | tf_op jit(solution)/shard_map/ppermute | solution.py:518
  50.8 6.1 %copy-start.1 = (f32[512,2048]{1,0:T(8,128)S(1)}, f32[512,2048]{1,0:T(8,128)}, u32[]{:S(2)}) copy-start(f32[512,2048]{1,0:T(8,128)} %copy-done) | copy-start | bytes 12582916
  50.8 6.1 %copy-start.3 = (f32[512,2048]{1,0:T(8,128)S(1)}, f32[512,2048]{1,0:T(8,128)}, u32[]{:S(2)}) copy-start(f32[512,2048]{1,0:T(8,128)} %copy-done.2) | copy-start | bytes 12582916
  50.8 6.1 %copy-start.5 = (bf16[2,512,512]{2,1,0:T(8,128)(2,1)S(1)}, bf16[2,512,512]{2,1,0:T(8,128)(2,1)}, u32[]{:S(2)}) copy-start(bf16[2,512,512]{2,1,0:T(8,128)(2,1)} %copy-done.4) | copy-start | bytes 3145732
  50.8 6.1 %copy-start.8 = (s32[2]{0:T(128)S(1)}, s32[2]{0:T(128)}, u32[]{:S(2)}) copy-start(s32[2]{0:T(128)} %len_ref.1) | copy-start | bytes 28

commit v7 on v6

--- a/solution.py
+++ b/solution.py
@@ -182,7 +182,7 @@
 
 def prepare_kernel(
     pld_ref, pbc_ref, bld_ref, bbc_ref,
-    hot_ref, pw_ref, plv_ref, plc_ref, bw_ref, blv_ref, blc_ref, reach_ref, *, width
+    hot_ref, pw_ref, plv_ref, plc_ref, bw_ref, blv_ref, blc_ref, reach_out, reach_ref, sems, *, width
 ):
     state = pbc_ref.shape[2]
 
@@ -200,6 +200,7 @@
     for g in range(hot_ref.shape[1] // 256):
         lane_head = quotient(iota((1, 256), 1), width) + g * (256 // width)
         hot_ref[:, pl.ds(g * 256, 256)] = jnp.where(row_head == lane_head, 1.0, 0.0).astype(BF16)
+    left = Copies(sems)
     upto = jnp.where(iota((BLOCK, 1), 0) <= iota((1, BLOCK), 1), 1.0, 0.0)
     runs = exact_dot(logs, upto)
     for k, (i, cut) in enumerate(cuts):
@@ -209,11 +210,13 @@
         entered = run[:, BLOCK - 1:BLOCK]
         reach = parts[k][1].astype(F32)[None, :, :] * jnp.exp(run)[:, None, :]
         reach_ref[i, cut, :] = reach.reshape(heads * state, BLOCK).T.astype(BF16)
+        left.start((k,), reach_ref.at[i, cut, :], reach_out.at[i, cut, :])
 
     cuts, logs, parts = collect(pld_ref, pbc_ref)
     heads = pld_ref.shape[1] // 2
     for k, w in enumerate(prepare(parts, logs, plv_ref, plc_ref, state, heads)):
         pw_ref[k // 2, k % 2] = w
+    left.wait_all()
 
 
 def prepare_all(prompt_logdec, prompt_bc, branch_logdec, branch_bc, branch_channels):
@@ -237,8 +240,11 @@
     out = pl.pallas_call(
         functools.partial(prepare_kernel, width=branch_channels // heads),
         in_specs=[whole] * 4,
-        out_specs=[pl.BlockSpec(shape, lambda rank=len(shape): (0,) * rank) for shape, _ in shapes],
+        out_specs=[
+            pl.BlockSpec(shape, lambda rank=len(shape): (0,) * rank) for shape, _ in shapes[:-1]
+        ] + [pl.BlockSpec(memory_space=pltpu.HBM)],
         out_shape=[jax.ShapeDtypeStruct(*shape) for shape in shapes],
+        scratch_shapes=[pltpu.VMEM(*shapes[-1]), pltpu.SemaphoreType.DMA((branch_cuts,))],
         compiler_params=pltpu.CompilerParams(vmem_limit_bytes=VMEM_LIMIT),
         cost_estimate=pl.CostEstimate(flops=10**8, bytes_accessed=10**6, transcendentals=0),
         name="prepare",
@@ -306,12 +312,12 @@
 
 def branch_kernel(x_in, *refs, which):
     ready = refs[:4]
-    own_ref, x_ref, s_ref, in_sems = refs[4:]
+    own_out, x_ref, own_ref, s_ref, in_sems, out_sems = refs[4:]
     positions, channels = x_ref.shape
     state = s_ref.shape[0]
     blocks = positions // BLOCK
     lanes = channels // in_sems.shape[1]
-    came = Copies(in_sems)
+    came, left = Copies(in_sems), Copies(out_sems)
     for b in range(blocks):
         for j in range(channels // lanes):
             spot = (pl.ds(b * BLOCK, BLOCK), pl.ds(j * lanes, lanes))
@@ -332,6 +338,7 @@
 
         def write(out):
             own_ref[here] = out
+            left.start((b, g), own_ref.at[here], own_out.at[here])
 
         def entering_of():
             return s_ref[:, cols] if b else jnp.zeros((state, 256), F32)
@@ -340,6 +347,7 @@
         return tile_job(ready, (at, at), g, x_of, entering_of, leave, write)
 
     run_tiles([job(b, g) for b in range(blocks) for g in range(channels // 256)])
+    left.wait_all()
 
 
 def branch_own(x, ready, which):
@@ -350,12 +358,14 @@
     return pl.pallas_call(
         functools.partial(branch_kernel, which=which),
         in_specs=[pl.BlockSpec(memory_space=pltpu.HBM)] + [whole] * 4,
-        out_specs=whole,
+        out_specs=pl.BlockSpec(memory_space=pltpu.HBM),
         out_shape=jax.ShapeDtypeStruct(x.shape[1:], F32),
         scratch_shapes=[
             pltpu.VMEM((positions, channels), BF16),
+            pltpu.VMEM((positions, channels), F32),
             pltpu.VMEM((state, channels), F32),
             pltpu.SemaphoreType.DMA((positions // BLOCK, channels // min(512, channels))),
+            pltpu.SemaphoreType.DMA((positions // BLOCK, channels // 256)),
         ],
         compiler_params=pltpu.CompilerParams(vmem_limit_bytes=VMEM_LIMIT),
         cost_estimate=pl.CostEstimate(

time: 60.9 us -> 65 us (1.067)
  Pallas kernels: 31.7 us -> 39.1 us
  waiting for transfers between devices: 2.61 us -> 0.02 us
    pallas_call x2, Pallas kernels: 10.1 us -> 16.6 us  [branch_own(): pl.pallas_call(functools.partial(branch_kernel, which=which), in_specs=[p...]
    ppermute x4, waiting for transfers between devices: 2.6 us -> 0.01 us  [swap_bit(): return lax.ppermute(value, 'ctx', [(k, k ^ bit) for k in range(size)])]
    pallas_call x1, Pallas kernels: 1.89 us -> 2.8 us  [prepare_all(): pl.pallas_call(functools.partial(prepare_kernel, width=branch_channels //...]
  transfers between devices with their start and end apart: 6 -> 6, of which waited for: 2 -> 0; matrix products, arithmetic and copies ran while one was open for 0% -> 0% of each run, Pallas kernels for 40% -> 48%
where the time goes in v7:
time: 65 us; the launch traced here: 64.6 us
  Pallas kernels  39.1 us (60%)
  starting transfers between devices  10.7 us (16%)
  local copies, waits for them, and re-layouts  9.89 us (15%)
  other arithmetic  2.96 us (5%)
  between operations  1.94 us (3%)
    pallas_call x2, Pallas kernels, branch_own(): pl.pallas_call(functools.partial(branch_kernel, which=which), in_specs=[p...  16.6 us
    pallas_call x2, Pallas kernels, prompt_half(): pl.pallas_call(functools.partial(prompt_kernel, skip=len(into)), in_specs...  11.8 us
    unnamed x44, local copies, waits for them, and re-layouts  7.08 us
    ppermute x2, starting transfers between devices, spread_step(): got = lax.ppermute(value, ('ctx', 'pair'), links)  6.04 us
    pallas_call x1, Pallas kernels, local_ends(): pl.pallas_call(functools.partial(ends_kernel, width=width, lanes=lanes),...  5.05 us
    ppermute x4, starting transfers between devices, swap_bit(): return lax.ppermute(value, 'ctx', [(k, k ^ bit) for k in range(size)])  4.63 us
    pallas_call x1, Pallas kernels, finish(): pl.pallas_call(functools.partial(finish_kernel, width=width), in_specs=[p...  2.9 us
    pallas_call x1, Pallas kernels, prepare_all(): pl.pallas_call(functools.partial(prepare_kernel, width=branch_channels //...  2.8 us
  transfers between devices with their start and end apart: 6, of which 0 were waited for; matrix products, arithmetic and copies ran while one was open for 0% of the time, Pallas kernels for 48%

profile of v7, /device:TPU:0, one launch (start us, length us, event | category | flops | bytes accessed | tf_op | source)
XLA Modules:
  0.0 64.6 jit_solution(9760475059417001118)
XLA Ops:
  0.6 0.0 copy-start.7
  0.6 0.0 copy-start.10
  0.7 0.0 copy-start.6
  0.7 0.0 copy-start.9
  0.7 5.1 %local_ends.1 = (f32[2,16,4096]{2,1,0:T(8,128)S(1)}, f32[2,8,4096]{2,1,0:T(8,128)S(1)}) custom-call(bf16[2,256,4096]{2,1,0:T(8,128)(2,1)} %refs_1_.3, f32[2,64,256]{2,1,0:T(8,128)} %pld_ref.1, bf16[2,2,16,256]{3,2,1,0:T(8,128)(2,1)} %pbc_ref.1), custom_call_target="tpu_custom_call" | custom-call | flops 268435456 | bytes 4194304 | tf_op jit(solution)/shard_map/local_ends/pallas_call | solution.py:124
  5.9 0.5 collective-permute-start
  6.4 0.0 copy-done.7
  6.4 0.0 copy-done.10
  6.4 0.0 copy-done.6
  6.4 0.0 copy-done.9
  6.4 2.8 %prepare.1 = (bf16[64,2048]{1,0:T(8,128)(2,1)S(1)}, bf16[2,2,528,64]{3,2,1,0:T(8,128)(2,1)S(1)}, bf16[2,384,256]{2,1,0:T(8,128)(2,1)S(1)}, bf16[2,256,128]{2,1,0...) custom-call(f32[2,64,256]{2,1,0:T(8,128)S(1)} %copy-done.6, ...), custom_call_target="tpu_custom_call" | custom-call | flops 100000000 | bytes 1000000 | tf_op jit(solution)/shard_map/prepare/pallas_call | solution.py:240
  9.2 0.0 copy-start.4
  9.2 1.0 %copy-done.4 = bf16[2,512,512]{2,1,0:T(8,128)(2,1)} copy-done((bf16[2,512,512]{2,1,0:T(8,128)(2,1)}, bf16[2,512,512]{2,1,0:T(8,128)(2,1)S(1)}, u32[]{:S(2)}) %copy-start.4) | copy-done | bytes 1048600
  10.2 0.0 collective-permute-done
  10.2 0.0 copy-start.13
  10.3 0.6 copy-done.13
  10.9 0.1 select_add_fusion.2
  11.0 0.0 copy-start.17
  11.0 0.7 %copy-done.17 = f32[2,16,2048]{2,1,0:T(8,128)} copy-done((f32[2,16,2048]{2,1,0:T(8,128)}, f32[2,16,2048]{2,1,0:T(8,128)S(1)}, u32[]{:S(2)}) %copy-start.17) | copy-done | bytes 262168
  11.7 0.7 %pad_maximum_fusion.1 = f32[34,2048]{1,0:T(8,128)} fusion(f32[2,2048]{1,0:T(2,128)S(1)} %get-tuple-element.99, f32[32,2048]{1,0:T(8,128)S(1)} %bitcast.34), kind=kLoop, calls=%fused_computation.2 | loop fusion | flops 69632 | bytes 557056 | tf_op jit(solution)/shard_map/concatenate | solution.py:502
  12.5 2.5 %collective-permute-start.1 = (f32[34,2048]{1,0:T(8,128)}, f32[34,2048]{1,0:T(8,128)}, u32[]{:S(2)}, u32[]{:S(2)}) collective-permute-start(f32[34,2048]{1,0:T(8,128)} %pad_maximum_fusion.1), channel_id=1, source_target_pairs={{0,8},{4,12},{8,0},{12,4},{16,24},{20,28},{24,16},{28,20},{1,9},{5... | collective-permute-start | bytes 835592 | tf_op jit(solution)/shard_map/ppermute | solution.py:497
  15.0 0.0 copy-start.18
  15.0 8.3 %branch_own.2.refs_0_ = f32[512,2048]{1,0:T(8,128)S(1)} custom-call(bf16[2,512,2048]{2,1,0:T(8,128)(2,1)} %x_in.1, bf16[64,2048]{1,0:T(8,128)(2,1)S(1)} %get-tuple-element.71.refs_0_.refs_2_, bf16[4,528,64]{2,1,0:T(8,128)(2,1)S(1)} %get-tuple-element.61.refs_1_, bf16[4,384,256]{2,1,0:T(8,128)(2,1)S(1)} %get-tuple-element.62.refs_2_, ...), custom_call_target="tpu_custom_call" | custom-call | flops 2415919104 | bytes 4194304 | tf_op jit(solution)/shard_map/branch_own/pallas_call | solution.py:358
  23.3 0.0 copy-start
  23.3 2.0 %copy-done = f32[512,2048]{1,0:T(8,128)} copy-done((f32[512,2048]{1,0:T(8,128)}, f32[512,2048]{1,0:T(8,128)S(1)}, u32[]{:S(2)}) %copy-start) | copy-done | bytes 4194328
  25.3 0.0 collective-permute-done.1
  25.3 1.0 %slice.43 = f32[32,2048]{1,0:T(8,128)S(1)} slice(f32[34,2048]{1,0:T(8,128)} %collective-permute-done.1), slice={[0:32], [0:2048]} | slice | bytes 524288 | tf_op jit(solution)/shard_map/slice | solution.py:508
  26.3 0.0 copy-start.15
  26.3 0.9 %select_exponential_fusion = (f32[2,2048]{1,0:T(2,128)S(1)}, f32[2,2048]{1,0:T(2,128)S(1)}) fusion(pred[]{:T(512)S(6)} %ne.17, f32[34,2048]{1,0:T(8,128)} %collective-permute-done.1), kind=kLoop, calls=%fused_computation.33 | loop fusion | flops 4096 | bytes 49153 | tf_op jit(solution)/shard_map/exp | solution.py:584
  27.3 0.0 copy-done.18
  27.3 0.1 select_add_fusion.1
  27.4 0.0 copy-start.11
  27.4 0.7 %copy-done.11 = f32[2,16,2048]{2,1,0:T(8,128)} copy-done((f32[2,16,2048]{2,1,0:T(8,128)}, f32[2,16,2048]{2,1,0:T(8,128)S(1)}, u32[]{:S(2)}) %copy-start.11) | copy-done | bytes 262168
  28.1 0.7 %pad_maximum_fusion.2 = f32[34,2048]{1,0:T(8,128)} fusion(f32[2,2048]{1,0:T(2,128)S(1)} %bitcast.40, f32[32,2048]{1,0:T(8,128)S(1)} %bitcast.29), kind=kLoop, calls=%fused_computation.3 | loop fusion | flops 69632 | bytes 557056 | tf_op jit(solution)/shard_map/concatenate | solution.py:502
  28.8 0.0 copy-done.15
  28.8 1.5 %collective-permute-start.2 = (f32[34,2048]{1,0:T(8,128)}, f32[34,2048]{1,0:T(8,128)}, u32[]{:S(2)}, u32[]{:S(2)}) collective-permute-start(f32[34,2048]{1,0:T(8,128)} %pad_maximum_fusion.2), channel_id=1, source_target_pairs={{0,16},{4,20},{8,24},{12,28},{16,0},{20,4},{24,8},{28,12},{1,17},{... | collective-permute-start | bytes 835592 | tf_op jit(solution)/shard_map/ppermute | solution.py:497
  30.3 0.0 copy-start.12
  30.3 8.3 %branch_own.3.refs_1_ = f32[512,2048]{1,0:T(8,128)S(1)} custom-call(bf16[2,512,2048]{2,1,0:T(8,128)(2,1)} %x_in.1, bf16[64,2048]{1,0:T(8,128)(2,1)S(1)} %get-tuple-element.71.refs_0_.refs_2_, bf16[4,528,64]{2,1,0:T(8,128)(2,1)S(1)} %get-tuple-element.61.refs_1_, bf16[4,384,256]{2,1,0:T(8,128)(2,1)S(1)} %get-tuple-element.62.refs_2_, ...), custom_call_target="tpu_custom_call" | custom-call | flops 2415919104 | bytes 4194304 | tf_op jit(solution)/shard_map/branch_own/pallas_call | solution.py:358
  38.7 0.0 copy-start.2
  38.7 2.0 %copy-done.2 = f32[512,2048]{1,0:T(8,128)} copy-done((f32[512,2048]{1,0:T(8,128)}, f32[512,2048]{1,0:T(8,128)S(1)}, u32[]{:S(2)}) %copy-start.2) | copy-done | bytes 4194328
  40.6 0.0 collective-permute-done.2
  40.6 0.8 %slice.44 = f32[2,2048]{1,0:T(2,128)S(1)} slice(f32[34,2048]{1,0:T(8,128)} %collective-permute-done.2), slice={[32:34], [0:2048]} | slice | bytes 32768 | tf_op jit(solution)/shard_map/slice | solution.py:508
  41.5 1.0 %slice.45 = f32[32,2048]{1,0:T(8,128)S(1)} slice(f32[34,2048]{1,0:T(8,128)} %collective-permute-done.2), slice={[0:32], [0:2048]} | slice | bytes 524288 | tf_op jit(solution)/shard_map/slice | solution.py:508
  42.5 0.0 copy-done.12
  42.5 0.0 copy-done.14
  42.5 0.0 copy-done.16
  42.5 0.1 fusion
  42.7 4.7 %collective-permute-start.3 = (f32[2,16,2048]{2,1,0:T(8,128)S(1)}, f32[2,16,2048]{2,1,0:T(8,128)S(1)}, u32[]{:S(2)}, u32[]{:S(2)}) collective-permute-start(f32[2,16,2048]{2,1,0:T(8,128)S(1)} %get-tuple-element.70), channel_id=1, source_target_pairs={{0,2},{4,6},{9,11},{13,15},{18,16},{22,20},{27,25},{31,29}} | collective-permute-start | bytes 786440 | tf_op jit(solution)/shard_map/ppermute | solution.py:528
  47.5 0.1 collective-permute-start.4
  47.5 5.8 %prompt_half.2.refs_7_ = bf16[2,256,4096]{2,1,0:T(8,128)(2,1)} custom-call(s32[1]{0:T(128)} %bitcast.6.refs_0_, bf16[2,256,4096]{2,1,0:T(8,128)(2,1)} %refs_1_.3, bf16[64,2048]{1,0:T(8,128)(2,1)S(1)} %get-tuple-element.71.refs_0_.refs_2_, bf16[2,2,528,64]{3,2,1,0:T(8,128)(2,1)S(1)} %get-tuple-element.72.refs_3_, ...), custom_call_target="tpu_custom_call" | custom-call | flops 2415919104 | bytes 4194304 | tf_op jit(solution)/shard_map/prompt_half/pallas_call | solution.py:433
  53.3 0.0 collective-permute-done.3
  53.4 0.0 collective-permute-done.4.refs_6_
  53.4 1.3 %collective-permute-start.5 = (f32[2,16,2048]{2,1,0:T(8,128)S(1)}, f32[2,16,2048]{2,1,0:T(8,128)S(1)}, u32[]{:S(2)}, u32[]{:S(2)}) collective-permute-start(f32[2,16,2048]{2,1,0:T(8,128)S(1)} %broadcast_select_fusion.1), channel_id=1, source_target_pairs={{0,1},{2,3},{4,5},{6,7},{9,8},{11,10},{13,12},{15,14},{18,19},{16,... | collective-permute-start | bytes 786440 | tf_op jit(solution)/shard_map/ppermute | solution.py:528
  55.4 0.0 copy-start.1
  55.4 0.0 copy-start.3
  55.4 0.0 copy-start.5
  55.4 0.0 copy-start.8
  55.4 6.0 %prompt_half.3 = bf16[2,256,4096]{2,1,0:T(8,128)(2,1)} custom-call(s32[1]{0:T(128)S(6)} %sub.9.refs_0_, bf16[2,256,4096]{2,1,0:T(8,128)(2,1)} %refs_1_.3, bf16[64,2048]{1,0:T(8,128)(2,1)S(1)} %get-tuple-element.71.refs_0_.refs_2_, bf16[2,2,528,64]{3,2,1,0:T(8,128)(2,1)S(1)} %get-tuple-element.72.refs_3_, ...), custom_call_target="tpu_custom_call", output_to_operand_aliasing={{}: (7, {})} | custom-call | flops 2415919104 | bytes 4194304 | tf_op jit(solution)/shard_map/prompt_half/pallas_call | solution.py:433
  61.4 0.0 collective-permute-done.5
  61.5 0.0 copy-done.1
  61.5 0.0 copy-done.3
  61.5 0.0 copy-done.5
  61.5 0.0 copy-done.8
  61.5 2.9 %branch_finish.1 = bf16[2,512,2048]{2,1,0:T(8,128)(2,1)} custom-call(s32[2]{0:T(128)S(1)} %copy-done.8, bf16[2,512,512]{2,1,0:T(8,128)(2,1)S(1)} %copy-done.5, f32[16,2048]{1,0:T(8,128)S(1)} %fusion.2.start_ref, f32[512,2048]{1,0:T(8,128)S(1)} %copy-done.1, f32[512,2048]{1,0:T(8,128)S(1)} %copy-done.3), custom_call_target="tpu_custom_call" | custom-call | flops 268435456 | bytes 8388608 | tf_op jit(solution)/shard_map/branch_finish/pallas_call | solution.py:480
  (19 shorter events, 0.4 us)
Async XLA Ops:
  0.6 5.7 %copy-start.7 = (bf16[2,2,16,256]{3,2,1,0:T(8,128)(2,1)S(1)}, bf16[2,2,16,256]{3,2,1,0:T(8,128)(2,1)}, u32[]{:S(2)}) copy-start(bf16[2,2,16,256]{3,2,1,0:T(8,128)(2,1)} %pbc_ref.1) | copy-start | bytes 98308
  0.6 5.7 %copy-start.10 = (bf16[2,2,16,512]{3,2,1,0:T(8,128)(2,1)S(1)}, bf16[2,2,16,512]{3,2,1,0:T(8,128)(2,1)}, u32[]{:S(2)}) copy-start(bf16[2,2,16,512]{3,2,1,0:T(8,128)(2,1)} %bbc_ref.1) | copy-start | bytes 196612
  0.7 5.7 %copy-start.6 = (f32[2,64,256]{2,1,0:T(8,128)S(1)}, f32[2,64,256]{2,1,0:T(8,128)}, u32[]{:S(2)}) copy-start(f32[2,64,256]{2,1,0:T(8,128)} %pld_ref.1) | copy-start | bytes 393220
  0.7 5.7 %copy-start.9 = (f32[2,32,512]{2,1,0:T(8,128)S(1)}, f32[2,32,512]{2,1,0:T(8,128)}, u32[]{:S(2)}) copy-start(f32[2,32,512]{2,1,0:T(8,128)} %bld_ref) | copy-start | bytes 393220
  5.9 4.4 %collective-permute-start = (f32[34,2048]{1,0:T(8,128)S(1)}, f32[34,2048]{1,0:T(8,128)S(1)}, u32[]{:S(2)}, u32[]{:S(2)}) collective-permute-start(f32[34,2048]{1,0:T(8,128)S(1)} %pad_maximum_fusion), channel_id=1, source_target_pairs={{0,4},{4,0},{8,12},{12,8},{16,20},{20,16},{24,28},{28,24},{1,5},{5... | collective-permute-start | bytes 835592 | tf_op jit(solution)/shard_map/ppermute | solution.py:497
  9.2 1.0 %copy-start.4 = (bf16[2,512,512]{2,1,0:T(8,128)(2,1)}, bf16[2,512,512]{2,1,0:T(8,128)(2,1)S(1)}, u32[]{:S(2)}) copy-start(bf16[2,512,512]{2,1,0:T(8,128)(2,1)S(1)} %get-tuple-element.83.reach_ref) | copy-start | bytes 3145732
  10.2 0.7 %copy-start.13 = (f32[32,2048]{1,0:T(8,128)}, f32[32,2048]{1,0:T(8,128)S(1)}, u32[]{:S(2)}) copy-start(f32[32,2048]{1,0:T(8,128)S(1)} %slice.41) | copy-start | bytes 786436
  11.0 0.7 %copy-start.17 = (f32[2,16,2048]{2,1,0:T(8,128)}, f32[2,16,2048]{2,1,0:T(8,128)S(1)}, u32[]{:S(2)}) copy-start(f32[2,16,2048]{2,1,0:T(8,128)S(1)} %select_add_fusion.2) | copy-start | bytes 786436
  12.5 12.8 %collective-permute-start.1 = (f32[34,2048]{1,0:T(8,128)}, f32[34,2048]{1,0:T(8,128)}, u32[]{:S(2)}, u32[]{:S(2)}) collective-permute-start(f32[34,2048]{1,0:T(8,128)} %pad_maximum_fusion.1), channel_id=1, source_target_pairs={{0,8},{4,12},{8,0},{12,4},{16,24},{20,28},{24,16},{28,20},{1,9},{5... | collective-permute-start | bytes 835592 | tf_op jit(solution)/shard_map/ppermute | solution.py:497
  15.0 12.3 %copy-start.18 = (f32[2,16,2048]{2,1,0:T(8,128)S(1)}, f32[2,16,2048]{2,1,0:T(8,128)}, u32[]{:S(2)}) copy-start(f32[2,16,2048]{2,1,0:T(8,128)} %copy-done.17) | copy-start | bytes 786436
  23.3 2.0 %copy-start = (f32[512,2048]{1,0:T(8,128)}, f32[512,2048]{1,0:T(8,128)S(1)}, u32[]{:S(2)}) copy-start(f32[512,2048]{1,0:T(8,128)S(1)} %branch_own.2.refs_0_) | copy-start | bytes 12582916
  26.3 2.5 %copy-start.15 = (f32[32,2048]{1,0:T(8,128)}, f32[32,2048]{1,0:T(8,128)S(1)}, u32[]{:S(2)}) copy-start(f32[32,2048]{1,0:T(8,128)S(1)} %slice.43) | copy-start | bytes 786436
  27.4 0.7 %copy-start.11 = (f32[2,16,2048]{2,1,0:T(8,128)}, f32[2,16,2048]{2,1,0:T(8,128)S(1)}, u32[]{:S(2)}) copy-start(f32[2,16,2048]{2,1,0:T(8,128)S(1)} %select_add_fusion.1) | copy-start | bytes 786436
  28.8 11.8 %collective-permute-start.2 = (f32[34,2048]{1,0:T(8,128)}, f32[34,2048]{1,0:T(8,128)}, u32[]{:S(2)}, u32[]{:S(2)}) collective-permute-start(f32[34,2048]{1,0:T(8,128)} %pad_maximum_fusion.2), channel_id=1, source_target_pairs={{0,16},{4,20},{8,24},{12,28},{16,0},{20,4},{24,8},{28,12},{1,17},{... | collective-permute-start | bytes 835592 | tf_op jit(solution)/shard_map/ppermute | solution.py:497
  30.3 12.2 %copy-start.12 = (f32[2,16,2048]{2,1,0:T(8,128)S(1)}, f32[2,16,2048]{2,1,0:T(8,128)}, u32[]{:S(2)}) copy-start(f32[2,16,2048]{2,1,0:T(8,128)} %copy-done.11) | copy-start | bytes 786436
  30.3 12.2 %copy-start.14 = (f32[32,2048]{1,0:T(8,128)S(1)}, f32[32,2048]{1,0:T(8,128)}, u32[]{:S(2)}) copy-start(f32[32,2048]{1,0:T(8,128)} %copy-done.13) | copy-start | bytes 786436
  30.3 12.2 %copy-start.16 = (f32[32,2048]{1,0:T(8,128)S(1)}, f32[32,2048]{1,0:T(8,128)}, u32[]{:S(2)}) copy-start(f32[32,2048]{1,0:T(8,128)} %copy-done.15) | copy-start | bytes 786436
  38.7 2.0 %copy-start.2 = (f32[512,2048]{1,0:T(8,128)}, f32[512,2048]{1,0:T(8,128)S(1)}, u32[]{:S(2)}) copy-start(f32[512,2048]{1,0:T(8,128)S(1)} %branch_own.3.refs_1_) | copy-start | bytes 12582916
  42.7 10.7 %collective-permute-start.3 = (f32[2,16,2048]{2,1,0:T(8,128)S(1)}, f32[2,16,2048]{2,1,0:T(8,128)S(1)}, u32[]{:S(2)}, u32[]{:S(2)}) collective-permute-start(f32[2,16,2048]{2,1,0:T(8,128)S(1)} %get-tuple-element.70), channel_id=1, source_target_pairs={{0,2},{4,6},{9,11},{13,15},{18,16},{22,20},{27,25},{31,29}} | collective-permute-start | bytes 786440 | tf_op jit(solution)/shard_map/ppermute | solution.py:528
  47.5 5.9 %collective-permute-start.4 = (f32[2,16,2048]{2,1,0:T(8,128)S(1)}, f32[2,16,2048]{2,1,0:T(8,128)S(1)}, u32[]{:S(2)}, u32[]{:S(2)}) collective-permute-start(f32[2,16,2048]{2,1,0:T(8,128)S(1)} %get-tuple-element.88), channel_id=1, source_target_pairs={{0,4},{4,0},{8,12},{12,8},{16,20},{20,16},{24,28},{28,24},{1,5},{5... | collective-permute-start | bytes 786440 | tf_op jit(solution)/shard_map/ppermute | solution.py:497
  53.4 8.0 %collective-permute-start.5 = (f32[2,16,2048]{2,1,0:T(8,128)S(1)}, f32[2,16,2048]{2,1,0:T(8,128)S(1)}, u32[]{:S(2)}, u32[]{:S(2)}) collective-permute-start(f32[2,16,2048]{2,1,0:T(8,128)S(1)} %broadcast_select_fusion.1), channel_id=1, source_target_pairs={{0,1},{2,3},{4,5},{6,7},{9,8},{11,10},{13,12},{15,14},{18,19},{16,... | collective-permute-start | bytes 786440 | tf_op jit(solution)/shard_map/ppermute | solution.py:528
  55.4 6.1 %copy-start.1 = (f32[512,2048]{1,0:T(8,128)S(1)}, f32[512,2048]{1,0:T(8,128)}, u32[]{:S(2)}) copy-start(f32[512,2048]{1,0:T(8,128)} %copy-done) | copy-start | bytes 12582916
  55.4 6.1 %copy-start.3 = (f32[512,2048]{1,0:T(8,128)S(1)}, f32[512,2048]{1,0:T(8,128)}, u32[]{:S(2)}) copy-start(f32[512,2048]{1,0:T(8,128)} %copy-done.2) | copy-start | bytes 12582916
  55.4 6.1 %copy-start.5 = (bf16[2,512,512]{2,1,0:T(8,128)(2,1)S(1)}, bf16[2,512,512]{2,1,0:T(8,128)(2,1)}, u32[]{:S(2)}) copy-start(bf16[2,512,512]{2,1,0:T(8,128)(2,1)} %copy-done.4) | copy-start | bytes 3145732
  55.4 6.1 %copy-start.8 = (s32[2]{0:T(128)S(1)}, s32[2]{0:T(128)}, u32[]{:S(2)}) copy-start(s32[2]{0:T(128)} %len_ref.1) | copy-start | bytes 28

commit v8 on v6

--- a/solution.py
+++ b/solution.py
@@ -175,75 +175,49 @@
     return scales
 
 
-def cuts_of(ld_ref):
-    count, _, positions = ld_ref.shape
-    return [(i, pl.ds(b * BLOCK, BLOCK)) for i in range(count) for b in range(positions // BLOCK)]
-
-
-def prepare_kernel(
-    pld_ref, pbc_ref, bld_ref, bbc_ref,
-    hot_ref, pw_ref, plv_ref, plc_ref, bw_ref, blv_ref, blc_ref, reach_ref, *, width
-):
-    state = pbc_ref.shape[2]
-
-    def collect(ld_ref, bc_ref):
-        cuts = cuts_of(ld_ref)
-        logs = jnp.concatenate([ld_ref[i, :, cut] for i, cut in cuts], axis=0)
-        return cuts, logs, [(bc_ref[0, i, :, cut], bc_ref[1, i, :, cut]) for i, cut in cuts]
-
-    cuts, logs, parts = collect(bld_ref, bbc_ref)
-    heads = bld_ref.shape[1]
-    blocks = len(cuts) // bld_ref.shape[0]
-    for k, w in enumerate(prepare(parts, logs, blv_ref, blc_ref, state, heads)):
-        bw_ref[k] = w
+def prepare_hot(hot_ref, heads, width):
     row_head = remainder(iota((2 * heads, 1), 0), heads)
     for g in range(hot_ref.shape[1] // 256):
         lane_head = quotient(iota((1, 256), 1), width) + g * (256 // width)
         hot_ref[:, pl.ds(g * 256, 256)] = jnp.where(row_head == lane_head, 1.0, 0.0).astype(BF16)
-    upto = jnp.where(iota((BLOCK, 1), 0) <= iota((1, BLOCK), 1), 1.0, 0.0)
-    runs = exact_dot(logs, upto)
-    for k, (i, cut) in enumerate(cuts):
-        run = runs[k * heads:(k + 1) * heads]
-        if k % blocks:
-            run = run + entered
-        entered = run[:, BLOCK - 1:BLOCK]
-        reach = parts[k][1].astype(F32)[None, :, :] * jnp.exp(run)[:, None, :]
-        reach_ref[i, cut, :] = reach.reshape(heads * state, BLOCK).T.astype(BF16)
-
-    cuts, logs, parts = collect(pld_ref, pbc_ref)
-    heads = pld_ref.shape[1] // 2
-    for k, w in enumerate(prepare(parts, logs, plv_ref, plc_ref, state, heads)):
-        pw_ref[k // 2, k % 2] = w
-
-
-def prepare_all(prompt_logdec, prompt_bc, branch_logdec, branch_bc, branch_channels):
-    state = prompt_bc.shape[2]
-    rows = BLOCK // CHUNK * state
-    prompt_cuts = prompt_logdec.shape[0] * (prompt_logdec.shape[2] // BLOCK)
-    branches, heads, positions = branch_logdec.shape
-    branch_cuts = branches * (positions // BLOCK)
-    half = prompt_logdec.shape[1] // 2
+
+
+def blocks_of(ld_ref, bc_ref):
+    count, _, positions = ld_ref.shape
+    cuts = [(i, pl.ds(b * BLOCK, BLOCK)) for i in range(count) for b in range(positions // BLOCK)]
+    logs = jnp.concatenate([ld_ref[i, :, cut] for i, cut in cuts], axis=0)
+    return cuts, logs, [(bc_ref[0, i, :, cut], bc_ref[1, i, :, cut]) for i, cut in cuts]
+
+
+def prepare_kernel(ld_ref, bc_ref, hot_ref, w_ref, lv_ref, lc_ref, *, width):
+    heads = ld_ref.shape[1] // 2
+    prepare_hot(hot_ref, heads, width)
+    _, logs, parts = blocks_of(ld_ref, bc_ref)
+    for k, w in enumerate(prepare(parts, logs, lv_ref, lc_ref, bc_ref.shape[2], heads)):
+        w_ref[k // 2, k % 2] = w
+
+
+def prepare_prompts(logdec, bc, channels):
+    count, heads, positions = logdec.shape
+    rows = BLOCK // CHUNK * bc.shape[2]
+    cuts = count * (positions // BLOCK)
+    half = heads // 2
     shapes = [
-        ((2 * heads, branch_channels), BF16),
-        ((prompt_cuts, 2, 2 * BLOCK + 16, 2 * half), BF16),
-        ((prompt_cuts, rows + BLOCK, BLOCK), BF16),
-        ((prompt_cuts, BLOCK, rows), BF16),
-        ((branch_cuts, 2 * BLOCK + 16, 2 * heads), BF16),
-        ((branch_cuts, rows + BLOCK, BLOCK), BF16),
-        ((branch_cuts, BLOCK, rows), BF16),
-        ((branches, positions, heads * state), BF16),
+        (2 * half, channels // 2),
+        (cuts, 2, 2 * BLOCK + 16, 2 * half),
+        (cuts, rows + BLOCK, BLOCK),
+        (cuts, BLOCK, rows),
     ]
     whole = pl.BlockSpec(memory_space=pltpu.VMEM)
-    out = pl.pallas_call(
-        functools.partial(prepare_kernel, width=branch_channels // heads),
-        in_specs=[whole] * 4,
-        out_specs=[pl.BlockSpec(shape, lambda rank=len(shape): (0,) * rank) for shape, _ in shapes],
-        out_shape=[jax.ShapeDtypeStruct(*shape) for shape in shapes],
+    return pl.pallas_call(
+        functools.partial(prepare_kernel, width=channels // heads),
+        in_specs=[whole] * 2,
+        out_specs=[pl.BlockSpec(shape, lambda rank=len(shape): (0,) * rank) for shape in shapes],
+        out_shape=[jax.ShapeDtypeStruct(shape, BF16) for shape in shapes],
         compiler_params=pltpu.CompilerParams(vmem_limit_bytes=VMEM_LIMIT),
         cost_estimate=pl.CostEstimate(flops=10**8, bytes_accessed=10**6, transcendentals=0),
         name="prepare",
-    )(prompt_logdec, prompt_bc, branch_logdec, branch_bc)
-    return out[:4], (out[0], *out[4:7]), out[7]
+    )(logdec, bc)
 
 
 def run_tiles(jobs):
@@ -257,7 +231,7 @@
             jobs[g - 2][2](passed.pop(g - 2))
 
 
-def tile_job(ready_refs, at, g, x_of, entering_of, leave, write):
+def tile_job(ready_refs, at, cols, x_of, entering_of, leave, write):
     hot_ref, w_ref, lv_ref, lc_ref = ready_refs
     w_at, at = at
     rows = lc_ref.shape[2]
@@ -265,7 +239,7 @@
     state = rows // chunks
 
     def scale():
-        wide = jnp.dot(w_ref[w_at], hot_ref[:, pl.ds(g * 256, 256)], preferred_element_type=F32)
+        wide = jnp.dot(w_ref[w_at], hot_ref[:, cols], preferred_element_type=F32)
         scaled = (x_of().astype(F32) * wide[:BLOCK]).astype(BF16)
         return scaled, wide[BLOCK:BLOCK + 16], wide[BLOCK + 16:]
 
@@ -304,64 +278,83 @@
             self.wait(key)
 
 
-def branch_kernel(x_in, *refs, which):
-    ready = refs[:4]
-    own_ref, x_ref, s_ref, in_sems = refs[4:]
-    positions, channels = x_ref.shape
+def branch_kernel(x_ref, ld_ref, bc_ref, *refs, skip, width):
+    own_ref, reach_ref, hot_ref, w_ref, lv_ref, lc_ref, s_ref = refs[skip:]
+    block, tile = pl.program_id(0), pl.program_id(1)
+    heads = ld_ref.shape[1]
+    lanes = x_ref.shape[2]
     state = s_ref.shape[0]
-    blocks = positions // BLOCK
-    lanes = channels // in_sems.shape[1]
-    came = Copies(in_sems)
-    for b in range(blocks):
-        for j in range(channels // lanes):
-            spot = (pl.ds(b * BLOCK, BLOCK), pl.ds(j * lanes, lanes))
-            came.start((b, j), x_in.at[(which, *spot)], x_ref.at[spot])
-
-    def job(b, g):
+
+    @pl.when((block == 0) & (tile == 0))
+    def _():
+        prepare_hot(hot_ref, heads, width)
+        cuts, logs, parts = blocks_of(ld_ref, bc_ref)
+        for k, w in enumerate(prepare(parts, logs, lv_ref, lc_ref, state, heads)):
+            w_ref[k] = w
+        upto = jnp.where(iota((BLOCK, 1), 0) <= iota((1, BLOCK), 1), 1.0, 0.0)
+        runs = exact_dot(logs, upto)
+        for k, (_, cut) in enumerate(cuts):
+            run = runs[k * heads:(k + 1) * heads]
+            if k:
+                run = run + entered
+            entered = run[:, BLOCK - 1:BLOCK]
+            reach = parts[k][1].astype(F32)[None, :, :] * jnp.exp(run)[:, None, :]
+            reach_ref[0, cut, :] = reach.reshape(heads * state, BLOCK).T.astype(BF16)
+
+    def job(g):
         cols = pl.ds(g * 256, 256)
-        here = (pl.ds(b * BLOCK, BLOCK), cols)
-
-        def x_of():
-            if g * 256 % lanes == 0:
-                came.wait((b, g * 256 // lanes))
-            return x_ref[here]
+        here = pl.ds(pl.multiple_of(tile * lanes + g * 256, 256), 256)
+
+        def entering_of():
+            return jnp.where(block == 0, 0.0, s_ref[:, here])
 
         def leave(carry):
-            if b < blocks - 1:
-                s_ref[:, cols] = carry
+            s_ref[:, here] = carry
 
         def write(out):
-            own_ref[here] = out
-
-        def entering_of():
-            return s_ref[:, cols] if b else jnp.zeros((state, 256), F32)
-
-        at = which * blocks + b
-        return tile_job(ready, (at, at), g, x_of, entering_of, leave, write)
-
-    run_tiles([job(b, g) for b in range(blocks) for g in range(channels // 256)])
-
-
-def branch_own(x, ready, which):
-    _, positions, channels = x.shape
-    state = ready[3].shape[2] * CHUNK // BLOCK
-    whole = pl.BlockSpec(memory_space=pltpu.VMEM)
+            own_ref[0, :, cols] = out
+
+        ready = (hot_ref, w_ref, lv_ref, lc_ref)
+        return tile_job(ready, (block, block), here, lambda: x_ref[0, :, cols], entering_of, leave, write)
+
+    run_tiles([job(g) for g in range(lanes // 256)])
+
+
+def branch_own(x, logdec, bc, which, into):
+    count, positions, channels = x.shape
+    heads, state = logdec.shape[1], bc.shape[2]
+    blocks, rows = positions // BLOCK, BLOCK // CHUNK * state
+    lanes = min(1024, channels)
     work = positions * channels
     return pl.pallas_call(
-        functools.partial(branch_kernel, which=which),
-        in_specs=[pl.BlockSpec(memory_space=pltpu.HBM)] + [whole] * 4,
-        out_specs=whole,
-        out_shape=jax.ShapeDtypeStruct(x.shape[1:], F32),
+        functools.partial(branch_kernel, skip=len(into), width=channels // heads),
+        grid=(blocks, channels // lanes),
+        in_specs=[
+            pl.BlockSpec((1, BLOCK, lanes), lambda b, j: (which, b, j)),
+            pl.BlockSpec((1, heads, positions), lambda b, j: (which, 0, 0)),
+            pl.BlockSpec((2, 1, state, positions), lambda b, j: (0, which, 0, 0)),
+        ] + [pl.BlockSpec(memory_space=pl.ANY)] * len(into),
+        out_specs=[
+            pl.BlockSpec((1, BLOCK, lanes), lambda b, j: (which, b, j)),
+            pl.BlockSpec((1, positions, heads * state), lambda b, j: (which, 0, 0)),
+        ],
+        out_shape=[
+            jax.ShapeDtypeStruct(x.shape, F32),
+            jax.ShapeDtypeStruct((count, positions, heads * state), BF16),
+        ],
         scratch_shapes=[
-            pltpu.VMEM((positions, channels), BF16),
+            pltpu.VMEM((2 * heads, channels), BF16),
+            pltpu.VMEM((blocks, 2 * BLOCK + 16, 2 * heads), BF16),
+            pltpu.VMEM((blocks, rows + BLOCK, BLOCK), BF16),
+            pltpu.VMEM((blocks, BLOCK, rows), BF16),
             pltpu.VMEM((state, channels), F32),
-            pltpu.SemaphoreType.DMA((positions // BLOCK, channels // min(512, channels))),
         ],
-        compiler_params=pltpu.CompilerParams(vmem_limit_bytes=VMEM_LIMIT),
+        input_output_aliases={3 + i: i for i in range(len(into))},
+        compiler_params=pltpu.CompilerParams(vmem_limit_bytes=32 * 1024 * 1024),
         cost_estimate=pl.CostEstimate(
             flops=2 * 1152 * work, bytes_accessed=4 * work, transcendentals=0),
         name="branch_own",
-    )(in_hbm(x), *ready)
+    )(in_hbm(x), logdec, bc, *into)
 
 
 def prompt_kernel(*refs, skip):
@@ -407,7 +400,7 @@
                 left.start((i, b, j), x_ref.at[staged], y_out.at[there])
 
         at = i * blocks + b
-        return tile_job(ready, ((at, half), at), g, x_of, entering_of, leave, write)
+        return tile_job(ready, ((at, half), at), pl.ds(g * 256, 256), x_of, entering_of, leave, write)
 
     run_tiles([job(i, b, g) for i in range(count) for b in range(blocks) for g in range(channels // 256)])
     left.wait_all()
@@ -438,8 +431,7 @@
     )(half, in_hbm(x), *ready, start, *into)
 
 
-def finish_kernel(len_ref, reach_ref, start_ref, *refs, width):
-    own_refs, (y_out, y_ref, sems) = refs[:-3], refs[-3:]
+def finish_kernel(len_ref, own_ref, reach_ref, start_ref, y_out, y_ref, sems, *, width):
     count, positions, channels = y_ref.shape
     state = start_ref.shape[0]
     group = 128 // state
@@ -457,19 +449,19 @@
                 term = jnp.dot(
                     reach_ref[i, rows, pl.ds(g * 128, 128)], starts[g], preferred_element_type=F32)
                 live = iota((BLOCK, span), 0) < len_ref[i] - b * BLOCK
-                y_ref[i, rows, cols] = jnp.where(live, own_refs[i][rows, cols] + term, 0.0).astype(BF16)
+                y_ref[i, rows, cols] = jnp.where(live, own_ref[i, rows, cols] + term, 0.0).astype(BF16)
                 left.start((i, b, g), y_ref.at[i, rows, cols], y_out.at[i, rows, cols])
     left.wait_all()
 
 
-def finish(lengths, reach, start, own):
-    count, (positions, channels) = len(own), own[0].shape
+def finish(lengths, own, reach, start):
+    count, positions, channels = own.shape
     state = start.shape[0]
     width = channels * state // reach.shape[2]
     whole = pl.BlockSpec(memory_space=pltpu.VMEM)
     return pl.pallas_call(
         functools.partial(finish_kernel, width=width),
-        in_specs=[pl.BlockSpec(memory_space=pltpu.SMEM)] + [whole] * (2 + count),
+        in_specs=[pl.BlockSpec(memory_space=pltpu.SMEM)] + [whole] * 3,
         out_specs=pl.BlockSpec(memory_space=pltpu.HBM),
         out_shape=jax.ShapeDtypeStruct((count, positions, channels), BF16),
         scratch_shapes=[
@@ -480,7 +472,7 @@
         cost_estimate=pl.CostEstimate(
             flops=2**28, bytes_accessed=2**23, transcendentals=0),
         name="branch_finish",
-    )(lengths, reach, start, *own)
+    )(lengths, own, reach, start)
 
 
 def swap_bit(value, bit, size):
@@ -546,11 +538,11 @@
     low, high = (end[:, :, :half], log[:, :1, :half]), (end[:, :, half:], log[:, :1, half:])
     keep = [jnp.where(odd, h, l) for l, h in zip(low, high)]
     send = [jnp.where(odd, l, h) for l, h in zip(low, high)]
-    got, (prompt_ready, branch_ready, reach) = beside(
+    got, ready = beside(
         lambda v: swap_bit(v, 1, size),
         pack(*send),
-        lambda ld: prepare_all(prompt_logdec, prompt_bc, ld, branch_bc, branch_x.shape[2]),
-        branch_logdec,
+        lambda logdec: prepare_prompts(logdec, prompt_bc, prompt_x.shape[2]),
+        prompt_logdec,
     )
     got = unpack(got, prompts)
     first, second = in_order(odd, keep, got)
@@ -568,7 +560,7 @@
         else:
             got, own = beside(
                 swap, pack(total, total_log),
-                lambda x, own: (*own, branch_own(x, branch_ready, which)), branch_x, own)
+                lambda x, own: branch_own(x, branch_logdec, branch_bc, which, own), branch_x, own)
         other = unpack(got, prompts)
         upper = (mine & bit) != 0
         before = jnp.where(upper, jnp.exp(before_log) * other[0] + before, before)
@@ -576,7 +568,7 @@
         total, total_log = join(*in_order(upper, (total, total_log), other))
         bit *= 2
     for which in works:
-        own = (*own, branch_own(branch_x, branch_ready, which))
+        own = branch_own(branch_x, branch_logdec, branch_bc, which, own)
 
     next_before = jnp.exp(first[1]) * before + first[0]
     keep = jnp.where(odd, next_before, before)
@@ -591,17 +583,17 @@
             side, entering = sides.pop(0)
             (got, has), prompt_y = beside(
                 step, total,
-                lambda entering, y: (prompt_half(side, prompt_x, prompt_ready, entering, y),), entering, prompt_y)
+                lambda entering, y: (prompt_half(side, prompt_x, ready, entering, y),), entering, prompt_y)
         else:
             got, has = step(total)
         total = jnp.where(has, total, got)
         hop //= 2
     for side, entering in sides:
-        prompt_y = (prompt_half(side, prompt_x, prompt_ready, entering, prompt_y),)
+        prompt_y = (prompt_half(side, prompt_x, ready, entering, prompt_y),)
     start = total[0]
     for which in range(1, prompts):
         start = jnp.where(branch_prompt[0] == which, total[which], start)
-    branch_y = finish(branch_len, reach, start, own)
+    branch_y = finish(branch_len, *own, start)
     return prompt_y[0], branch_y
 
 

time: 60.9 us -> 62.9 us (1.033)
  local copies, waits for them, and re-layouts: 9.89 us -> 12.8 us
  waiting for transfers between devices: 2.61 us -> 0.38 us
  other arithmetic: 2.96 us -> 3.96 us
    unnamed x44 -> x38, local copies, waits for them, and re-layouts: 7.08 us -> 10 us
    ppermute x4, waiting for transfers between devices: 2.6 us -> 0.37 us  [swap_bit(): return lax.ppermute(value, 'ctx', [(k, k ^ bit) for k in range(size)])]
    select_n x2, other arithmetic: 0.07 us -> 1.03 us  [body(): total = jnp.where(has, total, got)]
    select_n x1, other arithmetic: 0.14 us -> 0.93 us  [body(): others = swap_bit(jnp.where(odd, before, next_before), 1, size)]
    concatenate x3, other arithmetic: 1.52 us -> 0.8 us  [pack(): jnp.concatenate([states.reshape(-1, lanes), logs.reshape(-1, lanes)], axi...]
  transfers between devices with their start and end apart: 6 -> 6, of which waited for: 2 -> 1; matrix products, arithmetic and copies ran while one was open for 0% -> 2% of each run, Pallas kernels for 40% -> 39%
where the time goes in v8:
time: 62.9 us; the launch traced here: 62.3 us
  Pallas kernels  32.3 us (51%)
  local copies, waits for them, and re-layouts  12.8 us (20%)
  starting transfers between devices  11 us (17%)
  other arithmetic  3.96 us (6%)
  between operations  1.9 us (3%)
    pallas_call x2, Pallas kernels, prompt_half(): pl.pallas_call(functools.partial(prompt_kernel, skip=len(into)), in_specs...  11.8 us
    pallas_call x2, Pallas kernels, branch_own(): pl.pallas_call(functools.partial(branch_kernel, skip=len(into), width=cha...  11.7 us
    unnamed x38, local copies, waits for them, and re-layouts  10 us
    ppermute x2, starting transfers between devices, spread_step(): got = lax.ppermute(value, ('ctx', 'pair'), links)  5.99 us
    pallas_call x1, Pallas kernels, local_ends(): pl.pallas_call(functools.partial(ends_kernel, width=width, lanes=lanes),...  5.05 us
    ppermute x4, starting transfers between devices, swap_bit(): return lax.ppermute(value, 'ctx', [(k, k ^ bit) for k in range(size)])  5.03 us
    pallas_call x1, Pallas kernels, finish(): pl.pallas_call(functools.partial(finish_kernel, width=width), in_specs=[p...  2.89 us
    slice x3, local copies, waits for them, and re-layouts, unpack(): packed[:rows].reshape(count, rows // count, lanes)  1.95 us
  transfers between devices with their start and end apart: 6, of which 1 were waited for; matrix products, arithmetic and copies ran while one was open for 2% of the time, Pallas kernels for 39%

profile of v8, /device:TPU:0, one launch (start us, length us, event | category | flops | bytes accessed | tf_op | source)
XLA Modules:
  0.0 62.3 jit_solution(5615995581020195262)
XLA Ops:
  0.6 0.0 copy-start.4
  0.6 0.0 copy-start.6
  0.7 0.0 copy-start.3
  0.7 0.0 copy-start.5
  0.7 5.1 %local_ends.1 = (f32[2,16,4096]{2,1,0:T(8,128)S(1)}, f32[2,8,4096]{2,1,0:T(8,128)S(1)}) custom-call(bf16[2,256,4096]{2,1,0:T(8,128)(2,1)} %refs_1_.3, f32[2,64,256]{2,1,0:T(8,128)} %ld_ref.2, bf16[2,2,16,256]{3,2,1,0:T(8,128)(2,1)} %bc_ref.3), custom_call_target="tpu_custom_call" | custom-call | flops 268435456 | bytes 4194304 | tf_op jit(solution)/shard_map/local_ends/pallas_call | solution.py:124
  5.9 0.5 collective-permute-start
  6.4 0.0 copy-done.4
  6.4 0.0 copy-done.6
  6.4 0.9 %prepare.1 = (bf16[64,2048]{1,0:T(8,128)(2,1)S(1)}, bf16[2,2,528,64]{3,2,1,0:T(8,128)(2,1)S(1)}, bf16[2,384,256]{2,1,0:T(8,128)(2,1)S(1)}, bf16[2,256,128]{2,1,0:T(8,128)(2,1)S(1)}) custom-call(f32[2,64,256]{2,1,0:T(8,128)S(1)} %copy-done.4, bf16[2,2,16,256]{3,2,1,0:T(8,128)(2,1)S(1)} %copy-done.6), custom_call_target="tpu_custom_call" | custom-call | flops 100000000 | bytes 1000000 | tf_op jit(solution)/shard_map/prepare/pallas_call | solution.py:212
  7.3 0.4 collective-permute-done
  7.7 0.0 copy-start.8
  7.8 0.1 select_add_fusion.2
  7.8 0.0 copy-start.12
  7.9 2.9 %collective-permute-start.1 = (f32[34,2048]{1,0:T(8,128)S(1)}, f32[34,2048]{1,0:T(8,128)}, u32[]{:S(2)}, u32[]{:S(2)}) collective-permute-start(f32[34,2048]{1,0:T(8,128)S(1)} %pad_maximum_fusion.1), channel_id=1, source_target_pairs={{0,8},{4,12},{8,0},{12,4},{16,24},{20,28},{24,16},{28,20},{1,9},{5... | collective-permute-start | bytes 835592 | tf_op jit(solution)/shard_map/ppermute | solution.py:479
  10.8 0.0 copy-done.8
  10.8 0.0 copy-done.12
  10.8 0.0 copy-done.3
  10.8 0.0 copy-done.5
  10.8 0.0 copy-start.13
  10.8 5.8 %branch_own.2 = (f32[2,512,2048]{2,1,0:T(8,128)S(1)}, bf16[2,512,512]{2,1,0:T(8,128)(2,1)S(1)}) custom-call(bf16[2,512,2048]{2,1,0:T(8,128)(2,1)} %x_ref.3, f32[2,32,512]{2,1,0:T(8,128)S(1)} %copy-done.3, bf16[2,2,16,512]{3,2,1,0:T(8,128)(2,1)S(1)} %copy-done.5), custom_call_target="tpu_custom_call" | custom-call | flops 2415919104 | bytes 4194304 | tf_op jit(solution)/shard_map/branch_own/pallas_call | solution.py:329
  16.7 0.0 copy-start
  16.7 3.3 %copy-done = f32[2,512,2048]{2,1,0:T(8,128)} copy-done((f32[2,512,2048]{2,1,0:T(8,128)}, f32[2,512,2048]{2,1,0:T(8,128)S(1)}, u32[]{:S(2)}) %copy-start) | copy-done | bytes 8388632
  19.9 0.0 collective-permute-done.1
  19.9 1.0 %slice.43 = f32[32,2048]{1,0:T(8,128)S(1)} slice(f32[34,2048]{1,0:T(8,128)} %collective-permute-done.1), slice={[0:32], [0:2048]} | slice | bytes 524288 | tf_op jit(solution)/shard_map/slice | solution.py:490
  20.9 0.0 copy-start.10
  20.9 0.9 %select_exponential_fusion = (f32[2,2048]{1,0:T(2,128)S(1)}, f32[2,2048]{1,0:T(2,128)S(1)}) fusion(pred[]{:T(512)S(6)} %ne.17, f32[34,2048]{1,0:T(8,128)} %collective-permute-done.1), kind=kLoop, calls=%fused_computation.33 | loop fusion | flops 4096 | bytes 49153 | tf_op jit(solution)/shard_map/exp | solution.py:566
  21.9 0.0 copy-done.10
  21.9 0.0 copy-done.13
  21.9 0.1 select_add_fusion.1
  22.0 0.7 %pad_maximum_fusion.2 = f32[34,2048]{1,0:T(8,128)} fusion(f32[2,2048]{1,0:T(2,128)S(1)} %bitcast.41, f32[32,2048]{1,0:T(8,128)S(1)} %bitcast.31), kind=kLoop, calls=%fused_computation.3 | loop fusion | flops 69632 | bytes 557056 | tf_op jit(solution)/shard_map/concatenate | solution.py:484
  22.8 1.5 %collective-permute-start.2 = (f32[34,2048]{1,0:T(8,128)}, f32[34,2048]{1,0:T(8,128)}, u32[]{:S(2)}, u32[]{:S(2)}) collective-permute-start(f32[34,2048]{1,0:T(8,128)} %pad_maximum_fusion.2), channel_id=1, source_target_pairs={{0,16},{4,20},{8,24},{12,28},{16,0},{20,4},{24,8},{28,12},{1,17},{... | collective-permute-start | bytes 835592 | tf_op jit(solution)/shard_map/ppermute | solution.py:479
  24.3 0.0 copy-start.1
  24.3 3.4 %copy-done.1 = f32[2,512,2048]{2,1,0:T(8,128)S(1)} copy-done((f32[2,512,2048]{2,1,0:T(8,128)S(1)}, f32[2,512,2048]{2,1,0:T(8,128)}, u32[]{:S(2)}) %copy-start.1) | copy-done | bytes 8388632
  27.7 0.0 copy-start.9
  27.7 0.0 copy-start.11
  27.7 5.8 %branch_own.3 = (f32[2,512,2048]{2,1,0:T(8,128)S(1)}, bf16[2,512,512]{2,1,0:T(8,128)(2,1)S(1)}) custom-call(bf16[2,512,2048]{2,1,0:T(8,128)(2,1)} %x_ref.3, f32[2,32,512]{2,1,0:T(8,128)S(1)} %copy-done.3, bf16[2,2,16,512]{3,2,1,0:T(8,128)(2,1)S(1)} %copy-done.5, f32[2,512,2048]{2,1,0:T(8,128)S(1)} %copy-done.1, ...), custom_call_target="tpu_custom_call", output_to_operand_aliasing={{0}: (3, {}), {1}: (4, {})} | custom-call | flops 2415919104 | bytes 4194304 | tf_op jit(solution)/shard_map/branch_own/pallas_call | solution.py:329
  33.5 0.0 copy-start.2
  33.5 3.3 %copy-done.2 = f32[2,512,2048]{2,1,0:T(8,128)} copy-done((f32[2,512,2048]{2,1,0:T(8,128)}, f32[2,512,2048]{2,1,0:T(8,128)S(1)}, u32[]{:S(2)}) %copy-start.2) | copy-done | bytes 8388632
  36.8 0.0 collective-permute-done.2
  36.8 1.0 %slice.45 = f32[32,2048]{1,0:T(8,128)S(1)} slice(f32[34,2048]{1,0:T(8,128)} %collective-permute-done.2), slice={[0:32], [0:2048]} | slice | bytes 524288 | tf_op jit(solution)/shard_map/slice | solution.py:490
  37.7 0.8 %slice.44 = f32[2,2048]{1,0:T(2,128)S(1)} slice(f32[34,2048]{1,0:T(8,128)} %collective-permute-done.2), slice={[32:34], [0:2048]} | slice | bytes 32768 | tf_op jit(solution)/shard_map/slice | solution.py:490
  38.6 0.0 copy-done.9
  38.6 0.0 copy-done.11
  38.6 0.9 %fusion = (f32[2,16,2048]{2,1,0:T(8,128)}, f32[2,16,2048]{2,1,0:T(8,128)S(1)}, f32[2,16,2048]{2,1,0:T(8,128)}) fusion(f32[2,2048]{1,0:T(2,128)S(1)} %get-tuple-element.92, pred[]{:T(512)S(6)} %eq.15, f32[2,16,2048]{2,1,0:T(8,128)S(1)} %bitcast.33, f32[2,16,2048]{2,1,0:T(8,128)S(1)} %bitcast.35, pred[]{:T(512)S(6)} %ne.17, f32[2,16,2048]{2,1,0:T(8,128)S(1)} %bitcast.37, ...), kind=kLoop, calls=%fused_computation.5 | loop fusion | flops 917504 | bytes 2408451 | tf_op jit(solution)/shard_map/jit(_where)/select_n | solution.py:575
  39.6 4.5 %collective-permute-start.3 = (f32[2,16,2048]{2,1,0:T(8,128)}, f32[2,16,2048]{2,1,0:T(8,128)S(1)}, u32[]{:S(2)}, u32[]{:S(2)}) collective-permute-start(f32[2,16,2048]{2,1,0:T(8,128)} %get-tuple-element.65), channel_id=1, source_target_pairs={{0,2},{4,6},{9,11},{13,15},{18,16},{22,20},{27,25},{31,29}} | collective-permute-start | bytes 786440 | tf_op jit(solution)/shard_map/ppermute | solution.py:510
  44.1 0.1 collective-permute-start.4
  44.2 5.8 %prompt_half.2.refs_7_ = bf16[2,256,4096]{2,1,0:T(8,128)(2,1)} custom-call(s32[1]{0:T(128)} %bitcast.6.refs_0_, bf16[2,256,4096]{2,1,0:T(8,128)(2,1)} %refs_1_.3, bf16[64,2048]{1,0:T(8,128)(2,1)S(1)} %get-tuple-element.66.refs_2_, bf16[2,2,528,64]{3,2,1,0:T(8,128)(2,1)S(1)} %get-tuple-element.67.refs_3_, bf16[2,384,256]{2,1,0:T(8,128)(2,1)S(1)} %get-tuple-element.68.refs_4_, ...), custom_call_target="tpu_custom_call" | custom-call | flops 2415919104 | bytes 4194304 | tf_op jit(solution)/shard_map/prompt_half/pallas_call | solution.py:416
  50.0 0.0 collective-permute-done.3
  50.0 1.0 %broadcast_select_fusion.1 = f32[2,16,2048]{2,1,0:T(8,128)S(1)} fusion(f32[2,16,2048]{2,1,0:T(8,128)} %get-tuple-element.65, f32[2,16,2048]{2,1,0:T(8,128)S(1)} %collective-permute-done.3, pred[]{:T(512)S(6)} %eq.16), kind=kLoop, calls=%fused_computation.15 | loop fusion | flops 65536 | bytes 786433 | tf_op jit(solution)/shard_map/jit(_where)/select_n | solution.py:589
  51.0 0.0 collective-permute-done.4.refs_6_
  51.0 1.5 %collective-permute-start.5 = (f32[2,16,2048]{2,1,0:T(8,128)S(1)}, f32[2,16,2048]{2,1,0:T(8,128)S(1)}, u32[]{:S(2)}, u32[]{:S(2)}) collective-permute-start(f32[2,16,2048]{2,1,0:T(8,128)S(1)} %broadcast_select_fusion.1), channel_id=1, source_target_pairs={{0,1},{2,3},{4,5},{6,7},{9,8},{11,10},{13,12},{15,14},{18,19},{16,... | collective-permute-start | bytes 786440 | tf_op jit(solution)/shard_map/ppermute | solution.py:510
  53.2 0.0 slice-start
  53.2 0.0 slice-start.1
  53.2 0.0 copy-start.7
  53.2 6.0 %prompt_half.3 = bf16[2,256,4096]{2,1,0:T(8,128)(2,1)} custom-call(s32[1]{0:T(128)S(6)} %sub.9.refs_0_, bf16[2,256,4096]{2,1,0:T(8,128)(2,1)} %refs_1_.3, bf16[64,2048]{1,0:T(8,128)(2,1)S(1)} %get-tuple-element.66.refs_2_, bf16[2,2,528,64]{3,2,1,0:T(8,128)(2,1)S(1)} %get-tuple-element.67.refs_3_, ...), custom_call_target="tpu_custom_call", output_to_operand_aliasing={{}: (7, {})} | custom-call | flops 2415919104 | bytes 4194304 | tf_op jit(solution)/shard_map/prompt_half/pallas_call | solution.py:416
  59.2 0.0 collective-permute-done.5
  59.2 0.0 slice-done
  59.3 0.0 slice-done.1
  59.3 0.0 copy-done.7
  59.3 2.9 %branch_finish.1 = bf16[2,512,2048]{2,1,0:T(8,128)(2,1)} custom-call(s32[2]{0:T(128)S(1)} %copy-done.7, f32[2,512,2048]{2,1,0:T(8,128)S(1)} %bitcast.30, bf16[2,512,512]{2,1,0:T(8,128)(2,1)S(1)} %get-tuple-element.79.reach_ref, f32[16,2048]{1,0:T(8,128)S(1)} %fusion.2.start_ref), custom_call_target="tpu_custom_call" | custom-call | flops 268435456 | bytes 8388608 | tf_op jit(solution)/shard_map/branch_finish/pallas_call | solution.py:462
  (18 shorter events, 0.4 us)
Async XLA Ops:
  0.6 5.7 %copy-start.4 = (f32[2,64,256]{2,1,0:T(8,128)S(1)}, f32[2,64,256]{2,1,0:T(8,128)}, u32[]{:S(2)}) copy-start(f32[2,64,256]{2,1,0:T(8,128)} %ld_ref.2) | copy-start | bytes 393220
  0.6 5.7 %copy-start.6 = (bf16[2,2,16,256]{3,2,1,0:T(8,128)(2,1)S(1)}, bf16[2,2,16,256]{3,2,1,0:T(8,128)(2,1)}, u32[]{:S(2)}) copy-start(bf16[2,2,16,256]{3,2,1,0:T(8,128)(2,1)} %bc_ref.3) | copy-start | bytes 98308
  0.7 10.1 %copy-start.3 = (f32[2,32,512]{2,1,0:T(8,128)S(1)}, f32[2,32,512]{2,1,0:T(8,128)}, u32[]{:S(2)}) copy-start(f32[2,32,512]{2,1,0:T(8,128)} %ld_ref.4) | copy-start | bytes 393220
  0.7 10.1 %copy-start.5 = (bf16[2,2,16,512]{3,2,1,0:T(8,128)(2,1)S(1)}, bf16[2,2,16,512]{3,2,1,0:T(8,128)(2,1)}, u32[]{:S(2)}) copy-start(bf16[2,2,16,512]{3,2,1,0:T(8,128)(2,1)} %bc_ref.5) | copy-start | bytes 196612
  5.9 1.8 %collective-permute-start = (f32[34,2048]{1,0:T(8,128)S(1)}, f32[34,2048]{1,0:T(8,128)S(1)}, u32[]{:S(2)}, u32[]{:S(2)}) collective-permute-start(f32[34,2048]{1,0:T(8,128)S(1)} %pad_maximum_fusion), channel_id=1, source_target_pairs={{0,4},{4,0},{8,12},{12,8},{16,20},{20,16},{24,28},{28,24},{1,5},{5... | collective-permute-start | bytes 835592 | tf_op jit(solution)/shard_map/ppermute | solution.py:479
  7.7 3.1 %copy-start.8 = (f32[32,2048]{1,0:T(8,128)}, f32[32,2048]{1,0:T(8,128)S(1)}, u32[]{:S(2)}) copy-start(f32[32,2048]{1,0:T(8,128)S(1)} %slice.41) | copy-start | bytes 786436
  7.8 3.0 %copy-start.12 = (f32[2,16,2048]{2,1,0:T(8,128)}, f32[2,16,2048]{2,1,0:T(8,128)S(1)}, u32[]{:S(2)}) copy-start(f32[2,16,2048]{2,1,0:T(8,128)S(1)} %select_add_fusion.2) | copy-start | bytes 786436
  7.9 12.1 %collective-permute-start.1 = (f32[34,2048]{1,0:T(8,128)S(1)}, f32[34,2048]{1,0:T(8,128)}, u32[]{:S(2)}, u32[]{:S(2)}) collective-permute-start(f32[34,2048]{1,0:T(8,128)S(1)} %pad_maximum_fusion.1), channel_id=1, source_target_pairs={{0,8},{4,12},{8,0},{12,4},{16,24},{20,28},{24,16},{28,20},{1,9},{5... | collective-permute-start | bytes 835592 | tf_op jit(solution)/shard_map/ppermute | solution.py:479
  10.8 11.1 %copy-start.13 = (f32[2,16,2048]{2,1,0:T(8,128)S(1)}, f32[2,16,2048]{2,1,0:T(8,128)}, u32[]{:S(2)}) copy-start(f32[2,16,2048]{2,1,0:T(8,128)} %copy-done.12) | copy-start | bytes 786436
  16.7 3.3 %copy-start = (f32[2,512,2048]{2,1,0:T(8,128)}, f32[2,512,2048]{2,1,0:T(8,128)S(1)}, u32[]{:S(2)}) copy-start(f32[2,512,2048]{2,1,0:T(8,128)S(1)} %get-tuple-element.60.refs_0_) | copy-start | bytes 25165828
  20.9 1.0 %copy-start.10 = (f32[32,2048]{1,0:T(8,128)}, f32[32,2048]{1,0:T(8,128)S(1)}, u32[]{:S(2)}) copy-start(f32[32,2048]{1,0:T(8,128)S(1)} %slice.43) | copy-start | bytes 786436
  22.8 14.0 %collective-permute-start.2 = (f32[34,2048]{1,0:T(8,128)}, f32[34,2048]{1,0:T(8,128)}, u32[]{:S(2)}, u32[]{:S(2)}) collective-permute-start(f32[34,2048]{1,0:T(8,128)} %pad_maximum_fusion.2), channel_id=1, source_target_pairs={{0,16},{4,20},{8,24},{12,28},{16,0},{20,4},{24,8},{28,12},{1,17},{... | collective-permute-start | bytes 835592 | tf_op jit(solution)/shard_map/ppermute | solution.py:479
  24.3 3.4 %copy-start.1 = (f32[2,512,2048]{2,1,0:T(8,128)S(1)}, f32[2,512,2048]{2,1,0:T(8,128)}, u32[]{:S(2)}) copy-start(f32[2,512,2048]{2,1,0:T(8,128)} %copy-done) | copy-start | bytes 25165828
  27.7 11.0 %copy-start.9 = (f32[32,2048]{1,0:T(8,128)S(1)}, f32[32,2048]{1,0:T(8,128)}, u32[]{:S(2)}) copy-start(f32[32,2048]{1,0:T(8,128)} %copy-done.8) | copy-start | bytes 786436
  27.7 11.0 %copy-start.11 = (f32[32,2048]{1,0:T(8,128)S(1)}, f32[32,2048]{1,0:T(8,128)}, u32[]{:S(2)}) copy-start(f32[32,2048]{1,0:T(8,128)} %copy-done.10) | copy-start | bytes 786436
  33.5 3.3 %copy-start.2 = (f32[2,512,2048]{2,1,0:T(8,128)}, f32[2,512,2048]{2,1,0:T(8,128)S(1)}, u32[]{:S(2)}) copy-start(f32[2,512,2048]{2,1,0:T(8,128)S(1)} %get-tuple-element.78.own_ref) | copy-start | bytes 25165828
  39.6 10.4 %collective-permute-start.3 = (f32[2,16,2048]{2,1,0:T(8,128)}, f32[2,16,2048]{2,1,0:T(8,128)S(1)}, u32[]{:S(2)}, u32[]{:S(2)}) collective-permute-start(f32[2,16,2048]{2,1,0:T(8,128)} %get-tuple-element.65), channel_id=1, source_target_pairs={{0,2},{4,6},{9,11},{13,15},{18,16},{22,20},{27,25},{31,29}} | collective-permute-start | bytes 786440 | tf_op jit(solution)/shard_map/ppermute | solution.py:510
  44.1 6.9 %collective-permute-start.4 = (f32[2,16,2048]{2,1,0:T(8,128)}, f32[2,16,2048]{2,1,0:T(8,128)S(1)}, u32[]{:S(2)}, u32[]{:S(2)}) collective-permute-start(f32[2,16,2048]{2,1,0:T(8,128)} %get-tuple-element.82), channel_id=1, source_target_pairs={{0,4},{4,0},{8,12},{12,8},{16,20},{20,16},{24,28},{28,24},{1,5},{5... | collective-permute-start | bytes 786440 | tf_op jit(solution)/shard_map/ppermute | solution.py:479
  51.0 8.2 %collective-permute-start.5 = (f32[2,16,2048]{2,1,0:T(8,128)S(1)}, f32[2,16,2048]{2,1,0:T(8,128)S(1)}, u32[]{:S(2)}, u32[]{:S(2)}) collective-permute-start(f32[2,16,2048]{2,1,0:T(8,128)S(1)} %broadcast_select_fusion.1), channel_id=1, source_target_pairs={{0,1},{2,3},{4,5},{6,7},{9,8},{11,10},{13,12},{15,14},{18,19},{16,... | collective-permute-start | bytes 786440 | tf_op jit(solution)/shard_map/ppermute | solution.py:510
  53.2 6.1 %slice-start = ((s8[8388608]{0:T(1024)(128)(4,1)}), s8[4194304]{0:T(1024)(128)(4,1)S(1)}, s32[]{:S(2)}) async-start(s8[8388608]{0:T(1024)(128)(4,1)} %bitcast.29), calls=%async_computation | async-start | bytes 8388608
  53.2 6.1 %slice-start.1 = ((s8[8388608]{0:T(1024)(128)(4,1)}), s8[4194304]{0:T(1024)(128)(4,1)S(1)}, s32[]{:S(2)}) async-start(s8[8388608]{0:T(1024)(128)(4,1)} %bitcast.29), calls=%async_computation.1 | async-start | bytes 8388608
  53.2 6.1 %copy-start.7 = (s32[2]{0:T(128)S(1)}, s32[2]{0:T(128)}, u32[]{:S(2)}) copy-start(s32[2]{0:T(128)} %len_ref.1) | copy-start | bytes 28

commit v9 on v6

--- a/solution.py
+++ b/solution.py
@@ -509,15 +509,31 @@
 
 
 def spread_step(value, hop, ctx_size, pair_size):
-    owner = lax.axis_index("ctx") * pair_size // ctx_size
     known = [m for m in range(pair_size) if m & (2 * hop - 1) == 0]
     links = []
     for k in range(ctx_size):
         z = k * pair_size // ctx_size
         links += [(k * pair_size + (z ^ m), k * pair_size + (z ^ m ^ hop)) for m in known]
-    got = lax.ppermute(value, ("ctx", "pair"), links)
-    has = ((lax.axis_index("pair") ^ owner) & (2 * hop - 1)) == 0
-    return got, has
+    return lax.ppermute(value, ("ctx", "pair"), links)
+
+
+def halvings(size):
+    return [size >> k for k in range(1, size.bit_length())]
+
+
+def places(branch_prompt, prompts):
+    size, pair_size = lax.axis_size("ctx"), lax.axis_size("pair")
+    ctx, pair = lax.axis_index("ctx"), lax.axis_index("pair")
+    away = pair ^ lax.div(ctx * pair_size, size)
+    odd = ctx & 1
+    return {
+        "odd": odd == 1,
+        "half": jnp.reshape(odd, (1,)),
+        "other_half": jnp.reshape(1 - odd, (1,)),
+        "upper": {bit: (ctx & bit) != 0 for bit in halvings(size)[:-1]},
+        "has": {hop: (away & (2 * hop - 1)) == 0 for hop in halvings(pair_size)},
+        "chosen": [branch_prompt[0] == which for which in range(1, prompts)],
+    }
 
 
 def body(
@@ -533,8 +549,8 @@
     size, pair_size = lax.axis_size("ctx"), lax.axis_size("pair")
     prompts, branches = prompt_x.shape[0], branch_x.shape[0]
     assert size == 2 * pair_size and size & (size - 1) == 0 and branch_prompt.shape[0] == 1
-    mine = lax.axis_index("ctx")
-    odd = (mine & 1) == 1
+    place, prompt_logdec = lax.optimization_barrier((places(branch_prompt, prompts), prompt_logdec))
+    odd = place["odd"]
 
     def beside(exchange, value, work, *given):
         value, given = lax.optimization_barrier((value, given))
@@ -570,7 +586,7 @@
                 swap, pack(total, total_log),
                 lambda x, own: (*own, branch_own(x, branch_ready, which)), branch_x, own)
         other = unpack(got, prompts)
-        upper = (mine & bit) != 0
+        upper = place["upper"][bit]
         before = jnp.where(upper, jnp.exp(before_log) * other[0] + before, before)
         before_log = jnp.where(upper, before_log + other[1], before_log)
         total, total_log = join(*in_order(upper, (total, total_log), other))
@@ -581,26 +597,23 @@
     next_before = jnp.exp(first[1]) * before + first[0]
     keep = jnp.where(odd, next_before, before)
     others = swap_bit(jnp.where(odd, before, next_before), 1, size)
-    here = jnp.reshape(mine & 1, (1,))
-    sides = [(here, keep), (1 - here, others)]
+    sides = [(place["half"], keep), (place["other_half"], others)]
     prompt_y = ()
-    hop = pair_size // 2
-    while hop:
+    for hop in halvings(pair_size):
         step = functools.partial(spread_step, hop=hop, ctx_size=size, pair_size=pair_size)
         if sides:
             side, entering = sides.pop(0)
-            (got, has), prompt_y = beside(
+            got, prompt_y = beside(
                 step, total,
                 lambda entering, y: (prompt_half(side, prompt_x, prompt_ready, entering, y),), entering, prompt_y)
         else:
-            got, has = step(total)
-        total = jnp.where(has, total, got)
-        hop //= 2
+            got = step(total)
+        total = jnp.where(place["has"][hop], total, got)
     for side, entering in sides:
         prompt_y = (prompt_half(side, prompt_x, prompt_ready, entering, prompt_y),)
     start = total[0]
     for which in range(1, prompts):
-        start = jnp.where(branch_prompt[0] == which, total[which], start)
+        start = jnp.where(place["chosen"][which - 1], total[which], start)
     branch_y = finish(branch_len, reach, start, own)
     return prompt_y[0], branch_y
 

time: 60.9 us -> 52.6 us (0.86)
  local copies, waits for them, and re-layouts: 9.89 us -> 0.16 us
  waiting for transfers between devices: 2.61 us -> 6.74 us
  other arithmetic: 2.96 us -> 0.58 us
    unnamed x44 -> x16, local copies, waits for them, and re-layouts: 7.08 us -> 0.09 us
    ppermute x4, waiting for transfers between devices: 2.6 us -> 6.08 us  [swap_bit(): return lax.ppermute(value, 'ctx', [(k, k ^ bit) for k in range(size)])]
    slice x3, local copies, waits for them, and re-layouts: 1.95 us -> 0.05 us  [unpack(): packed[:rows].reshape(count, rows // count, lanes)]
    concatenate x3, other arithmetic: 1.52 us -> 0.07 us  [pack(): jnp.concatenate([states.reshape(-1, lanes), logs.reshape(-1, lanes)], axi...]
    exp x1, other arithmetic: 0.93 us -> 0.02 us  [body(): before = jnp.where(upper, jnp.exp(before_log) * other[0] + before, before)]
    slice x2, local copies, waits for them, and re-layouts: 0.85 us -> 0.01 us  [unpack(): packed[rows:].reshape(count, 1, lanes)]
    ppermute x2, waiting for transfers between devices: 0.01 us -> 0.65 us  [spread_step(): return lax.ppermute(value, ('ctx', 'pair'), links)]
  transfers between devices with their start and end apart: 6 -> 6, of which waited for: 2 -> 3; matrix products, arithmetic and copies ran while one was open for 0% -> 0% of each run, Pallas kernels for 40% -> 45%
where the time goes in v9:
time: 52.6 us; the launch traced here: 51.7 us
  Pallas kernels  31.3 us (60%)
  starting transfers between devices  11.1 us (21%)
  waiting for transfers between devices  6.74 us (13%)
  between operations  1.85 us (4%)
  other arithmetic  0.58 us (1%)
    pallas_call x2, Pallas kernels, prompt_half(): pl.pallas_call(functools.partial(prompt_kernel, skip=len(into)), in_specs...  11.6 us
    pallas_call x2, Pallas kernels, branch_own(): pl.pallas_call(functools.partial(branch_kernel, which=which), in_specs=[p...  9.99 us
    ppermute x4, waiting for transfers between devices, swap_bit(): return lax.ppermute(value, 'ctx', [(k, k ^ bit) for k in range(size)])  6.08 us
    ppermute x2, starting transfers between devices, spread_step(): return lax.ppermute(value, ('ctx', 'pair'), links)  6.04 us
    ppermute x4, starting transfers between devices, swap_bit(): return lax.ppermute(value, 'ctx', [(k, k ^ bit) for k in range(size)])  5.02 us
    pallas_call x1, Pallas kernels, local_ends(): pl.pallas_call(functools.partial(ends_kernel, width=width, lanes=lanes),...  4.9 us
    pallas_call x1, Pallas kernels, finish(): pl.pallas_call(functools.partial(finish_kernel, width=width), in_specs=[p...  2.89 us
    pallas_call x1, Pallas kernels, prepare_all(): pl.pallas_call(functools.partial(prepare_kernel, width=branch_channels //...  1.89 us
  transfers between devices with their start and end apart: 6, of which 3 were waited for; matrix products, arithmetic and copies ran while one was open for 0% of the time, Pallas kernels for 45%

profile of v9, /device:TPU:0, one launch (start us, length us, event | category | flops | bytes accessed | tf_op | source)
XLA Modules:
  0.0 51.7 jit_solution(9099827480255044308)
XLA Ops:
  0.6 0.0 copy-start
  0.6 0.0 copy-start.1
  0.7 0.0 copy-start.3
  0.7 0.0 copy-start.4
  1.4 4.9 %local_ends.1 = (f32[2,16,4096]{2,1,0:T(8,128)S(1)}, f32[2,8,4096]{2,1,0:T(8,128)S(1)}) custom-call(bf16[2,256,4096]{2,1,0:T(8,128)(2,1)} %refs_1_.3, f32[2,64,256]{2,1,0:T(8,128)} %pld_ref, bf16[2,2,16,256]{3,2,1,0:T(8,128)(2,1)} %pbc_ref.1), custom_call_target="tpu_custom_call" | custom-call | flops 268435456 | bytes 4194304 | tf_op jit(solution)/shard_map/local_ends/pallas_call | solution.py:124
  6.4 0.5 %collective-permute-start = (f32[34,2048]{1,0:T(8,128)S(1)}, f32[34,2048]{1,0:T(8,128)S(1)}, u32[]{:S(2)}, u32[]{:S(2)}) collective-permute-start(f32[34,2048]{1,0:T(8,128)S(1)} %pad_maximum_fusion), channel_id=1, source_target_pairs={{0,4},{4,0},{8,12},{12,8},{16,20},{20,16},{24,28},{28,24},{1,5},{5... | collective-permute-start | bytes 835592 | tf_op jit(solution)/shard_map/ppermute | solution.py:487
  6.9 0.0 copy-done
  6.9 0.0 copy-done.1
  6.9 0.0 copy-done.3
  6.9 0.0 copy-done.4
  7.0 1.9 %prepare.1 = (bf16[64,2048]{1,0:T(8,128)(2,1)S(1)}, bf16[2,2,528,64]{3,2,1,0:T(8,128)(2,1)S(1)}, bf16[2,384,256]{2,1,0:T(8,128)(2,1)S(1)}, bf16[2,256,128]{2,1,0...) custom-call(f32[2,64,256]{2,1,0:T(8,128)S(1)} %copy-done, ...), custom_call_target="tpu_custom_call" | custom-call | flops 100000000 | bytes 1000000 | tf_op jit(solution)/shard_map/prepare/pallas_call | solution.py:237
  8.9 0.0 collective-permute-done
  9.0 0.1 select_add_fusion.2
  9.1 2.6 %collective-permute-start.1 = (f32[34,2048]{1,0:T(8,128)S(1)}, f32[34,2048]{1,0:T(8,128)S(1)}, u32[]{:S(2)}, u32[]{:S(2)}) collective-permute-start(f32[34,2048]{1,0:T(8,128)S(1)} %pad_maximum_fusion.1), channel_id=1, source_target_pairs={{0,8},{4,12},{8,0},{12,4},{16,24},{20,28},{24,16},{28,20},{1,9},{5... | collective-permute-start | bytes 835592 | tf_op jit(solution)/shard_map/ppermute | solution.py:487
  11.7 5.0 %branch_own.2.refs_0_ = f32[512,2048]{1,0:T(8,128)S(1)} custom-call(bf16[2,512,2048]{2,1,0:T(8,128)(2,1)} %x_in.1, bf16[64,2048]{1,0:T(8,128)(2,1)S(1)} %get-tuple-element.84.refs_0_.refs_2_, bf16[4,528,64]{2,1,0:T(8,128)(2,1)S(1)} %get-tuple-element.73.refs_1_, bf16[4,384,256]{2,1,0:T(8,128)(2,1)S(1)} %get-tuple-element.74.refs_2_, ...), custom_call_target="tpu_custom_call" | custom-call | flops 2415919104 | bytes 4194304 | tf_op jit(solution)/shard_map/branch_own/pallas_call | solution.py:350
  16.7 3.3 %collective-permute-done.1 = f32[34,2048]{1,0:T(8,128)S(1)} collective-permute-done((f32[34,2048]{1,0:T(8,128)S(1)}, f32[34,2048]{1,0:T(8,128)S(1)}, u32[]{:S(2)}, u32[]{:S(2)}) %collective-permute-start.1) | collective-permute-done | bytes 278560 | tf_op jit(solution)/shard_map/ppermute | solution.py:487
  20.2 1.8 %collective-permute-start.2 = (f32[34,2048]{1,0:T(8,128)S(1)}, f32[34,2048]{1,0:T(8,128)S(1)}, u32[]{:S(2)}, u32[]{:S(2)}) collective-permute-start(f32[34,2048]{1,0:T(8,128)S(1)} %pad_maximum_fusion.2), channel_id=1, source_target_pairs={{0,16},{4,20},{8,24},{12,28},{16,0},{20,4},{24,8},{28,12},{1,17},{... | collective-permute-start | bytes 835592 | tf_op jit(solution)/shard_map/ppermute | solution.py:487
  22.1 5.0 %branch_own.3.refs_1_ = f32[512,2048]{1,0:T(8,128)S(1)} custom-call(bf16[2,512,2048]{2,1,0:T(8,128)(2,1)} %x_in.1, bf16[64,2048]{1,0:T(8,128)(2,1)S(1)} %get-tuple-element.84.refs_0_.refs_2_, bf16[4,528,64]{2,1,0:T(8,128)(2,1)S(1)} %get-tuple-element.73.refs_1_, bf16[4,384,256]{2,1,0:T(8,128)(2,1)S(1)} %get-tuple-element.74.refs_2_, ...), custom_call_target="tpu_custom_call" | custom-call | flops 2415919104 | bytes 4194304 | tf_op jit(solution)/shard_map/branch_own/pallas_call | solution.py:350
  27.1 2.7 %collective-permute-done.2 = f32[34,2048]{1,0:T(8,128)S(1)} collective-permute-done((f32[34,2048]{1,0:T(8,128)S(1)}, f32[34,2048]{1,0:T(8,128)S(1)}, u32[]{:S(2)}, u32[]{:S(2)}) %collective-permute-start.2) | collective-permute-done | bytes 278560 | tf_op jit(solution)/shard_map/ppermute | solution.py:487
  29.9 0.1 fusion
  30.0 4.7 %collective-permute-start.3 = (f32[2,16,2048]{2,1,0:T(8,128)S(1)}, f32[2,16,2048]{2,1,0:T(8,128)S(1)}, u32[]{:S(2)}, u32[]{:S(2)}) collective-permute-start(f32[2,16,2048]{2,1,0:T(8,128)S(1)} %get-tuple-element.82), channel_id=1, source_target_pairs={{0,2},{4,6},{9,11},{13,15},{18,16},{22,20},{27,25},{31,29}} | collective-permute-start | bytes 786440 | tf_op jit(solution)/shard_map/ppermute | solution.py:517
  34.8 0.1 collective-permute-start.4
  34.9 5.8 %prompt_half.2.refs_7_ = bf16[2,256,4096]{2,1,0:T(8,128)(2,1)} custom-call(s32[1]{0:T(128)} %bitcast.1.refs_0_, bf16[2,256,4096]{2,1,0:T(8,128)(2,1)} %refs_1_.3, bf16[64,2048]{1,0:T(8,128)(2,1)S(1)} %get-tuple-element.84.refs_0_.refs_2_, bf16[2,2,528,64]{3,2,1,0:T(8,128)(2,1)S(1)} %get-tuple-element.85.refs_3_, ...), custom_call_target="tpu_custom_call" | custom-call | flops 2415919104 | bytes 4194304 | tf_op jit(solution)/shard_map/prompt_half/pallas_call | solution.py:423
  40.7 0.0 collective-permute-done.3
  40.7 0.0 copy-start.2
  40.7 0.0 collective-permute-done.4.refs_6_
  40.8 1.3 %collective-permute-start.5 = (f32[2,16,2048]{2,1,0:T(8,128)S(1)}, f32[2,16,2048]{2,1,0:T(8,128)S(1)}, u32[]{:S(2)}, u32[]{:S(2)}) collective-permute-start(f32[2,16,2048]{2,1,0:T(8,128)S(1)} %broadcast_select_fusion.2), channel_id=1, source_target_pairs={{0,1},{2,3},{4,5},{6,7},{9,8},{11,10},{13,12},{15,14},{18,19},{16,... | collective-permute-start | bytes 786440 | tf_op jit(solution)/shard_map/ppermute | solution.py:517
  42.1 5.8 %prompt_half.3 = bf16[2,256,4096]{2,1,0:T(8,128)(2,1)} custom-call(s32[1]{0:T(128)} %bitcast.2.refs_0_, bf16[2,256,4096]{2,1,0:T(8,128)(2,1)} %refs_1_.3, bf16[64,2048]{1,0:T(8,128)(2,1)S(1)} %get-tuple-element.84.refs_0_.refs_2_, bf16[2,2,528,64]{3,2,1,0:T(8,128)(2,1)S(1)} %get-tuple-element.85.refs_3_, ...), custom_call_target="tpu_custom_call", output_to_operand_aliasing={{}: (7, {})} | custom-call | flops 2415919104 | bytes 4194304 | tf_op jit(solution)/shard_map/prompt_half/pallas_call | solution.py:423
  47.9 0.7 %collective-permute-done.5 = f32[2,16,2048]{2,1,0:T(8,128)S(1)} collective-permute-done((f32[2,16,2048]{2,1,0:T(8,128)S(1)}, f32[2,16,2048]{2,1,0:T(8,128)S(1)}, u32[]{:S(2)}, u32[]{:S(2)}) %collective-permute-start.5) | collective-permute-done | bytes 262176 | tf_op jit(solution)/shard_map/ppermute | solution.py:517
  48.6 0.0 copy-done.2
  48.6 2.9 %branch_finish.1 = bf16[2,512,2048]{2,1,0:T(8,128)(2,1)} custom-call(s32[2]{0:T(128)S(1)} %copy-done.2, bf16[2,512,512]{2,1,0:T(8,128)(2,1)S(1)} %get-tuple-element.96.reach_ref, f32[16,2048]{1,0:T(8,128)S(1)} %fusion.2.start_ref, f32[512,2048]{1,0:T(8,128)S(1)} %branch_own.2.refs_0_, f32[512,2048]{1,0:T(8,128)S(1)} %branch_own.3.refs_1_), custom_call_target="tpu_custom_call" | custom-call | flops 268435456 | bytes 8388608 | tf_op jit(solution)/shard_map/branch_finish/pallas_call | solution.py:470
  (24 shorter events, 0.5 us)
Async XLA Ops:
  0.6 6.3 %copy-start = (f32[2,64,256]{2,1,0:T(8,128)S(1)}, f32[2,64,256]{2,1,0:T(8,128)}, u32[]{:S(2)}) copy-start(f32[2,64,256]{2,1,0:T(8,128)} %pld_ref) | copy-start | bytes 393220
  0.6 6.3 %copy-start.1 = (bf16[2,2,16,256]{3,2,1,0:T(8,128)(2,1)S(1)}, bf16[2,2,16,256]{3,2,1,0:T(8,128)(2,1)}, u32[]{:S(2)}) copy-start(bf16[2,2,16,256]{3,2,1,0:T(8,128)(2,1)} %pbc_ref.1) | copy-start | bytes 98308
  0.7 6.3 %copy-start.3 = (f32[2,32,512]{2,1,0:T(8,128)S(1)}, f32[2,32,512]{2,1,0:T(8,128)}, u32[]{:S(2)}) copy-start(f32[2,32,512]{2,1,0:T(8,128)} %bld_ref) | copy-start | bytes 393220
  0.7 6.3 %copy-start.4 = (bf16[2,2,16,512]{3,2,1,0:T(8,128)(2,1)S(1)}, bf16[2,2,16,512]{3,2,1,0:T(8,128)(2,1)}, u32[]{:S(2)}) copy-start(bf16[2,2,16,512]{3,2,1,0:T(8,128)(2,1)} %bbc_ref.1) | copy-start | bytes 196612
  6.4 2.4 %collective-permute-start = (f32[34,2048]{1,0:T(8,128)S(1)}, f32[34,2048]{1,0:T(8,128)S(1)}, u32[]{:S(2)}, u32[]{:S(2)}) collective-permute-start(f32[34,2048]{1,0:T(8,128)S(1)} %pad_maximum_fusion), channel_id=1, source_target_pairs={{0,4},{4,0},{8,12},{12,8},{16,20},{20,16},{24,28},{28,24},{1,5},{5... | collective-permute-start | bytes 835592 | tf_op jit(solution)/shard_map/ppermute | solution.py:487
  9.1 10.9 %collective-permute-start.1 = (f32[34,2048]{1,0:T(8,128)S(1)}, f32[34,2048]{1,0:T(8,128)S(1)}, u32[]{:S(2)}, u32[]{:S(2)}) collective-permute-start(f32[34,2048]{1,0:T(8,128)S(1)} %pad_maximum_fusion.1), channel_id=1, source_target_pairs={{0,8},{4,12},{8,0},{12,4},{16,24},{20,28},{24,16},{28,20},{1,9},{5... | collective-permute-start | bytes 835592 | tf_op jit(solution)/shard_map/ppermute | solution.py:487
  20.2 9.6 %collective-permute-start.2 = (f32[34,2048]{1,0:T(8,128)S(1)}, f32[34,2048]{1,0:T(8,128)S(1)}, u32[]{:S(2)}, u32[]{:S(2)}) collective-permute-start(f32[34,2048]{1,0:T(8,128)S(1)} %pad_maximum_fusion.2), channel_id=1, source_target_pairs={{0,16},{4,20},{8,24},{12,28},{16,0},{20,4},{24,8},{28,12},{1,17},{... | collective-permute-start | bytes 835592 | tf_op jit(solution)/shard_map/ppermute | solution.py:487
  30.0 10.6 %collective-permute-start.3 = (f32[2,16,2048]{2,1,0:T(8,128)S(1)}, f32[2,16,2048]{2,1,0:T(8,128)S(1)}, u32[]{:S(2)}, u32[]{:S(2)}) collective-permute-start(f32[2,16,2048]{2,1,0:T(8,128)S(1)} %get-tuple-element.82), channel_id=1, source_target_pairs={{0,2},{4,6},{9,11},{13,15},{18,16},{22,20},{27,25},{31,29}} | collective-permute-start | bytes 786440 | tf_op jit(solution)/shard_map/ppermute | solution.py:517
  34.8 6.0 %collective-permute-start.4 = (f32[2,16,2048]{2,1,0:T(8,128)S(1)}, f32[2,16,2048]{2,1,0:T(8,128)S(1)}, u32[]{:S(2)}, u32[]{:S(2)}) collective-permute-start(f32[2,16,2048]{2,1,0:T(8,128)S(1)} %get-tuple-element.102), channel_id=1, source_target_pairs={{0,4},{4,0},{8,12},{12,8},{16,20},{20,16},{24,28},{28,24},{1,5},{5... | collective-permute-start | bytes 786440 | tf_op jit(solution)/shard_map/ppermute | solution.py:487
  40.7 7.9 %copy-start.2 = (s32[2]{0:T(128)S(1)}, s32[2]{0:T(128)}, u32[]{:S(2)}) copy-start(s32[2]{0:T(128)} %len_ref.1) | copy-start | bytes 28
  40.8 7.8 %collective-permute-start.5 = (f32[2,16,2048]{2,1,0:T(8,128)S(1)}, f32[2,16,2048]{2,1,0:T(8,128)S(1)}, u32[]{:S(2)}, u32[]{:S(2)}) collective-permute-start(f32[2,16,2048]{2,1,0:T(8,128)S(1)} %broadcast_select_fusion.2), channel_id=1, source_target_pairs={{0,1},{2,3},{4,5},{6,7},{9,8},{11,10},{13,12},{15,14},{18,19},{16,... | collective-permute-start | bytes 786440 | tf_op jit(solution)/shard_map/ppermute | solution.py:517

commit v10 on v9

--- a/solution.py
+++ b/solution.py
@@ -124,13 +124,13 @@
     return pl.pallas_call(
         functools.partial(ends_kernel, width=width, lanes=lanes),
         in_specs=[pl.BlockSpec(memory_space=pltpu.HBM)] * 3,
-        out_specs=[whole, whole],
+        out_specs=[whole, whole, whole],
         out_shape=[
             jax.ShapeDtypeStruct((count, state, channels), F32),
             jax.ShapeDtypeStruct((count, 8, channels), F32),
+            jax.ShapeDtypeStruct(x.shape, BF16),
         ],
         scratch_shapes=[
-            pltpu.VMEM(x.shape, BF16),
             pltpu.VMEM(logdec.shape, F32),
             pltpu.VMEM(bc.shape[1:], BF16),
             pltpu.VMEM((count, heads * state, positions), BF16),
@@ -180,26 +180,32 @@
     return [(i, pl.ds(b * BLOCK, BLOCK)) for i in range(count) for b in range(positions // BLOCK)]
 
 
-def prepare_kernel(
-    pld_ref, pbc_ref, bld_ref, bbc_ref,
-    hot_ref, pw_ref, plv_ref, plc_ref, bw_ref, blv_ref, blc_ref, reach_ref, *, width
-):
-    state = pbc_ref.shape[2]
-
-    def collect(ld_ref, bc_ref):
-        cuts = cuts_of(ld_ref)
-        logs = jnp.concatenate([ld_ref[i, :, cut] for i, cut in cuts], axis=0)
-        return cuts, logs, [(bc_ref[0, i, :, cut], bc_ref[1, i, :, cut]) for i, cut in cuts]
-
-    cuts, logs, parts = collect(bld_ref, bbc_ref)
-    heads = bld_ref.shape[1]
-    blocks = len(cuts) // bld_ref.shape[0]
-    for k, w in enumerate(prepare(parts, logs, blv_ref, blc_ref, state, heads)):
-        bw_ref[k] = w
+def prepare_hot(hot_ref, heads, width):
     row_head = remainder(iota((2 * heads, 1), 0), heads)
     for g in range(hot_ref.shape[1] // 256):
         lane_head = quotient(iota((1, 256), 1), width) + g * (256 // width)
         hot_ref[:, pl.ds(g * 256, 256)] = jnp.where(row_head == lane_head, 1.0, 0.0).astype(BF16)
+
+
+def blocks_of(ld_ref, bc_ref):
+    cuts = cuts_of(ld_ref)
+    logs = jnp.concatenate([ld_ref[i, :, cut] for i, cut in cuts], axis=0)
+    return cuts, logs, [(bc_ref[0, i, :, cut], bc_ref[1, i, :, cut]) for i, cut in cuts]
+
+
+def prompt_prepare_kernel(ld_ref, bc_ref, w_ref, lv_ref, lc_ref):
+    _, logs, parts = blocks_of(ld_ref, bc_ref)
+    for k, w in enumerate(prepare(parts, logs, lv_ref, lc_ref, bc_ref.shape[2], ld_ref.shape[1] // 2)):
+        w_ref[k // 2, k % 2] = w
+
+
+def branch_prepare_kernel(ld_ref, bc_ref, hot_ref, w_ref, lv_ref, lc_ref, reach_ref, *, width):
+    heads, state = ld_ref.shape[1], bc_ref.shape[2]
+    blocks = ld_ref.shape[2] // BLOCK
+    cuts, logs, parts = blocks_of(ld_ref, bc_ref)
+    for k, w in enumerate(prepare(parts, logs, lv_ref, lc_ref, state, heads)):
+        w_ref[k] = w
+    prepare_hot(hot_ref, heads, width)
     upto = jnp.where(iota((BLOCK, 1), 0) <= iota((1, BLOCK), 1), 1.0, 0.0)
     runs = exact_dot(logs, upto)
     for k, (i, cut) in enumerate(cuts):
@@ -210,40 +216,41 @@
         reach = parts[k][1].astype(F32)[None, :, :] * jnp.exp(run)[:, None, :]
         reach_ref[i, cut, :] = reach.reshape(heads * state, BLOCK).T.astype(BF16)
 
-    cuts, logs, parts = collect(pld_ref, pbc_ref)
-    heads = pld_ref.shape[1] // 2
-    for k, w in enumerate(prepare(parts, logs, plv_ref, plc_ref, state, heads)):
-        pw_ref[k // 2, k % 2] = w
-
-
-def prepare_all(prompt_logdec, prompt_bc, branch_logdec, branch_bc, branch_channels):
-    state = prompt_bc.shape[2]
-    rows = BLOCK // CHUNK * state
-    prompt_cuts = prompt_logdec.shape[0] * (prompt_logdec.shape[2] // BLOCK)
-    branches, heads, positions = branch_logdec.shape
-    branch_cuts = branches * (positions // BLOCK)
-    half = prompt_logdec.shape[1] // 2
-    shapes = [
-        ((2 * heads, branch_channels), BF16),
-        ((prompt_cuts, 2, 2 * BLOCK + 16, 2 * half), BF16),
-        ((prompt_cuts, rows + BLOCK, BLOCK), BF16),
-        ((prompt_cuts, BLOCK, rows), BF16),
-        ((branch_cuts, 2 * BLOCK + 16, 2 * heads), BF16),
-        ((branch_cuts, rows + BLOCK, BLOCK), BF16),
-        ((branch_cuts, BLOCK, rows), BF16),
-        ((branches, positions, heads * state), BF16),
-    ]
+
+def prepare_call(kernel, shapes, name, logdec, bc):
     whole = pl.BlockSpec(memory_space=pltpu.VMEM)
-    out = pl.pallas_call(
-        functools.partial(prepare_kernel, width=branch_channels // heads),
-        in_specs=[whole] * 4,
-        out_specs=[pl.BlockSpec(shape, lambda rank=len(shape): (0,) * rank) for shape, _ in shapes],
-        out_shape=[jax.ShapeDtypeStruct(*shape) for shape in shapes],
+    return pl.pallas_call(
+        kernel,
+        in_specs=[whole] * 2,
+        out_specs=[whole] * len(shapes),
+        out_shape=[jax.ShapeDtypeStruct(shape, BF16) for shape in shapes],
         compiler_params=pltpu.CompilerParams(vmem_limit_bytes=VMEM_LIMIT),
         cost_estimate=pl.CostEstimate(flops=10**8, bytes_accessed=10**6, transcendentals=0),
-        name="prepare",
-    )(prompt_logdec, prompt_bc, branch_logdec, branch_bc)
-    return out[:4], (out[0], *out[4:7]), out[7]
+        name=name,
+    )(logdec, bc)
+
+
+def prepare_prompts(logdec, bc):
+    count, heads, positions = logdec.shape
+    cuts, rows = count * (positions // BLOCK), BLOCK // CHUNK * bc.shape[2]
+    shapes = [(cuts, 2, 2 * BLOCK + 16, heads), (cuts, rows + BLOCK, BLOCK), (cuts, BLOCK, rows)]
+    return prepare_call(prompt_prepare_kernel, shapes, "prompt_prepare", logdec, bc)
+
+
+def prepare_branches(logdec, bc, channels):
+    count, heads, positions = logdec.shape
+    state = bc.shape[2]
+    cuts, rows = count * (positions // BLOCK), BLOCK // CHUNK * state
+    shapes = [
+        (2 * heads, channels),
+        (cuts, 2 * BLOCK + 16, 2 * heads),
+        (cuts, rows + BLOCK, BLOCK),
+        (cuts, BLOCK, rows),
+        (count, positions, heads * state),
+    ]
+    kernel = functools.partial(branch_prepare_kernel, width=channels // heads)
+    out = prepare_call(kernel, shapes, "branch_prepare", logdec, bc)
+    return out[:4], out[4]
 
 
 def run_tiles(jobs):
@@ -365,34 +372,18 @@
 
 
 def prompt_kernel(*refs, skip):
-    half_ref, x_in, *ready, start_ref = refs[:7]
-    y_out, x_ref, in_sems, out_sems = refs[7 + skip:]
-    count, positions, channels = x_ref.shape
+    half_ref, x_ref, *ready, start_ref = refs[:7]
+    y_out, y_ref, sems = refs[7 + skip:]
+    count, positions, channels = y_ref.shape
     blocks = positions // BLOCK
-    lanes = channels // in_sems.shape[2]
     half = half_ref[0]
-    came, left = Copies(in_sems), Copies(out_sems)
+    left = Copies(sems)
     entered = {}
 
-    def spots(i, b, j):
-        there = pl.ds(pl.multiple_of(half * channels + j * lanes, lanes), lanes)
+    def job(i, b, g):
         rows = pl.ds(b * BLOCK, BLOCK)
-        return (i, rows, there), (i, rows, pl.ds(j * lanes, lanes))
-
-    for i in range(count):
-        for b in range(blocks):
-            for j in range(channels // lanes):
-                there, here = spots(i, b, j)
-                came.start((i, b, j), x_in.at[there], x_ref.at[here])
-
-    def job(i, b, g):
-        here = (i, pl.ds(b * BLOCK, BLOCK), pl.ds(g * 256, 256))
-        j = g * 256 // lanes
-
-        def x_of():
-            if g * 256 % lanes == 0:
-                came.wait((i, b, j))
-            return x_ref[here]
+        here = (i, rows, pl.ds(g * 256, 256))
+        there = (i, rows, pl.ds(pl.multiple_of(half * channels + g * 256, 256), 256))
 
         def leave(carry):
             entered[i, g] = carry
@@ -401,13 +392,11 @@
             return entered[i, g] if b else start_ref[i, :, pl.ds(g * 256, 256)]
 
         def write(out):
-            x_ref[here] = out.astype(BF16)
-            if (g + 1) * 256 % lanes == 0:
-                there, staged = spots(i, b, j)
-                left.start((i, b, j), x_ref.at[staged], y_out.at[there])
+            y_ref[here] = out.astype(BF16)
+            left.start((i, b, g), y_ref.at[here], y_out.at[there])
 
         at = i * blocks + b
-        return tile_job(ready, ((at, half), at), g, x_of, entering_of, leave, write)
+        return tile_job(ready, ((at, half), at), g, lambda: x_ref[there], entering_of, leave, write)
 
     run_tiles([job(i, b, g) for i in range(count) for b in range(blocks) for g in range(channels // 256)])
     left.wait_all()
@@ -418,37 +407,38 @@
     part = channels // 2
     whole = pl.BlockSpec(memory_space=pltpu.VMEM)
     hbm = pl.BlockSpec(memory_space=pltpu.HBM)
-    parts = (count, positions // BLOCK, part // min(512, part))
     work = count * positions * part
     return pl.pallas_call(
         functools.partial(prompt_kernel, skip=len(into)),
-        in_specs=[pl.BlockSpec(memory_space=pltpu.SMEM), hbm] + [whole] * 5 + [hbm] * len(into),
+        in_specs=[pl.BlockSpec(memory_space=pltpu.SMEM)] + [whole] * 6 + [hbm] * len(into),
         out_specs=hbm,
         out_shape=jax.ShapeDtypeStruct(x.shape, BF16),
         scratch_shapes=[
             pltpu.VMEM((count, positions, part), BF16),
-            pltpu.SemaphoreType.DMA(parts),
-            pltpu.SemaphoreType.DMA(parts),
+            pltpu.SemaphoreType.DMA((count, positions // BLOCK, part // 256)),
         ],
         input_output_aliases={7 + i: i for i in range(len(into))},
         compiler_params=pltpu.CompilerParams(vmem_limit_bytes=VMEM_LIMIT),
         cost_estimate=pl.CostEstimate(
             flops=2 * 1152 * work, bytes_accessed=4 * work, transcendentals=0),
         name="prompt_half",
-    )(half, in_hbm(x), *ready, start, *into)
-
-
-def finish_kernel(len_ref, reach_ref, start_ref, *refs, width):
+    )(half, x, *ready, start, *into)
+
+
+def finish_kernel(len_ref, prompt_ref, reach_ref, total_ref, *refs, width):
     own_refs, (y_out, y_ref, sems) = refs[:-3], refs[-3:]
     count, positions, channels = y_ref.shape
-    state = start_ref.shape[0]
+    prompts, state, _ = total_ref.shape
     group = 128 // state
     span = group * width
     left = Copies(sems)
     own_head = quotient(iota((128, 1), 0), state) == quotient(iota((1, span), 1), width)
     starts = []
     for g in range(channels // span):
-        start = jnp.concatenate([start_ref[:, pl.ds(g * span, span)]] * group, axis=0)
+        start = total_ref[0, :, pl.ds(g * span, span)]
+        for which in range(1, prompts):
+            start = jnp.where(prompt_ref[0] == which, total_ref[which, :, pl.ds(g * span, span)], start)
+        start = jnp.concatenate([start] * group, axis=0)
         starts.append(jnp.where(own_head, start, 0.0).astype(BF16))
     for i in range(count):
         for g in range(channels // span):
@@ -462,14 +452,14 @@
     left.wait_all()
 
 
-def finish(lengths, reach, start, own):
+def finish(lengths, prompt, reach, total, own):
     count, (positions, channels) = len(own), own[0].shape
-    state = start.shape[0]
+    state = total.shape[1]
     width = channels * state // reach.shape[2]
     whole = pl.BlockSpec(memory_space=pltpu.VMEM)
     return pl.pallas_call(
         functools.partial(finish_kernel, width=width),
-        in_specs=[pl.BlockSpec(memory_space=pltpu.SMEM)] + [whole] * (2 + count),
+        in_specs=[pl.BlockSpec(memory_space=pltpu.SMEM)] * 2 + [whole] * (2 + count),
         out_specs=pl.BlockSpec(memory_space=pltpu.HBM),
         out_shape=jax.ShapeDtypeStruct((count, positions, channels), BF16),
         scratch_shapes=[
@@ -480,7 +470,7 @@
         cost_estimate=pl.CostEstimate(
             flops=2**28, bytes_accessed=2**23, transcendentals=0),
         name="branch_finish",
-    )(lengths, reach, start, *own)
+    )(lengths, prompt, reach, total, *own)
 
 
 def swap_bit(value, bit, size):
@@ -488,14 +478,14 @@
 
 
 def pack(states, logs):
-    lanes = states.shape[-1]
-    return jnp.concatenate([states.reshape(-1, lanes), logs.reshape(-1, lanes)], axis=0)
+    states = states.reshape(-1, states.shape[-1])
+    return jnp.concatenate([states, logs.reshape(states.shape[0], -1)], axis=1)
 
 
 def unpack(packed, count):
-    lanes = packed.shape[-1]
-    rows = packed.shape[0] - count
-    return packed[:rows].reshape(count, rows // count, lanes), packed[rows:].reshape(count, 1, lanes)
+    rows = packed.shape[0] // count
+    lanes = packed.shape[1] * rows // (rows + 1)
+    return packed[:, :lanes].reshape(count, rows, lanes), packed[:, lanes:].reshape(count, 1, lanes)
 
 
 def in_order(upper, mine, other):
@@ -521,7 +511,7 @@
     return [size >> k for k in range(1, size.bit_length())]
 
 
-def places(branch_prompt, prompts):
+def places():
     size, pair_size = lax.axis_size("ctx"), lax.axis_size("pair")
     ctx, pair = lax.axis_index("ctx"), lax.axis_index("pair")
     away = pair ^ lax.div(ctx * pair_size, size)
@@ -532,7 +522,6 @@
         "other_half": jnp.reshape(1 - odd, (1,)),
         "upper": {bit: (ctx & bit) != 0 for bit in halvings(size)[:-1]},
         "has": {hop: (away & (2 * hop - 1)) == 0 for hop in halvings(pair_size)},
-        "chosen": [branch_prompt[0] == which for which in range(1, prompts)],
     }
 
 
@@ -549,7 +538,7 @@
     size, pair_size = lax.axis_size("ctx"), lax.axis_size("pair")
     prompts, branches = prompt_x.shape[0], branch_x.shape[0]
     assert size == 2 * pair_size and size & (size - 1) == 0 and branch_prompt.shape[0] == 1
-    place, prompt_logdec = lax.optimization_barrier((places(branch_prompt, prompts), prompt_logdec))
+    place, prompt_logdec = lax.optimization_barrier((places(), prompt_logdec))
     odd = place["odd"]
 
     def beside(exchange, value, work, *given):
@@ -557,15 +546,15 @@
         got = exchange(value)
         return lax.optimization_barrier((got, work(*given)))
 
-    end, log = local_ends(prompt_x, prompt_logdec, prompt_bc)
+    end, log, held = local_ends(prompt_x, prompt_logdec, prompt_bc)
     half = end.shape[2] // 2
     low, high = (end[:, :, :half], log[:, :1, :half]), (end[:, :, half:], log[:, :1, half:])
     keep = [jnp.where(odd, h, l) for l, h in zip(low, high)]
     send = [jnp.where(odd, l, h) for l, h in zip(low, high)]
-    got, (prompt_ready, branch_ready, reach) = beside(
+    got, (ready, reach) = beside(
         lambda v: swap_bit(v, 1, size),
         pack(*send),
-        lambda ld: prepare_all(prompt_logdec, prompt_bc, ld, branch_bc, branch_x.shape[2]),
+        lambda logdec: prepare_branches(logdec, branch_bc, branch_x.shape[2]),
         branch_logdec,
     )
     got = unpack(got, prompts)
@@ -573,26 +562,32 @@
     total, total_log = join(first, second)
     before, before_log = jnp.zeros_like(total), jnp.zeros_like(total_log)
 
-    own = ()
-    works = iter(range(branches))
+    def part(which):
+        def work(x, logdec):
+            own = branch_own(x, ready, which)
+            return own, prepare_prompts(logdec, prompt_bc) if which == branches - 1 else None
+
+        return work
+
+    done = []
     bit = 2
     while bit < size:
-        which = next(works, None)
         swap = functools.partial(swap_bit, bit=bit, size=size)
-        if which is None:
+        if len(done) < branches:
+            got, out = beside(swap, pack(total, total_log), part(len(done)), branch_x, prompt_logdec)
+            done.append(out)
+        else:
             got = swap(pack(total, total_log))
-        else:
-            got, own = beside(
-                swap, pack(total, total_log),
-                lambda x, own: (*own, branch_own(x, branch_ready, which)), branch_x, own)
         other = unpack(got, prompts)
         upper = place["upper"][bit]
         before = jnp.where(upper, jnp.exp(before_log) * other[0] + before, before)
         before_log = jnp.where(upper, before_log + other[1], before_log)
         total, total_log = join(*in_order(upper, (total, total_log), other))
         bit *= 2
-    for which in works:
-        own = (*own, branch_own(branch_x, branch_ready, which))
+    while len(done) < branches:
+        done.append(part(len(done))(branch_x, prompt_logdec))
+    own = [out[0] for out in done]
+    prompt_ready = (ready[0], *done[-1][1])
 
     next_before = jnp.exp(first[1]) * before + first[0]
     keep = jnp.where(odd, next_before, before)
@@ -605,16 +600,13 @@
             side, entering = sides.pop(0)
             got, prompt_y = beside(
                 step, total,
-                lambda entering, y: (prompt_half(side, prompt_x, prompt_ready, entering, y),), entering, prompt_y)
+                lambda entering, y: (prompt_half(side, held, prompt_ready, entering, y),), entering, prompt_y)
         else:
             got = step(total)
         total = jnp.where(place["has"][hop], total, got)
     for side, entering in sides:
-        prompt_y = (prompt_half(side, prompt_x, prompt_ready, entering, prompt_y),)
-    start = total[0]
-    for which in range(1, prompts):
-        start = jnp.where(place["chosen"][which - 1], total[which], start)
-    branch_y = finish(branch_len, reach, start, own)
+        prompt_y = (prompt_half(side, held, prompt_ready, entering, prompt_y),)
+    branch_y = finish(branch_len, branch_prompt, reach, total, own)
     return prompt_y[0], branch_y
 
 

time: 52.6 us -> 54.8 us (1.042)
  local copies, waits for them, and re-layouts: 0.16 us -> 9.22 us
  waiting for transfers between devices: 6.74 us -> 2.38 us
  Pallas kernels: 31.3 us -> 27.3 us
  other arithmetic: 0.58 us -> 1.9 us
    unnamed x16 -> x41, local copies, waits for them, and re-layouts: 0.09 us -> 6.16 us
    ppermute x4, waiting for transfers between devices: 6.08 us -> 0.16 us  [swap_bit(): return lax.ppermute(value, 'ctx', [(k, k ^ bit) for k in range(size)])]
    pallas_call x2, Pallas kernels: 11.6 us -> 7.18 us  [prompt_half(): pl.pallas_call(functools.partial(prompt_kernel, skip=len(into)), in_specs...]
    slice x5, local copies, waits for them, and re-layouts: 0.07 us -> 1.73 us  [the longest x3 1 us: unpack(): packed[:, :lanes].reshape(count, rows, lanes)]
    ppermute x2, waiting for transfers between devices: 0.65 us -> 2.22 us  [spread_step(): return lax.ppermute(value, ('ctx', 'pair'), links)]
    exp x0 -> x1, local copies, waits for them, and re-layouts: none -> 1.34 us  [body(): before = jnp.where(upper, jnp.exp(before_log) * other[0] + before, before)]
    concatenate x3, other arithmetic: 0.07 us -> 0.77 us  [pack(): return jnp.concatenate([states, logs.reshape(states.shape[0], -1)], axis=1)]
    exp x1, other arithmetic: 0.02 us -> 0.66 us  [body(): before = jnp.where(upper, jnp.exp(before_log) * other[0] + before, before)]
  transfers between devices with their start and end apart: 6 -> 6, of which waited for: 3 -> 3; matrix products, arithmetic and copies ran while one was open for 0% -> 3% of each run, Pallas kernels for 45% -> 36%
where the time goes in v10:
time: 54.8 us; the launch traced here: 53.8 us
  Pallas kernels  27.3 us (50%)
  starting transfers between devices  11.1 us (20%)
  local copies, waits for them, and re-layouts  9.22 us (17%)
  waiting for transfers between devices  2.38 us (4%)
  other arithmetic  1.9 us (3%)
  between operations  1.9 us (3%)
    pallas_call x2, Pallas kernels, branch_own(): pl.pallas_call(functools.partial(branch_kernel, which=which), in_specs=[p...  10.1 us
    pallas_call x2, Pallas kernels, prompt_half(): pl.pallas_call(functools.partial(prompt_kernel, skip=len(into)), in_specs...  7.18 us
    unnamed x41, local copies, waits for them, and re-layouts  6.16 us
    ppermute x2, starting transfers between devices, spread_step(): return lax.ppermute(value, ('ctx', 'pair'), links)  5.99 us
    ppermute x4, starting transfers between devices, swap_bit(): return lax.ppermute(value, 'ctx', [(k, k ^ bit) for k in range(size)])  5.12 us
    pallas_call x1, Pallas kernels, local_ends(): pl.pallas_call(functools.partial(ends_kernel, width=width, lanes=lanes),...  4.92 us
    pallas_call x1, Pallas kernels, finish(): pl.pallas_call(functools.partial(finish_kernel, width=width), in_specs=[p...  2.89 us
    ppermute x2, waiting for transfers between devices, spread_step(): return lax.ppermute(value, ('ctx', 'pair'), links)  2.22 us
  transfers between devices with their start and end apart: 6, of which 3 were waited for; matrix products, arithmetic and copies ran while one was open for 3% of the time, Pallas kernels for 36%

profile of v10, /device:TPU:0, one launch (start us, length us, event | category | flops | bytes accessed | tf_op | source)
XLA Modules:
  0.0 53.8 jit_solution(11882797043096132743)
XLA Ops:
  0.6 0.0 copy-start.7
  0.7 0.0 copy-start.8
  0.7 4.9 %local_ends.1 = (f32[2,16,4096]{2,1,0:T(8,128)S(1)}, f32[2,8,4096]{2,1,0:T(8,128)S(1)}, bf16[2,256,4096]{2,1,0:T(8,128)(2,1)S(1)}) custom-call(bf16[2,256,4096]{2,1,0:T(8,128)(2,1)} %x_ref.1, f32[2,64,256]{2,1,0:T(8,128)} %ld_ref.1, bf16[2,2,16,256]{3,2,1,0:T(8,128)(2,1)} %bc_ref.3), custom_call_target="tpu_custom_call" | custom-call | flops 268435456 | bytes 4194304 | tf_op jit(solution)/shard_map/local_ends/pallas_call | solution.py:124
  5.6 0.0 copy-start
  5.6 2.0 %copy-done = bf16[2,256,4096]{2,1,0:T(8,128)(2,1)} copy-done((bf16[2,256,4096]{2,1,0:T(8,128)(2,1)}, bf16[2,256,4096]{2,1,0:T(8,128)(2,1)S(1)}, u32[]{:S(2)}) %copy-start) | copy-done | bytes 4194328
  7.7 0.5 collective-permute-start
  8.2 0.0 copy-done.7
  8.2 0.0 copy-done.8
  8.2 1.3 %branch_prepare.1 = (bf16[64,2048]{1,0:T(8,128)(2,1)S(1)}, bf16[4,528,64]{2,1,0:T(8,128)(2,1)S(1)}, bf16[4,384,256]{2,1,0:T(8,128)(2,1)S(1)}, bf16[4,256,128]{2,1,0:T(8,128)(2,1)S(1)}, bf16[2,512,512]{2,1,0:T(8,128)(2,1)S(1)}) custom-call(f32[2,32,512]{2,1,0:T(8,128)S(1)} %copy-done.7, bf16[2,2,16,512]{3,2,1,0:T(8,128)(2,1)S(1)} %copy-done.8), custom_call_target="tpu_custom_call" | custom-call | flops 100000000 | bytes 1000000 | tf_op jit(solution)/shard_map/branch_prepare/pallas_call | solution.py:222
  9.5 0.0 collective-permute-done
  9.6 0.0 copy-start.9
  9.7 0.6 %copy_bitcast_fusion = (f32[2,2048]{1,0:T(2,128)}, f32[2,2048]{1,0:T(2,128)S(1)}) fusion(f32[2,1,2048]{2,1,0:T(1,128)S(1)} %get-tuple-element.102, f32[2,1,2048]{2,1,0:T(1,128)S(1)} %get-tuple-element.104), kind=kLoop, calls=%fused_computation.24 | loop fusion | bytes 65536
  10.3 0.1 select_add_fusion.2
  10.4 0.0 copy-done.9
  10.4 0.0 copy-start.4
  10.4 2.8 %collective-permute-start.1 = (f32[32,2176]{1,0:T(8,128)S(1)}, f32[32,2176]{1,0:T(8,128)S(1)}, u32[]{:S(2)}, u32[]{:S(2)}) collective-permute-start(f32[32,2176]{1,0:T(8,128)S(1)} %pad_maximum_fusion.1), channel_id=1, source_target_pairs={{0,8},{4,12},{8,0},{12,4},{16,24},{20,28},{24,16},{28,20},{1,9},{5... | collective-permute-start | bytes 835592 | tf_op jit(solution)/shard_map/ppermute | solution.py:477
  13.2 5.0 %branch_own.2.refs_0_ = f32[512,2048]{1,0:T(8,128)S(1)} custom-call(bf16[2,512,2048]{2,1,0:T(8,128)(2,1)} %x_in.1, bf16[64,2048]{1,0:T(8,128)(2,1)S(1)} %get-tuple-element.67.refs_0_.refs_2_, bf16[4,528,64]{2,1,0:T(8,128)(2,1)S(1)} %get-tuple-element.68.refs_1_, bf16[4,384,256]{2,1,0:T(8,128)(2,1)S(1)} %get-tuple-element.69.refs_2_, ...), custom_call_target="tpu_custom_call" | custom-call | flops 2415919104 | bytes 4194304 | tf_op jit(solution)/shard_map/branch_own/pallas_call | solution.py:357
  18.2 0.0 copy-start.2
  18.2 2.0 %copy-done.2 = f32[512,2048]{1,0:T(8,128)} copy-done((f32[512,2048]{1,0:T(8,128)}, f32[512,2048]{1,0:T(8,128)S(1)}, u32[]{:S(2)}) %copy-start.2) | copy-done | bytes 4194328
  20.1 0.2 collective-permute-done.1
  20.3 0.0 copy-start.11
  20.3 0.7 %select_exponential_fusion = (f32[32,128]{1,0:T(8,128)}, f32[32,128]{1,0:T(8,128)S(1)}) fusion(pred[]{:T(512)S(6)} %ne.6, f32[32,2176]{1,0:T(8,128)S(1)} %collective-permute-done.1), kind=kLoop, calls=%fused_computation.28 | loop fusion | flops 4096 | bytes 49153 | tf_op jit(solution)/shard_map/exp | solution.py:583
  21.0 0.0 copy-start.15
  21.1 0.0 copy-done.11
  21.1 0.1 select_add_fusion.1
  21.1 0.0 copy-start.13
  21.1 0.7 %copy-done.13 = f32[2,16,2048]{2,1,0:T(8,128)} copy-done((f32[2,16,2048]{2,1,0:T(8,128)}, f32[2,16,2048]{2,1,0:T(8,128)S(1)}, u32[]{:S(2)}) %copy-start.13) | copy-done | bytes 262168
  21.8 0.7 %pad_maximum_fusion.2 = f32[32,2176]{1,0:T(8,128)} fusion(f32[32,128]{1,0:T(8,128)S(1)} %bitcast.32, f32[32,2048]{1,0:T(8,128)S(1)} %bitcast.28), kind=kLoop, calls=%fused_computation.3 | loop fusion | flops 69632 | bytes 557056 | tf_op jit(solution)/shard_map/concatenate | solution.py:482
  22.6 0.0 copy-done.15
  22.6 1.8 %collective-permute-start.2 = (f32[32,2176]{1,0:T(8,128)}, f32[32,2176]{1,0:T(8,128)}, u32[]{:S(2)}, u32[]{:S(2)}) collective-permute-start(f32[32,2176]{1,0:T(8,128)} %pad_maximum_fusion.2), channel_id=1, source_target_pairs={{0,16},{4,20},{8,24},{12,28},{16,0},{20,4},{24,8},{28,12},{1,17},{... | collective-permute-start | bytes 835592 | tf_op jit(solution)/shard_map/ppermute | solution.py:477
  24.3 1.3 %exp.28 = f32[2,2048]{1,0:T(2,128)} reshape(f32[32,128]{1,0:T(8,128)} %get-tuple-element.100) | data formatting | bytes 32768 | tf_op jit(solution)/shard_map/exp | solution.py:583
  25.7 0.0 copy-done.4
  25.7 0.8 %copy-done.5 = bf16[2,2,16,256]{3,2,1,0:T(8,128)(2,1)S(1)} copy-done((bf16[2,2,16,256]{3,2,1,0:T(8,128)(2,1)S(1)}, bf16[2,2,16,256]{3,2,1,0:T(8,128)(2,1)}, u32[]{:S(2)}) %copy-start.5) | copy-done | bytes 32792
  26.4 0.9 %prompt_prepare.1 = (bf16[2,2,528,64]{3,2,1,0:T(8,128)(2,1)S(1)}, bf16[2,384,256]{2,1,0:T(8,128)(2,1)S(1)}, bf16[2,256,128]{2,1,0:T(8,128)(2,1)S(1)}) custom-call(f32[2,64,256]{2,1,0:T(8,128)S(1)} %copy-done.4, bf16[2,2,16,256]{3,2,1,0:T(8,128)(2,1)S(1)} %copy-done.5), custom_call_target="tpu_custom_call" | custom-call | flops 100000000 | bytes 1000000 | tf_op jit(solution)/shard_map/prompt_prepare/pallas_call | solution.py:222
  27.3 0.0 copy-start.16
  27.3 0.0 copy-start.10
  27.3 0.0 copy-start.12
  27.3 0.0 copy-start.14
  27.3 0.0 copy-start.17
  27.4 0.0 copy-start.18
  27.4 0.0 copy-start.1
  27.4 5.2 %branch_own.3.refs_1_ = f32[512,2048]{1,0:T(8,128)S(1)} custom-call(bf16[2,512,2048]{2,1,0:T(8,128)(2,1)} %x_in.1, bf16[64,2048]{1,0:T(8,128)(2,1)S(1)} %get-tuple-element.67.refs_0_.refs_2_, bf16[4,528,64]{2,1,0:T(8,128)(2,1)S(1)} %get-tuple-element.68.refs_1_, bf16[4,384,256]{2,1,0:T(8,128)(2,1)S(1)} %get-tuple-element.69.refs_2_, ...), custom_call_target="tpu_custom_call" | custom-call | flops 2415919104 | bytes 4194304 | tf_op jit(solution)/shard_map/branch_own/pallas_call | solution.py:357
  32.5 0.0 collective-permute-done.2
  32.6 0.7 %slice.38 = f32[32,128]{1,0:T(8,128)S(1)} slice(f32[32,2176]{1,0:T(8,128)} %collective-permute-done.2), slice={[0:32], [2048:2176]} | slice | bytes 32768 | tf_op jit(solution)/shard_map/slice | solution.py:488
  33.3 1.0 %slice.39 = f32[32,2048]{1,0:T(8,128)S(1)} slice(f32[32,2176]{1,0:T(8,128)} %collective-permute-done.2), slice={[0:32], [0:2048]} | slice | bytes 524288 | tf_op jit(solution)/shard_map/slice | solution.py:488
  34.2 0.0 copy-done.16
  34.3 0.0 copy-done.10
  34.3 0.0 copy-done.12
  34.3 0.0 copy-done.14
  34.3 0.0 copy-done.17
  34.3 0.0 copy-done.18
  34.4 0.1 fusion
  34.5 4.7 %collective-permute-start.3 = (f32[2,16,2048]{2,1,0:T(8,128)S(1)}, f32[2,16,2048]{2,1,0:T(8,128)S(1)}, u32[]{:S(2)}, u32[]{:S(2)}) collective-permute-start(f32[2,16,2048]{2,1,0:T(8,128)S(1)} %get-tuple-element.79), channel_id=1, source_target_pairs={{0,2},{4,6},{9,11},{13,15},{18,16},{22,20},{27,25},{31,29}} | collective-permute-start | bytes 786440 | tf_op jit(solution)/shard_map/ppermute | solution.py:507
  39.2 0.1 collective-permute-start.4
  39.3 0.0 copy-done.1
  39.3 3.6 %prompt_half.2.refs_7_ = bf16[2,256,4096]{2,1,0:T(8,128)(2,1)} custom-call(s32[1]{0:T(128)} %bitcast.refs_0_, bf16[2,256,4096]{2,1,0:T(8,128)(2,1)S(1)} %copy-done.1, bf16[64,2048]{1,0:T(8,128)(2,1)S(1)} %get-tuple-element.67.refs_0_.refs_2_, bf16[2,2,528,64]{3,2,1,0:T(8,128)(2,1)S(1)} %get-tuple-element.82.refs_3_, ...), custom_call_target="tpu_custom_call" | custom-call | flops 2415919104 | bytes 4194304 | tf_op jit(solution)/shard_map/prompt_half/pallas_call | solution.py:411
  42.9 1.2 %collective-permute-done.3 = f32[2,16,2048]{2,1,0:T(8,128)S(1)} collective-permute-done((f32[2,16,2048]{2,1,0:T(8,128)S(1)}, f32[2,16,2048]{2,1,0:T(8,128)S(1)}, u32[]{:S(2)}, u32[]{:S(2)}) %collective-permute-start.3) | collective-permute-done | bytes 262176 | tf_op jit(solution)/shard_map/ppermute | solution.py:507
  44.1 0.0 collective-permute-done.4.refs_6_
  44.1 1.3 %collective-permute-start.5 = (f32[2,16,2048]{2,1,0:T(8,128)S(1)}, f32[2,16,2048]{2,1,0:T(8,128)S(1)}, u32[]{:S(2)}, u32[]{:S(2)}) collective-permute-start(f32[2,16,2048]{2,1,0:T(8,128)S(1)} %broadcast_select_fusion.2), channel_id=1, source_target_pairs={{0,1},{2,3},{4,5},{6,7},{9,8},{11,10},{13,12},{15,14},{18,19},{16,... | collective-permute-start | bytes 786440 | tf_op jit(solution)/shard_map/ppermute | solution.py:507
  46.1 0.0 copy-start.3
  46.1 0.0 copy-start.6
  46.1 3.6 %prompt_half.3 = bf16[2,256,4096]{2,1,0:T(8,128)(2,1)} custom-call(s32[1]{0:T(128)} %bitcast.1.refs_0_, bf16[2,256,4096]{2,1,0:T(8,128)(2,1)S(1)} %copy-done.1, bf16[64,2048]{1,0:T(8,128)(2,1)S(1)} %get-tuple-element.67.refs_0_.refs_2_, bf16[2,2,528,64]{3,2,1,0:T(8,128)(2,1)S(1)} %get-tuple-element.82.refs_3_, ...), custom_call_target="tpu_custom_call", output_to_operand_aliasing={{}: (7, {})} | custom-call | flops 2415919104 | bytes 4194304 | tf_op jit(solution)/shard_map/prompt_half/pallas_call | solution.py:411
  49.7 1.0 %collective-permute-done.5 = f32[2,16,2048]{2,1,0:T(8,128)S(1)} collective-permute-done((f32[2,16,2048]{2,1,0:T(8,128)S(1)}, f32[2,16,2048]{2,1,0:T(8,128)S(1)}, u32[]{:S(2)}, u32[]{:S(2)}) %collective-permute-start.5) | collective-permute-done | bytes 262176 | tf_op jit(solution)/shard_map/ppermute | solution.py:507
  50.8 2.9 %branch_finish.1 = bf16[2,512,2048]{2,1,0:T(8,128)(2,1)} custom-call(s32[2]{0:T(128)S(1)} %copy-done.6, s32[1]{0:T(128)S(6)} %copy.22.prompt_ref, bf16[2,512,512]{2,1,0:T(8,128)(2,1)S(1)} %get-tuple-element.93.reach_ref, f32[2,16,2048]{2,1,0:T(8,128)S(1)} %broadcast_select_fusion.total_ref, f32[512,2048]{1,0:T(8,128)S(1)} %copy-done.3, ...), custom_call_target="tpu_custom_call" | custom-call | flops 268435456 | bytes 8388608 | tf_op jit(solution)/shard_map/branch_finish/pallas_call | solution.py:460
  (17 shorter events, 0.3 us)
Async XLA Ops:
  0.6 7.6 %copy-start.7 = (f32[2,32,512]{2,1,0:T(8,128)S(1)}, f32[2,32,512]{2,1,0:T(8,128)}, u32[]{:S(2)}) copy-start(f32[2,32,512]{2,1,0:T(8,128)} %ld_ref) | copy-start | bytes 393220
  0.7 7.6 %copy-start.8 = (bf16[2,2,16,512]{3,2,1,0:T(8,128)(2,1)S(1)}, bf16[2,2,16,512]{3,2,1,0:T(8,128)(2,1)}, u32[]{:S(2)}) copy-start(bf16[2,2,16,512]{3,2,1,0:T(8,128)(2,1)} %bc_ref.2) | copy-start | bytes 196612
  5.6 2.0 %copy-start = (bf16[2,256,4096]{2,1,0:T(8,128)(2,1)}, bf16[2,256,4096]{2,1,0:T(8,128)(2,1)S(1)}, u32[]{:S(2)}) copy-start(bf16[2,256,4096]{2,1,0:T(8,128)(2,1)S(1)} %get-tuple-element.81.refs_1_) | copy-start | bytes 12582916
  7.7 1.9 %collective-permute-start = (f32[32,2176]{1,0:T(8,128)S(1)}, f32[32,2176]{1,0:T(8,128)S(1)}, u32[]{:S(2)}, u32[]{:S(2)}) collective-permute-start(f32[32,2176]{1,0:T(8,128)S(1)} %pad_maximum_fusion), channel_id=1, source_target_pairs={{0,4},{4,0},{8,12},{12,8},{16,20},{20,16},{24,28},{28,24},{1,5},{5... | collective-permute-start | bytes 835592 | tf_op jit(solution)/shard_map/ppermute | solution.py:477
  9.6 0.8 %copy-start.9 = (f32[32,2048]{1,0:T(8,128)}, f32[32,2048]{1,0:T(8,128)S(1)}, u32[]{:S(2)}) copy-start(f32[32,2048]{1,0:T(8,128)S(1)} %slice.35) | copy-start | bytes 786436
  10.4 15.3 %copy-start.4 = (f32[2,64,256]{2,1,0:T(8,128)S(1)}, f32[2,64,256]{2,1,0:T(8,128)}, u32[]{:S(2)}) copy-start(f32[2,64,256]{2,1,0:T(8,128)} %ld_ref.1) | copy-start | bytes 393220
  10.4 9.9 %collective-permute-start.1 = (f32[32,2176]{1,0:T(8,128)S(1)}, f32[32,2176]{1,0:T(8,128)S(1)}, u32[]{:S(2)}, u32[]{:S(2)}) collective-permute-start(f32[32,2176]{1,0:T(8,128)S(1)} %pad_maximum_fusion.1), channel_id=1, source_target_pairs={{0,8},{4,12},{8,0},{12,4},{16,24},{20,28},{24,16},{28,20},{1,9},{5... | collective-permute-start | bytes 835592 | tf_op jit(solution)/shard_map/ppermute | solution.py:477
  18.2 2.0 %copy-start.2 = (f32[512,2048]{1,0:T(8,128)}, f32[512,2048]{1,0:T(8,128)S(1)}, u32[]{:S(2)}) copy-start(f32[512,2048]{1,0:T(8,128)S(1)} %branch_own.2.refs_0_) | copy-start | bytes 12582916
  20.3 0.7 %copy-start.11 = (f32[32,2048]{1,0:T(8,128)}, f32[32,2048]{1,0:T(8,128)S(1)}, u32[]{:S(2)}) copy-start(f32[32,2048]{1,0:T(8,128)S(1)} %slice.37) | copy-start | bytes 786436
  21.0 1.6 %copy-start.15 = (f32[2,1,2048]{2,1,0:T(1,128)}, f32[2,1,2048]{2,1,0:T(1,128)S(1)}, u32[]{:S(2)}) copy-start(f32[2,1,2048]{2,1,0:T(1,128)S(1)} %get-tuple-element.106) | copy-start | bytes 49156
  21.1 0.7 %copy-start.13 = (f32[2,16,2048]{2,1,0:T(8,128)}, f32[2,16,2048]{2,1,0:T(8,128)S(1)}, u32[]{:S(2)}) copy-start(f32[2,16,2048]{2,1,0:T(8,128)S(1)} %select_add_fusion.1) | copy-start | bytes 786436
  22.6 10.0 %collective-permute-start.2 = (f32[32,2176]{1,0:T(8,128)}, f32[32,2176]{1,0:T(8,128)}, u32[]{:S(2)}, u32[]{:S(2)}) collective-permute-start(f32[32,2176]{1,0:T(8,128)} %pad_maximum_fusion.2), channel_id=1, source_target_pairs={{0,16},{4,20},{8,24},{12,28},{16,0},{20,4},{24,8},{28,12},{1,17},{... | collective-permute-start | bytes 835592 | tf_op jit(solution)/shard_map/ppermute | solution.py:477
  25.7 0.8 %copy-start.5 = (bf16[2,2,16,256]{3,2,1,0:T(8,128)(2,1)S(1)}, bf16[2,2,16,256]{3,2,1,0:T(8,128)(2,1)}, u32[]{:S(2)}) copy-start(bf16[2,2,16,256]{3,2,1,0:T(8,128)(2,1)} %bc_ref.3) | copy-start | bytes 98308
  27.3 6.9 %copy-start.16 = (f32[2,1,2048]{2,1,0:T(1,128)S(1)}, f32[2,1,2048]{2,1,0:T(1,128)}, u32[]{:S(2)}) copy-start(f32[2,1,2048]{2,1,0:T(1,128)} %copy-done.15) | copy-start | bytes 49156
  27.3 7.0 %copy-start.10 = (f32[32,2048]{1,0:T(8,128)S(1)}, f32[32,2048]{1,0:T(8,128)}, u32[]{:S(2)}) copy-start(f32[32,2048]{1,0:T(8,128)} %copy-done.9) | copy-start | bytes 786436
  27.3 7.0 %copy-start.12 = (f32[32,2048]{1,0:T(8,128)S(1)}, f32[32,2048]{1,0:T(8,128)}, u32[]{:S(2)}) copy-start(f32[32,2048]{1,0:T(8,128)} %copy-done.11) | copy-start | bytes 786436
  27.3 7.0 %copy-start.14 = (f32[2,16,2048]{2,1,0:T(8,128)S(1)}, f32[2,16,2048]{2,1,0:T(8,128)}, u32[]{:S(2)}) copy-start(f32[2,16,2048]{2,1,0:T(8,128)} %copy-done.13) | copy-start | bytes 786436
  27.3 7.0 %copy-start.17 = (f32[2,2048]{1,0:T(2,128)S(1)}, f32[2,2048]{1,0:T(2,128)}, u32[]{:S(2)}) copy-start(f32[2,2048]{1,0:T(2,128)} %exp.28) | copy-start | bytes 49156
  27.4 7.0 %copy-start.18 = (f32[2,2048]{1,0:T(2,128)S(1)}, f32[2,2048]{1,0:T(2,128)}, u32[]{:S(2)}) copy-start(f32[2,2048]{1,0:T(2,128)} %get-tuple-element.108) | copy-start | bytes 49156
  27.4 11.9 %copy-start.1 = (bf16[2,256,4096]{2,1,0:T(8,128)(2,1)S(1)}, bf16[2,256,4096]{2,1,0:T(8,128)(2,1)}, u32[]{:S(2)}) copy-start(bf16[2,256,4096]{2,1,0:T(8,128)(2,1)} %copy-done) | copy-start | bytes 12582916
  34.5 9.6 %collective-permute-start.3 = (f32[2,16,2048]{2,1,0:T(8,128)S(1)}, f32[2,16,2048]{2,1,0:T(8,128)S(1)}, u32[]{:S(2)}, u32[]{:S(2)}) collective-permute-start(f32[2,16,2048]{2,1,0:T(8,128)S(1)} %get-tuple-element.79), channel_id=1, source_target_pairs={{0,2},{4,6},{9,11},{13,15},{18,16},{22,20},{27,25},{31,29}} | collective-permute-start | bytes 786440 | tf_op jit(solution)/shard_map/ppermute | solution.py:507
  39.2 4.9 %collective-permute-start.4 = (f32[2,16,2048]{2,1,0:T(8,128)S(1)}, f32[2,16,2048]{2,1,0:T(8,128)S(1)}, u32[]{:S(2)}, u32[]{:S(2)}) collective-permute-start(f32[2,16,2048]{2,1,0:T(8,128)S(1)} %get-tuple-element.98), channel_id=1, source_target_pairs={{0,4},{4,0},{8,12},{12,8},{16,20},{20,16},{24,28},{28,24},{1,5},{5... | collective-permute-start | bytes 786440 | tf_op jit(solution)/shard_map/ppermute | solution.py:477
  44.1 6.6 %collective-permute-start.5 = (f32[2,16,2048]{2,1,0:T(8,128)S(1)}, f32[2,16,2048]{2,1,0:T(8,128)S(1)}, u32[]{:S(2)}, u32[]{:S(2)}) collective-permute-start(f32[2,16,2048]{2,1,0:T(8,128)S(1)} %broadcast_select_fusion.2), channel_id=1, source_target_pairs={{0,1},{2,3},{4,5},{6,7},{9,8},{11,10},{13,12},{15,14},{18,19},{16,... | collective-permute-start | bytes 786440 | tf_op jit(solution)/shard_map/ppermute | solution.py:507
  46.1 4.7 %copy-start.3 = (f32[512,2048]{1,0:T(8,128)S(1)}, f32[512,2048]{1,0:T(8,128)}, u32[]{:S(2)}) copy-start(f32[512,2048]{1,0:T(8,128)} %copy-done.2) | copy-start | bytes 12582916
  46.1 4.7 %copy-start.6 = (s32[2]{0:T(128)S(1)}, s32[2]{0:T(128)}, u32[]{:S(2)}) copy-start(s32[2]{0:T(128)} %len_ref.1) | copy-start | bytes 28

commit v11 on v10

--- a/solution.py
+++ b/solution.py
@@ -473,19 +473,9 @@
     )(lengths, prompt, reach, total, *own)
 
 
-def swap_bit(value, bit, size):
-    return lax.ppermute(value, "ctx", [(k, k ^ bit) for k in range(size)])
-
-
-def pack(states, logs):
-    states = states.reshape(-1, states.shape[-1])
-    return jnp.concatenate([states, logs.reshape(states.shape[0], -1)], axis=1)
-
-
-def unpack(packed, count):
-    rows = packed.shape[0] // count
-    lanes = packed.shape[1] * rows // (rows + 1)
-    return packed[:, :lanes].reshape(count, rows, lanes), packed[:, lanes:].reshape(count, 1, lanes)
+def swap_bit(values, bit, size):
+    links = [(k, k ^ bit) for k in range(size)]
+    return jax.tree.map(lambda value: lax.ppermute(value, "ctx", links), values)
 
 
 def in_order(upper, mine, other):
@@ -536,7 +526,7 @@
     branch_len,
 ):
     size, pair_size = lax.axis_size("ctx"), lax.axis_size("pair")
-    prompts, branches = prompt_x.shape[0], branch_x.shape[0]
+    branches = branch_x.shape[0]
     assert size == 2 * pair_size and size & (size - 1) == 0 and branch_prompt.shape[0] == 1
     place, prompt_logdec = lax.optimization_barrier((places(), prompt_logdec))
     odd = place["odd"]
@@ -553,11 +543,10 @@
     send = [jnp.where(odd, l, h) for l, h in zip(low, high)]
     got, (ready, reach) = beside(
         lambda v: swap_bit(v, 1, size),
-        pack(*send),
+        send,
         lambda logdec: prepare_branches(logdec, branch_bc, branch_x.shape[2]),
         branch_logdec,
     )
-    got = unpack(got, prompts)
     first, second = in_order(odd, keep, got)
     total, total_log = join(first, second)
     before, before_log = jnp.zeros_like(total), jnp.zeros_like(total_log)
@@ -574,11 +563,10 @@
     while bit < size:
         swap = functools.partial(swap_bit, bit=bit, size=size)
         if len(done) < branches:
-            got, out = beside(swap, pack(total, total_log), part(len(done)), branch_x, prompt_logdec)
+            other, out = beside(swap, (total, total_log), part(len(done)), branch_x, prompt_logdec)
             done.append(out)
         else:
-            got = swap(pack(total, total_log))
-        other = unpack(got, prompts)
+            other = swap((total, total_log))
         upper = place["upper"][bit]
         before = jnp.where(upper, jnp.exp(before_log) * other[0] + before, before)
         before_log = jnp.where(upper, before_log + other[1], before_log)

time: 54.8 us -> 46.4 us (0.85)
  local copies, waits for them, and re-layouts: 9.22 us -> 0.08 us
  waiting for transfers between devices: 2.38 us -> 4.25 us
  other arithmetic: 1.9 us -> 0.46 us
  starting transfers between devices: 11.1 us -> 11.9 us
    unnamed x41 -> x14, local copies, waits for them, and re-layouts: 6.16 us -> 0.08 us
    ppermute x4 -> x7, waiting for transfers between devices: 0.16 us -> 2.01 us  [swap_bit(): return jax.tree.map(lambda value: lax.ppermute(value, 'ctx', links), values)]
    slice x5 -> x0, local copies, waits for them, and re-layouts: 1.73 us -> none  [the longest x3 1 us: unpack(): packed[:, :lanes].reshape(count, rows, lanes)]
    exp x1 -> x0, local copies, waits for them, and re-layouts: 1.34 us -> none  [body(): before = jnp.where(upper, jnp.exp(before_log) * other[0] + before, before)]
    concatenate x3 -> x0, other arithmetic: 0.77 us -> none  [pack(): return jnp.concatenate([states, logs.reshape(states.shape[0], -1)], axis=1)]
    ppermute x4 -> x7, starting transfers between devices: 5.12 us -> 5.82 us  [swap_bit(): return jax.tree.map(lambda value: lax.ppermute(value, 'ctx', links), values)]
    exp x1 -> x0, other arithmetic: 0.66 us -> none  [body(): before = jnp.where(upper, jnp.exp(before_log) * other[0] + before, before)]
  transfers between devices with their start and end apart: 6 -> 9, of which waited for: 3 -> 4; matrix products, arithmetic and copies ran while one was open for 3% -> 0% of each run, Pallas kernels for 36% -> 42%
where the time goes in v11:
time: 46.4 us; the launch traced here: 45.6 us
  Pallas kernels  27.2 us (59%)
  starting transfers between devices  11.9 us (26%)
  waiting for transfers between devices  4.25 us (9%)
  between operations  1.72 us (4%)
    pallas_call x2, Pallas kernels, branch_own(): pl.pallas_call(functools.partial(branch_kernel, which=which), in_specs=[p...  9.99 us
    pallas_call x2, Pallas kernels, prompt_half(): pl.pallas_call(functools.partial(prompt_kernel, skip=len(into)), in_specs...  7.18 us
    ppermute x2, starting transfers between devices, spread_step(): return lax.ppermute(value, ('ctx', 'pair'), links)  6.08 us
    ppermute x7, starting transfers between devices, swap_bit(): return jax.tree.map(lambda value: lax.ppermute(value, 'ctx', links), values)  5.82 us
    pallas_call x1, Pallas kernels, local_ends(): pl.pallas_call(functools.partial(ends_kernel, width=width, lanes=lanes),...  4.92 us
    pallas_call x1, Pallas kernels, finish(): pl.pallas_call(functools.partial(finish_kernel, width=width), in_specs=[p...  2.89 us
    ppermute x2, waiting for transfers between devices, spread_step(): return lax.ppermute(value, ('ctx', 'pair'), links)  2.24 us
    pallas_call x2, Pallas kernels, prepare_call(): pl.pallas_call(kernel, in_specs=[whole] * 2, out_specs=[whole] * len(shap...  2.18 us
  transfers between devices with their start and end apart: 9, of which 4 were waited for; matrix products, arithmetic and copies ran while one was open for 0% of the time, Pallas kernels for 42%

profile of v11, /device:TPU:0, one launch (start us, length us, event | category | flops | bytes accessed | tf_op | source)
XLA Modules:
  0.0 45.6 jit_solution(13357224054798444517)
XLA Ops:
  0.6 0.0 copy-start.3
  0.6 0.0 copy-start.4
  0.7 4.9 %local_ends.1 = (f32[2,16,4096]{2,1,0:T(8,128)S(1)}, f32[2,8,4096]{2,1,0:T(8,128)S(1)}, bf16[2,256,4096]{2,1,0:T(8,128)(2,1)S(1)}) custom-call(bf16[2,256,4096]{2,1,0:T(8,128)(2,1)} %x_ref.1, f32[2,64,256]{2,1,0:T(8,128)} %ld_ref.1, bf16[2,2,16,256]{3,2,1,0:T(8,128)(2,1)} %bc_ref.3), custom_call_target="tpu_custom_call" | custom-call | flops 268435456 | bytes 4194304 | tf_op jit(solution)/shard_map/local_ends/pallas_call | solution.py:124
  5.7 0.5 %collective-permute-start = (f32[2,16,2048]{2,1,0:T(8,128)S(1)}, f32[2,16,2048]{2,1,0:T(8,128)S(1)}, u32[]{:S(2)}, u32[]{:S(2)}) collective-permute-start(f32[2,16,2048]{2,1,0:T(8,128)S(1)} %slice_select_fusion.1), channel_id=1, source_target_pairs={{0,4},{4,0},{8,12},{12,8},{16,20},{20,16},{24,28},{28,24},{1,5},{5... | collective-permute-start | bytes 786440 | tf_op jit(solution)/shard_map/ppermute | solution.py:478
  6.2 0.1 collective-permute-start.1
  6.3 0.0 copy-done.3
  6.3 0.0 copy-done.4
  6.3 1.3 %branch_prepare.1 = (bf16[64,2048]{1,0:T(8,128)(2,1)S(1)}, bf16[4,528,64]{2,1,0:T(8,128)(2,1)S(1)}, bf16[4,384,256]{2,1,0:T(8,128)(2,1)S(1)}, bf16[4,256,128]{2,1,0:T(8,128)(2,1)S(1)}, bf16[2,512,512]{2,1,0:T(8,128)(2,1)S(1)}) custom-call(f32[2,32,512]{2,1,0:T(8,128)S(1)} %copy-done.3, bf16[2,2,16,512]{3,2,1,0:T(8,128)(2,1)S(1)} %copy-done.4), custom_call_target="tpu_custom_call" | custom-call | flops 100000000 | bytes 1000000 | tf_op jit(solution)/shard_map/branch_prepare/pallas_call | solution.py:222
  7.6 0.0 collective-permute-done.1
  7.6 0.0 collective-permute-done
  7.7 0.1 select_add_fusion.2
  7.7 3.0 %collective-permute-start.2 = (f32[2,16,2048]{2,1,0:T(8,128)S(1)}, f32[2,16,2048]{2,1,0:T(8,128)S(1)}, u32[]{:S(2)}, u32[]{:S(2)}) collective-permute-start(f32[2,16,2048]{2,1,0:T(8,128)S(1)} %select_add_fusion.2), channel_id=1, source_target_pairs={{0,8},{4,12},{8,0},{12,4},{16,24},{20,28},{24,16},{28,20},{1,9},{5... | collective-permute-start | bytes 786440 | tf_op jit(solution)/shard_map/ppermute | solution.py:478
  10.7 0.1 collective-permute-start.3
  10.8 5.0 %branch_own.2.refs_0_ = f32[512,2048]{1,0:T(8,128)S(1)} custom-call(bf16[2,512,2048]{2,1,0:T(8,128)(2,1)} %x_in.1, bf16[64,2048]{1,0:T(8,128)(2,1)S(1)} %get-tuple-element.76.refs_0_.refs_2_, bf16[4,528,64]{2,1,0:T(8,128)(2,1)S(1)} %get-tuple-element.77.refs_1_, bf16[4,384,256]{2,1,0:T(8,128)(2,1)S(1)} %get-tuple-element.78.refs_2_, ...), custom_call_target="tpu_custom_call" | custom-call | flops 2415919104 | bytes 4194304 | tf_op jit(solution)/shard_map/branch_own/pallas_call | solution.py:357
  15.8 1.8 %collective-permute-done.3 = f32[2,1,2048]{2,1,0:T(1,128)S(1)} collective-permute-done((f32[2,1,2048]{2,1,0:T(1,128)S(1)}, f32[2,1,2048]{2,1,0:T(1,128)S(1)}, u32[]{:S(2)}, u32[]{:S(2)}) %collective-permute-start.3) | collective-permute-done | bytes 16416 | tf_op jit(solution)/shard_map/ppermute | solution.py:478
  17.6 0.0 collective-permute-done.2
  17.8 0.0 copy-start
  17.8 0.0 copy-start.1
  17.8 1.8 %collective-permute-start.4 = (f32[2,16,2048]{2,1,0:T(8,128)S(1)}, f32[2,16,2048]{2,1,0:T(8,128)S(1)}, u32[]{:S(2)}, u32[]{:S(2)}) collective-permute-start(f32[2,16,2048]{2,1,0:T(8,128)S(1)} %select_add_fusion.1), channel_id=1, source_target_pairs={{0,16},{4,20},{8,24},{12,28},{16,0},{20,4},{24,8},{28,12},{1,17},{... | collective-permute-start | bytes 786440 | tf_op jit(solution)/shard_map/ppermute | solution.py:478
  19.6 0.3 collective-permute-start.5
  19.9 5.0 %branch_own.3.refs_1_ = f32[512,2048]{1,0:T(8,128)S(1)} custom-call(bf16[2,512,2048]{2,1,0:T(8,128)(2,1)} %x_in.1, bf16[64,2048]{1,0:T(8,128)(2,1)S(1)} %get-tuple-element.76.refs_0_.refs_2_, bf16[4,528,64]{2,1,0:T(8,128)(2,1)S(1)} %get-tuple-element.77.refs_1_, bf16[4,384,256]{2,1,0:T(8,128)(2,1)S(1)} %get-tuple-element.78.refs_2_, ...), custom_call_target="tpu_custom_call" | custom-call | flops 2415919104 | bytes 4194304 | tf_op jit(solution)/shard_map/branch_own/pallas_call | solution.py:357
  24.9 0.0 copy-done
  24.9 0.0 copy-done.1
  24.9 0.9 %prompt_prepare.1 = (bf16[2,2,528,64]{3,2,1,0:T(8,128)(2,1)S(1)}, bf16[2,384,256]{2,1,0:T(8,128)(2,1)S(1)}, bf16[2,256,128]{2,1,0:T(8,128)(2,1)S(1)}) custom-call(f32[2,64,256]{2,1,0:T(8,128)S(1)} %copy-done, bf16[2,2,16,256]{3,2,1,0:T(8,128)(2,1)S(1)} %copy-done.1), custom_call_target="tpu_custom_call" | custom-call | flops 100000000 | bytes 1000000 | tf_op jit(solution)/shard_map/prompt_prepare/pallas_call | solution.py:222
  25.8 0.2 collective-permute-done.5
  26.0 0.0 collective-permute-done.4
  26.0 0.1 fusion
  26.2 4.8 %collective-permute-start.6 = (f32[2,16,2048]{2,1,0:T(8,128)S(1)}, f32[2,16,2048]{2,1,0:T(8,128)S(1)}, u32[]{:S(2)}, u32[]{:S(2)}) collective-permute-start(f32[2,16,2048]{2,1,0:T(8,128)S(1)} %get-tuple-element.91), channel_id=1, source_target_pairs={{0,2},{4,6},{9,11},{13,15},{18,16},{22,20},{27,25},{31,29}} | collective-permute-start | bytes 786440 | tf_op jit(solution)/shard_map/ppermute | solution.py:497
  30.9 0.1 collective-permute-start.7
  31.0 3.6 %prompt_half.2.refs_7_ = bf16[2,256,4096]{2,1,0:T(8,128)(2,1)} custom-call(s32[1]{0:T(128)} %bitcast.refs_0_, bf16[2,256,4096]{2,1,0:T(8,128)(2,1)S(1)} %get-tuple-element.93.refs_1_, bf16[64,2048]{1,0:T(8,128)(2,1)S(1)} %get-tuple-element.76.refs_0_.refs_2_, bf16[2,2,528,64]{3,2,1,0:T(8,128)(2,1)S(1)} %get-tuple-element.94.refs_3_, ...), custom_call_target="tpu_custom_call" | custom-call | flops 2415919104 | bytes 4194304 | tf_op jit(solution)/shard_map/prompt_half/pallas_call | solution.py:411
  34.6 0.5 %collective-permute-done.6 = f32[2,16,2048]{2,1,0:T(8,128)S(1)} collective-permute-done((f32[2,16,2048]{2,1,0:T(8,128)S(1)}, f32[2,16,2048]{2,1,0:T(8,128)S(1)}, u32[]{:S(2)}, u32[]{:S(2)}) %collective-permute-start.6) | collective-permute-done | bytes 262176 | tf_op jit(solution)/shard_map/ppermute | solution.py:497
  35.2 0.0 collective-permute-done.7.refs_6_
  35.2 1.3 %collective-permute-start.8 = (f32[2,16,2048]{2,1,0:T(8,128)S(1)}, f32[2,16,2048]{2,1,0:T(8,128)S(1)}, u32[]{:S(2)}, u32[]{:S(2)}) collective-permute-start(f32[2,16,2048]{2,1,0:T(8,128)S(1)} %broadcast_select_fusion.2), channel_id=1, source_target_pairs={{0,1},{2,3},{4,5},{6,7},{9,8},{11,10},{13,12},{15,14},{18,19},{16,... | collective-permute-start | bytes 786440 | tf_op jit(solution)/shard_map/ppermute | solution.py:497
  37.1 0.0 copy-start.2
  37.1 3.6 %prompt_half.3 = bf16[2,256,4096]{2,1,0:T(8,128)(2,1)} custom-call(s32[1]{0:T(128)} %bitcast.1.refs_0_, bf16[2,256,4096]{2,1,0:T(8,128)(2,1)S(1)} %get-tuple-element.93.refs_1_, bf16[64,2048]{1,0:T(8,128)(2,1)S(1)} %get-tuple-element.76.refs_0_.refs_2_, bf16[2,2,528,64]{3,2,1,0:T(8,128)(2,1)S(1)} %get-tuple-element.94.refs_3_, ...), custom_call_target="tpu_custom_call", output_to_operand_aliasing={{}: (7, {})} | custom-call | flops 2415919104 | bytes 4194304 | tf_op jit(solution)/shard_map/prompt_half/pallas_call | solution.py:411
  40.8 1.7 %collective-permute-done.8 = f32[2,16,2048]{2,1,0:T(8,128)S(1)} collective-permute-done((f32[2,16,2048]{2,1,0:T(8,128)S(1)}, f32[2,16,2048]{2,1,0:T(8,128)S(1)}, u32[]{:S(2)}, u32[]{:S(2)}) %collective-permute-start.8) | collective-permute-done | bytes 262176 | tf_op jit(solution)/shard_map/ppermute | solution.py:497
  42.5 0.0 copy-done.2
  42.5 2.9 %branch_finish.1 = bf16[2,512,2048]{2,1,0:T(8,128)(2,1)} custom-call(s32[2]{0:T(128)S(1)} %copy-done.2, s32[1]{0:T(128)S(6)} %copy.25.prompt_ref, bf16[2,512,512]{2,1,0:T(8,128)(2,1)S(1)} %get-tuple-element.105.reach_ref, f32[2,16,2048]{2,1,0:T(8,128)S(1)} %broadcast_select_fusion.total_ref, f32[512,2048]{1,0:T(8,128)S(1)} %branch_own.2.refs_0_, ...), custom_call_target="tpu_custom_call" | custom-call | flops 268435456 | bytes 8388608 | tf_op jit(solution)/shard_map/branch_finish/pallas_call | solution.py:460
  (12 shorter events, 0.3 us)
Async XLA Ops:
  0.6 5.6 %copy-start.3 = (f32[2,32,512]{2,1,0:T(8,128)S(1)}, f32[2,32,512]{2,1,0:T(8,128)}, u32[]{:S(2)}) copy-start(f32[2,32,512]{2,1,0:T(8,128)} %ld_ref) | copy-start | bytes 393220
  0.6 5.6 %copy-start.4 = (bf16[2,2,16,512]{3,2,1,0:T(8,128)(2,1)S(1)}, bf16[2,2,16,512]{3,2,1,0:T(8,128)(2,1)}, u32[]{:S(2)}) copy-start(bf16[2,2,16,512]{3,2,1,0:T(8,128)(2,1)} %bc_ref.2) | copy-start | bytes 196612
  5.7 1.9 %collective-permute-start = (f32[2,16,2048]{2,1,0:T(8,128)S(1)}, f32[2,16,2048]{2,1,0:T(8,128)S(1)}, u32[]{:S(2)}, u32[]{:S(2)}) collective-permute-start(f32[2,16,2048]{2,1,0:T(8,128)S(1)} %slice_select_fusion.1), channel_id=1, source_target_pairs={{0,4},{4,0},{8,12},{12,8},{16,20},{20,16},{24,28},{28,24},{1,5},{5... | collective-permute-start | bytes 786440 | tf_op jit(solution)/shard_map/ppermute | solution.py:478
  6.2 1.4 %collective-permute-start.1 = (f32[2,1,2048]{2,1,0:T(1,128)S(1)}, f32[2,1,2048]{2,1,0:T(1,128)S(1)}, u32[]{:S(2)}, u32[]{:S(2)}) collective-permute-start(f32[2,1,2048]{2,1,0:T(1,128)S(1)} %broadcast_select_fusion.5), channel_id=1, source_target_pairs={{0,4},{4,0},{8,12},{12,8},{16,20},{20,16},{24,28},{28,24},{1,5},{5... | collective-permute-start | bytes 49160 | tf_op jit(solution)/shard_map/ppermute | solution.py:478
  7.7 9.9 %collective-permute-start.2 = (f32[2,16,2048]{2,1,0:T(8,128)S(1)}, f32[2,16,2048]{2,1,0:T(8,128)S(1)}, u32[]{:S(2)}, u32[]{:S(2)}) collective-permute-start(f32[2,16,2048]{2,1,0:T(8,128)S(1)} %select_add_fusion.2), channel_id=1, source_target_pairs={{0,8},{4,12},{8,0},{12,4},{16,24},{20,28},{24,16},{28,20},{1,9},{5... | collective-permute-start | bytes 786440 | tf_op jit(solution)/shard_map/ppermute | solution.py:478
  10.7 6.9 %collective-permute-start.3 = (f32[2,1,2048]{2,1,0:T(1,128)S(1)}, f32[2,1,2048]{2,1,0:T(1,128)S(1)}, u32[]{:S(2)}, u32[]{:S(2)}) collective-permute-start(f32[2,1,2048]{2,1,0:T(1,128)S(1)} %get-tuple-element.74), channel_id=1, source_target_pairs={{0,8},{4,12},{8,0},{12,4},{16,24},{20,28},{24,16},{28,20},{1,9},{5... | collective-permute-start | bytes 49160 | tf_op jit(solution)/shard_map/ppermute | solution.py:478
  17.8 7.1 %copy-start = (f32[2,64,256]{2,1,0:T(8,128)S(1)}, f32[2,64,256]{2,1,0:T(8,128)}, u32[]{:S(2)}) copy-start(f32[2,64,256]{2,1,0:T(8,128)} %ld_ref.1) | copy-start | bytes 393220
  17.8 7.1 %copy-start.1 = (bf16[2,2,16,256]{3,2,1,0:T(8,128)(2,1)S(1)}, bf16[2,2,16,256]{3,2,1,0:T(8,128)(2,1)}, u32[]{:S(2)}) copy-start(bf16[2,2,16,256]{3,2,1,0:T(8,128)(2,1)} %bc_ref.3) | copy-start | bytes 98308
  17.8 8.2 %collective-permute-start.4 = (f32[2,16,2048]{2,1,0:T(8,128)S(1)}, f32[2,16,2048]{2,1,0:T(8,128)S(1)}, u32[]{:S(2)}, u32[]{:S(2)}) collective-permute-start(f32[2,16,2048]{2,1,0:T(8,128)S(1)} %select_add_fusion.1), channel_id=1, source_target_pairs={{0,16},{4,20},{8,24},{12,28},{16,0},{20,4},{24,8},{28,12},{1,17},{... | collective-permute-start | bytes 786440 | tf_op jit(solution)/shard_map/ppermute | solution.py:478
  19.6 6.3 %collective-permute-start.5 = (f32[2,1,2048]{2,1,0:T(1,128)S(1)}, f32[2,1,2048]{2,1,0:T(1,128)S(1)}, u32[]{:S(2)}, u32[]{:S(2)}) collective-permute-start(f32[2,1,2048]{2,1,0:T(1,128)S(1)} %get-tuple-element.83), channel_id=1, source_target_pairs={{0,16},{4,20},{8,24},{12,28},{16,0},{20,4},{24,8},{28,12},{1,17},{... | collective-permute-start | bytes 49160 | tf_op jit(solution)/shard_map/ppermute | solution.py:478
  26.2 9.0 %collective-permute-start.6 = (f32[2,16,2048]{2,1,0:T(8,128)S(1)}, f32[2,16,2048]{2,1,0:T(8,128)S(1)}, u32[]{:S(2)}, u32[]{:S(2)}) collective-permute-start(f32[2,16,2048]{2,1,0:T(8,128)S(1)} %get-tuple-element.91), channel_id=1, source_target_pairs={{0,2},{4,6},{9,11},{13,15},{18,16},{22,20},{27,25},{31,29}} | collective-permute-start | bytes 786440 | tf_op jit(solution)/shard_map/ppermute | solution.py:497
  30.9 4.2 %collective-permute-start.7 = (f32[2,16,2048]{2,1,0:T(8,128)S(1)}, f32[2,16,2048]{2,1,0:T(8,128)S(1)}, u32[]{:S(2)}, u32[]{:S(2)}) collective-permute-start(f32[2,16,2048]{2,1,0:T(8,128)S(1)} %get-tuple-element.110), channel_id=1, source_target_pairs={{0,4},{4,0},{8,12},{12,8},{16,20},{20,16},{24,28},{28,24},{1,5},{5... | collective-permute-start | bytes 786440 | tf_op jit(solution)/shard_map/ppermute | solution.py:478
  35.2 7.3 %collective-permute-start.8 = (f32[2,16,2048]{2,1,0:T(8,128)S(1)}, f32[2,16,2048]{2,1,0:T(8,128)S(1)}, u32[]{:S(2)}, u32[]{:S(2)}) collective-permute-start(f32[2,16,2048]{2,1,0:T(8,128)S(1)} %broadcast_select_fusion.2), channel_id=1, source_target_pairs={{0,1},{2,3},{4,5},{6,7},{9,8},{11,10},{13,12},{15,14},{18,19},{16,... | collective-permute-start | bytes 786440 | tf_op jit(solution)/shard_map/ppermute | solution.py:497
  37.1 5.4 %copy-start.2 = (s32[2]{0:T(128)S(1)}, s32[2]{0:T(128)}, u32[]{:S(2)}) copy-start(s32[2]{0:T(128)} %len_ref.1) | copy-start | bytes 28

commit v12 on v11

--- a/solution.py
+++ b/solution.py
@@ -92,14 +92,19 @@
         push_ref[i] = push.reshape(heads * state, positions).astype(BF16)
     group = 256 // width
     lane_head = quotient(iota((1, 256), 1), width)
-    for i in range(count):
-        totals = lax.dot_general(
-            jnp.ones((16, positions), F32), ld_ref[i], (((1,), (1,)), ((), ())),
-            preferred_element_type=F32, precision=lax.Precision.HIGHEST)
-        for j in range(tiles):
-            cols = pl.ds(j * lanes, lanes)
-            pick = iota((heads, 1), 0) == quotient(iota((1, lanes), 1), width) + j * (lanes // width)
-            log_ref[i, :, cols] = split_dot(totals, jnp.where(pick, 1.0, 0.0).astype(BF16))[:8]
+    high = logs.astype(BF16)
+    middle = (logs - high.astype(F32)).astype(BF16)
+    low = (logs - high.astype(F32) - middle.astype(F32)).astype(BF16)
+    totals = sum(
+        lax.dot_general(
+            jnp.ones((16, positions), BF16), part, (((1,), (1,)), ((), ())), preferred_element_type=F32)
+        for part in (high, middle, low))
+    totals = jnp.concatenate([totals[:8, i * heads:(i + 1) * heads] for i in range(count)], axis=0)
+    for j in range(tiles):
+        pick = iota((heads, 1), 0) == quotient(iota((1, lanes), 1), width) + j * (lanes // width)
+        wide = split_dot(totals, jnp.where(pick, 1.0, 0.0).astype(BF16))
+        for i in range(count):
+            log_ref[i, :, pl.ds(j * lanes, lanes)] = wide[8 * i:8 * i + 8]
     for i in range(count):
         for j in range(tiles):
             copies[i, j].wait()
@@ -199,7 +204,8 @@
         w_ref[k // 2, k % 2] = w
 
 
-def branch_prepare_kernel(ld_ref, bc_ref, hot_ref, w_ref, lv_ref, lc_ref, reach_ref, *, width):
+def branch_prepare_kernel(prompt_ref, ld_ref, bc_ref, hot_ref, w_ref, lv_ref, lc_ref, reach_ref, row_ref, *, width):
+    row_ref[...] = jnp.full(row_ref.shape, prompt_ref[0], jnp.int32).astype(F32)
     heads, state = ld_ref.shape[1], bc_ref.shape[2]
     blocks = ld_ref.shape[2] // BLOCK
     cuts, logs, parts = blocks_of(ld_ref, bc_ref)
@@ -217,40 +223,43 @@
         reach_ref[i, cut, :] = reach.reshape(heads * state, BLOCK).T.astype(BF16)
 
 
-def prepare_call(kernel, shapes, name, logdec, bc):
+def prepare_call(kernel, shapes, name, *args):
     whole = pl.BlockSpec(memory_space=pltpu.VMEM)
+    scalars = [pl.BlockSpec(memory_space=pltpu.SMEM)] * (len(args) - 2)
     return pl.pallas_call(
         kernel,
-        in_specs=[whole] * 2,
+        in_specs=scalars + [whole] * 2,
         out_specs=[whole] * len(shapes),
-        out_shape=[jax.ShapeDtypeStruct(shape, BF16) for shape in shapes],
+        out_shape=[jax.ShapeDtypeStruct(*shape) for shape in shapes],
         compiler_params=pltpu.CompilerParams(vmem_limit_bytes=VMEM_LIMIT),
         cost_estimate=pl.CostEstimate(flops=10**8, bytes_accessed=10**6, transcendentals=0),
         name=name,
-    )(logdec, bc)
+    )(*args)
 
 
 def prepare_prompts(logdec, bc):
     count, heads, positions = logdec.shape
     cuts, rows = count * (positions // BLOCK), BLOCK // CHUNK * bc.shape[2]
     shapes = [(cuts, 2, 2 * BLOCK + 16, heads), (cuts, rows + BLOCK, BLOCK), (cuts, BLOCK, rows)]
+    shapes = [(shape, BF16) for shape in shapes]
     return prepare_call(prompt_prepare_kernel, shapes, "prompt_prepare", logdec, bc)
 
 
-def prepare_branches(logdec, bc, channels):
+def prepare_branches(prompt, logdec, bc, channels):
     count, heads, positions = logdec.shape
     state = bc.shape[2]
     cuts, rows = count * (positions // BLOCK), BLOCK // CHUNK * state
     shapes = [
-        (2 * heads, channels),
-        (cuts, 2 * BLOCK + 16, 2 * heads),
-        (cuts, rows + BLOCK, BLOCK),
-        (cuts, BLOCK, rows),
-        (count, positions, heads * state),
+        ((2 * heads, channels), BF16),
+        ((cuts, 2 * BLOCK + 16, 2 * heads), BF16),
+        ((cuts, rows + BLOCK, BLOCK), BF16),
+        ((cuts, BLOCK, rows), BF16),
+        ((count, positions, heads * state), BF16),
+        ((1, channels), F32),
     ]
     kernel = functools.partial(branch_prepare_kernel, width=channels // heads)
-    out = prepare_call(kernel, shapes, "branch_prepare", logdec, bc)
-    return out[:4], out[4]
+    out = prepare_call(kernel, shapes, "branch_prepare", prompt, logdec, bc)
+    return out[:4], out[4], out[5]
 
 
 def run_tiles(jobs):
@@ -425,41 +434,37 @@
     )(half, x, *ready, start, *into)
 
 
-def finish_kernel(len_ref, prompt_ref, reach_ref, total_ref, *refs, width):
+def finish_kernel(len_ref, reach_ref, start_ref, *refs, width):
     own_refs, (y_out, y_ref, sems) = refs[:-3], refs[-3:]
     count, positions, channels = y_ref.shape
-    prompts, state, _ = total_ref.shape
+    state = start_ref.shape[0]
     group = 128 // state
     span = group * width
     left = Copies(sems)
     own_head = quotient(iota((128, 1), 0), state) == quotient(iota((1, span), 1), width)
-    starts = []
     for g in range(channels // span):
-        start = total_ref[0, :, pl.ds(g * span, span)]
-        for which in range(1, prompts):
-            start = jnp.where(prompt_ref[0] == which, total_ref[which, :, pl.ds(g * span, span)], start)
-        start = jnp.concatenate([start] * group, axis=0)
-        starts.append(jnp.where(own_head, start, 0.0).astype(BF16))
-    for i in range(count):
-        for g in range(channels // span):
+        cols = pl.ds(g * span, span)
+        start = jnp.concatenate([start_ref[:, cols]] * group, axis=0)
+        start = jnp.where(own_head, start, 0.0).astype(BF16)
+        for i in range(count):
             for b in range(positions // BLOCK):
-                rows, cols = pl.ds(b * BLOCK, BLOCK), pl.ds(g * span, span)
+                rows = pl.ds(b * BLOCK, BLOCK)
                 term = jnp.dot(
-                    reach_ref[i, rows, pl.ds(g * 128, 128)], starts[g], preferred_element_type=F32)
+                    reach_ref[i, rows, pl.ds(g * 128, 128)], start, preferred_element_type=F32)
                 live = iota((BLOCK, span), 0) < len_ref[i] - b * BLOCK
                 y_ref[i, rows, cols] = jnp.where(live, own_refs[i][rows, cols] + term, 0.0).astype(BF16)
                 left.start((i, b, g), y_ref.at[i, rows, cols], y_out.at[i, rows, cols])
     left.wait_all()
 
 
-def finish(lengths, prompt, reach, total, own):
+def finish(lengths, reach, start, own):
     count, (positions, channels) = len(own), own[0].shape
-    state = total.shape[1]
+    state = start.shape[0]
     width = channels * state // reach.shape[2]
     whole = pl.BlockSpec(memory_space=pltpu.VMEM)
     return pl.pallas_call(
         functools.partial(finish_kernel, width=width),
-        in_specs=[pl.BlockSpec(memory_space=pltpu.SMEM)] * 2 + [whole] * (2 + count),
+        in_specs=[pl.BlockSpec(memory_space=pltpu.SMEM)] + [whole] * (2 + count),
         out_specs=pl.BlockSpec(memory_space=pltpu.HBM),
         out_shape=jax.ShapeDtypeStruct((count, positions, channels), BF16),
         scratch_shapes=[
@@ -470,7 +475,7 @@
         cost_estimate=pl.CostEstimate(
             flops=2**28, bytes_accessed=2**23, transcendentals=0),
         name="branch_finish",
-    )(lengths, prompt, reach, total, *own)
+    )(lengths, reach, start, *own)
 
 
 def swap_bit(values, bit, size):
@@ -541,16 +546,22 @@
     low, high = (end[:, :, :half], log[:, :1, :half]), (end[:, :, half:], log[:, :1, half:])
     keep = [jnp.where(odd, h, l) for l, h in zip(low, high)]
     send = [jnp.where(odd, l, h) for l, h in zip(low, high)]
-    got, (ready, reach) = beside(
+    got, (ready, reach, row) = beside(
         lambda v: swap_bit(v, 1, size),
         send,
-        lambda logdec: prepare_branches(logdec, branch_bc, branch_x.shape[2]),
+        lambda logdec: prepare_branches(branch_prompt, logdec, branch_bc, branch_x.shape[2]),
         branch_logdec,
     )
     first, second = in_order(odd, keep, got)
     total, total_log = join(first, second)
     before, before_log = jnp.zeros_like(total), jnp.zeros_like(total_log)
 
+    def chosen(total, row):
+        out = total[0]
+        for which in range(1, total.shape[0]):
+            out = jnp.where(row == which, total[which], out)
+        return out
+
     def part(which):
         def work(x, logdec):
             own = branch_own(x, ready, which)
@@ -562,7 +573,14 @@
     bit = 2
     while bit < size:
         swap = functools.partial(swap_bit, bit=bit, size=size)
-        if len(done) < branches:
+        if not done:
+            def with_row(values):
+                return swap(values[:2]), lax.ppermute(values[2], "pair", [(z, z ^ 1) for z in range(pair_size)])
+
+            (other, next_row), out = beside(
+                with_row, (total, total_log, row), part(0), branch_x, prompt_logdec)
+            done.append(out)
+        elif len(done) < branches:
             other, out = beside(swap, (total, total_log), part(len(done)), branch_x, prompt_logdec)
             done.append(out)
         else:
@@ -584,17 +602,20 @@
     prompt_y = ()
     for hop in halvings(pair_size):
         step = functools.partial(spread_step, hop=hop, ctx_size=size, pair_size=pair_size)
+        value = total if hop > 1 else chosen(total, next_row)
         if sides:
             side, entering = sides.pop(0)
             got, prompt_y = beside(
-                step, total,
+                step, value,
                 lambda entering, y: (prompt_half(side, held, prompt_ready, entering, y),), entering, prompt_y)
         else:
-            got = step(total)
-        total = jnp.where(place["has"][hop], total, got)
+            got = step(value)
+        if hop > 1:
+            total = jnp.where(place["has"][hop], total, got)
     for side, entering in sides:
         prompt_y = (prompt_half(side, held, prompt_ready, entering, prompt_y),)
-    branch_y = finish(branch_len, branch_prompt, reach, total, own)
+    start = jnp.where(place["has"][1], chosen(total, row), got)
+    branch_y = finish(branch_len, reach, start, own)
     return prompt_y[0], branch_y
 
 

time: 46.4 us -> 44.1 us (0.950)
  waiting for transfers between devices: 4.25 us -> 0.49 us
  starting transfers between devices: 11.9 us -> 13.9 us
    ppermute x7, waiting for transfers between devices: 2.01 us -> 0.02 us  [swap_bit(): return jax.tree.map(lambda value: lax.ppermute(value, 'ctx', links), values)]
    ppermute x2, waiting for transfers between devices: 2.24 us -> 0.47 us  [spread_step(): return lax.ppermute(value, ('ctx', 'pair'), links)]
    ppermute x0 -> x1, starting transfers between devices: none -> 1.58 us  [with_row(): lax.ppermute(values[2], 'pair', [(z, z ^ 1) for z in range(pair_size)])]
    ppermute x7, starting transfers between devices: 5.82 us -> 6.34 us  [swap_bit(): return jax.tree.map(lambda value: lax.ppermute(value, 'ctx', links), values)]
  transfers between devices with their start and end apart: 9 -> 10, of which waited for: 4 -> 1; matrix products, arithmetic and copies ran while one was open for 0% -> 0% of each run, Pallas kernels for 42% -> 45%
where the time goes in v12:
time: 44.1 us; the launch traced here: 43.7 us
  Pallas kernels  26.9 us (61%)
  starting transfers between devices  13.9 us (32%)
  between operations  1.79 us (4%)
  other arithmetic  0.58 us (1%)
  waiting for transfers between devices  0.49 us (1%)
    pallas_call x2, Pallas kernels, branch_own(): pl.pallas_call(functools.partial(branch_kernel, which=which), in_specs=[p...  10.1 us
    pallas_call x2, Pallas kernels, prompt_half(): pl.pallas_call(functools.partial(prompt_kernel, skip=len(into)), in_specs...  7.2 us
    ppermute x7, starting transfers between devices, swap_bit(): return jax.tree.map(lambda value: lax.ppermute(value, 'ctx', links), values)  6.34 us
    ppermute x2, starting transfers between devices, spread_step(): return lax.ppermute(value, ('ctx', 'pair'), links)  5.98 us
    pallas_call x1, Pallas kernels, local_ends(): pl.pallas_call(functools.partial(ends_kernel, width=width, lanes=lanes),...  4.55 us
    pallas_call x1, Pallas kernels, finish(): pl.pallas_call(functools.partial(finish_kernel, width=width), in_specs=[p...  2.89 us
    pallas_call x2, Pallas kernels, prepare_call(): pl.pallas_call(kernel, in_specs=scalars + [whole] * 2, out_specs=[whole]...  2.18 us
    ppermute x1, starting transfers between devices, with_row(): lax.ppermute(values[2], 'pair', [(z, z ^ 1) for z in range(pair_size)])  1.58 us
  transfers between devices with their start and end apart: 10, of which 1 were waited for; matrix products, arithmetic and copies ran while one was open for 0% of the time, Pallas kernels for 45%

profile of v12, /device:TPU:0, one launch (start us, length us, event | category | flops | bytes accessed | tf_op | source)
XLA Modules:
  0.0 43.7 jit_solution(9475335005740613143)
XLA Ops:
  0.6 0.0 copy-start.3
  0.6 0.0 copy-start.4
  0.7 4.5 %local_ends.1 = (f32[2,16,4096]{2,1,0:T(8,128)S(1)}, f32[2,8,4096]{2,1,0:T(8,128)S(1)}, bf16[2,256,4096]{2,1,0:T(8,128)(2,1)S(1)}) custom-call(bf16[2,256,4096]{2,1,0:T(8,128)(2,1)} %x_ref.1, f32[2,64,256]{2,1,0:T(8,128)} %ld_ref.1, bf16[2,2,16,256]{3,2,1,0:T(8,128)(2,1)} %bc_ref.3), custom_call_target="tpu_custom_call" | custom-call | flops 268435456 | bytes 4194304 | tf_op jit(solution)/shard_map/local_ends/pallas_call | solution.py:129
  5.3 0.5 %collective-permute-start = (f32[2,16,2048]{2,1,0:T(8,128)S(1)}, f32[2,16,2048]{2,1,0:T(8,128)S(1)}, u32[]{:S(2)}, u32[]{:S(2)}) collective-permute-start(f32[2,16,2048]{2,1,0:T(8,128)S(1)} %slice_select_fusion.1), channel_id=1, source_target_pairs={{0,4},{4,0},{8,12},{12,8},{16,20},{20,16},{24,28},{28,24},{1,5},{5... | collective-permute-start | bytes 786440 | tf_op jit(solution)/shard_map/ppermute | solution.py:483
  5.8 0.1 collective-permute-start.1
  6.5 0.0 copy-done.3
  6.5 0.0 copy-done.4
  6.6 1.3 %branch_prepare.1 = (bf16[64,2048]{1,0:T(8,128)(2,1)S(1)}, bf16[4,528,64]{2,1,0:T(8,128)(2,1)S(1)}, bf16[4,384,256]{2,1,0:T(8,128)(2,1)S(1)}, bf16[4,256,128]{2,...) custom-call(s32[1]{0:T(128)S(6)} %copy.25.prompt_ref, f32[2,32,512]{2,1,0:T(8,128)S(1)} %copy-done.3, ...), custom_call_target="tpu_custom_call" | custom-call | flops 100000000 | bytes 1000000 | tf_op jit(solution)/shard_map/branch_prepare/pallas_call | solution.py:229
  7.9 0.0 collective-permute-done.1
  7.9 0.0 collective-permute-done
  8.0 0.1 select_add_fusion.2
  8.1 3.0 %collective-permute-start.2 = (f32[2,16,2048]{2,1,0:T(8,128)S(1)}, f32[2,16,2048]{2,1,0:T(8,128)S(1)}, u32[]{:S(2)}, u32[]{:S(2)}) collective-permute-start(f32[2,16,2048]{2,1,0:T(8,128)S(1)} %select_add_fusion.2), channel_id=1, source_target_pairs={{0,8},{4,12},{8,0},{12,4},{16,24},{20,28},{24,16},{28,20},{1,9},{5... | collective-permute-start | bytes 786440 | tf_op jit(solution)/shard_map/ppermute | solution.py:483
  11.0 1.6 %collective-permute-start.4 = (f32[1,2048]{1,0:T(1,128)S(1)}, f32[1,2048]{1,0:T(1,128)S(1)}, u32[]{:S(2)}, u32[]{:S(2)}) collective-permute-start(f32[1,2048]{1,0:T(1,128)S(1)} %get-tuple-element.78), channel_id=1, source_target_pairs={{0,1},{1,0},{2,3},{3,2},{4,5},{5,4},{6,7},{7,6},{8,9},{9,8},{10,11... | collective-permute-start | bytes 24584 | tf_op jit(solution)/shard_map/ppermute | solution.py:578
  12.6 0.5 %collective-permute-start.3 = (f32[2,1,2048]{2,1,0:T(1,128)S(1)}, f32[2,1,2048]{2,1,0:T(1,128)S(1)}, u32[]{:S(2)}, u32[]{:S(2)}) collective-permute-start(f32[2,1,2048]{2,1,0:T(1,128)S(1)} %get-tuple-element.77), channel_id=1, source_target_pairs={{0,8},{4,12},{8,0},{12,4},{16,24},{20,28},{24,16},{28,20},{1,9},{5... | collective-permute-start | bytes 49160 | tf_op jit(solution)/shard_map/ppermute | solution.py:483
  13.2 5.0 %branch_own.2.refs_0_ = f32[512,2048]{1,0:T(8,128)S(1)} custom-call(bf16[2,512,2048]{2,1,0:T(8,128)(2,1)} %x_in.1, bf16[64,2048]{1,0:T(8,128)(2,1)S(1)} %get-tuple-element.80.refs_0_.refs_2_, bf16[4,528,64]{2,1,0:T(8,128)(2,1)S(1)} %get-tuple-element.81.refs_1_, bf16[4,384,256]{2,1,0:T(8,128)(2,1)S(1)} %get-tuple-element.82.refs_2_, ...), custom_call_target="tpu_custom_call" | custom-call | flops 2415919104 | bytes 4194304 | tf_op jit(solution)/shard_map/branch_own/pallas_call | solution.py:366
  18.2 0.0 collective-permute-done.4
  18.2 0.0 collective-permute-done.3
  18.2 0.0 collective-permute-done.2
  18.2 0.1 fusion.4
  18.3 1.6 %collective-permute-start.5 = (f32[2,16,2048]{2,1,0:T(8,128)S(1)}, f32[2,16,2048]{2,1,0:T(8,128)S(1)}, u32[]{:S(2)}, u32[]{:S(2)}) collective-permute-start(f32[2,16,2048]{2,1,0:T(8,128)S(1)} %select_add_fusion.1), channel_id=1, source_target_pairs={{0,16},{4,20},{8,24},{12,28},{16,0},{20,4},{24,8},{28,12},{1,17},{... | collective-permute-start | bytes 786440 | tf_op jit(solution)/shard_map/ppermute | solution.py:483
  20.0 0.0 copy-start
  20.0 0.0 copy-start.1
  20.0 0.6 %collective-permute-start.6 = (f32[2,1,2048]{2,1,0:T(1,128)S(1)}, f32[2,1,2048]{2,1,0:T(1,128)S(1)}, u32[]{:S(2)}, u32[]{:S(2)}) collective-permute-start(f32[2,1,2048]{2,1,0:T(1,128)S(1)} %get-tuple-element.91), channel_id=1, source_target_pairs={{0,16},{4,20},{8,24},{12,28},{16,0},{20,4},{24,8},{28,12},{1,17},{... | collective-permute-start | bytes 49160 | tf_op jit(solution)/shard_map/ppermute | solution.py:483
  20.6 5.0 %branch_own.3.refs_1_ = f32[512,2048]{1,0:T(8,128)S(1)} custom-call(bf16[2,512,2048]{2,1,0:T(8,128)(2,1)} %x_in.1, bf16[64,2048]{1,0:T(8,128)(2,1)S(1)} %get-tuple-element.80.refs_0_.refs_2_, bf16[4,528,64]{2,1,0:T(8,128)(2,1)S(1)} %get-tuple-element.81.refs_1_, bf16[4,384,256]{2,1,0:T(8,128)(2,1)S(1)} %get-tuple-element.82.refs_2_, ...), custom_call_target="tpu_custom_call" | custom-call | flops 2415919104 | bytes 4194304 | tf_op jit(solution)/shard_map/branch_own/pallas_call | solution.py:366
  25.6 0.0 copy-done
  25.6 0.0 copy-done.1
  25.6 0.9 %prompt_prepare.1 = (bf16[2,2,528,64]{3,2,1,0:T(8,128)(2,1)S(1)}, bf16[2,384,256]{2,1,0:T(8,128)(2,1)S(1)}, bf16[2,256,128]{2,1,0:T(8,128)(2,1)S(1)}) custom-call(f32[2,64,256]{2,1,0:T(8,128)S(1)} %copy-done, bf16[2,2,16,256]{3,2,1,0:T(8,128)(2,1)S(1)} %copy-done.1), custom_call_target="tpu_custom_call" | custom-call | flops 100000000 | bytes 1000000 | tf_op jit(solution)/shard_map/prompt_prepare/pallas_call | solution.py:229
  26.5 0.0 collective-permute-done.6
  26.5 0.0 collective-permute-done.5
  26.6 0.1 fusion
  26.7 4.7 %collective-permute-start.7 = (f32[2,16,2048]{2,1,0:T(8,128)S(1)}, f32[2,16,2048]{2,1,0:T(8,128)S(1)}, u32[]{:S(2)}, u32[]{:S(2)}) collective-permute-start(f32[2,16,2048]{2,1,0:T(8,128)S(1)} %get-tuple-element.99), channel_id=1, source_target_pairs={{0,2},{4,6},{9,11},{13,15},{18,16},{22,20},{27,25},{31,29}} | collective-permute-start | bytes 786440 | tf_op jit(solution)/shard_map/ppermute | solution.py:502
  31.5 0.1 collective-permute-start.8
  31.5 3.6 %prompt_half.2.refs_7_ = bf16[2,256,4096]{2,1,0:T(8,128)(2,1)} custom-call(s32[1]{0:T(128)} %bitcast.refs_0_, bf16[2,256,4096]{2,1,0:T(8,128)(2,1)S(1)} %get-tuple-element.101.refs_1_, bf16[64,2048]{1,0:T(8,128)(2,1)S(1)} %get-tuple-element.80.refs_0_.refs_2_, bf16[2,2,528,64]{3,2,1,0:T(8,128)(2,1)S(1)} %get-tuple-element.102.refs_3_, ...), custom_call_target="tpu_custom_call" | custom-call | flops 2415919104 | bytes 4194304 | tf_op jit(solution)/shard_map/prompt_half/pallas_call | solution.py:420
  35.1 0.5 %collective-permute-done.7 = f32[2,16,2048]{2,1,0:T(8,128)S(1)} collective-permute-done((f32[2,16,2048]{2,1,0:T(8,128)S(1)}, f32[2,16,2048]{2,1,0:T(8,128)S(1)}, u32[]{:S(2)}, u32[]{:S(2)}) %collective-permute-start.7) | collective-permute-done | bytes 262176 | tf_op jit(solution)/shard_map/ppermute | solution.py:502
  35.7 0.0 copy-start.2
  35.7 0.0 collective-permute-done.8.refs_6_
  35.7 1.3 %collective-permute-start.9 = (f32[16,2048]{1,0:T(8,128)S(1)}, f32[16,2048]{1,0:T(8,128)S(1)}, u32[]{:S(2)}, u32[]{:S(2)}) collective-permute-start(f32[16,2048]{1,0:T(8,128)S(1)} %fusion.2), channel_id=1, source_target_pairs={{0,1},{2,3},{4,5},{6,7},{9,8},{11,10},{13,12},{15,14},{18,19},{16,... | collective-permute-start | bytes 393224 | tf_op jit(solution)/shard_map/ppermute | solution.py:502
  37.0 3.6 %prompt_half.3 = bf16[2,256,4096]{2,1,0:T(8,128)(2,1)} custom-call(s32[1]{0:T(128)} %bitcast.1.refs_0_, bf16[2,256,4096]{2,1,0:T(8,128)(2,1)S(1)} %get-tuple-element.101.refs_1_, bf16[64,2048]{1,0:T(8,128)(2,1)S(1)} %get-tuple-element.80.refs_0_.refs_2_, bf16[2,2,528,64]{3,2,1,0:T(8,128)(2,1)S(1)} %get-tuple-element.102.refs_3_, ...), custom_call_target="tpu_custom_call", output_to_operand_aliasing={{}: (7, {})} | custom-call | flops 2415919104 | bytes 4194304 | tf_op jit(solution)/shard_map/prompt_half/pallas_call | solution.py:420
  40.6 0.0 collective-permute-done.9
  40.7 0.0 copy-done.2
  40.7 2.9 %branch_finish.1 = bf16[2,512,2048]{2,1,0:T(8,128)(2,1)} custom-call(s32[2]{0:T(128)S(1)} %copy-done.2, bf16[2,512,512]{2,1,0:T(8,128)(2,1)S(1)} %get-tuple-element.113.reach_ref, f32[16,2048]{1,0:T(8,128)S(1)} %select_select_fusion.start_ref, f32[512,2048]{1,0:T(8,128)S(1)} %branch_own.2.refs_0_, f32[512,2048]{1,0:T(8,128)S(1)} %branch_own.3.refs_1_), custom_call_target="tpu_custom_call" | custom-call | flops 268435456 | bytes 8388608 | tf_op jit(solution)/shard_map/branch_finish/pallas_call | solution.py:465
  (14 shorter events, 0.4 us)
Async XLA Ops:
  0.6 5.9 %copy-start.3 = (f32[2,32,512]{2,1,0:T(8,128)S(1)}, f32[2,32,512]{2,1,0:T(8,128)}, u32[]{:S(2)}) copy-start(f32[2,32,512]{2,1,0:T(8,128)} %ld_ref) | copy-start | bytes 393220
  0.6 5.9 %copy-start.4 = (bf16[2,2,16,512]{3,2,1,0:T(8,128)(2,1)S(1)}, bf16[2,2,16,512]{3,2,1,0:T(8,128)(2,1)}, u32[]{:S(2)}) copy-start(bf16[2,2,16,512]{3,2,1,0:T(8,128)(2,1)} %bc_ref.2) | copy-start | bytes 196612
  5.3 2.6 %collective-permute-start = (f32[2,16,2048]{2,1,0:T(8,128)S(1)}, f32[2,16,2048]{2,1,0:T(8,128)S(1)}, u32[]{:S(2)}, u32[]{:S(2)}) collective-permute-start(f32[2,16,2048]{2,1,0:T(8,128)S(1)} %slice_select_fusion.1), channel_id=1, source_target_pairs={{0,4},{4,0},{8,12},{12,8},{16,20},{20,16},{24,28},{28,24},{1,5},{5... | collective-permute-start | bytes 786440 | tf_op jit(solution)/shard_map/ppermute | solution.py:483
  5.8 2.1 %collective-permute-start.1 = (f32[2,1,2048]{2,1,0:T(1,128)S(1)}, f32[2,1,2048]{2,1,0:T(1,128)S(1)}, u32[]{:S(2)}, u32[]{:S(2)}) collective-permute-start(f32[2,1,2048]{2,1,0:T(1,128)S(1)} %broadcast_select_fusion.8), channel_id=1, source_target_pairs={{0,4},{4,0},{8,12},{12,8},{16,20},{20,16},{24,28},{28,24},{1,5},{5... | collective-permute-start | bytes 49160 | tf_op jit(solution)/shard_map/ppermute | solution.py:483
  8.1 10.2 %collective-permute-start.2 = (f32[2,16,2048]{2,1,0:T(8,128)S(1)}, f32[2,16,2048]{2,1,0:T(8,128)S(1)}, u32[]{:S(2)}, u32[]{:S(2)}) collective-permute-start(f32[2,16,2048]{2,1,0:T(8,128)S(1)} %select_add_fusion.2), channel_id=1, source_target_pairs={{0,8},{4,12},{8,0},{12,4},{16,24},{20,28},{24,16},{28,20},{1,9},{5... | collective-permute-start | bytes 786440 | tf_op jit(solution)/shard_map/ppermute | solution.py:483
  11.0 7.2 %collective-permute-start.4 = (f32[1,2048]{1,0:T(1,128)S(1)}, f32[1,2048]{1,0:T(1,128)S(1)}, u32[]{:S(2)}, u32[]{:S(2)}) collective-permute-start(f32[1,2048]{1,0:T(1,128)S(1)} %get-tuple-element.78), channel_id=1, source_target_pairs={{0,1},{1,0},{2,3},{3,2},{4,5},{5,4},{6,7},{7,6},{8,9},{9,8},{10,11... | collective-permute-start | bytes 24584 | tf_op jit(solution)/shard_map/ppermute | solution.py:578
  12.6 5.6 %collective-permute-start.3 = (f32[2,1,2048]{2,1,0:T(1,128)S(1)}, f32[2,1,2048]{2,1,0:T(1,128)S(1)}, u32[]{:S(2)}, u32[]{:S(2)}) collective-permute-start(f32[2,1,2048]{2,1,0:T(1,128)S(1)} %get-tuple-element.77), channel_id=1, source_target_pairs={{0,8},{4,12},{8,0},{12,4},{16,24},{20,28},{24,16},{28,20},{1,9},{5... | collective-permute-start | bytes 49160 | tf_op jit(solution)/shard_map/ppermute | solution.py:483
  18.3 8.2 %collective-permute-start.5 = (f32[2,16,2048]{2,1,0:T(8,128)S(1)}, f32[2,16,2048]{2,1,0:T(8,128)S(1)}, u32[]{:S(2)}, u32[]{:S(2)}) collective-permute-start(f32[2,16,2048]{2,1,0:T(8,128)S(1)} %select_add_fusion.1), channel_id=1, source_target_pairs={{0,16},{4,20},{8,24},{12,28},{16,0},{20,4},{24,8},{28,12},{1,17},{... | collective-permute-start | bytes 786440 | tf_op jit(solution)/shard_map/ppermute | solution.py:483
  20.0 5.7 %copy-start = (f32[2,64,256]{2,1,0:T(8,128)S(1)}, f32[2,64,256]{2,1,0:T(8,128)}, u32[]{:S(2)}) copy-start(f32[2,64,256]{2,1,0:T(8,128)} %ld_ref.1) | copy-start | bytes 393220
  20.0 5.7 %copy-start.1 = (bf16[2,2,16,256]{3,2,1,0:T(8,128)(2,1)S(1)}, bf16[2,2,16,256]{3,2,1,0:T(8,128)(2,1)}, u32[]{:S(2)}) copy-start(bf16[2,2,16,256]{3,2,1,0:T(8,128)(2,1)} %bc_ref.3) | copy-start | bytes 98308
  20.0 6.5 %collective-permute-start.6 = (f32[2,1,2048]{2,1,0:T(1,128)S(1)}, f32[2,1,2048]{2,1,0:T(1,128)S(1)}, u32[]{:S(2)}, u32[]{:S(2)}) collective-permute-start(f32[2,1,2048]{2,1,0:T(1,128)S(1)} %get-tuple-element.91), channel_id=1, source_target_pairs={{0,16},{4,20},{8,24},{12,28},{16,0},{20,4},{24,8},{28,12},{1,17},{... | collective-permute-start | bytes 49160 | tf_op jit(solution)/shard_map/ppermute | solution.py:483
  26.7 8.9 %collective-permute-start.7 = (f32[2,16,2048]{2,1,0:T(8,128)S(1)}, f32[2,16,2048]{2,1,0:T(8,128)S(1)}, u32[]{:S(2)}, u32[]{:S(2)}) collective-permute-start(f32[2,16,2048]{2,1,0:T(8,128)S(1)} %get-tuple-element.99), channel_id=1, source_target_pairs={{0,2},{4,6},{9,11},{13,15},{18,16},{22,20},{27,25},{31,29}} | collective-permute-start | bytes 786440 | tf_op jit(solution)/shard_map/ppermute | solution.py:502
  31.5 4.2 %collective-permute-start.8 = (f32[2,16,2048]{2,1,0:T(8,128)S(1)}, f32[2,16,2048]{2,1,0:T(8,128)S(1)}, u32[]{:S(2)}, u32[]{:S(2)}) collective-permute-start(f32[2,16,2048]{2,1,0:T(8,128)S(1)} %get-tuple-element.118), channel_id=1, source_target_pairs={{0,4},{4,0},{8,12},{12,8},{16,20},{20,16},{24,28},{28,24},{1,5},{5... | collective-permute-start | bytes 786440 | tf_op jit(solution)/shard_map/ppermute | solution.py:483
  35.7 5.0 %copy-start.2 = (s32[2]{0:T(128)S(1)}, s32[2]{0:T(128)}, u32[]{:S(2)}) copy-start(s32[2]{0:T(128)} %len_ref.1) | copy-start | bytes 28
  35.7 4.9 %collective-permute-start.9 = (f32[16,2048]{1,0:T(8,128)S(1)}, f32[16,2048]{1,0:T(8,128)S(1)}, u32[]{:S(2)}, u32[]{:S(2)}) collective-permute-start(f32[16,2048]{1,0:T(8,128)S(1)} %fusion.2), channel_id=1, source_target_pairs={{0,1},{2,3},{4,5},{6,7},{9,8},{11,10},{13,12},{15,14},{18,19},{16,... | collective-permute-start | bytes 393224 | tf_op jit(solution)/shard_map/ppermute | solution.py:502

commit v13 on v12

--- a/solution.py
+++ b/solution.py
@@ -86,10 +86,6 @@
     logs = jnp.concatenate([ld_ref[i] for i in range(count)], axis=0)
     after = jnp.where(iota((positions, 1), 0) > iota((1, positions), 1), 1.0, 0.0)
     to_end = jnp.exp(exact_dot(logs, after)) * gain_of(logs)
-    for i in range(count):
-        b_rows = b_ref[i].astype(F32)
-        push = b_rows[None, :, :] * to_end[i * heads:(i + 1) * heads][:, None, :]
-        push_ref[i] = push.reshape(heads * state, positions).astype(BF16)
     group = 256 // width
     lane_head = quotient(iota((1, 256), 1), width)
     high = logs.astype(BF16)
@@ -106,6 +102,9 @@
         for i in range(count):
             log_ref[i, :, pl.ds(j * lanes, lanes)] = wide[8 * i:8 * i + 8]
     for i in range(count):
+        b_rows = b_ref[i].astype(F32)
+        push = b_rows[None, :, :] * to_end[i * heads:(i + 1) * heads][:, None, :]
+        push_ref[i] = push.reshape(heads * state, positions).astype(BF16)
         for j in range(tiles):
             copies[i, j].wait()
             for g in range(lanes // 256):
@@ -129,7 +128,7 @@
     return pl.pallas_call(
         functools.partial(ends_kernel, width=width, lanes=lanes),
         in_specs=[pl.BlockSpec(memory_space=pltpu.HBM)] * 3,
-        out_specs=[whole, whole, whole],
+        out_specs=[whole] * 3,
         out_shape=[
             jax.ShapeDtypeStruct((count, state, channels), F32),
             jax.ShapeDtypeStruct((count, 8, channels), F32),
@@ -204,14 +203,19 @@
         w_ref[k // 2, k % 2] = w
 
 
-def branch_prepare_kernel(prompt_ref, ld_ref, bc_ref, hot_ref, w_ref, lv_ref, lc_ref, reach_ref, row_ref, *, width):
+def branch_prepare_kernel(prompt_ref, ld_ref, bc_ref, hot_ref, w_ref, lv_ref, lc_ref, row_ref, *, width):
     row_ref[...] = jnp.full(row_ref.shape, prompt_ref[0], jnp.int32).astype(F32)
+    heads, state = ld_ref.shape[1], bc_ref.shape[2]
+    _, logs, parts = blocks_of(ld_ref, bc_ref)
+    for k, w in enumerate(prepare(parts, logs, lv_ref, lc_ref, state, heads)):
+        w_ref[k] = w
+    prepare_hot(hot_ref, heads, width)
+
+
+def branch_reach_kernel(ld_ref, bc_ref, reach_ref):
     heads, state = ld_ref.shape[1], bc_ref.shape[2]
     blocks = ld_ref.shape[2] // BLOCK
     cuts, logs, parts = blocks_of(ld_ref, bc_ref)
-    for k, w in enumerate(prepare(parts, logs, lv_ref, lc_ref, state, heads)):
-        w_ref[k] = w
-    prepare_hot(hot_ref, heads, width)
     upto = jnp.where(iota((BLOCK, 1), 0) <= iota((1, BLOCK), 1), 1.0, 0.0)
     runs = exact_dot(logs, upto)
     for k, (i, cut) in enumerate(cuts):
@@ -247,19 +251,23 @@
 
 def prepare_branches(prompt, logdec, bc, channels):
     count, heads, positions = logdec.shape
-    state = bc.shape[2]
-    cuts, rows = count * (positions // BLOCK), BLOCK // CHUNK * state
+    cuts, rows = count * (positions // BLOCK), BLOCK // CHUNK * bc.shape[2]
     shapes = [
         ((2 * heads, channels), BF16),
         ((cuts, 2 * BLOCK + 16, 2 * heads), BF16),
         ((cuts, rows + BLOCK, BLOCK), BF16),
         ((cuts, BLOCK, rows), BF16),
-        ((count, positions, heads * state), BF16),
         ((1, channels), F32),
     ]
     kernel = functools.partial(branch_prepare_kernel, width=channels // heads)
     out = prepare_call(kernel, shapes, "branch_prepare", prompt, logdec, bc)
-    return out[:4], out[4], out[5]
+    return out[:4], out[4]
+
+
+def branch_reach(logdec, bc):
+    count, heads, positions = logdec.shape
+    shapes = [((count, positions, heads * bc.shape[2]), BF16)]
+    return prepare_call(branch_reach_kernel, shapes, "branch_reach", logdec, bc)[0]
 
 
 def run_tiles(jobs):
@@ -546,7 +554,7 @@
     low, high = (end[:, :, :half], log[:, :1, :half]), (end[:, :, half:], log[:, :1, half:])
     keep = [jnp.where(odd, h, l) for l, h in zip(low, high)]
     send = [jnp.where(odd, l, h) for l, h in zip(low, high)]
-    got, (ready, reach, row) = beside(
+    got, (ready, row) = beside(
         lambda v: swap_bit(v, 1, size),
         send,
         lambda logdec: prepare_branches(branch_prompt, logdec, branch_bc, branch_x.shape[2]),
@@ -563,9 +571,13 @@
         return out
 
     def part(which):
-        def work(x, logdec):
+        def work(x, prompt_logdec, branch_logdec):
             own = branch_own(x, ready, which)
-            return own, prepare_prompts(logdec, prompt_bc) if which == branches - 1 else None
+            return (
+                own,
+                branch_reach(branch_logdec, branch_bc) if which == 0 else None,
+                prepare_prompts(prompt_logdec, prompt_bc) if which == branches - 1 else None,
+            )
 
         return work
 
@@ -578,10 +590,11 @@
                 return swap(values[:2]), lax.ppermute(values[2], "pair", [(z, z ^ 1) for z in range(pair_size)])
 
             (other, next_row), out = beside(
-                with_row, (total, total_log, row), part(0), branch_x, prompt_logdec)
+                with_row, (total, total_log, row), part(0), branch_x, prompt_logdec, branch_logdec)
             done.append(out)
         elif len(done) < branches:
-            other, out = beside(swap, (total, total_log), part(len(done)), branch_x, prompt_logdec)
+            other, out = beside(
+                swap, (total, total_log), part(len(done)), branch_x, prompt_logdec, branch_logdec)
             done.append(out)
         else:
             other = swap((total, total_log))
@@ -591,9 +604,9 @@
         total, total_log = join(*in_order(upper, (total, total_log), other))
         bit *= 2
     while len(done) < branches:
-        done.append(part(len(done))(branch_x, prompt_logdec))
+        done.append(part(len(done))(branch_x, prompt_logdec, branch_logdec))
     own = [out[0] for out in done]
-    prompt_ready = (ready[0], *done[-1][1])
+    reach, prompt_ready = done[0][1], (ready[0], *done[-1][2])
 
     next_before = jnp.exp(first[1]) * before + first[0]
     keep = jnp.where(odd, next_before, before)

time: 44.1 us -> 44.4 us (level)
    pallas_call x2 -> x3, Pallas kernels: 2.18 us -> 2.41 us  [prepare_call(): pl.pallas_call(kernel, in_specs=scalars + [whole] * 2, out_specs=[whole]...]
where the time goes in v13:
time: 44.4 us; the launch traced here: 44.2 us
  Pallas kernels  27.2 us (61%)
  starting transfers between devices  13.9 us (31%)
  between operations  1.79 us (4%)
  waiting for transfers between devices  0.66 us (1%)
  other arithmetic  0.59 us (1%)
    pallas_call x2, Pallas kernels, branch_own(): pl.pallas_call(functools.partial(branch_kernel, which=which), in_specs=[p...  10.1 us
    pallas_call x2, Pallas kernels, prompt_half(): pl.pallas_call(functools.partial(prompt_kernel, skip=len(into)), in_specs...  7.21 us
    ppermute x7, starting transfers between devices, swap_bit(): return jax.tree.map(lambda value: lax.ppermute(value, 'ctx', links), values)  6.34 us
    ppermute x2, starting transfers between devices, spread_step(): return lax.ppermute(value, ('ctx', 'pair'), links)  5.99 us
    pallas_call x1, Pallas kernels, local_ends(): pl.pallas_call(functools.partial(ends_kernel, width=width, lanes=lanes),...  4.59 us
    pallas_call x1, Pallas kernels, finish(): pl.pallas_call(functools.partial(finish_kernel, width=width), in_specs=[p...  2.89 us
    pallas_call x3, Pallas kernels, prepare_call(): pl.pallas_call(kernel, in_specs=scalars + [whole] * 2, out_specs=[whole]...  2.41 us
    ppermute x1, starting transfers between devices, with_row(): lax.ppermute(values[2], 'pair', [(z, z ^ 1) for z in range(pair_size)])  1.58 us
  transfers between devices with their start and end apart: 10, of which 1 were waited for; matrix products, arithmetic and copies ran while one was open for 0% of the time, Pallas kernels for 45%

profile of v13, /device:TPU:0, one launch (start us, length us, event | category | flops | bytes accessed | tf_op | source)
XLA Modules:
  0.0 44.2 jit_solution(6832346022100245231)
XLA Ops:
  0.6 0.0 copy-start
  0.6 0.0 copy-start.2
  0.7 4.6 %local_ends.1 = (f32[2,16,4096]{2,1,0:T(8,128)S(1)}, f32[2,8,4096]{2,1,0:T(8,128)S(1)}, bf16[2,256,4096]{2,1,0:T(8,128)(2,1)S(1)}) custom-call(bf16[2,256,4096]{2,1,0:T(8,128)(2,1)} %x_ref.1, f32[2,64,256]{2,1,0:T(8,128)} %ld_ref.2, bf16[2,2,16,256]{3,2,1,0:T(8,128)(2,1)} %bc_ref.5), custom_call_target="tpu_custom_call" | custom-call | flops 268435456 | bytes 4194304 | tf_op jit(solution)/shard_map/local_ends/pallas_call | solution.py:128
  5.3 0.5 %collective-permute-start = (f32[2,16,2048]{2,1,0:T(8,128)S(1)}, f32[2,16,2048]{2,1,0:T(8,128)S(1)}, u32[]{:S(2)}, u32[]{:S(2)}) collective-permute-start(f32[2,16,2048]{2,1,0:T(8,128)S(1)} %slice_select_fusion.1), channel_id=1, source_target_pairs={{0,4},{4,0},{8,12},{12,8},{16,20},{20,16},{24,28},{28,24},{1,5},{5... | collective-permute-start | bytes 786440 | tf_op jit(solution)/shard_map/ppermute | solution.py:491
  5.8 0.1 collective-permute-start.1
  6.6 0.0 copy-done
  6.6 0.0 copy-done.2
  6.6 0.9 %branch_prepare.1 = (bf16[64,2048]{1,0:T(8,128)(2,1)S(1)}, bf16[4,528,64]{2,1,0:T(8,128)(2,1)S(1)}, bf16[4,384,256]{2,1,0:T(8,128)(2,1)S(1)}, bf16[4,256,128]{2,1,0:T(8,128)(2,1)S(1)}, f32[1,2048]{1,0:T(1,128)S(1)}) custom-call(s32[1]{0:T(128)S(6)} %copy.25.prompt_ref, f32[2,32,512]{2,1,0:T(8,128)S(1)} %copy-done, bf16[2,2,16,512]{3,2,1,0:T(8,128)(2,1)S(1)} %copy-done.2), custom_call_target="tpu_custom_call" | custom-call | flops 100000000 | bytes 1000000 | tf_op jit(solution)/shard_map/branch_prepare/pallas_call | solution.py:233
  7.5 0.0 collective-permute-done.1
  7.5 0.0 collective-permute-done
  7.6 0.1 select_add_fusion.2
  7.7 3.0 %collective-permute-start.2 = (f32[2,16,2048]{2,1,0:T(8,128)S(1)}, f32[2,16,2048]{2,1,0:T(8,128)S(1)}, u32[]{:S(2)}, u32[]{:S(2)}) collective-permute-start(f32[2,16,2048]{2,1,0:T(8,128)S(1)} %select_add_fusion.2), channel_id=1, source_target_pairs={{0,8},{4,12},{8,0},{12,4},{16,24},{20,28},{24,16},{28,20},{1,9},{5... | collective-permute-start | bytes 786440 | tf_op jit(solution)/shard_map/ppermute | solution.py:491
  10.7 1.6 %collective-permute-start.4 = (f32[1,2048]{1,0:T(1,128)S(1)}, f32[1,2048]{1,0:T(1,128)S(1)}, u32[]{:S(2)}, u32[]{:S(2)}) collective-permute-start(f32[1,2048]{1,0:T(1,128)S(1)} %get-tuple-element.77), channel_id=1, source_target_pairs={{0,1},{1,0},{2,3},{3,2},{4,5},{5,4},{6,7},{7,6},{8,9},{9,8},{10,11... | collective-permute-start | bytes 24584 | tf_op jit(solution)/shard_map/ppermute | solution.py:590
  12.2 0.5 %collective-permute-start.3 = (f32[2,1,2048]{2,1,0:T(1,128)S(1)}, f32[2,1,2048]{2,1,0:T(1,128)S(1)}, u32[]{:S(2)}, u32[]{:S(2)}) collective-permute-start(f32[2,1,2048]{2,1,0:T(1,128)S(1)} %get-tuple-element.76), channel_id=1, source_target_pairs={{0,8},{4,12},{8,0},{12,4},{16,24},{20,28},{24,16},{28,20},{1,9},{5... | collective-permute-start | bytes 49160 | tf_op jit(solution)/shard_map/ppermute | solution.py:491
  12.8 5.0 %branch_own.2.refs_0_ = f32[512,2048]{1,0:T(8,128)S(1)} custom-call(bf16[2,512,2048]{2,1,0:T(8,128)(2,1)} %x_in.1, bf16[64,2048]{1,0:T(8,128)(2,1)S(1)} %get-tuple-element.79.refs_0_.refs_2_, bf16[4,528,64]{2,1,0:T(8,128)(2,1)S(1)} %get-tuple-element.80.refs_1_, bf16[4,384,256]{2,1,0:T(8,128)(2,1)S(1)} %get-tuple-element.81.refs_2_, ...), custom_call_target="tpu_custom_call" | custom-call | flops 2415919104 | bytes 4194304 | tf_op jit(solution)/shard_map/branch_own/pallas_call | solution.py:374
  17.8 0.6 %branch_reach.1.reach_ref = bf16[2,512,512]{2,1,0:T(8,128)(2,1)S(1)} custom-call(f32[2,32,512]{2,1,0:T(8,128)S(1)} %copy-done, bf16[2,2,16,512]{3,2,1,0:T(8,128)(2,1)S(1)} %copy-done.2), custom_call_target="tpu_custom_call" | custom-call | flops 100000000 | bytes 1000000 | tf_op jit(solution)/shard_map/branch_reach/pallas_call | solution.py:233
  18.5 0.0 collective-permute-done.4
  18.5 0.0 collective-permute-done.3
  18.5 0.0 collective-permute-done.2
  18.5 0.1 fusion.4
  18.6 1.6 %collective-permute-start.5 = (f32[2,16,2048]{2,1,0:T(8,128)S(1)}, f32[2,16,2048]{2,1,0:T(8,128)S(1)}, u32[]{:S(2)}, u32[]{:S(2)}) collective-permute-start(f32[2,16,2048]{2,1,0:T(8,128)S(1)} %select_add_fusion.1), channel_id=1, source_target_pairs={{0,16},{4,20},{8,24},{12,28},{16,0},{20,4},{24,8},{28,12},{1,17},{... | collective-permute-start | bytes 786440 | tf_op jit(solution)/shard_map/ppermute | solution.py:491
  20.2 0.0 copy-start.1
  20.2 0.0 copy-start.3
  20.3 0.6 %collective-permute-start.6 = (f32[2,1,2048]{2,1,0:T(1,128)S(1)}, f32[2,1,2048]{2,1,0:T(1,128)S(1)}, u32[]{:S(2)}, u32[]{:S(2)}) collective-permute-start(f32[2,1,2048]{2,1,0:T(1,128)S(1)} %get-tuple-element.91), channel_id=1, source_target_pairs={{0,16},{4,20},{8,24},{12,28},{16,0},{20,4},{24,8},{28,12},{1,17},{... | collective-permute-start | bytes 49160 | tf_op jit(solution)/shard_map/ppermute | solution.py:491
  20.8 5.0 %branch_own.3.refs_1_ = f32[512,2048]{1,0:T(8,128)S(1)} custom-call(bf16[2,512,2048]{2,1,0:T(8,128)(2,1)} %x_in.1, bf16[64,2048]{1,0:T(8,128)(2,1)S(1)} %get-tuple-element.79.refs_0_.refs_2_, bf16[4,528,64]{2,1,0:T(8,128)(2,1)S(1)} %get-tuple-element.80.refs_1_, bf16[4,384,256]{2,1,0:T(8,128)(2,1)S(1)} %get-tuple-element.81.refs_2_, ...), custom_call_target="tpu_custom_call" | custom-call | flops 2415919104 | bytes 4194304 | tf_op jit(solution)/shard_map/branch_own/pallas_call | solution.py:374
  25.9 0.0 copy-done.1
  25.9 0.0 copy-done.3
  25.9 0.9 %prompt_prepare.1 = (bf16[2,2,528,64]{3,2,1,0:T(8,128)(2,1)S(1)}, bf16[2,384,256]{2,1,0:T(8,128)(2,1)S(1)}, bf16[2,256,128]{2,1,0:T(8,128)(2,1)S(1)}) custom-call(f32[2,64,256]{2,1,0:T(8,128)S(1)} %copy-done.1, bf16[2,2,16,256]{3,2,1,0:T(8,128)(2,1)S(1)} %copy-done.3), custom_call_target="tpu_custom_call" | custom-call | flops 100000000 | bytes 1000000 | tf_op jit(solution)/shard_map/prompt_prepare/pallas_call | solution.py:233
  26.8 0.0 collective-permute-done.6
  26.8 0.0 collective-permute-done.5
  26.9 0.1 fusion
  27.0 4.7 %collective-permute-start.7 = (f32[2,16,2048]{2,1,0:T(8,128)S(1)}, f32[2,16,2048]{2,1,0:T(8,128)S(1)}, u32[]{:S(2)}, u32[]{:S(2)}) collective-permute-start(f32[2,16,2048]{2,1,0:T(8,128)S(1)} %get-tuple-element.99), channel_id=1, source_target_pairs={{0,2},{4,6},{9,11},{13,15},{18,16},{22,20},{27,25},{31,29}} | collective-permute-start | bytes 786440 | tf_op jit(solution)/shard_map/ppermute | solution.py:510
  31.7 0.1 collective-permute-start.8
  31.8 3.6 %prompt_half.2.refs_7_ = bf16[2,256,4096]{2,1,0:T(8,128)(2,1)} custom-call(s32[1]{0:T(128)} %bitcast.refs_0_, bf16[2,256,4096]{2,1,0:T(8,128)(2,1)S(1)} %get-tuple-element.101.refs_1_, bf16[64,2048]{1,0:T(8,128)(2,1)S(1)} %get-tuple-element.79.refs_0_.refs_2_, bf16[2,2,528,64]{3,2,1,0:T(8,128)(2,1)S(1)} %get-tuple-element.102.refs_3_, ...), custom_call_target="tpu_custom_call" | custom-call | flops 2415919104 | bytes 4194304 | tf_op jit(solution)/shard_map/prompt_half/pallas_call | solution.py:428
  35.4 0.6 %collective-permute-done.7 = f32[2,16,2048]{2,1,0:T(8,128)S(1)} collective-permute-done((f32[2,16,2048]{2,1,0:T(8,128)S(1)}, f32[2,16,2048]{2,1,0:T(8,128)S(1)}, u32[]{:S(2)}, u32[]{:S(2)}) %collective-permute-start.7) | collective-permute-done | bytes 262176 | tf_op jit(solution)/shard_map/ppermute | solution.py:510
  36.1 0.0 copy-start.4
  36.1 0.0 collective-permute-done.8.refs_6_
  36.1 1.3 %collective-permute-start.9 = (f32[16,2048]{1,0:T(8,128)S(1)}, f32[16,2048]{1,0:T(8,128)S(1)}, u32[]{:S(2)}, u32[]{:S(2)}) collective-permute-start(f32[16,2048]{1,0:T(8,128)S(1)} %fusion.2), channel_id=1, source_target_pairs={{0,1},{2,3},{4,5},{6,7},{9,8},{11,10},{13,12},{15,14},{18,19},{16,... | collective-permute-start | bytes 393224 | tf_op jit(solution)/shard_map/ppermute | solution.py:510
  37.4 3.6 %prompt_half.3 = bf16[2,256,4096]{2,1,0:T(8,128)(2,1)} custom-call(s32[1]{0:T(128)} %bitcast.1.refs_0_, bf16[2,256,4096]{2,1,0:T(8,128)(2,1)S(1)} %get-tuple-element.101.refs_1_, bf16[64,2048]{1,0:T(8,128)(2,1)S(1)} %get-tuple-element.79.refs_0_.refs_2_, bf16[2,2,528,64]{3,2,1,0:T(8,128)(2,1)S(1)} %get-tuple-element.102.refs_3_, ...), custom_call_target="tpu_custom_call", output_to_operand_aliasing={{}: (7, {})} | custom-call | flops 2415919104 | bytes 4194304 | tf_op jit(solution)/shard_map/prompt_half/pallas_call | solution.py:428
  41.1 0.0 collective-permute-done.9
  41.1 0.0 copy-done.4
  41.1 2.9 %branch_finish.1 = bf16[2,512,2048]{2,1,0:T(8,128)(2,1)} custom-call(s32[2]{0:T(128)S(1)} %copy-done.4, bf16[2,512,512]{2,1,0:T(8,128)(2,1)S(1)} %branch_reach.1.reach_ref, f32[16,2048]{1,0:T(8,128)S(1)} %select_select_fusion.start_ref, f32[512,2048]{1,0:T(8,128)S(1)} %branch_own.2.refs_0_, f32[512,2048]{1,0:T(8,128)S(1)} %branch_own.3.refs_1_), custom_call_target="tpu_custom_call" | custom-call | flops 268435456 | bytes 8388608 | tf_op jit(solution)/shard_map/branch_finish/pallas_call | solution.py:473
  (14 shorter events, 0.4 us)
Async XLA Ops:
  0.6 6.0 %copy-start = (f32[2,32,512]{2,1,0:T(8,128)S(1)}, f32[2,32,512]{2,1,0:T(8,128)}, u32[]{:S(2)}) copy-start(f32[2,32,512]{2,1,0:T(8,128)} %ld_ref.1) | copy-start | bytes 393220
  0.6 6.0 %copy-start.2 = (bf16[2,2,16,512]{3,2,1,0:T(8,128)(2,1)S(1)}, bf16[2,2,16,512]{3,2,1,0:T(8,128)(2,1)}, u32[]{:S(2)}) copy-start(bf16[2,2,16,512]{3,2,1,0:T(8,128)(2,1)} %bc_ref.4) | copy-start | bytes 196612
  5.3 2.2 %collective-permute-start = (f32[2,16,2048]{2,1,0:T(8,128)S(1)}, f32[2,16,2048]{2,1,0:T(8,128)S(1)}, u32[]{:S(2)}, u32[]{:S(2)}) collective-permute-start(f32[2,16,2048]{2,1,0:T(8,128)S(1)} %slice_select_fusion.1), channel_id=1, source_target_pairs={{0,4},{4,0},{8,12},{12,8},{16,20},{20,16},{24,28},{28,24},{1,5},{5... | collective-permute-start | bytes 786440 | tf_op jit(solution)/shard_map/ppermute | solution.py:491
  5.8 1.7 %collective-permute-start.1 = (f32[2,1,2048]{2,1,0:T(1,128)S(1)}, f32[2,1,2048]{2,1,0:T(1,128)S(1)}, u32[]{:S(2)}, u32[]{:S(2)}) collective-permute-start(f32[2,1,2048]{2,1,0:T(1,128)S(1)} %broadcast_select_fusion.8), channel_id=1, source_target_pairs={{0,4},{4,0},{8,12},{12,8},{16,20},{20,16},{24,28},{28,24},{1,5},{5... | collective-permute-start | bytes 49160 | tf_op jit(solution)/shard_map/ppermute | solution.py:491
  7.7 10.8 %collective-permute-start.2 = (f32[2,16,2048]{2,1,0:T(8,128)S(1)}, f32[2,16,2048]{2,1,0:T(8,128)S(1)}, u32[]{:S(2)}, u32[]{:S(2)}) collective-permute-start(f32[2,16,2048]{2,1,0:T(8,128)S(1)} %select_add_fusion.2), channel_id=1, source_target_pairs={{0,8},{4,12},{8,0},{12,4},{16,24},{20,28},{24,16},{28,20},{1,9},{5... | collective-permute-start | bytes 786440 | tf_op jit(solution)/shard_map/ppermute | solution.py:491
  10.7 7.8 %collective-permute-start.4 = (f32[1,2048]{1,0:T(1,128)S(1)}, f32[1,2048]{1,0:T(1,128)S(1)}, u32[]{:S(2)}, u32[]{:S(2)}) collective-permute-start(f32[1,2048]{1,0:T(1,128)S(1)} %get-tuple-element.77), channel_id=1, source_target_pairs={{0,1},{1,0},{2,3},{3,2},{4,5},{5,4},{6,7},{7,6},{8,9},{9,8},{10,11... | collective-permute-start | bytes 24584 | tf_op jit(solution)/shard_map/ppermute | solution.py:590
  12.2 6.2 %collective-permute-start.3 = (f32[2,1,2048]{2,1,0:T(1,128)S(1)}, f32[2,1,2048]{2,1,0:T(1,128)S(1)}, u32[]{:S(2)}, u32[]{:S(2)}) collective-permute-start(f32[2,1,2048]{2,1,0:T(1,128)S(1)} %get-tuple-element.76), channel_id=1, source_target_pairs={{0,8},{4,12},{8,0},{12,4},{16,24},{20,28},{24,16},{28,20},{1,9},{5... | collective-permute-start | bytes 49160 | tf_op jit(solution)/shard_map/ppermute | solution.py:491
  18.6 8.2 %collective-permute-start.5 = (f32[2,16,2048]{2,1,0:T(8,128)S(1)}, f32[2,16,2048]{2,1,0:T(8,128)S(1)}, u32[]{:S(2)}, u32[]{:S(2)}) collective-permute-start(f32[2,16,2048]{2,1,0:T(8,128)S(1)} %select_add_fusion.1), channel_id=1, source_target_pairs={{0,16},{4,20},{8,24},{12,28},{16,0},{20,4},{24,8},{28,12},{1,17},{... | collective-permute-start | bytes 786440 | tf_op jit(solution)/shard_map/ppermute | solution.py:491
  20.2 5.7 %copy-start.1 = (f32[2,64,256]{2,1,0:T(8,128)S(1)}, f32[2,64,256]{2,1,0:T(8,128)}, u32[]{:S(2)}) copy-start(f32[2,64,256]{2,1,0:T(8,128)} %ld_ref.2) | copy-start | bytes 393220
  20.2 5.7 %copy-start.3 = (bf16[2,2,16,256]{3,2,1,0:T(8,128)(2,1)S(1)}, bf16[2,2,16,256]{3,2,1,0:T(8,128)(2,1)}, u32[]{:S(2)}) copy-start(bf16[2,2,16,256]{3,2,1,0:T(8,128)(2,1)} %bc_ref.5) | copy-start | bytes 98308
  20.3 6.5 %collective-permute-start.6 = (f32[2,1,2048]{2,1,0:T(1,128)S(1)}, f32[2,1,2048]{2,1,0:T(1,128)S(1)}, u32[]{:S(2)}, u32[]{:S(2)}) collective-permute-start(f32[2,1,2048]{2,1,0:T(1,128)S(1)} %get-tuple-element.91), channel_id=1, source_target_pairs={{0,16},{4,20},{8,24},{12,28},{16,0},{20,4},{24,8},{28,12},{1,17},{... | collective-permute-start | bytes 49160 | tf_op jit(solution)/shard_map/ppermute | solution.py:491
  27.0 9.1 %collective-permute-start.7 = (f32[2,16,2048]{2,1,0:T(8,128)S(1)}, f32[2,16,2048]{2,1,0:T(8,128)S(1)}, u32[]{:S(2)}, u32[]{:S(2)}) collective-permute-start(f32[2,16,2048]{2,1,0:T(8,128)S(1)} %get-tuple-element.99), channel_id=1, source_target_pairs={{0,2},{4,6},{9,11},{13,15},{18,16},{22,20},{27,25},{31,29}} | collective-permute-start | bytes 786440 | tf_op jit(solution)/shard_map/ppermute | solution.py:510
  31.7 4.4 %collective-permute-start.8 = (f32[2,16,2048]{2,1,0:T(8,128)S(1)}, f32[2,16,2048]{2,1,0:T(8,128)S(1)}, u32[]{:S(2)}, u32[]{:S(2)}) collective-permute-start(f32[2,16,2048]{2,1,0:T(8,128)S(1)} %get-tuple-element.118), channel_id=1, source_target_pairs={{0,4},{4,0},{8,12},{12,8},{16,20},{20,16},{24,28},{28,24},{1,5},{5... | collective-permute-start | bytes 786440 | tf_op jit(solution)/shard_map/ppermute | solution.py:491
  36.1 5.0 %copy-start.4 = (s32[2]{0:T(128)S(1)}, s32[2]{0:T(128)}, u32[]{:S(2)}) copy-start(s32[2]{0:T(128)} %len_ref.1) | copy-start | bytes 28
  36.1 4.9 %collective-permute-start.9 = (f32[16,2048]{1,0:T(8,128)S(1)}, f32[16,2048]{1,0:T(8,128)S(1)}, u32[]{:S(2)}, u32[]{:S(2)}) collective-permute-start(f32[16,2048]{1,0:T(8,128)S(1)} %fusion.2), channel_id=1, source_target_pairs={{0,1},{2,3},{4,5},{6,7},{9,8},{11,10},{13,12},{15,14},{18,19},{16,... | collective-permute-start | bytes 393224 | tf_op jit(solution)/shard_map/ppermute | solution.py:510
